TPU v7x, 512 devices: a whole 4x4x16 slice. The times are simulated.
512 devices in a mesh: row: 32 (over z, x_hi), col: 16 (over x_lo, y, core).
Axes of the slice: x: 4 (x_hi: 2, x_lo: 2; x = x_hi * 2 + x_lo), y: 4, z: 16, core: 2. Of those that a mesh axis runs over, the one named last changes fastest.
Arguments:
- tokens: bfloat16 [8192, 8192], P('row', 'col'), may hold values from -560 to 560
- norm_gain: bfloat16 [8192], P('col'), may hold values from 0.25 to 1.75
- w_query: bfloat16 [8192, 4096], P('row', 'col'), may hold values from -21 to 21
- w_key: bfloat16 [8192, 512], P('row'), may hold values from -1 to 1
- w_value: bfloat16 [8192, 512], P('row'), may hold values from -0.0625 to 0.0625
Outputs:
- attended: bfloat16 [8192, 4096], P('row', 'col')
All inputs are finite; a program needn't handle non-finite values.
Results may differ from a plain program's by a relative error of at most 0.008.
Values may be sent and summed in bfloat16 or wider, within the bound.
No kernel may reach another device: no remote copies, remote signals or barrier semaphores. Data moves between devices by JAX's collectives and lax.ppermute only.
A program may use at most 64 MiB of HBM per device.

v0:
```python
import math

import jax
import jax.numpy as jnp
from jax import lax
from jax.sharding import PartitionSpec as P

HEAD = 128
GROUP = 8


def on_device(tokens, norm_gain, w_query, w_key, w_value):
    tok_rows = tokens.shape[0]
    whole_rows, whole_gain = (
        lax.all_gather(tokens, "col", axis=1, tiled=True),
        lax.all_gather(norm_gain, "col", axis=0, tiled=True),
    )
    states = whole_rows.astype(jnp.float32)
    mean_sq = jnp.mean(states * states, axis=1, keepdims=True)
    normed = (states * lax.rsqrt(mean_sq + 1e-05) * whole_gain.astype(jnp.float32)[None, :]).astype(
        jnp.bfloat16
    )
    q_width = w_query.shape[1]
    heads_here = q_width // HEAD
    kv_index = lax.axis_index("col") * heads_here // GROUP
    key_cols = lax.dynamic_slice_in_dim(w_key, kv_index * HEAD, HEAD, 1)
    value_cols = lax.dynamic_slice_in_dim(w_value, kv_index * HEAD, HEAD, 1)
    pieces = (
        lax.all_gather(w_query, "row", axis=0, tiled=True),
        lax.all_gather(key_cols, "row", axis=0, tiled=True),
        lax.all_gather(value_cols, "row", axis=0, tiled=True),
    )
    q_sum, k_sum, v_sum = tuple(
        (jnp.dot(normed, piece, preferred_element_type=jnp.float32) for piece in pieces)
    )
    queries = q_sum.astype(jnp.bfloat16)
    key_own = k_sum.astype(jnp.bfloat16)
    value_own = v_sum.astype(jnp.bfloat16)
    half_rows = tok_rows // 2
    row_here = lax.axis_index("row")
    local_steps = jnp.arange(half_rows, dtype=jnp.int32)
    query_parts = (queries[:half_rows], queries[half_rows:])
    position_parts = (
        row_here * tok_rows + local_steps,
        row_here * tok_rows + half_rows + local_steps,
    )
    query_heads = tuple((part.reshape(half_rows, heads_here, HEAD) for part in query_parts))
    factor = HEAD ** (-0.5)

    def update(carry, q_part, pos_part, key_block, value_block, block_start):
        run_max, run_total, accum = carry
        scores = (
            jnp.einsum("qhd,kd->hqk", q_part, key_block, preferred_element_type=jnp.float32)
            * factor
        )
        key_pos = block_start + jnp.arange(key_block.shape[0], dtype=jnp.int32)
        causal = (pos_part[:, None] >= key_pos[None, :])[None, :, :]
        masked = jnp.where(causal, scores, -1e30)
        new_max = jnp.maximum(run_max, jnp.max(masked, axis=2))
        weights = jnp.where(causal, jnp.exp(scores - new_max[:, :, None]), 0.0)
        rescale = jnp.exp(run_max - new_max)
        run_total = run_total * rescale + jnp.sum(weights, axis=2)
        mixed = jnp.einsum(
            "hqk,kd->hqd",
            weights.astype(jnp.bfloat16),
            value_block,
            preferred_element_type=jnp.float32,
        )
        accum = accum * rescale[:, :, None] + mixed
        return (new_max, run_total, accum)

    def guarded(carry, q_part, pos_part, key_block, value_block, block_start):
        return lax.cond(
            block_start <= pos_part[-1],
            lambda state: update(state, q_part, pos_part, key_block, value_block, block_start),
            lambda state: state,
            carry,
        )

    blank = (
        jnp.full((heads_here, half_rows), -1e30, jnp.float32),
        jnp.zeros((heads_here, half_rows), jnp.float32),
        jnp.zeros((heads_here, half_rows, HEAD), jnp.float32),
    )
    empty = (blank, blank)
    key_rows, value_rows = (
        lax.all_gather(key_own, "row", axis=0, tiled=True),
        lax.all_gather(value_own, "row", axis=0, tiled=True),
    )
    carry = empty
    key_count = key_rows.shape[0]
    block_size = math.gcd(key_count, 512)
    block_count = key_count // block_size
    key_blocks = key_rows.reshape(block_count, block_size, HEAD)
    value_blocks = value_rows.reshape(block_count, block_size, HEAD)
    starts = 0 + block_size * jnp.arange(block_count, dtype=jnp.int32)

    def step_block(state, packet):
        return (
            tuple(
                (
                    guarded(
                        state[index],
                        query_heads[index],
                        position_parts[index],
                        packet[0],
                        packet[1],
                        packet[2],
                    )
                    for index in range(2)
                )
            ),
            None,
        )

    carry, _ = lax.scan(step_block, carry, (key_blocks, value_blocks, starts))

    def finish(state):
        result = (state[2] / state[1][:, :, None]).astype(jnp.bfloat16)
        return jnp.transpose(result, (1, 0, 2)).reshape(half_rows, heads_here * HEAD)

    first_out = finish(carry[0])
    second_out = finish(carry[1])
    return jnp.concatenate([first_out, second_out], axis=0)


def solution(mesh):
    return jax.shard_map(
        on_device,
        mesh=mesh,
        in_specs=(P("row", "col"), P("col"), P("row", "col"), P("row", None), P("row", None)),
        out_specs=P("row", "col"),
        check_vma=False,
    )
```

profile of v0, /device:TPU:480, one launch (start us, length us, event | category | flops | bytes accessed | tf_op | source)
XLA Modules:
  0.0 956.6 jit_solution(929438333669941718)
XLA Ops:
  11.0 19.9 %all-gather = bf16[16,1,512]{2,1,0:T(2,128)(2,1)S(1)} all-gather(bf16[1,1,512]{2,1,0:T(2,128)(2,1)S(1)} %reshape.99), channel_id=1, replica_groups=mesh['row'=32,'col'=16] {'col'}, dimensions={0}, use_global_device_ids=true | all-gather | bytes 17408 | tf_op jit(solution)/shard_map/all_gather | solution.py:16
  31.0 22.6 %all-gather.8.cloned.1.call-done = bf16[256,8192]{1,0:T(8,128)(2,1)} async-done(((bf16[256,512]{1,0:T(8,128)(2,1)}), bf16[256,8192]{1,0:T(8,128)(2,1)}) %all-gather.8.cloned.1.call-update) | async-done | bytes 4194320 | tf_op jit(solution)/shard_map/all_gather | solution.py:15
  53.6 3.1 fusion.20
  56.7 148.2 %all-gather.10.cloned.1.call-done = bf16[8192,128]{1,0:T(8,128)(2,1)} async-done(((bf16[256,128]{1,0:T(8,128)(2,1)}), bf16[8192,128]{1,0:T(8,128)(2,1)}) %all-gather.10.cloned.1.call-update) | async-done | bytes 2097168 | tf_op jit(solution)/shard_map/all_gather | solution.py:30
  204.9 4.9 convolution_convert_fusion.2
  209.9 142.6 %all-gather.14.cloned.1.call-done = bf16[8192,128]{1,0:T(8,128)(2,1)} async-done(((bf16[256,128]{1,0:T(8,128)(2,1)}), bf16[8192,128]{1,0:T(8,128)(2,1)}) %all-gather.14.cloned.1.call-update) | async-done | bytes 2097168 | tf_op jit(solution)/shard_map/all_gather | solution.py:31
  352.5 4.9 convolution_convert_fusion.1
  357.5 156.8 %all-gather.18.cloned.1.call-done = bf16[8192,256]{1,0:T(8,128)(2,1)} async-done(((bf16[256,256]{1,0:T(8,128)(2,1)}), bf16[8192,256]{1,0:T(8,128)(2,1)}) %all-gather.18.cloned.1.call-update) | async-done | bytes 4194320 | tf_op jit(solution)/shard_map/all_gather | solution.py:29
  514.3 5.6 convolution_convert_fusion
  520.2 141.5 %all-gather.12.cloned.1.call-done = bf16[8192,128]{1,0:T(8,128)(2,1)} async-done(((bf16[256,128]{1,0:T(8,128)(2,1)}), bf16[8192,128]{1,0:T(8,128)(2,1)}) %all-gather.12.cloned.1.call-update) | async-done | bytes 2097168 | tf_op jit(solution)/shard_map/all_gather | solution.py:87
  661.7 147.5 %all-gather.16.cloned.1.call-done = bf16[8192,128]{1,0:T(8,128)(2,1)} async-done(((bf16[256,128]{1,0:T(8,128)(2,1)}), bf16[8192,128]{1,0:T(8,128)(2,1)}) %all-gather.16.cloned.1.call-update) | async-done | bytes 2097168 | tf_op jit(solution)/shard_map/all_gather | solution.py:88
  809.2 139.7 %while.20 = (s32[]{:T(128)}, f32[2,128]{1,0:T(2,128)S(1)}, f32[2,128]{1,0:T(2,128)S(1)}, f32[2,128,128]{2,1,0:T(8,128)S(1)}, f32[2,128]{1,0:T(2,128)S(1)}, /*ind...) while((s32[]{:T(128)}, f32[2,128]{1,0:T(2,128)S(1)}, ...), condition=%wide.region_10.11_spmd, body=%wide.region_1.10_spmd.sunk | while | flops 136841216 | bytes 5416393 | solution.py:116
  814.7 1.6 conditional.4
  825.0 1.6 conditional.5
  833.7 1.6 conditional.5
  842.5 1.6 conditional.5
  849.6 1.6 conditional.4
  858.3 1.6 conditional.4
  859.9 1.6 conditional.5
  867.1 1.6 conditional.4
  868.7 1.6 conditional.5
  875.8 1.6 conditional.4
  877.4 1.6 conditional.5
  886.1 1.6 conditional.5
  893.3 1.6 conditional.4
  903.6 1.6 conditional.5
  910.7 1.6 conditional.4
  919.5 1.6 conditional.4
  921.1 1.6 conditional.5
  928.2 1.6 conditional.4
  929.8 1.6 conditional.5
  936.9 1.6 conditional.4
  (367 shorter events, 120.5 us)
Async XLA Ops:
  6.5 1.0 copy-start
  6.5 47.0 %all-gather.8.cloned.1.call-start = ((), (), s32[]{:S(2)}) async-start(), calls=%async_computation | async-start | bytes 4456448 | tf_op jit(solution)/shard_map/all_gather | solution.py:15
  7.3 197.6 %all-gather.10.cloned.1.call-start = ((), (), s32[]{:S(2)}) async-start(), calls=%async_computation.1 | async-start | bytes 2162688 | tf_op jit(solution)/shard_map/all_gather | solution.py:30
  8.1 344.3 %all-gather.14.cloned.1.call-start = ((), (), s32[]{:S(2)}) async-start(), calls=%async_computation.3 | async-start | bytes 2162688 | tf_op jit(solution)/shard_map/all_gather | solution.py:31
  9.7 504.6 %all-gather.18.cloned.1.call-start = ((), (), s32[]{:S(2)}) async-start(), calls=%async_computation.5 | async-start | bytes 4325376 | tf_op jit(solution)/shard_map/all_gather | solution.py:29
  10.3 651.4 %all-gather.12.cloned.1.call-start = ((), (), s32[]{:S(2)}) async-start(), calls=%async_computation.2 | async-start | bytes 2162688 | tf_op jit(solution)/shard_map/all_gather | solution.py:87
  209.8 599.3 %all-gather.16.cloned.1.call-start = ((), (), s32[]{:S(2)}) async-start(), calls=%async_computation.4 | async-start | bytes 2162688 | tf_op jit(solution)/shard_map/all_gather | solution.py:88
Sparse Core Ops, SparseCore 0:
  9.5 44.0 all-gather.7
  56.7 148.1 all-gather.9
  208.0 144.4 all-gather.13
  355.4 158.8 all-gather.17
  517.3 144.3 all-gather.11
  664.6 144.4 all-gather.15
where the time goes:
time: 958 us; the launch traced here: 957 us
  waiting for transfers between devices  760 us (79%)
  local copies, waits for them, and re-layouts  49.3 us (5%)
  loops' own time  44.2 us (5%)
  matrix products  35.3 us (4%)
  other arithmetic  33.6 us (4%)
  blocking collectives  19.9 us (2%)
  between operations  13.6 us (1%)
    all_gather x1, waiting for transfers between devices, on_device(): lax.all_gather(w_query, 'row', axis=0, tiled=True)  157 us
    all_gather x1, waiting for transfers between devices, on_device(): lax.all_gather(key_cols, 'row', axis=0, tiled=True)  148 us
    all_gather x1, waiting for transfers between devices, on_device(): lax.all_gather(value_own, 'row', axis=0, tiled=True)  147 us
    all_gather x1, waiting for transfers between devices, on_device(): lax.all_gather(value_cols, 'row', axis=0, tiled=True)  143 us
    all_gather x1, waiting for transfers between devices, on_device(): lax.all_gather(key_own, 'row', axis=0, tiled=True)  141 us
    another operation x1, loops' own time, on_device(): carry, _ = lax.scan(step_block, carry, (key_blocks, value_blocks, starts))  42.3 us
    all_gather x1, waiting for transfers between devices, on_device(): lax.all_gather(tokens, 'col', axis=1, tiled=True)  22.6 us
    add x32, other arithmetic, update(): key_pos = block_start + jnp.arange(key_block.shape[0], dtype=jnp.int32)  20.8 us
  transfers between devices with their start and end apart: 6, of which 6 were waited for; matrix products, arithmetic and copies ran while one was open for 2% of the time, Pallas kernels for 0%

commit v1 on v0

v1 whole, which is shorter than its diff:
```python
import functools
import math

import jax
import jax.numpy as jnp
from jax import lax
from jax.experimental import pallas as pl
from jax.experimental.pallas import tpu as pltpu
from jax.sharding import Mesh
from jax.sharding import PartitionSpec as P

HEAD = 128
GROUP = 8
EPS = 1e-05
ROW = ("zh", "zl", "xh")
COL = ("xl", "yh", "yl", "core")
F32 = jnp.float32
BF16 = jnp.bfloat16


def gather(x, axes, n):
    return lax.all_to_all(jnp.broadcast_to(x[None], (n, *x.shape)), axes, 0, 0)


def swap(x):
    return lax.ppermute(x, "core", [(0, 1), (1, 0)])


def attend_kernel(place, q_ref, mine_ref, other_ref, out_ref, q_all, m_ref, l_ref, acc_ref):
    z, xh, core = place[0], place[1], place[2]
    rows = q_ref.shape[0]
    scale = HEAD**-0.5 * math.log2(math.e)
    q_all[:rows] = q_ref[:, :HEAD]
    q_all[rows:] = q_ref[:, HEAD:]
    m_ref[...] = jnp.full(m_ref.shape, -1e30, F32)
    l_ref[...] = jnp.zeros(l_ref.shape, F32)
    acc_ref[...] = jnp.zeros(acc_ref.shape, F32)
    chunk = mine_ref.shape[3]
    half = 4 * chunk

    def block(zi, masked):
        zl, zh = lax.rem(zi, 4), lax.div(zi, 4)
        kv = jnp.concatenate(
            [mine_ref[:, zl, zh].reshape(half, 2 * HEAD), other_ref[:, zl, zh].reshape(half, 2 * HEAD)], axis=0
        )
        s = lax.dot_general(q_all[...], kv[:, :HEAD], (((1,), (1,)), ((), ())), preferred_element_type=F32)
        if masked:
            slot = lax.broadcasted_iota(jnp.int32, s.shape, 1)
            within = lax.rem(slot, half)
            owner = jnp.where(slot < half, core, 1 - core)
            key_pos = (lax.div(within, chunk) * 2 + owner) * chunk + lax.rem(within, chunk)
            query_pos = xh * rows + lax.rem(lax.broadcasted_iota(jnp.int32, s.shape, 0), rows)
            s = jnp.where(key_pos <= query_pos, s, -1e30)
        m_old = m_ref[...]
        m_new = jnp.maximum(m_old, jnp.max(s, axis=1, keepdims=True))
        alpha = jnp.exp2((m_old - m_new) * scale)
        total = l_ref[...] * alpha
        weights = []
        for j in range(0, s.shape[1], HEAD):
            w = jnp.exp2((s[:, j : j + HEAD] - m_new) * scale)
            total = total + w
            weights.append(w.astype(BF16))
        p = jnp.concatenate(weights, axis=1)
        l_ref[...] = total
        m_ref[...] = m_new
        acc_ref[...] = acc_ref[...] * alpha + jnp.dot(p, kv[:, HEAD:], preferred_element_type=F32)

    @pl.loop(0, z)
    def _(zi):
        block(zi, False)

    block(z, True)
    total = jnp.sum(l_ref[...], axis=1, keepdims=True)
    result = (acc_ref[...] / total).astype(BF16)
    out_ref[:, :HEAD] = result[:rows]
    out_ref[:, HEAD:] = result[rows:]


def attend(place, q, mine, other):
    rows = q.shape[0]
    vmem = pl.BlockSpec(memory_space=pltpu.VMEM)
    return pl.pallas_call(
        attend_kernel,
        out_shape=jax.ShapeDtypeStruct(q.shape, BF16),
        in_specs=[pl.BlockSpec(memory_space=pltpu.SMEM), vmem, vmem, vmem],
        out_specs=vmem,
        scratch_shapes=[
            pltpu.VMEM((2 * rows, HEAD), BF16),
            pltpu.VMEM((2 * rows, HEAD), F32),
            pltpu.VMEM((2 * rows, HEAD), F32),
            pltpu.VMEM((2 * rows, HEAD), F32),
        ],
        compiler_params=pltpu.CompilerParams(vmem_limit_bytes=40 * 1024 * 1024),
        cost_estimate=pl.CostEstimate(flops=2**31, bytes_accessed=2**22, transcendentals=2**22),
    )(place, q, mine, other)


def on_device(tokens, norm_gain, w_query, w_key, w_value):
    at = lax.axis_index
    z, xh, core = at(("zh", "zl")), at("xh"), at("core")
    rows, feats = tokens.shape
    q_cols = w_query.shape[1]
    half = w_query.shape[0] // 2

    with jax.named_scope("weights"):
        wq = lax.all_to_all(w_query.reshape(2, half, q_cols), "core", 0, 0)
        head = at(("xl", "yh"))
        start = (core * half, head * HEAD)
        wkv = jnp.where(
            at("yl") == 0,
            lax.dynamic_slice(w_key, start, (half, HEAD)),
            lax.dynamic_slice(w_value, start, (half, HEAD)),
        )
        weights = lax.all_gather(
            jnp.concatenate([wkv, wq[0], wq[1]], axis=1), ("zh", "zl"), axis=0, tiled=True
        )

    with jax.named_scope("norm"):
        states = tokens.astype(F32)
        own = jnp.sum(states * states, axis=1).reshape(2, rows // 2)
        mean_sq = jnp.sum(gather(own, COL, 16), axis=0).reshape(rows, 1) / (feats * 16)
        normed = (states * lax.rsqrt(mean_sq + EPS) * norm_gain.astype(F32)[None, :]).astype(BF16)

    with jax.named_scope("spread"):
        quarters = jnp.transpose(normed.reshape(rows, 4, feats // 4), (1, 0, 2))
        quarters = lax.all_to_all(quarters, ("xh", "core"), 0, 0)
        whole = gather(quarters, ("xl", "yh", "yl"), 8)
        whole = whole.reshape(8, 2, 2, rows, feats // 4)
        whole = jnp.transpose(whole, (1, 3, 0, 2, 4)).reshape(2 * rows, 4 * feats)

    with jax.named_scope("project_kv"):
        kv_sum = jnp.dot(whole, weights[:, :HEAD], preferred_element_type=F32)
        parts = lax.all_to_all(kv_sum.reshape(8, rows // 4, HEAD), ("xh", "yl", "core"), 0, 0)
        parts = jnp.sum(parts.reshape(2, 2, 2, rows // 4, HEAD), axis=(0, 2)).astype(BF16)
        kv = jnp.concatenate([parts[0], parts[1]], axis=1)

    with jax.named_scope("gather_kv"):
        kv = gather(gather(kv, "zh", 4), "zl", 4)
        mine = gather(kv, ("xh", "yl"), 4)
        other = swap(mine)

    with jax.named_scope("project_q"):
        q_sum = jnp.dot(whole, weights[:, HEAD:], preferred_element_type=F32)
        q_sum = q_sum.reshape(2 * rows, 2, q_cols)
        q_keep = lax.dynamic_index_in_dim(q_sum, core, 1, keepdims=False)
        q_send = lax.dynamic_index_in_dim(q_sum, 1 - core, 1, keepdims=False)
        q_sum = (q_keep + swap(q_send)).reshape(2, rows, q_cols)
        q_keep = lax.dynamic_index_in_dim(q_sum, xh, 0, keepdims=False)
        q_send = lax.dynamic_index_in_dim(q_sum, 1 - xh, 0, keepdims=False)
        q = (q_keep + lax.ppermute(q_send, "xh", [(0, 1), (1, 0)])).astype(BF16)

    with jax.named_scope("attend"):
        place = jnp.stack([z, xh, core]).astype(jnp.int32)
        return attend(place, q, mine, other)


def solution(mesh):
    fine = Mesh(mesh.devices.reshape(4, 4, 2, 2, 2, 2, 2), ("zh", "zl", "xh", "xl", "yh", "yl", "core"))
    return jax.shard_map(
        on_device,
        mesh=fine,
        in_specs=(P(ROW, COL), P(COL), P(ROW, COL), P(ROW, None), P(ROW, None)),
        out_specs=P(ROW, COL),
        check_vma=False,
    )
```

time: 958 us -> 218 us (0.23)
  waiting for transfers between devices: 760 us -> 49.8 us
  blocking collectives: 19.9 us -> 89.1 us
  loops' own time: 44.2 us -> 0 us
  matrix products: 35.3 us -> 5.88 us
  local copies, waits for them, and re-layouts: 49.3 us -> 20.7 us
  other arithmetic: 33.6 us -> 5.61 us
  starting transfers between devices: 0.21 us -> 20.2 us
  Pallas kernels: 0 us -> 11.9 us
    all_gather x6 -> x1, waiting for transfers between devices: 759 us -> 12.1 us  [on_device(): lax.all_gather(jnp.concatenate([wkv, wq[0], wq[1]], axis=1), ('zh', 'zl')...]
    all_to_all x0 -> x5, blocking collectives: none -> 89.1 us  [the longest x3 64.9 us: gather(): return lax.all_to_all(jnp.broadcast_to(x[None], (n, *x.shape)), axes, 0, 0)]
    another operation x33 -> x0, loops' own time: 44.2 us -> none  [the longest x1 42.3 us: on_device(): carry, _ = lax.scan(step_block, carry, (key_blocks, value_blocks, starts))]
    dot_general x67 -> x2, matrix products: 35.3 us -> 5.88 us  [the longest x1 3.5 us: on_device(): q_sum = jnp.dot(whole, weights[:, HEAD:], preferred_element_type=F32)]
    all_to_all x0 -> x3, waiting for transfers between devices: none -> 27.5 us  [the longest x2 27 us: gather(): return lax.all_to_all(jnp.broadcast_to(x[None], (n, *x.shape)), axes, 0, 0)]
    slice x33 -> x0, local copies, waits for them, and re-layouts: 20.7 us -> none  [the longest x32 20.7 us: guarded(): pos_part[-1]]
    add x66 -> x1, other arithmetic: 21.3 us -> 1.11 us  [on_device(): q_sum = (q_keep + swap(q_send)).reshape(2, rows, q_cols)]
    all_gather x1 -> x0, blocking collectives: 19.9 us -> none  [on_device(): lax.all_gather(norm_gain, 'col', axis=0, tiled=True)]
  transfers between devices with their start and end apart: 6 -> 7, of which waited for: 6 -> 6; matrix products, arithmetic and copies ran while one was open for 2% -> 12% of each run, Pallas kernels for 0% -> 0%
where the time goes in v1:
time: 218 us; the launch traced here: 217 us
  blocking collectives  89.1 us (41%)
  waiting for transfers between devices  49.8 us (23%)
  local copies, waits for them, and re-layouts  20.7 us (9%)
  starting transfers between devices  20.2 us (9%)
  between operations  13.6 us (6%)
  Pallas kernels  11.9 us (5%)
  matrix products  5.88 us (3%)
  other arithmetic  5.61 us (3%)
    all_to_all x3, blocking collectives, gather(): return lax.all_to_all(jnp.broadcast_to(x[None], (n, *x.shape)), axes, 0, 0)  64.9 us
    all_to_all x2, waiting for transfers between devices, gather(): return lax.all_to_all(jnp.broadcast_to(x[None], (n, *x.shape)), axes, 0, 0)  27 us
    all_to_all x1, blocking collectives, on_device(): lax.all_to_all(kv_sum.reshape(8, rows // 4, HEAD), ('xh', 'yl', 'core'),...  12.9 us
    all_gather x1, waiting for transfers between devices, on_device(): lax.all_gather(jnp.concatenate([wkv, wq[0], wq[1]], axis=1), ('zh', 'zl')...  12.1 us
    pallas_call x1, Pallas kernels, attend(): pl.pallas_call(attend_kernel, out_shape=jax.ShapeDtypeStruct(q.shape, BF1...  11.9 us
    all_to_all x1, blocking collectives, on_device(): quarters = lax.all_to_all(quarters, ('xh', 'core'), 0, 0)  11.3 us
    all_to_all x2, starting transfers between devices, gather(): return lax.all_to_all(jnp.broadcast_to(x[None], (n, *x.shape)), axes, 0, 0)  9.11 us
    ppermute x1, waiting for transfers between devices, on_device(): q = (q_keep + lax.ppermute(q_send, 'xh', [(0, 1), (1, 0)])).astype(BF16)  8.56 us
  transfers between devices with their start and end apart: 7, of which 6 were waited for; matrix products, arithmetic and copies ran while one was open for 12% of the time, Pallas kernels for 0%

profile of v1, /device:TPU:480, one launch (start us, length us, event | category | flops | bytes accessed | tf_op | source)
XLA Modules:
  0.0 216.8 jit_solution(9027703059739413858)
XLA Ops:
  6.5 3.4 %all-to-all-start.3 = ((bf16[2,128,256]{2,1,0:T(8,128)(2,1)}), bf16[2,128,256]{2,1,0:T(8,128)(2,1)S(1)}, u32[]{:S(2)}, u32[]{:S(2)}) async-start(bf16[2,128,256]{2,1,0:T(8,128)(2,1)} %bitcast.51), calls=%async_computation.3 | async-start | bytes 262144 | tf_op jit(solution)/shard_map/weights/all_to_all | solution.py:106
  10.0 0.8 dynamic-slice_select_fusion
  11.4 0.7 pad_maximum_fusion
  12.1 1.1 fusion
  13.8 5.5 %all-to-all-start = ((f32[16,2,128]{2,1,0:T(2,128)}), f32[16,2,128]{2,1,0:T(2,128)S(1)}, u32[]{:S(2)}, u32[]{:S(2)}) async-start(f32[16,2,128]{2,1,0:T(2,128)} %broadcast_in_dim.13), calls=%async_computation | async-start | bytes 32768 | tf_op jit(solution)/shard_map/norm/all_to_all | solution.py:22
  19.3 0.7 convert_element_type.16
  20.0 5.4 %all-to-all-done = f32[16,2,128]{2,1,0:T(2,128)S(1)} async-done(((f32[16,2,128]{2,1,0:T(2,128)}), f32[16,2,128]{2,1,0:T(2,128)S(1)}, u32[]{:S(2)}, u32[]{:S(2)}) %all-to-all-start) | async-done | bytes 16416 | tf_op jit(solution)/shard_map/norm/all_to_all | solution.py:22
  25.4 1.1 bitcast_bitcast_fusion
  26.5 11.3 %all_to_all.40 = bf16[4,256,128]{2,1,0:T(8,128)(2,1)S(1)} all-to-all(bf16[4,256,128]{2,1,0:T(8,128)(2,1)S(1)} %bitcast_bitcast_fusion), channel_id=1, replica_groups=mesh['zh'=4,'zl'=4,'xh'=2,'xl'=2,'yh'=2,'yl'=2,'core'=2] {'xh','core'}, dimensions={0} | all-to-all | bytes 524288 | tf_op jit(solution)/shard_map/spread/all_to_all | solution.py:126
  38.3 29.5 %all_to_all.41 = bf16[8,4,256,128]{3,2,1,0:T(8,128)(2,1)S(1)} all-to-all(bf16[8,4,256,128]{3,2,1,0:T(8,128)(2,1)S(1)} %broadcast_in_dim.14), channel_id=1, replica_groups=mesh['zh'=4,'zl'=4,'xh'=2,'xl'=2,'yh'=2,'yl'=2,'core'=2] {'xl','yh','yl'}, dimensions={0} | all-to-all | bytes 4194304 | tf_op jit(solution)/shard_map/spread/all_to_all | solution.py:22
  67.9 2.2 copy.18
  70.1 3.1 %dot_general.15 = bf16[8,64,2048]{2,1,0:T(8,128)(2,1)} reshape(bf16[2,256,8,2,128]{4,3,2,1,0:T(2,128)(2,1)S(1)} %copy.18) | data formatting | bytes 4194304 | tf_op jit(solution)/shard_map/project_kv/dot_general | solution.py:132
  73.2 12.1 %all-gather.2.cloned.1.call-done = bf16[2048,640]{1,0:T(8,128)(2,1)} async-done(((bf16[128,640]{1,0:T(8,128)(2,1)}), bf16[2048,640]{1,0:T(8,128)(2,1)}) %all-gather.2.cloned.1.call-update) | async-done | bytes 2621456 | tf_op jit(solution)/shard_map/weights/all_gather | solution.py:114
  85.3 2.4 %fusion.3 = f32[8,64,128]{2,1,0:T(8,128)S(1)} fusion(bf16[8,64,2048]{2,1,0:T(8,128)(2,1)} %dot_general.15, bf16[2048,640]{1,0:T(8,128)(2,1)} %all-gather.2.cloned.1.call-done), kind=kOutput, calls=%fused_computation.7 | convolution fusion | flops 268435456 | bytes 2883584 | tf_op jit(solution)/shard_map/project_kv/dot_general | solution.py:132
  87.7 12.9 %all_to_all.42 = f32[8,64,128]{2,1,0:T(8,128)S(1)} all-to-all(f32[8,64,128]{2,1,0:T(8,128)S(1)} %fusion.3), channel_id=1, replica_groups=mesh['zh'=4,'zl'=4,'xh'=2,'xl'=2,'yh'=2,'yl'=2,'core'=2] {'xh','yl','core'}, dimensions={0} | all-to-all | bytes 524288 | tf_op jit(solution)/shard_map/project_kv/all_to_all | solution.py:133
  100.6 18.3 %all_to_all.43 = bf16[4,64,256]{2,1,0:T(8,128)(2,1)S(1)} all-to-all(bf16[4,64,256]{2,1,0:T(8,128)(2,1)S(1)} %broadcast_in_dim.15), channel_id=1, replica_groups=mesh['zh'=4,'zl'=4,'xh'=2,'xl'=2,'yh'=2,'yl'=2,'core'=2] {'zh'}, dimensions={0} | all-to-all | bytes 262144 | tf_op jit(solution)/shard_map/gather_kv/all_to_all | solution.py:22
  119.0 17.0 %all_to_all.44 = bf16[4,4,64,256]{3,2,1,0:T(8,128)(2,1)S(1)} all-to-all(bf16[4,4,64,256]{3,2,1,0:T(8,128)(2,1)S(1)} %broadcast_in_dim.16), channel_id=1, replica_groups=mesh['zh'=4,'zl'=4,'xh'=2,'xl'=2,'yh'=2,'yl'=2,'core'=2] {'zl'}, dimensions={0} | all-to-all | bytes 1048576 | tf_op jit(solution)/shard_map/gather_kv/all_to_all | solution.py:22
  136.0 1.7 broadcast_in_dim.17
  137.7 3.6 %all-to-all-start.7 = ((bf16[4,4,4,64,256]{4,3,2,1,0:T(8,128)(2,1)}), bf16[4,4,4,64,256]{4,3,2,1,0:T(8,128)(2,1)S(1)}, u32[]{:S(2)}, u32[]{:S(2)}) async-start(bf16[4,4,4,64,256]{4,3,2,1,0:T(8,128)(2,1)} %broadcast_in_dim.17), calls=%async_computation.7 | async-start | bytes 4194304 | tf_op jit(solution)/shard_map/gather_kv/all_to_all | solution.py:22
  141.3 4.5 %reshape.53 = bf16[512,2048,1]{1,0,2:T(8,128)(2,1)} reshape(bf16[2,256,8,2,128]{4,3,2,1,0:T(2,128)(2,1)} %copy-done) | data formatting | bytes 4194304 | tf_op jit(solution)/shard_map/spread/reshape | solution.py:129
  145.8 21.6 %all-to-all-done.7.mine_ref = bf16[4,4,4,64,256]{4,3,2,1,0:T(8,128)(2,1)S(1)} async-done(((bf16[4,4,4,64,256]{4,3,2,1,0:T(8,128)(2,1)}), bf16[4,4,4,64,256]{4,3,2,1,0:T(8,128)(2,1)S(1)}, u32[]{:S(2)}, u32[]{:S(2)}) %all-to-all-start.7) | async-done | bytes 2097184 | tf_op jit(solution)/shard_map/gather_kv/all_to_all | solution.py:22
  167.4 1.9 collective-permute-start.2
  169.3 3.1 %slice_bitcast_fusion = bf16[512,2048]{0,1:T(8,128)(2,1)} fusion(bf16[2048,640]{1,0:T(8,128)(2,1)} %all-gather.2.cloned.1.call-done), kind=kLoop, calls=%fused_computation | loop fusion | bytes 4194304 | tf_op jit(solution)/shard_map/project_q/dot_general | solution.py:143
  172.4 4.0 %copy.19 = bf16[512,2048]{1,0:T(8,128)(2,1)} copy(bf16[512,2048]{0,1:T(8,128)(2,1)} %slice_bitcast_fusion) | data formatting | bytes 4194304 | tf_op jit(solution)/shard_map/project_q/dot_general | solution.py:143
  176.4 3.5 %fusion.6 = f32[512,2,256]{2,0,1:T(8,128)S(1)} fusion(bf16[512,2048,1]{1,0,2:T(8,128)(2,1)} %reshape.53, bf16[2,256,2048]{2,1,0:T(8,128)(2,1)} %bitcast.47), kind=kOutput, calls=%fused_computation.24 | convolution fusion | flops 1073741824 | bytes 5242880 | tf_op jit(solution)/shard_map/project_q/dot_general | solution.py:143
  179.9 1.0 copy-done.1
  180.9 2.4 %collective-permute-start = (f32[512,256]{1,0:T(8,128)S(1)}, f32[512,256]{1,0:T(8,128)S(1)}, u32[]{:S(2)}, u32[]{:S(2)}) collective-permute-start(f32[512,256]{1,0:T(8,128)S(1)} %dynamic-slice_bitcast_fusion), channel_id=1, source_target_pairs={{0,1},{1,0},{2,3},{3,2},{4,5},{5,4},{6,7},{7,6},{8,9},{9,8},{10,11... | collective-permute-start | bytes 1572872 | tf_op jit(solution)/shard_map/project_q/ppermute | solution.py:26
  183.4 1.5 collective-permute-done
  184.9 1.1 bitcast_add_fusion
  186.0 3.3 %collective-permute-start.1 = (f32[256,256]{1,0:T(8,128)S(1)}, f32[256,256]{1,0:T(8,128)S(1)}, u32[]{:S(2)}, u32[]{:S(2)}) collective-permute-start(f32[256,256]{1,0:T(8,128)S(1)} %dynamic-slice_bitcast_fusion.1), channel_id=1, source_target_pairs={{0,16},{16,0},{1,17},{17,1},{2,18},{18,2},{3,19},{19,3},{4,20},{20... | collective-permute-start | bytes 786440 | tf_op jit(solution)/shard_map/project_q/ppermute | solution.py:150
  189.4 8.6 %collective-permute-done.1 = f32[256,256]{1,0:T(8,128)S(1)} collective-permute-done((f32[256,256]{1,0:T(8,128)S(1)}, f32[256,256]{1,0:T(8,128)S(1)}, u32[]{:S(2)}, u32[]{:S(2)}) %collective-permute-start.1) | collective-permute-done | bytes 262176 | tf_op jit(solution)/shard_map/project_q/ppermute | solution.py:150
  198.0 11.9 %attend.1 = bf16[256,256]{1,0:T(8,128)(2,1)} custom-call(s32[3]{0:T(128)S(1)} %pad_add_fusion.place, bf16[256,256]{1,0:T(8,128)(2,1)S(1)} %fusion.5.q_ref, bf16[4,4,4,64,256]{4,3,2,1,0:T(8,128)(2,1)S(1)} %all-to-all-done.7.mine_ref, bf16[4,4,4,64,256]{4,3,2,1,0:T(8,128)(2,1)} %collective-permute-done.2.other_ref), custom_call_target="tpu_custom_call" | custom-call | flops 2147483648 | bytes 4194304 | tf_op jit(solution)/shard_map/attend/pallas_call | solution.py:82
  (21 shorter events, 2.0 us)
Async XLA Ops:
  6.5 4.8 %all-to-all-start.3 = ((bf16[2,128,256]{2,1,0:T(8,128)(2,1)}), bf16[2,128,256]{2,1,0:T(8,128)(2,1)S(1)}, u32[]{:S(2)}, u32[]{:S(2)}) async-start(bf16[2,128,256]{2,1,0:T(8,128)(2,1)} %bitcast.51), calls=%async_computation.3 | async-start | bytes 262144 | tf_op jit(solution)/shard_map/weights/all_to_all | solution.py:106
  9.9 75.4 %all-gather.2.cloned.1.call-start = ((), (), s32[]{:S(2)}) async-start(), calls=%async_computation.8 | async-start | bytes 2785280 | tf_op jit(solution)/shard_map/weights/all_gather | solution.py:114
  13.8 11.6 %all-to-all-start = ((f32[16,2,128]{2,1,0:T(2,128)}), f32[16,2,128]{2,1,0:T(2,128)S(1)}, u32[]{:S(2)}, u32[]{:S(2)}) async-start(f32[16,2,128]{2,1,0:T(2,128)} %broadcast_in_dim.13), calls=%async_computation | async-start | bytes 32768 | tf_op jit(solution)/shard_map/norm/all_to_all | solution.py:22
  70.0 17.6 %copy-start = (bf16[2,256,8,2,128]{4,3,2,1,0:T(2,128)(2,1)}, bf16[2,256,8,2,128]{4,3,2,1,0:T(2,128)(2,1)S(1)}, u32[]{:S(2)}) copy-start(bf16[2,256,8,2,128]{4,3,2,1,0:T(2,128)(2,1)S(1)} %copy.18) | copy-start | bytes 6291460
  137.7 29.7 %all-to-all-start.7 = ((bf16[4,4,4,64,256]{4,3,2,1,0:T(8,128)(2,1)}), bf16[4,4,4,64,256]{4,3,2,1,0:T(8,128)(2,1)S(1)}, u32[]{:S(2)}, u32[]{:S(2)}) async-start(bf16[4,4,4,64,256]{4,3,2,1,0:T(8,128)(2,1)} %broadcast_in_dim.17), calls=%async_computation.7 | async-start | bytes 4194304 | tf_op jit(solution)/shard_map/gather_kv/all_to_all | solution.py:22
  167.4 30.7 %collective-permute-start.2 = (bf16[4,4,4,64,256]{4,3,2,1,0:T(8,128)(2,1)S(1)}, bf16[4,4,4,64,256]{4,3,2,1,0:T(8,128)(2,1)}, u32[]{:S(2)}, u32[]{:S(2)}) collective-permute-start(bf16[4,4,4,64,256]{4,3,2,1,0:T(8,128)(2,1)S(1)} %all-to-all-done.7.mine_ref), channel_id=1, source_target_pairs={{0,1},{1,0},{2,3},{3,2},{4,5},{5,4},{6,7},{7,6},{8,9},{9,8},{10,11... | collective-permute-start | bytes 6291464 | tf_op jit(solution)/shard_map/gather_kv/ppermute | solution.py:26
  179.9 1.0 copy-start.1
  180.9 3.9 %collective-permute-start = (f32[512,256]{1,0:T(8,128)S(1)}, f32[512,256]{1,0:T(8,128)S(1)}, u32[]{:S(2)}, u32[]{:S(2)}) collective-permute-start(f32[512,256]{1,0:T(8,128)S(1)} %dynamic-slice_bitcast_fusion), channel_id=1, source_target_pairs={{0,1},{1,0},{2,3},{3,2},{4,5},{5,4},{6,7},{7,6},{8,9},{9,8},{10,11... | collective-permute-start | bytes 1572872 | tf_op jit(solution)/shard_map/project_q/ppermute | solution.py:26
  186.0 12.0 %collective-permute-start.1 = (f32[256,256]{1,0:T(8,128)S(1)}, f32[256,256]{1,0:T(8,128)S(1)}, u32[]{:S(2)}, u32[]{:S(2)}) collective-permute-start(f32[256,256]{1,0:T(8,128)S(1)} %dynamic-slice_bitcast_fusion.1), channel_id=1, source_target_pairs={{0,16},{16,0},{1,17},{17,1},{2,18},{18,2},{3,19},{19,3},{4,20},{20... | collective-permute-start | bytes 786440 | tf_op jit(solution)/shard_map/project_q/ppermute | solution.py:150
Sparse Core Ops, SparseCore 0:
  12.8 72.4 all-gather.1

commit v2 on v1

--- a/solution.py
+++ b/solution.py
@@ -95,25 +95,39 @@
     )(place, q, mine, other)
 
 
+def kv_kernel(t_ref, w_ref, out_ref):
+    for head in range(out_ref.shape[1]):
+        w = jnp.concatenate([w_ref[:, at : at + HEAD] for at in (head * HEAD, head * HEAD + w_ref.shape[1] // 2)], axis=1)
+        part = jnp.dot(t_ref[...], w, preferred_element_type=F32)
+        out_ref[:, head] = part.reshape(out_ref.shape[0], *out_ref.shape[2:])
+
+
+def kv_partial(t, w):
+    vmem = pl.BlockSpec(memory_space=pltpu.VMEM)
+    rows, depth = t.shape
+    return pl.pallas_call(
+        kv_kernel,
+        out_shape=jax.ShapeDtypeStruct((2, 4, 4, rows // 8, 2 * HEAD), F32),
+        in_specs=[vmem, vmem],
+        out_specs=vmem,
+        compiler_params=pltpu.CompilerParams(vmem_limit_bytes=40 * 1024 * 1024),
+        cost_estimate=pl.CostEstimate(flops=2 * rows * depth * w.shape[1], bytes_accessed=3 * 2**20, transcendentals=0),
+    )(t, w)
+
+
 def on_device(tokens, norm_gain, w_query, w_key, w_value):
     at = lax.axis_index
     z, xh, core = at(("zh", "zl")), at("xh"), at("core")
     rows, feats = tokens.shape
-    q_cols = w_query.shape[1]
-    half = w_query.shape[0] // 2
+    half = feats // 2
 
     with jax.named_scope("weights"):
-        wq = lax.all_to_all(w_query.reshape(2, half, q_cols), "core", 0, 0)
-        head = at(("xl", "yh"))
-        start = (core * half, head * HEAD)
-        wkv = jnp.where(
-            at("yl") == 0,
-            lax.dynamic_slice(w_key, start, (half, HEAD)),
-            lax.dynamic_slice(w_value, start, (half, HEAD)),
-        )
-        weights = lax.all_gather(
-            jnp.concatenate([wkv, wq[0], wq[1]], axis=1), ("zh", "zl"), axis=0, tiled=True
-        )
+        wkv = jnp.concatenate([w_key, w_value], axis=1)
+        turn = [
+            ((a * 2 + x) * 16 + b, (b * 2 + x) * 16 + a) for a in range(16) for x in range(2) for b in range(16)
+        ]
+        wkv = lax.ppermute(wkv, ROW + COL, turn)
+        wq = lax.all_gather(w_query, ("zh", "zl"), axis=0, tiled=True)
 
     with jax.named_scope("norm"):
         states = tokens.astype(F32)
@@ -122,36 +136,31 @@
         normed = (states * lax.rsqrt(mean_sq + EPS) * norm_gain.astype(F32)[None, :]).astype(BF16)
 
     with jax.named_scope("spread"):
-        quarters = jnp.transpose(normed.reshape(rows, 4, feats // 4), (1, 0, 2))
-        quarters = lax.all_to_all(quarters, ("xh", "core"), 0, 0)
-        whole = gather(quarters, ("xl", "yh", "yl"), 8)
-        whole = whole.reshape(8, 2, 2, rows, feats // 4)
-        whole = jnp.transpose(whole, (1, 3, 0, 2, 4)).reshape(2 * rows, 4 * feats)
+        keep = lax.dynamic_slice_in_dim(normed, xh * half, half, 1)
+        send = lax.dynamic_slice_in_dim(normed, (1 - xh) * half, half, 1)
+        came = lax.ppermute(send, "xh", [(0, 1), (1, 0)])
+        both = jnp.where(xh == 0, jnp.concatenate([keep, came]), jnp.concatenate([came, keep]))
+        whole = lax.all_gather(both, COL, axis=1, tiled=True)
 
     with jax.named_scope("project_kv"):
-        kv_sum = jnp.dot(whole, weights[:, :HEAD], preferred_element_type=F32)
-        parts = lax.all_to_all(kv_sum.reshape(8, rows // 4, HEAD), ("xh", "yl", "core"), 0, 0)
-        parts = jnp.sum(parts.reshape(2, 2, 2, rows // 4, HEAD), axis=(0, 2)).astype(BF16)
-        kv = jnp.concatenate([parts[0], parts[1]], axis=1)
+        kv_sum = kv_partial(both, wkv).reshape(32, rows // 4, 2 * HEAD)
+        parts = lax.all_to_all(kv_sum, ("xh",) + COL, 0, 0)
+        kv = jnp.sum(parts, axis=0).astype(BF16)
 
     with jax.named_scope("gather_kv"):
         kv = gather(gather(kv, "zh", 4), "zl", 4)
         mine = gather(kv, ("xh", "yl"), 4)
-        other = swap(mine)
 
     with jax.named_scope("project_q"):
-        q_sum = jnp.dot(whole, weights[:, HEAD:], preferred_element_type=F32)
-        q_sum = q_sum.reshape(2 * rows, 2, q_cols)
-        q_keep = lax.dynamic_index_in_dim(q_sum, core, 1, keepdims=False)
-        q_send = lax.dynamic_index_in_dim(q_sum, 1 - core, 1, keepdims=False)
-        q_sum = (q_keep + swap(q_send)).reshape(2, rows, q_cols)
+        q_sum = jnp.dot(whole, wq, preferred_element_type=F32).reshape(2, rows, -1)
         q_keep = lax.dynamic_index_in_dim(q_sum, xh, 0, keepdims=False)
         q_send = lax.dynamic_index_in_dim(q_sum, 1 - xh, 0, keepdims=False)
         q = (q_keep + lax.ppermute(q_send, "xh", [(0, 1), (1, 0)])).astype(BF16)
 
     with jax.named_scope("attend"):
+        mine, q = lax.optimization_barrier((mine, q))
         place = jnp.stack([z, xh, core]).astype(jnp.int32)
-        return attend(place, q, mine, other)
+        return attend(place, q, mine, swap(mine))
 
 
 def solution(mesh):

time: 218 us -> 263 us (1.21)
  the two profiles are of different devices: /device:TPU:480 before, /device:TPU:1 now
where the time goes in v2:
time: 263 us
  blocking collectives  155 us (59%)
  waiting for transfers between devices  51 us (19%)
  starting transfers between devices  27.1 us (10%)
  between operations  13.6 us (5%)
  other arithmetic  5.62 us (2%)
  matrix products  4.12 us (2%)
  Pallas kernels  3.4 us (1%)
  local copies, waits for them, and re-layouts  3.29 us (1%)
    all_to_all x1, blocking collectives, on_device(): parts = lax.all_to_all(kv_sum, ('xh',) + COL, 0, 0)  116 us
    all_to_all x2, blocking collectives, gather(): return lax.all_to_all(jnp.broadcast_to(x[None], (n, *x.shape)), axes, 0, 0)  38.9 us
    ppermute x1, waiting for transfers between devices, on_device(): q = (q_keep + lax.ppermute(q_send, 'xh', [(0, 1), (1, 0)])).astype(BF16)  21.1 us
    ppermute x1, waiting for transfers between devices, on_device(): wkv = lax.ppermute(wkv, ROW + COL, turn)  14.1 us
    all_to_all x2, starting transfers between devices, gather(): return lax.all_to_all(jnp.broadcast_to(x[None], (n, *x.shape)), axes, 0, 0)  13.8 us
    ppermute x1, waiting for transfers between devices, on_device(): came = lax.ppermute(send, 'xh', [(0, 1), (1, 0)])  6.15 us
  transfers between devices with their start and end apart: 8, of which 5 were waited for; matrix products, arithmetic and copies ran while one was open for 5% of the time, Pallas kernels for 0%

profile of v2, /device:TPU:1, one launch (start us, length us, event | category | flops | bytes accessed | tf_op | source)
XLA Modules:
  0.0 262.7 jit_solution(204769606247648592)
XLA Ops:
  6.5 0.7 all-gather.5.cloned.1.call-update
  7.3 1.1 fusion
  8.3 0.6 broadcast_in_dim.11
  9.0 10.2 %all-to-all-start = ((f32[16,2,128]{2,1,0:T(2,128)}), f32[16,2,128]{2,1,0:T(2,128)S(1)}, u32[]{:S(2)}, u32[]{:S(2)}) async-start(f32[16,2,128]{2,1,0:T(2,128)} %broadcast_in_dim.11), calls=%async_computation | async-start | bytes 32768 | tf_op jit(solution)/shard_map/norm/all_to_all | solution.py:22
  19.1 0.0 all-gather.3.cloned.1.call-start
  19.2 0.7 convert_element_type.20
  19.9 5.1 %all-to-all-done = f32[16,2,128]{2,1,0:T(2,128)S(1)} async-done(((f32[16,2,128]{2,1,0:T(2,128)}), f32[16,2,128]{2,1,0:T(2,128)S(1)}, u32[]{:S(2)}, u32[]{:S(2)}) %all-to-all-start) | async-done | bytes 16416 | tf_op jit(solution)/shard_map/norm/all_to_all | solution.py:22
  25.0 1.1 fusion.2
  26.1 1.9 collective-permute-start
  28.1 6.1 %collective-permute-done = bf16[256,256]{1,0:T(8,128)(2,1)S(1)} collective-permute-done((bf16[256,256]{1,0:T(8,128)(2,1)S(1)}, bf16[256,256]{1,0:T(8,128)(2,1)S(1)}, u32[]{:S(2)}, u32[]{:S(2)}) %collective-permute-start) | collective-permute-done | bytes 131104 | tf_op jit(solution)/shard_map/spread/ppermute | solution.py:141
  34.2 0.8 maximum_select_fusion.t_ref
  35.1 0.0 all-gather.3.cloned.1.call-update
  35.1 0.1 pad_maximum_fusion
  35.2 1.9 collective-permute-start.1
  37.1 14.1 %collective-permute-done.1.w_ref = bf16[256,1024]{1,0:T(8,128)(2,1)S(1)} collective-permute-done((bf16[256,1024]{1,0:T(8,128)(2,1)S(1)}, bf16[256,1024]{1,0:T(8,128)(2,1)S(1)}, u32[]{:S(2)}, u32[]{:S(2)}) %collective-permute-start.1) | collective-permute-done | bytes 524320 | tf_op jit(solution)/shard_map/weights/ppermute | solution.py:129
  51.2 0.9 copy-done
  52.1 0.4 project_kv.1
  52.5 115.6 %all_to_all.25 = f32[32,64,256]{2,1,0:T(8,128)} all-to-all(f32[32,64,256]{2,1,0:T(8,128)S(1)} %bitcast.16), channel_id=1, replica_groups=mesh['zh'=4,'zl'=4,'xh'=2,'xl'=2,'yh'=2,'yl'=2,'core'=2] {'xh','xl','yh'..., dimensions={0} | all-to-all | bytes 4194304 | tf_op jit(solution)/shard_map/project_kv/all_to_all | solution.py:147
  168.2 1.7 reduce_sum.29
  169.9 21.8 %all_to_all.26 = bf16[4,64,256]{2,1,0:T(8,128)(2,1)S(1)} all-to-all(bf16[4,64,256]{2,1,0:T(8,128)(2,1)S(1)} %broadcast_in_dim.12), channel_id=1, replica_groups=mesh['zh'=4,'zl'=4,'xh'=2,'xl'=2,'yh'=2,'yl'=2,'core'=2] {'zh'}, dimensions={0} | all-to-all | bytes 262144 | tf_op jit(solution)/shard_map/gather_kv/all_to_all | solution.py:22
  191.7 17.2 %all_to_all.27 = bf16[4,4,64,256]{3,2,1,0:T(8,128)(2,1)S(1)} all-to-all(bf16[4,4,64,256]{3,2,1,0:T(8,128)(2,1)S(1)} %broadcast_in_dim.13), channel_id=1, replica_groups=mesh['zh'=4,'zl'=4,'xh'=2,'xl'=2,'yh'=2,'yl'=2,'core'=2] {'zl'}, dimensions={0} | all-to-all | bytes 1048576 | tf_op jit(solution)/shard_map/gather_kv/all_to_all | solution.py:22
  208.9 1.6 broadcast_in_dim.14
  210.5 3.6 %all-to-all-start.4 = ((bf16[4,4,4,64,256]{4,3,2,1,0:T(8,128)(2,1)}), bf16[4,4,4,64,256]{4,3,2,1,0:T(8,128)(2,1)S(1)}, u32[]{:S(2)}, u32[]{:S(2)}) async-start(bf16[4,4,4,64,256]{4,3,2,1,0:T(8,128)(2,1)} %broadcast_in_dim.14), calls=%async_computation.4 | async-start | bytes 4194304 | tf_op jit(solution)/shard_map/gather_kv/all_to_all | solution.py:22
  214.1 0.0 all-gather.5.cloned.1.call-done
  214.1 0.0 all-gather.3.cloned.1.call-done
  214.2 4.1 %fusion.4 = f32[512,256]{1,0:T(8,128)S(1)} fusion(bf16[512,4096]{1,0:T(8,128)(2,1)} %all-gather.3.cloned.1.call-done, bf16[4096,256]{1,0:T(8,128)(2,1)} %all-gather.5.cloned.1.call-done), kind=kOutput, calls=%fused_computation.14 | convolution fusion | flops 1073741824 | bytes 6815744 | tf_op jit(solution)/shard_map/project_q/dot_general | solution.py:155
  218.3 4.8 %collective-permute-start.2 = (f32[256,256]{1,0:T(8,128)S(1)}, f32[256,256]{1,0:T(8,128)S(1)}, u32[]{:S(2)}, u32[]{:S(2)}) collective-permute-start(f32[256,256]{1,0:T(8,128)S(1)} %dynamic-slice_bitcast_fusion), channel_id=1, source_target_pairs={{0,16},{16,0},{1,17},{17,1},{2,18},{18,2},{3,19},{19,3},{4,20},{20... | collective-permute-start | bytes 786440 | tf_op jit(solution)/shard_map/project_q/ppermute | solution.py:158
  223.1 21.1 %collective-permute-done.2 = f32[256,256]{1,0:T(8,128)S(1)} collective-permute-done((f32[256,256]{1,0:T(8,128)S(1)}, f32[256,256]{1,0:T(8,128)S(1)}, u32[]{:S(2)}, u32[]{:S(2)}) %collective-permute-start.2) | collective-permute-done | bytes 262176 | tf_op jit(solution)/shard_map/project_q/ppermute | solution.py:158
  244.3 4.7 %collective-permute-start.3 = (bf16[4,4,4,64,256]{4,3,2,1,0:T(8,128)(2,1)S(1)}, bf16[4,4,4,64,256]{4,3,2,1,0:T(8,128)(2,1)}, u32[]{:S(2)}, u32[]{:S(2)}) collective-permute-start(bf16[4,4,4,64,256]{4,3,2,1,0:T(8,128)(2,1)S(1)} %all-to-all-done.4.mine_ref), channel_id=1, source_target_pairs={{0,1},{1,0},{2,3},{3,2},{4,5},{5,4},{6,7},{7,6},{8,9},{9,8},{10,11... | collective-permute-start | bytes 6291464 | tf_op jit(solution)/shard_map/attend/ppermute | solution.py:26
  249.0 0.1 pad_add_fusion.place
  249.1 3.8 %collective-permute-done.3.other_ref = bf16[4,4,4,64,256]{4,3,2,1,0:T(8,128)(2,1)} collective-permute-done((bf16[4,4,4,64,256]{4,3,2,1,0:T(8,128)(2,1)S(1)}, bf16[4,4,4,64,256]{4,3,2,1,0:T(8,128)(2,1)}, u32[]{:S(2)}, u32[]{:S(2)}) %collective-permute-start.3) | collective-permute-done | bytes 2097184 | tf_op jit(solution)/shard_map/attend/ppermute | solution.py:26
  252.9 3.0 %attend.1 = bf16[256,256]{1,0:T(8,128)(2,1)} custom-call(s32[3]{0:T(128)S(1)} %pad_add_fusion.place, bf16[256,256]{1,0:T(8,128)(2,1)S(1)} %fusion.3.q_ref, bf16[4,4,4,64,256]{4,3,2,1,0:T(8,128)(2,1)S(1)} %all-to-all-done.4.mine_ref, bf16[4,4,4,64,256]{4,3,2,1,0:T(8,128)(2,1)} %collective-permute-done.3.other_ref), custom_call_target="tpu_custom_call" | custom-call | flops 2147483648 | bytes 4194304 | tf_op jit(solution)/shard_map/attend/pallas_call | solution.py:82
  (14 shorter events, 0.2 us)
Async XLA Ops:
  6.5 28.5 %copy-start.1 = (bf16[256,512]{1,0:T(8,128)(2,1)S(1)}, bf16[256,512]{1,0:T(8,128)(2,1)}, u32[]{:S(2)}) copy-start(bf16[256,512]{1,0:T(8,128)(2,1)} %param.9) | copy-start | bytes 786436
  6.5 28.6 %copy-start.2 = (bf16[256,512]{1,0:T(8,128)(2,1)S(1)}, bf16[256,512]{1,0:T(8,128)(2,1)}, u32[]{:S(2)}) copy-start(bf16[256,512]{1,0:T(8,128)(2,1)} %param.8) | copy-start | bytes 786436
  6.5 207.6 %all-gather.5.cloned.1.call-start = ((), (), s32[]{:S(2)}) async-start(), calls=%async_computation.6 | async-start | bytes 2228224 | tf_op jit(solution)/shard_map/weights/all_gather | solution.py:130
  9.0 16.0 %all-to-all-start = ((f32[16,2,128]{2,1,0:T(2,128)}), f32[16,2,128]{2,1,0:T(2,128)S(1)}, u32[]{:S(2)}, u32[]{:S(2)}) async-start(f32[16,2,128]{2,1,0:T(2,128)} %broadcast_in_dim.11), calls=%async_computation | async-start | bytes 32768 | tf_op jit(solution)/shard_map/norm/all_to_all | solution.py:22
  19.1 195.0 %all-gather.3.cloned.1.call-start = ((), (), s32[]{:S(2)}) async-start(), calls=%async_computation.5 | async-start | bytes 4456448 | tf_op jit(solution)/shard_map/spread/all_gather | solution.py:143
  26.1 8.1 %collective-permute-start = (bf16[256,256]{1,0:T(8,128)(2,1)S(1)}, bf16[256,256]{1,0:T(8,128)(2,1)S(1)}, u32[]{:S(2)}, u32[]{:S(2)}) collective-permute-start(bf16[256,256]{1,0:T(8,128)(2,1)S(1)} %get-tuple-element.10), channel_id=1, source_target_pairs={{0,16},{16,0},{1,17},{17,1},{2,18},{18,2},{3,19},{19,3},{4,20},{20... | collective-permute-start | bytes 393224 | tf_op jit(solution)/shard_map/spread/ppermute | solution.py:141
  35.2 16.0 %collective-permute-start.1 = (bf16[256,1024]{1,0:T(8,128)(2,1)S(1)}, bf16[256,1024]{1,0:T(8,128)(2,1)S(1)}, u32[]{:S(2)}, u32[]{:S(2)}) collective-permute-start(bf16[256,1024]{1,0:T(8,128)(2,1)S(1)} %pad_maximum_fusion), channel_id=1, source_target_pairs={{0,0},{1,32},{2,64},{3,96},{4,128},{5,160},{6,192},{7,224},{8,256}... | collective-permute-start | bytes 1572872 | tf_op jit(solution)/shard_map/weights/ppermute | solution.py:129
  51.2 0.9 copy-start
  210.5 33.8 %all-to-all-start.4 = ((bf16[4,4,4,64,256]{4,3,2,1,0:T(8,128)(2,1)}), bf16[4,4,4,64,256]{4,3,2,1,0:T(8,128)(2,1)S(1)}, u32[]{:S(2)}, u32[]{:S(2)}) async-start(bf16[4,4,4,64,256]{4,3,2,1,0:T(8,128)(2,1)} %broadcast_in_dim.14), calls=%async_computation.4 | async-start | bytes 4194304 | tf_op jit(solution)/shard_map/gather_kv/all_to_all | solution.py:22
  218.3 25.9 %collective-permute-start.2 = (f32[256,256]{1,0:T(8,128)S(1)}, f32[256,256]{1,0:T(8,128)S(1)}, u32[]{:S(2)}, u32[]{:S(2)}) collective-permute-start(f32[256,256]{1,0:T(8,128)S(1)} %dynamic-slice_bitcast_fusion), channel_id=1, source_target_pairs={{0,16},{16,0},{1,17},{17,1},{2,18},{18,2},{3,19},{19,3},{4,20},{20... | collective-permute-start | bytes 786440 | tf_op jit(solution)/shard_map/project_q/ppermute | solution.py:158
  244.3 8.6 %collective-permute-start.3 = (bf16[4,4,4,64,256]{4,3,2,1,0:T(8,128)(2,1)S(1)}, bf16[4,4,4,64,256]{4,3,2,1,0:T(8,128)(2,1)}, u32[]{:S(2)}, u32[]{:S(2)}) collective-permute-start(bf16[4,4,4,64,256]{4,3,2,1,0:T(8,128)(2,1)S(1)} %all-to-all-done.4.mine_ref), channel_id=1, source_target_pairs={{0,1},{1,0},{2,3},{3,2},{4,5},{5,4},{6,7},{7,6},{8,9},{9,8},{10,11... | collective-permute-start | bytes 6291464 | tf_op jit(solution)/shard_map/attend/ppermute | solution.py:26
Sparse Core Ops, SparseCore 0:
  9.4 136.5 all-gather.4
  148.1 58.6 all-gather.2

commit v3 on v1

--- a/solution.py
+++ b/solution.py
@@ -95,15 +95,90 @@
     )(place, q, mine, other)
 
 
+def kv_kernel(parts_ref, w_ref, t_ref, kv_ref):
+    rows = t_ref.shape[1]
+    blocks = parts_ref.shape[1]
+    for xh in range(2):
+        squares = jnp.zeros((6, HEAD), F32)
+        for c in range(blocks):
+            squares += parts_ref[xh, c, rows : rows + 6].astype(F32)
+        mean_sq = (squares[4:6] + squares[2:4] + squares[0:2]) / (blocks * 4 * HEAD)
+        inverse = lax.rsqrt(mean_sq + EPS)
+        inverse = jnp.concatenate(
+            [jnp.transpose(jnp.broadcast_to(inverse[i : i + 1], (HEAD, HEAD))) for i in range(2)], axis=0
+        )
+        total = jnp.zeros((rows, HEAD), F32)
+        for c in range(0, blocks, 2):
+            for d in (c, c + 1):
+                gain = parts_ref[xh, d, rows + 6 : rows + 7].astype(F32)
+                t = parts_ref[xh, d, :rows].astype(F32) * inverse * gain
+                t_ref[xh, :, d * HEAD : (d + 1) * HEAD] = t.astype(BF16)
+            w = jnp.concatenate([w_ref[d % 4, d // 4] for d in (c, c + 1)], axis=0)
+            total += jnp.dot(t_ref[xh, :, c * HEAD : (c + 2) * HEAD], w, preferred_element_type=F32)
+        kv_ref[xh] = total
+
+
+def project_kv(parts, w, rows):
+    vmem = pl.BlockSpec(memory_space=pltpu.VMEM)
+    blocks = parts.shape[1]
+    return pl.pallas_call(
+        kv_kernel,
+        out_shape=(
+            jax.ShapeDtypeStruct((2, rows, blocks * HEAD), BF16),
+            jax.ShapeDtypeStruct((2, rows, HEAD), F32),
+        ),
+        in_specs=[vmem, vmem],
+        out_specs=(vmem, vmem),
+        compiler_params=pltpu.CompilerParams(vmem_limit_bytes=40 * 1024 * 1024),
+        cost_estimate=pl.CostEstimate(flops=2**28, bytes_accessed=5 * 2**20, transcendentals=0),
+    )(parts, w)
+
+
+def q_kernel(place, mine_ref, other_ref, w_ref, out_ref):
+    core = place[2]
+    rows = mine_ref.shape[1]
+    half = w_ref.shape[1] // 2
+    for xh in range(2):
+        total = jnp.zeros((rows, w_ref.shape[2]), F32)
+        for c in range(w_ref.shape[0]):
+            t = jnp.concatenate([ref[xh, :, c * half : (c + 1) * half] for ref in (mine_ref, other_ref)], axis=1)
+            w = jnp.concatenate(
+                [w_ref[c, pl.ds(pl.multiple_of(at * half, half), half)] for at in (core, 1 - core)], axis=0
+            )
+            total += jnp.dot(t, w, preferred_element_type=F32)
+        out_ref[xh] = total
+
+
+def project_q(place, mine, other, w):
+    vmem = pl.BlockSpec(memory_space=pltpu.VMEM)
+    return pl.pallas_call(
+        q_kernel,
+        out_shape=jax.ShapeDtypeStruct((*mine.shape[:2], w.shape[2]), F32),
+        in_specs=[pl.BlockSpec(memory_space=pltpu.SMEM), vmem, vmem, vmem],
+        out_specs=vmem,
+        compiler_params=pltpu.CompilerParams(vmem_limit_bytes=40 * 1024 * 1024),
+        cost_estimate=pl.CostEstimate(flops=2**30, bytes_accessed=6 * 2**20, transcendentals=0),
+    )(place, mine, other, w)
+
+
+def three(x):
+    out = []
+    for _ in range(3):
+        piece = lax.reduce_precision(x, 8, 7)
+        out.append(piece.astype(BF16))
+        x = x - piece
+    return out
+
+
 def on_device(tokens, norm_gain, w_query, w_key, w_value):
     at = lax.axis_index
     z, xh, core = at(("zh", "zl")), at("xh"), at("core")
+    place = jnp.stack([z, xh, core]).astype(jnp.int32)
     rows, feats = tokens.shape
-    q_cols = w_query.shape[1]
-    half = w_query.shape[0] // 2
+    half = w_key.shape[0] // 2
 
     with jax.named_scope("weights"):
-        wq = lax.all_to_all(w_query.reshape(2, half, q_cols), "core", 0, 0)
+        wq = lax.all_gather(w_query, ("zh", "zl"), axis=0)
         head = at(("xl", "yh"))
         start = (core * half, head * HEAD)
         wkv = jnp.where(
@@ -111,47 +186,43 @@
             lax.dynamic_slice(w_key, start, (half, HEAD)),
             lax.dynamic_slice(w_value, start, (half, HEAD)),
         )
-        weights = lax.all_gather(
-            jnp.concatenate([wkv, wq[0], wq[1]], axis=1), ("zh", "zl"), axis=0, tiled=True
-        )
-
-    with jax.named_scope("norm"):
+        wkv = lax.all_gather(lax.all_gather(wkv, "zh"), "zl")
+
+    with jax.named_scope("spread"):
         states = tokens.astype(F32)
-        own = jnp.sum(states * states, axis=1).reshape(2, rows // 2)
-        mean_sq = jnp.sum(gather(own, COL, 16), axis=0).reshape(rows, 1) / (feats * 16)
-        normed = (states * lax.rsqrt(mean_sq + EPS) * norm_gain.astype(F32)[None, :]).astype(BF16)
-
-    with jax.named_scope("spread"):
-        quarters = jnp.transpose(normed.reshape(rows, 4, feats // 4), (1, 0, 2))
-        quarters = lax.all_to_all(quarters, ("xh", "core"), 0, 0)
-        whole = gather(quarters, ("xl", "yh", "yl"), 8)
-        whole = whole.reshape(8, 2, 2, rows, feats // 4)
-        whole = jnp.transpose(whole, (1, 3, 0, 2, 4)).reshape(2 * rows, 4 * feats)
+        squares = jnp.concatenate([p.reshape(2, HEAD) for p in three(jnp.sum(states * states, axis=1))])
+        quarters = jnp.transpose(tokens.reshape(rows, 4, HEAD), (1, 0, 2))
+        extra = jnp.concatenate(
+            [
+                jnp.broadcast_to(squares[None], (4, 6, HEAD)),
+                norm_gain.reshape(4, 1, HEAD),
+                jnp.zeros((4, 9, HEAD), BF16),
+            ],
+            axis=1,
+        )
+        quarters = jnp.concatenate([quarters, extra], axis=1).reshape(2, 1, 2, rows + 16, HEAD)
+        parts = jnp.broadcast_to(quarters, (2, 8, 2, rows + 16, HEAD)).reshape(32, rows + 16, HEAD)
+        parts = lax.all_to_all(parts, ("xh",) + COL, 0, 0).reshape(2, 16, rows + 16, HEAD)
 
     with jax.named_scope("project_kv"):
-        kv_sum = jnp.dot(whole, weights[:, :HEAD], preferred_element_type=F32)
-        parts = lax.all_to_all(kv_sum.reshape(8, rows // 4, HEAD), ("xh", "yl", "core"), 0, 0)
-        parts = jnp.sum(parts.reshape(2, 2, 2, rows // 4, HEAD), axis=(0, 2)).astype(BF16)
-        kv = jnp.concatenate([parts[0], parts[1]], axis=1)
+        whole, kv_sum = project_kv(parts, wkv, rows)
+        chunks = lax.all_to_all(kv_sum.reshape(8, rows // 4, HEAD), ("xh", "yl", "core"), 0, 0)
+        chunks = jnp.sum(chunks.reshape(2, 2, 2, rows // 4, HEAD), axis=(0, 2)).astype(BF16)
+        kv = jnp.concatenate([chunks[0], chunks[1]], axis=1)
 
     with jax.named_scope("gather_kv"):
-        kv = gather(gather(kv, "zh", 4), "zl", 4)
+        kv = lax.all_gather(lax.all_gather(kv, "zh"), "zl")
         mine = gather(kv, ("xh", "yl"), 4)
-        other = swap(mine)
 
     with jax.named_scope("project_q"):
-        q_sum = jnp.dot(whole, weights[:, HEAD:], preferred_element_type=F32)
-        q_sum = q_sum.reshape(2 * rows, 2, q_cols)
-        q_keep = lax.dynamic_index_in_dim(q_sum, core, 1, keepdims=False)
-        q_send = lax.dynamic_index_in_dim(q_sum, 1 - core, 1, keepdims=False)
-        q_sum = (q_keep + swap(q_send)).reshape(2, rows, q_cols)
+        q_sum = project_q(place, whole, swap(whole), wq)
         q_keep = lax.dynamic_index_in_dim(q_sum, xh, 0, keepdims=False)
         q_send = lax.dynamic_index_in_dim(q_sum, 1 - xh, 0, keepdims=False)
         q = (q_keep + lax.ppermute(q_send, "xh", [(0, 1), (1, 0)])).astype(BF16)
 
     with jax.named_scope("attend"):
-        place = jnp.stack([z, xh, core]).astype(jnp.int32)
-        return attend(place, q, mine, other)
+        mine, q = lax.optimization_barrier((mine, q))
+        return attend(place, q, mine, swap(mine))
 
 
 def solution(mesh):

time: 218 us -> 165 us (0.76)
  the two profiles are of different devices: /device:TPU:480 before, /device:TPU:1 now
where the time goes in v3:
time: 165 us; the launch traced here: 164 us
  blocking collectives  78.6 us (48%)
  starting transfers between devices  33.8 us (20%)
  waiting for transfers between devices  21.3 us (13%)
  between operations  13.5 us (8%)
  Pallas kernels  7.8 us (5%)
  local copies, waits for them, and re-layouts  6 us (4%)
  other arithmetic  3.18 us (2%)
    all_gather x2, blocking collectives, on_device(): wkv = lax.all_gather(lax.all_gather(wkv, 'zh'), 'zl')  37.3 us
    all_gather x2, blocking collectives, on_device(): kv = lax.all_gather(lax.all_gather(kv, 'zh'), 'zl')  29.7 us
    ppermute x1, waiting for transfers between devices, on_device(): q = (q_keep + lax.ppermute(q_send, 'xh', [(0, 1), (1, 0)])).astype(BF16)  16.9 us
    ppermute x2, starting transfers between devices, swap(): return lax.ppermute(x, 'core', [(0, 1), (1, 0)])  14.7 us
    all_to_all x1, blocking collectives, on_device(): lax.all_to_all(kv_sum.reshape(8, rows // 4, HEAD), ('xh', 'yl', 'core'),...  11.6 us
    all_to_all x1, starting transfers between devices, on_device(): lax.all_to_all(parts, ('xh',) + COL, 0, 0).reshape(2, 16, rows + 16, HEAD)  10.6 us
    ppermute x1, starting transfers between devices, on_device(): q = (q_keep + lax.ppermute(q_send, 'xh', [(0, 1), (1, 0)])).astype(BF16)  4.83 us
    ppermute x2, waiting for transfers between devices, swap(): return lax.ppermute(x, 'core', [(0, 1), (1, 0)])  3.77 us
  transfers between devices with their start and end apart: 6, of which 2 were waited for; matrix products, arithmetic and copies ran while one was open for 2% of the time, Pallas kernels for 4%

profile of v3, /device:TPU:1, one launch (start us, length us, event | category | flops | bytes accessed | tf_op | source)
XLA Modules:
  0.0 164.2 jit_solution(5120000093894219268)
XLA Ops:
  6.5 1.1 multiply_reduce_fusion
  7.6 1.0 reshape.30
  8.7 0.1 pad.5.clone
  8.8 1.2 maximum_bitcast_fusion
  10.0 1.7 %broadcast_in_dim.25 = bf16[2,8,2,272,128]{4,3,2,1,0:T(8,128)(2,1)} broadcast(bf16[2,2,272,128]{3,2,1,0:T(8,128)(2,1)S(1)} %copy.7), dimensions={0,2,3,4} | broadcast | bytes 2506752 | tf_op jit(solution)/shard_map/spread/broadcast_in_dim | solution.py:204
  11.6 10.6 %all-to-all-start = ((bf16[32,272,128]{2,1,0:T(8,128)(2,1)}), bf16[32,272,128]{2,1,0:T(8,128)(2,1)S(1)}, u32[]{:S(2)}, u32[]{:S(2)}) async-start(bf16[32,272,128]{2,1,0:T(8,128)(2,1)} %bitcast.39), calls=%async_computation | async-start | bytes 4456448 | tf_op jit(solution)/shard_map/spread/all_to_all | solution.py:205
  22.2 0.0 all-gather.7.cloned.1.call-start
  22.3 0.7 all-gather.7.cloned.1.call-update
  23.0 0.8 dynamic-slice_select_fusion
  23.8 21.8 %all-gather = bf16[512,128]{1,0:T(8,128)(2,1)S(1)} all-gather(bf16[128,128]{1,0:T(8,128)(2,1)S(1)} %dynamic-slice_select_fusion), channel_id=2, replica_groups=mesh['zh'=4,'zl'=4,'xh'=2,'xl'=2,'yh'=2,'yl'=2,'core'=2] {'zh'}, dimensions={0}, use_global_device_ids=true | all-gather | bytes 163840 | tf_op jit(solution)/shard_map/weights/all_gather | solution.py:189
  45.6 15.5 %all-gather.1 = bf16[16,128,128]{2,1,0:T(8,128)(2,1)S(1)} all-gather(bf16[4,128,128]{2,1,0:T(8,128)(2,1)S(1)} %bitcast.43), channel_id=3, replica_groups=mesh['zh'=4,'zl'=4,'xh'=2,'xl'=2,'yh'=2,'yl'=2,'core'=2] {'zl'}, dimensions={0}, use_global_device_ids=true | all-gather | bytes 655360 | tf_op jit(solution)/shard_map/weights/all_gather | solution.py:189
  61.1 0.0 all-to-all-done
  61.1 2.4 %project_kv.1 = (bf16[2,256,2048]{2,1,0:T(8,128)(2,1)}, f32[2,256,128]{2,1,0:T(8,128)S(1)}) custom-call(bf16[2,16,272,128]{3,2,1,0:T(8,128)(2,1)S(1)} %bitcast.35, bf16[4,4,128,128]{3,2,1,0:T(8,128)(2,1)S(1)} %bitcast.37), custom_call_target="tpu_custom_call" | custom-call | flops 268435456 | bytes 5242880 | tf_op jit(solution)/shard_map/project_kv/pallas_call | solution.py:124
  63.5 6.8 %collective-permute-start = (bf16[2,256,2048]{2,1,0:T(8,128)(2,1)}, bf16[2,256,2048]{2,1,0:T(8,128)(2,1)}, u32[]{:S(2)}, u32[]{:S(2)}) collective-permute-start(bf16[2,256,2048]{2,1,0:T(8,128)(2,1)} %get-tuple-element.10.mine_ref), channel_id=1, source_target_pairs={{0,1},{1,0},{2,3},{3,2},{4,5},{5,4},{6,7},{7,6},{8,9},{9,8},{10,11... | collective-permute-start | bytes 6291464 | tf_op jit(solution)/shard_map/project_q/ppermute | solution.py:26
  70.3 11.6 %all_to_all.15 = f32[8,64,128]{2,1,0:T(8,128)S(1)} all-to-all(f32[8,64,128]{2,1,0:T(8,128)S(1)} %bitcast.38), channel_id=1, replica_groups=mesh['zh'=4,'zl'=4,'xh'=2,'xl'=2,'yh'=2,'yl'=2,'core'=2] {'xh','yl','core'}, dimensions={0} | all-to-all | bytes 524288 | tf_op jit(solution)/shard_map/project_kv/all_to_all | solution.py:209
  82.0 16.4 %all-gather.2 = bf16[256,256]{1,0:T(8,128)(2,1)S(1)} all-gather(bf16[64,256]{1,0:T(8,128)(2,1)S(1)} %pad_maximum_fusion), channel_id=4, replica_groups=mesh['zh'=4,'zl'=4,'xh'=2,'xl'=2,'yh'=2,'yl'=2,'core'=2] {'zh'}, dimensions={0}, use_global_device_ids=true | all-gather | bytes 163840 | tf_op jit(solution)/shard_map/gather_kv/all_gather | solution.py:214
  98.4 13.2 %all-gather.3 = bf16[16,64,256]{2,1,0:T(8,128)(2,1)S(1)} all-gather(bf16[4,64,256]{2,1,0:T(8,128)(2,1)S(1)} %bitcast.44), channel_id=5, replica_groups=mesh['zh'=4,'zl'=4,'xh'=2,'xl'=2,'yh'=2,'yl'=2,'core'=2] {'zl'}, dimensions={0}, use_global_device_ids=true | all-gather | bytes 655360 | tf_op jit(solution)/shard_map/gather_kv/all_gather | solution.py:214
  111.7 1.6 broadcast_in_dim.26
  113.2 3.6 %all-to-all-start.2 = ((bf16[4,4,4,64,256]{4,3,2,1,0:T(8,128)(2,1)}), bf16[4,4,4,64,256]{4,3,2,1,0:T(8,128)(2,1)S(1)}, u32[]{:S(2)}, u32[]{:S(2)}) async-start(bf16[4,4,4,64,256]{4,3,2,1,0:T(8,128)(2,1)} %broadcast_in_dim.26), calls=%async_computation.2 | async-start | bytes 4194304 | tf_op jit(solution)/shard_map/gather_kv/all_to_all | solution.py:22
  116.8 0.1 pad_add_fusion.place
  116.9 0.0 all-gather.7.cloned.1.call-done
  116.9 0.0 collective-permute-done.other_ref
  116.9 0.0 copy-start
  116.9 1.6 copy-done
  118.5 3.5 %project_q.1 = f32[2,256,256]{2,1,0:T(8,128)S(1)} custom-call(s32[3]{0:T(128)S(1)} %pad_add_fusion.place, bf16[2,256,2048]{2,1,0:T(8,128)(2,1)} %get-tuple-element.10.mine_ref, bf16[2,256,2048]{2,1,0:T(8,128)(2,1)} %collective-permute-done.other_ref, bf16[16,256,256]{2,1,0:T(8,128)(2,1)S(1)} %bitcast.36), custom_call_target="tpu_custom_call" | custom-call | flops 1073741824 | bytes 6291456 | tf_op jit(solution)/shard_map/project_q/pallas_call | solution.py:154
  122.0 4.8 %collective-permute-start.1 = (f32[256,256]{1,0:T(8,128)S(1)}, f32[256,256]{1,0:T(8,128)S(1)}, u32[]{:S(2)}, u32[]{:S(2)}) collective-permute-start(f32[256,256]{1,0:T(8,128)S(1)} %dynamic-slice_bitcast_fusion), channel_id=1, source_target_pairs={{0,16},{16,0},{1,17},{17,1},{2,18},{18,2},{3,19},{19,3},{4,20},{20... | collective-permute-start | bytes 786440 | tf_op jit(solution)/shard_map/project_q/ppermute | solution.py:221
  126.9 16.9 %collective-permute-done.1 = f32[256,256]{1,0:T(8,128)S(1)} collective-permute-done((f32[256,256]{1,0:T(8,128)S(1)}, f32[256,256]{1,0:T(8,128)S(1)}, u32[]{:S(2)}, u32[]{:S(2)}) %collective-permute-start.1) | collective-permute-done | bytes 262176 | tf_op jit(solution)/shard_map/project_q/ppermute | solution.py:221
  143.8 0.0 all-to-all-done.2.mine_ref
  143.8 7.9 %collective-permute-start.2 = (bf16[4,4,4,64,256]{4,3,2,1,0:T(8,128)(2,1)S(1)}, bf16[4,4,4,64,256]{4,3,2,1,0:T(8,128)(2,1)S(1)}, u32[]{:S(2)}, u32[]{:S(2)}) collective-permute-start(bf16[4,4,4,64,256]{4,3,2,1,0:T(8,128)(2,1)S(1)} %all-to-all-done.2.mine_ref), channel_id=1, source_target_pairs={{0,1},{1,0},{2,3},{3,2},{4,5},{5,4},{6,7},{7,6},{8,9},{9,8},{10,11... | collective-permute-start | bytes 6291464 | tf_op jit(solution)/shard_map/attend/ppermute | solution.py:26
  151.7 3.8 %collective-permute-done.2.other_ref = bf16[4,4,4,64,256]{4,3,2,1,0:T(8,128)(2,1)S(1)} collective-permute-done((bf16[4,4,4,64,256]{4,3,2,1,0:T(8,128)(2,1)S(1)}, bf16[4,4,4,64,256]{4,3,2,1,0:T(8,128)(2,1)S(1)}, u32[]{:S(2)}, u32[]{:S(2)}) %collective-permute-start.2) | collective-permute-done | bytes 2097184 | tf_op jit(solution)/shard_map/attend/ppermute | solution.py:26
  155.5 1.9 %attend.1 = bf16[256,256]{1,0:T(8,128)(2,1)} custom-call(s32[3]{0:T(128)S(1)} %pad_add_fusion.place, bf16[256,256]{1,0:T(8,128)(2,1)S(1)} %fusion.q_ref, bf16[4,4,4,64,256]{4,3,2,1,0:T(8,128)(2,1)S(1)} %all-to-all-done.2.mine_ref, bf16[4,4,4,64,256]{4,3,2,1,0:T(8,128)(2,1)S(1)} %collective-permute-done.2.other_ref), custom_call_target="tpu_custom_call" | custom-call | flops 2147483648 | bytes 4194304 | tf_op jit(solution)/shard_map/attend/pallas_call | solution.py:82
  (10 shorter events, 0.2 us)
Async XLA Ops:
  11.6 49.5 %all-to-all-start = ((bf16[32,272,128]{2,1,0:T(8,128)(2,1)}), bf16[32,272,128]{2,1,0:T(8,128)(2,1)S(1)}, u32[]{:S(2)}, u32[]{:S(2)}) async-start(bf16[32,272,128]{2,1,0:T(8,128)(2,1)} %bitcast.39), calls=%async_computation | async-start | bytes 4456448 | tf_op jit(solution)/shard_map/spread/all_to_all | solution.py:205
  22.2 94.7 %all-gather.7.cloned.1.call-start = ((), (), s32[]{:S(2)}) async-start(), calls=%async_computation.3 | async-start | bytes 2228224 | tf_op jit(solution)/shard_map/weights/all_gather | solution.py:181
  63.5 53.4 %collective-permute-start = (bf16[2,256,2048]{2,1,0:T(8,128)(2,1)}, bf16[2,256,2048]{2,1,0:T(8,128)(2,1)}, u32[]{:S(2)}, u32[]{:S(2)}) collective-permute-start(bf16[2,256,2048]{2,1,0:T(8,128)(2,1)} %get-tuple-element.10.mine_ref), channel_id=1, source_target_pairs={{0,1},{1,0},{2,3},{3,2},{4,5},{5,4},{6,7},{7,6},{8,9},{9,8},{10,11... | collective-permute-start | bytes 6291464 | tf_op jit(solution)/shard_map/project_q/ppermute | solution.py:26
  113.2 30.6 %all-to-all-start.2 = ((bf16[4,4,4,64,256]{4,3,2,1,0:T(8,128)(2,1)}), bf16[4,4,4,64,256]{4,3,2,1,0:T(8,128)(2,1)S(1)}, u32[]{:S(2)}, u32[]{:S(2)}) async-start(bf16[4,4,4,64,256]{4,3,2,1,0:T(8,128)(2,1)} %broadcast_in_dim.26), calls=%async_computation.2 | async-start | bytes 4194304 | tf_op jit(solution)/shard_map/gather_kv/all_to_all | solution.py:22
  116.9 1.6 copy-start
  122.0 21.7 %collective-permute-start.1 = (f32[256,256]{1,0:T(8,128)S(1)}, f32[256,256]{1,0:T(8,128)S(1)}, u32[]{:S(2)}, u32[]{:S(2)}) collective-permute-start(f32[256,256]{1,0:T(8,128)S(1)} %dynamic-slice_bitcast_fusion), channel_id=1, source_target_pairs={{0,16},{16,0},{1,17},{17,1},{2,18},{18,2},{3,19},{19,3},{4,20},{20... | collective-permute-start | bytes 786440 | tf_op jit(solution)/shard_map/project_q/ppermute | solution.py:221
  143.8 11.7 %collective-permute-start.2 = (bf16[4,4,4,64,256]{4,3,2,1,0:T(8,128)(2,1)S(1)}, bf16[4,4,4,64,256]{4,3,2,1,0:T(8,128)(2,1)S(1)}, u32[]{:S(2)}, u32[]{:S(2)}) collective-permute-start(bf16[4,4,4,64,256]{4,3,2,1,0:T(8,128)(2,1)S(1)} %all-to-all-done.2.mine_ref), channel_id=1, source_target_pairs={{0,1},{1,0},{2,3},{3,2},{4,5},{5,4},{6,7},{7,6},{8,9},{9,8},{10,11... | collective-permute-start | bytes 6291464 | tf_op jit(solution)/shard_map/attend/ppermute | solution.py:26
Sparse Core Ops, SparseCore 0:
  25.1 69.3 all-gather.6

commit v4 on v3

v4 whole, which is shorter than its diff:
```python
import functools
import math

import jax
import jax.numpy as jnp
from jax import lax
from jax.experimental import pallas as pl
from jax.experimental.pallas import tpu as pltpu
from jax.sharding import Mesh
from jax.sharding import PartitionSpec as P

HEAD = 128
GROUP = 8
EPS = 1e-05
ROW = ("zh", "zl", "xh")
COL = ("xl", "yh", "yl", "core")
F32 = jnp.float32
BF16 = jnp.bfloat16


def gather(x, axes, n):
    return lax.all_to_all(jnp.broadcast_to(x[None], (n, *x.shape)), axes, 0, 0)


def swap(x):
    return lax.ppermute(x, "core", [(0, 1), (1, 0)])


def attend_kernel(place, own_ref, pair_ref, mine_ref, other_ref, out_ref, m_ref, l_ref, acc_ref):
    z, xh, yl, core = place[0], place[1], place[2], place[3]
    rows = own_ref.shape[1]
    scale = HEAD**-0.5 * math.log2(math.e)
    m_ref[...] = jnp.full(m_ref.shape, -1e30, F32)
    l_ref[...] = jnp.zeros(l_ref.shape, F32)
    acc_ref[...] = jnp.zeros(acc_ref.shape, F32)
    chunk = mine_ref.shape[2]
    half = 4 * chunk

    def block(group, masked):
        kv = jnp.concatenate(
            [mine_ref[:, group].reshape(half, 2 * HEAD), other_ref[:, group].reshape(half, 2 * HEAD)], axis=0
        )
        if masked:
            shape = (2 * rows, 2 * half)
            slot = lax.broadcasted_iota(jnp.int32, shape, 1)
            within = lax.rem(slot, half)
            owner = jnp.where(slot < half, core, 1 - core) + 4 * xh + 2 * yl
            key_pos = lax.div(within, chunk) * (2 * rows) + owner * chunk + lax.rem(within, chunk)
            query_pos = lax.rem(z, 4) * (2 * rows) + lax.broadcasted_iota(jnp.int32, shape, 0)
            seen = key_pos <= query_pos
        for head in range(4):
            q_ref = (own_ref, pair_ref)[head // 2]
            at = head % 2 * HEAD
            q = q_ref[:, :, at : at + HEAD].reshape(2 * rows, HEAD)
            s = lax.dot_general(q, kv[:, :HEAD], (((1,), (1,)), ((), ())), preferred_element_type=F32)
            if masked:
                s = jnp.where(seen, s, -1e30)
            m_old = m_ref[head]
            m_new = jnp.maximum(m_old, jnp.max(s, axis=1, keepdims=True))
            alpha = jnp.exp2((m_old - m_new) * scale)
            total = l_ref[head] * alpha
            weights = []
            for j in range(0, s.shape[1], HEAD):
                w = jnp.exp2((s[:, j : j + HEAD] - m_new) * scale)
                total = total + w
                weights.append(w.astype(BF16))
            p = jnp.concatenate(weights, axis=1)
            l_ref[head] = total
            m_ref[head] = m_new
            acc_ref[head] = acc_ref[head] * alpha + jnp.dot(p, kv[:, HEAD:], preferred_element_type=F32)

    mine_group = lax.div(z, 4)

    @pl.loop(0, mine_group)
    def _(group):
        block(group, False)

    block(mine_group, True)
    lane = lax.broadcasted_iota(jnp.int32, (2 * rows, HEAD), 1)
    for side in range(2):
        to = yl if side == 0 else 1 - yl
        stats = jnp.zeros((2 * rows, HEAD), F32)
        for i in range(2):
            head = side * 2 + i
            total = jnp.sum(l_ref[head], axis=1, keepdims=True)
            stats = jnp.where(lane == i, m_ref[head] * scale + jnp.log2(total), stats)
            part = acc_ref[head] / total
            for x in range(2):
                out_ref[2 * x + to, :rows, i * HEAD : (i + 1) * HEAD] = part[x * rows : (x + 1) * rows]
        for x in range(2):
            out_ref[2 * x + to, rows:, :] = jnp.transpose(stats[x * rows : (x + 1) * rows])[:8]


def attend(place, own, pair, mine, other):
    rows, cols = own.shape[1:]
    vmem = pl.BlockSpec(memory_space=pltpu.VMEM)
    return pl.pallas_call(
        attend_kernel,
        out_shape=jax.ShapeDtypeStruct((4, rows + 8, cols), F32),
        in_specs=[pl.BlockSpec(memory_space=pltpu.SMEM), vmem, vmem, vmem, vmem],
        out_specs=vmem,
        scratch_shapes=[pltpu.VMEM((4, 2 * rows, HEAD), F32)] * 3,
        compiler_params=pltpu.CompilerParams(vmem_limit_bytes=40 * 1024 * 1024),
        cost_estimate=pl.CostEstimate(flops=2**31, bytes_accessed=2**22, transcendentals=2**22),
    )(place, own, pair, mine, other)


def merge_kernel(parts_ref, out_ref):
    rows = out_ref.shape[0]
    n = parts_ref.shape[0]
    sums = [parts_ref[i, rows:, :] for i in range(n)]
    most = functools.reduce(jnp.maximum, sums)
    shares = [jnp.exp2(s - most) for s in sums]
    total = functools.reduce(jnp.add, shares)
    columns = [jnp.transpose(jnp.concatenate([s / total] * (HEAD // 8), axis=0)) for s in shares]
    for i in range(2):
        at = slice(i * HEAD, (i + 1) * HEAD)
        out_ref[:, at] = sum(columns[k][:, i : i + 1] * parts_ref[k, :rows, at] for k in range(n)).astype(BF16)


def merge(parts):
    vmem = pl.BlockSpec(memory_space=pltpu.VMEM)
    return pl.pallas_call(
        merge_kernel,
        out_shape=jax.ShapeDtypeStruct((parts.shape[1] - 8, parts.shape[2]), BF16),
        in_specs=[vmem],
        out_specs=vmem,
        compiler_params=pltpu.CompilerParams(vmem_limit_bytes=40 * 1024 * 1024),
    )(parts)


def prep_kernel(tokens_ref, gain_ref, out_ref):
    rows = tokens_ref.shape[0]
    states = tokens_ref[...].astype(F32)
    sums = jnp.sum(states * states, axis=1, keepdims=True)
    left = jnp.transpose(jnp.broadcast_to(sums, (rows, HEAD)))[:1]
    left = jnp.concatenate([left[:, :HEAD], left[:, HEAD:]], axis=0)
    pieces = []
    for _ in range(3):
        piece = left.astype(BF16).astype(F32)
        pieces.append(piece)
        left = left - piece
    for q in range(4):
        at = slice(q * HEAD, (q + 1) * HEAD)
        gain = gain_ref[:, at].astype(F32)
        extra = jnp.concatenate([*pieces, gain, jnp.zeros((9, HEAD), F32)], axis=0).astype(BF16)
        for to in range(out_ref.shape[1]):
            out_ref[q // 2, to, q % 2, :rows] = tokens_ref[:, at]
            out_ref[q // 2, to, q % 2, rows:] = extra


def prep(tokens, gain):
    vmem = pl.BlockSpec(memory_space=pltpu.VMEM)
    return pl.pallas_call(
        prep_kernel,
        out_shape=jax.ShapeDtypeStruct((2, 8, 2, tokens.shape[0] + 16, HEAD), BF16),
        in_specs=[vmem, vmem],
        out_specs=vmem,
        compiler_params=pltpu.CompilerParams(vmem_limit_bytes=40 * 1024 * 1024),
    )(tokens, gain)


def kv_kernel(parts_ref, w_ref, t_ref, kv_ref):
    rows = t_ref.shape[1]
    blocks = parts_ref.shape[1]
    for xh in range(2):
        extra = [parts_ref[xh, c, rows:].astype(F32) for c in range(blocks)]
        squares = functools.reduce(jnp.add, extra)
        mean_sq = (squares[4:6] + squares[2:4] + squares[0:2]) / (blocks * 4 * HEAD)
        inverse = lax.rsqrt(mean_sq + EPS)
        inverse = jnp.concatenate(
            [jnp.transpose(jnp.broadcast_to(inverse[i : i + 1], (HEAD, HEAD))) for i in range(2)], axis=0
        )
        total = jnp.zeros((rows, HEAD), F32)
        for c in range(0, blocks, 2):
            for d in (c, c + 1):
                t = parts_ref[xh, d, :rows].astype(F32) * inverse * extra[d][6:7]
                t_ref[xh, :, d * HEAD : (d + 1) * HEAD] = t.astype(BF16)
            w = jnp.concatenate([w_ref[d % 4, d // 4] for d in (c, c + 1)], axis=0)
            total += jnp.dot(t_ref[xh, :, c * HEAD : (c + 2) * HEAD], w, preferred_element_type=F32)
        kv_ref[xh] = total


def project_kv(parts, w, rows):
    vmem = pl.BlockSpec(memory_space=pltpu.VMEM)
    blocks = parts.shape[1]
    return pl.pallas_call(
        kv_kernel,
        out_shape=(
            jax.ShapeDtypeStruct((2, rows, blocks * HEAD), BF16),
            jax.ShapeDtypeStruct((2, rows, HEAD), F32),
        ),
        in_specs=[vmem, vmem],
        out_specs=(vmem, vmem),
        compiler_params=pltpu.CompilerParams(vmem_limit_bytes=40 * 1024 * 1024),
        cost_estimate=pl.CostEstimate(flops=2**28, bytes_accessed=5 * 2**20, transcendentals=0),
    )(parts, w)


def q_kernel(place, mine_ref, other_ref, w_ref, out_ref):
    core = place[3]
    rows = mine_ref.shape[1]
    half = w_ref.shape[1] // 2
    for xh in range(2):
        total = jnp.zeros((rows, w_ref.shape[2]), F32)
        for c in range(w_ref.shape[0]):
            t = jnp.concatenate([ref[xh, :, c * half : (c + 1) * half] for ref in (mine_ref, other_ref)], axis=1)
            w = jnp.concatenate(
                [w_ref[c, pl.ds(pl.multiple_of(at * half, half), half)] for at in (core, 1 - core)], axis=0
            )
            total += jnp.dot(t, w, preferred_element_type=F32)
        out_ref[xh] = total


def project_q(place, mine, other, w):
    vmem = pl.BlockSpec(memory_space=pltpu.VMEM)
    return pl.pallas_call(
        q_kernel,
        out_shape=jax.ShapeDtypeStruct((*mine.shape[:2], w.shape[2]), F32),
        in_specs=[pl.BlockSpec(memory_space=pltpu.SMEM), vmem, vmem, vmem],
        out_specs=vmem,
        compiler_params=pltpu.CompilerParams(vmem_limit_bytes=40 * 1024 * 1024),
        cost_estimate=pl.CostEstimate(flops=2**30, bytes_accessed=6 * 2**20, transcendentals=0),
    )(place, mine, other, w)


def on_device(tokens, norm_gain, w_query, w_key, w_value):
    at = lax.axis_index
    core = at("core")
    place = jnp.stack([at(("zh", "zl")), at("xh"), at("yl"), core]).astype(jnp.int32)
    rows, feats = tokens.shape
    half = w_key.shape[0] // 2

    with jax.named_scope("weights"):
        wq = lax.all_gather(w_query, ("zh", "zl"), axis=0)
        head = at(("xl", "yh"))
        start = (core * half, head * HEAD)
        wkv = jnp.where(
            at("yl") == 0,
            lax.dynamic_slice(w_key, start, (half, HEAD)),
            lax.dynamic_slice(w_value, start, (half, HEAD)),
        )
        wkv = lax.all_gather(lax.all_gather(wkv, "zh"), "zl")

    with jax.named_scope("spread"):
        parts = prep(tokens, norm_gain.reshape(1, feats))
        parts = lax.all_to_all(parts.reshape(32, rows + 16, HEAD), ("xh",) + COL, 0, 0)
        parts = parts.reshape(2, 16, rows + 16, HEAD)

    with jax.named_scope("project_kv"):
        whole, kv_sum = project_kv(parts, wkv, rows)
        chunks = lax.all_to_all(kv_sum.reshape(8, rows // 4, HEAD), ("xh", "yl", "core"), 0, 0)
        chunks = jnp.sum(chunks.reshape(2, 2, 2, rows // 4, HEAD), axis=(0, 2)).astype(BF16)
        kv = jnp.concatenate([chunks[0], chunks[1]], axis=1)

    with jax.named_scope("gather_kv"):
        kv = gather(gather(kv, "zh", 4), "zl", 4)

    with jax.named_scope("project_q"):
        q = project_q(place, whole, swap(whole), wq)
        q = (q + lax.ppermute(q, "xh", [(0, 1), (1, 0)])).astype(BF16)
        pair = lax.ppermute(q, "yl", [(0, 1), (1, 0)])

    with jax.named_scope("attend"):
        out = attend(place, q, pair, kv, swap(kv))
        return merge(lax.all_to_all(out, ("xh", "yl"), 0, 0))


def solution(mesh):
    fine = Mesh(mesh.devices.reshape(4, 4, 2, 2, 2, 2, 2), ("zh", "zl", "xh", "xl", "yh", "yl", "core"))
    return jax.shard_map(
        on_device,
        mesh=fine,
        in_specs=(P(ROW, COL), P(COL), P(ROW, COL), P(ROW, None), P(ROW, None)),
        out_specs=P(ROW, COL),
        check_vma=False,
    )
```

time: 165 us -> 164 us (level)
  the two profiles are of different devices: /device:TPU:1 before, /device:TPU:16 now
where the time goes in v4:
time: 164 us; the launch traced here: 163 us
  blocking collectives  94.4 us (58%)
  starting transfers between devices  23.3 us (14%)
  waiting for transfers between devices  15.6 us (10%)
  between operations  13.5 us (8%)
  Pallas kernels  9.66 us (6%)
  local copies, waits for them, and re-layouts  5.42 us (3%)
    all_gather x2, blocking collectives, on_device(): wkv = lax.all_gather(lax.all_gather(wkv, 'zh'), 'zl')  41.5 us
    all_to_all x1, blocking collectives, gather(): return lax.all_to_all(jnp.broadcast_to(x[None], (n, *x.shape)), axes, 0, 0)  23.2 us
    all_to_all x1, blocking collectives, on_device(): return merge(lax.all_to_all(out, ('xh', 'yl'), 0, 0))  17.5 us
    all_to_all x1, blocking collectives, on_device(): lax.all_to_all(kv_sum.reshape(8, rows // 4, HEAD), ('xh', 'yl', 'core'),...  12.2 us
    all_to_all x1, starting transfers between devices, on_device(): lax.all_to_all(parts.reshape(32, rows + 16, HEAD), ('xh',) + COL, 0, 0)  9.44 us
    ppermute x1, waiting for transfers between devices, on_device(): pair = lax.ppermute(q, 'yl', [(0, 1), (1, 0)])  5.69 us
    ppermute x1, waiting for transfers between devices, on_device(): q = (q + lax.ppermute(q, 'xh', [(0, 1), (1, 0)])).astype(BF16)  4.91 us
    all_to_all x1, waiting for transfers between devices, gather(): return lax.all_to_all(jnp.broadcast_to(x[None], (n, *x.shape)), axes, 0, 0)  4.32 us
  transfers between devices with their start and end apart: 7, of which 3 were waited for; matrix products, arithmetic and copies ran while one was open for 1% of the time, Pallas kernels for 3%

profile of v4, /device:TPU:16, one launch (start us, length us, event | category | flops | bytes accessed | tf_op | source)
XLA Modules:
  0.0 162.9 jit_solution(16001929599479477366)
XLA Ops:
  6.5 0.7 reshape.17.gain_ref
  7.2 0.9 copy-done.2
  8.2 0.3 spread.1
  8.5 1.3 copy-done
  9.8 9.4 %all-to-all-start = ((bf16[32,272,128]{2,1,0:T(8,128)(2,1)}), bf16[32,272,128]{2,1,0:T(8,128)(2,1)S(1)}, u32[]{:S(2)}, u32[]{:S(2)}) async-start(bf16[32,272,128]{2,1,0:T(8,128)(2,1)} %bitcast.16), calls=%async_computation | async-start | bytes 4456448 | tf_op jit(solution)/shard_map/spread/all_to_all | solution.py:247
  19.3 0.0 all-gather.5.cloned.1.call-start
  19.3 0.7 all-gather.5.cloned.1.call-update
  20.0 0.8 dynamic-slice_select_fusion
  20.8 23.9 %all-gather = bf16[512,128]{1,0:T(8,128)(2,1)S(1)} all-gather(bf16[128,128]{1,0:T(8,128)(2,1)S(1)} %dynamic-slice_select_fusion), channel_id=2, replica_groups=mesh['zh'=4,'zl'=4,'xh'=2,'xl'=2,'yh'=2,'yl'=2,'core'=2] {'zh'}, dimensions={0}, use_global_device_ids=true | all-gather | bytes 163840 | tf_op jit(solution)/shard_map/weights/all_gather | solution.py:243
  44.8 17.6 %all-gather.1 = bf16[16,128,128]{2,1,0:T(8,128)(2,1)S(1)} all-gather(bf16[4,128,128]{2,1,0:T(8,128)(2,1)S(1)} %bitcast.21), channel_id=3, replica_groups=mesh['zh'=4,'zl'=4,'xh'=2,'xl'=2,'yh'=2,'yl'=2,'core'=2] {'zl'}, dimensions={0}, use_global_device_ids=true | all-gather | bytes 655360 | tf_op jit(solution)/shard_map/weights/all_gather | solution.py:243
  62.3 0.0 all-to-all-done
  62.3 2.4 %project_kv.1 = (bf16[2,256,2048]{2,1,0:T(8,128)(2,1)}, f32[2,256,128]{2,1,0:T(8,128)S(1)}) custom-call(bf16[2,16,272,128]{3,2,1,0:T(8,128)(2,1)S(1)} %bitcast.15, bf16[4,4,128,128]{3,2,1,0:T(8,128)(2,1)S(1)} %bitcast.18), custom_call_target="tpu_custom_call" | custom-call | flops 268435456 | bytes 5242880 | tf_op jit(solution)/shard_map/project_kv/pallas_call | solution.py:187
  64.7 1.9 %collective-permute-start = (bf16[2,256,2048]{2,1,0:T(8,128)(2,1)}, bf16[2,256,2048]{2,1,0:T(8,128)(2,1)S(1)}, u32[]{:S(2)}, u32[]{:S(2)}) collective-permute-start(bf16[2,256,2048]{2,1,0:T(8,128)(2,1)} %get-tuple-element.7.mine_ref), channel_id=1, source_target_pairs={{0,1},{1,0},{2,3},{3,2},{4,5},{5,4},{6,7},{7,6},{8,9},{9,8},{10,11... | collective-permute-start | bytes 6291464 | tf_op jit(solution)/shard_map/project_q/ppermute | solution.py:26
  66.7 12.2 %all_to_all.25 = f32[8,64,128]{2,1,0:T(8,128)S(1)} all-to-all(f32[8,64,128]{2,1,0:T(8,128)S(1)} %bitcast.19), channel_id=1, replica_groups=mesh['zh'=4,'zl'=4,'xh'=2,'xl'=2,'yh'=2,'yl'=2,'core'=2] {'xh','yl','core'}, dimensions={0} | all-to-all | bytes 524288 | tf_op jit(solution)/shard_map/project_kv/all_to_all | solution.py:252
  78.9 23.2 %all_to_all.26 = bf16[4,64,256]{2,1,0:T(8,128)(2,1)S(1)} all-to-all(bf16[4,64,256]{2,1,0:T(8,128)(2,1)S(1)} %broadcast_in_dim.4), channel_id=1, replica_groups=mesh['zh'=4,'zl'=4,'xh'=2,'xl'=2,'yh'=2,'yl'=2,'core'=2] {'zh'}, dimensions={0} | all-to-all | bytes 262144 | tf_op jit(solution)/shard_map/gather_kv/all_to_all | solution.py:22
  102.1 0.8 broadcast_in_dim.5
  102.9 3.5 %all-to-all-start.3 = ((bf16[4,4,64,256]{3,2,1,0:T(8,128)(2,1)}), bf16[4,4,64,256]{3,2,1,0:T(8,128)(2,1)S(1)}, u32[]{:S(2)}, u32[]{:S(2)}) async-start(bf16[4,4,64,256]{3,2,1,0:T(8,128)(2,1)} %broadcast_in_dim.5), calls=%async_computation.3 | async-start | bytes 1048576 | tf_op jit(solution)/shard_map/gather_kv/all_to_all | solution.py:22
  106.4 0.1 pad_add_fusion.place
  106.5 0.0 collective-permute-done.other_ref
  106.5 1.6 copy-done.1
  108.1 2.8 %project_q.1 = f32[2,256,256]{2,1,0:T(8,128)S(1)} custom-call(s32[4]{0:T(128)S(1)} %pad_add_fusion.place, bf16[2,256,2048]{2,1,0:T(8,128)(2,1)} %get-tuple-element.7.mine_ref, bf16[2,256,2048]{2,1,0:T(8,128)(2,1)S(1)} %collective-permute-done.other_ref, bf16[16,256,256]{2,1,0:T(8,128)(2,1)S(1)} %bitcast.17), custom_call_target="tpu_custom_call" | custom-call | flops 1073741824 | bytes 6291456 | tf_op jit(solution)/shard_map/project_q/pallas_call | solution.py:217
  110.9 4.0 %collective-permute-start.1 = (f32[2,256,256]{2,1,0:T(8,128)S(1)}, f32[2,256,256]{2,1,0:T(8,128)S(1)}, u32[]{:S(2)}, u32[]{:S(2)}) collective-permute-start(f32[2,256,256]{2,1,0:T(8,128)S(1)} %project_q.1), channel_id=1, source_target_pairs={{0,16},{16,0},{1,17},{17,1},{2,18},{18,2},{3,19},{19,3},{4,20},{20... | collective-permute-start | bytes 1572872 | tf_op jit(solution)/shard_map/project_q/ppermute | solution.py:261
  115.0 4.3 %all-to-all-done.3.mine_ref = bf16[4,4,64,256]{3,2,1,0:T(8,128)(2,1)S(1)} async-done(((bf16[4,4,64,256]{3,2,1,0:T(8,128)(2,1)}), bf16[4,4,64,256]{3,2,1,0:T(8,128)(2,1)S(1)}, u32[]{:S(2)}, u32[]{:S(2)}) %all-to-all-start.3) | async-done | bytes 524320 | tf_op jit(solution)/shard_map/gather_kv/all_to_all | solution.py:22
  119.3 1.9 %collective-permute-start.3 = (bf16[4,4,64,256]{3,2,1,0:T(8,128)(2,1)S(1)}, bf16[4,4,64,256]{3,2,1,0:T(8,128)(2,1)S(1)}, u32[]{:S(2)}, u32[]{:S(2)}) collective-permute-start(bf16[4,4,64,256]{3,2,1,0:T(8,128)(2,1)S(1)} %all-to-all-done.3.mine_ref), channel_id=1, source_target_pairs={{0,1},{1,0},{2,3},{3,2},{4,5},{5,4},{6,7},{7,6},{8,9},{9,8},{10,11... | collective-permute-start | bytes 1572872 | tf_op jit(solution)/shard_map/attend/ppermute | solution.py:26
  121.2 4.9 %collective-permute-done.1 = f32[2,256,256]{2,1,0:T(8,128)S(1)} collective-permute-done((f32[2,256,256]{2,1,0:T(8,128)S(1)}, f32[2,256,256]{2,1,0:T(8,128)S(1)}, u32[]{:S(2)}, u32[]{:S(2)}) %collective-permute-start.1) | collective-permute-done | bytes 524320 | tf_op jit(solution)/shard_map/project_q/ppermute | solution.py:261
  126.1 0.1 add_convert_fusion.own_ref
  126.2 2.6 %collective-permute-start.2 = (bf16[2,256,256]{2,1,0:T(8,128)(2,1)S(1)}, bf16[2,256,256]{2,1,0:T(8,128)(2,1)S(1)}, u32[]{:S(2)}, u32[]{:S(2)}) collective-permute-start(bf16[2,256,256]{2,1,0:T(8,128)(2,1)S(1)} %add_convert_fusion.own_ref), channel_id=1, source_target_pairs={{0,2},{2,0},{1,3},{3,1},{4,6},{6,4},{5,7},{7,5},{8,10},{10,8},{9,1... | collective-permute-start | bytes 786440 | tf_op jit(solution)/shard_map/project_q/ppermute | solution.py:262
  128.7 0.0 collective-permute-done.3.other_ref
  128.8 5.7 %collective-permute-done.2.pair_ref = bf16[2,256,256]{2,1,0:T(8,128)(2,1)S(1)} collective-permute-done((bf16[2,256,256]{2,1,0:T(8,128)(2,1)S(1)}, bf16[2,256,256]{2,1,0:T(8,128)(2,1)S(1)}, u32[]{:S(2)}, u32[]{:S(2)}) %collective-permute-start.2) | collective-permute-done | bytes 262176 | tf_op jit(solution)/shard_map/project_q/ppermute | solution.py:262
  134.4 2.9 %attend.2 = f32[4,264,256]{2,1,0:T(8,128)S(1)} custom-call(s32[4]{0:T(128)S(1)} %pad_add_fusion.place, bf16[2,256,256]{2,1,0:T(8,128)(2,1)S(1)} %add_convert_fusion.own_ref, bf16[2,256,256]{2,1,0:T(8,128)(2,1)S(1)} %collective-permute-done.2.pair_ref, bf16[4,4,64,256]{3,2,1,0:T(8,128)(2,1)S(1)} %all-to-all-done.3.mine_ref, ...), custom_call_target="tpu_custom_call" | custom-call | flops 2147483648 | bytes 4194304 | tf_op jit(solution)/shard_map/attend/pallas_call | solution.py:97
  137.4 17.5 %all_to_all.27.parts_ref = f32[4,264,256]{2,1,0:T(8,128)S(1)} all-to-all(f32[4,264,256]{2,1,0:T(8,128)S(1)} %attend.2), channel_id=1, replica_groups=mesh['zh'=4,'zl'=4,'xh'=2,'xl'=2,'yh'=2,'yl'=2,'core'=2] {'xh','yl'}, dimensions={0} | all-to-all | bytes 2162688 | tf_op jit(solution)/shard_map/attend/all_to_all | solution.py:266
  154.9 1.2 attend.3
  (8 shorter events, 0.0 us)
Async XLA Ops:
  7.2 0.9 copy-start.2
  8.5 1.3 copy-start
  9.8 52.5 %all-to-all-start = ((bf16[32,272,128]{2,1,0:T(8,128)(2,1)}), bf16[32,272,128]{2,1,0:T(8,128)(2,1)S(1)}, u32[]{:S(2)}, u32[]{:S(2)}) async-start(bf16[32,272,128]{2,1,0:T(8,128)(2,1)} %bitcast.16), calls=%async_computation | async-start | bytes 4456448 | tf_op jit(solution)/shard_map/spread/all_to_all | solution.py:247
  19.3 87.2 %all-gather.5.cloned.1.call-start = ((), (), s32[]{:S(2)}) async-start(), calls=%async_computation.5 | async-start | bytes 2228224 | tf_op jit(solution)/shard_map/weights/all_gather | solution.py:235
  64.7 41.8 %collective-permute-start = (bf16[2,256,2048]{2,1,0:T(8,128)(2,1)}, bf16[2,256,2048]{2,1,0:T(8,128)(2,1)S(1)}, u32[]{:S(2)}, u32[]{:S(2)}) collective-permute-start(bf16[2,256,2048]{2,1,0:T(8,128)(2,1)} %get-tuple-element.7.mine_ref), channel_id=1, source_target_pairs={{0,1},{1,0},{2,3},{3,2},{4,5},{5,4},{6,7},{7,6},{8,9},{9,8},{10,11... | collective-permute-start | bytes 6291464 | tf_op jit(solution)/shard_map/project_q/ppermute | solution.py:26
  102.9 16.3 %all-to-all-start.3 = ((bf16[4,4,64,256]{3,2,1,0:T(8,128)(2,1)}), bf16[4,4,64,256]{3,2,1,0:T(8,128)(2,1)S(1)}, u32[]{:S(2)}, u32[]{:S(2)}) async-start(bf16[4,4,64,256]{3,2,1,0:T(8,128)(2,1)} %broadcast_in_dim.5), calls=%async_computation.3 | async-start | bytes 1048576 | tf_op jit(solution)/shard_map/gather_kv/all_to_all | solution.py:22
  106.5 1.6 copy-start.1
  110.9 15.2 %collective-permute-start.1 = (f32[2,256,256]{2,1,0:T(8,128)S(1)}, f32[2,256,256]{2,1,0:T(8,128)S(1)}, u32[]{:S(2)}, u32[]{:S(2)}) collective-permute-start(f32[2,256,256]{2,1,0:T(8,128)S(1)} %project_q.1), channel_id=1, source_target_pairs={{0,16},{16,0},{1,17},{17,1},{2,18},{18,2},{3,19},{19,3},{4,20},{20... | collective-permute-start | bytes 1572872 | tf_op jit(solution)/shard_map/project_q/ppermute | solution.py:261
  119.3 9.5 %collective-permute-start.3 = (bf16[4,4,64,256]{3,2,1,0:T(8,128)(2,1)S(1)}, bf16[4,4,64,256]{3,2,1,0:T(8,128)(2,1)S(1)}, u32[]{:S(2)}, u32[]{:S(2)}) collective-permute-start(bf16[4,4,64,256]{3,2,1,0:T(8,128)(2,1)S(1)} %all-to-all-done.3.mine_ref), channel_id=1, source_target_pairs={{0,1},{1,0},{2,3},{3,2},{4,5},{5,4},{6,7},{7,6},{8,9},{9,8},{10,11... | collective-permute-start | bytes 1572872 | tf_op jit(solution)/shard_map/attend/ppermute | solution.py:26
  126.2 8.3 %collective-permute-start.2 = (bf16[2,256,256]{2,1,0:T(8,128)(2,1)S(1)}, bf16[2,256,256]{2,1,0:T(8,128)(2,1)S(1)}, u32[]{:S(2)}, u32[]{:S(2)}) collective-permute-start(bf16[2,256,256]{2,1,0:T(8,128)(2,1)S(1)} %add_convert_fusion.own_ref), channel_id=1, source_target_pairs={{0,2},{2,0},{1,3},{3,1},{4,6},{6,4},{5,7},{7,5},{8,10},{10,8},{9,1... | collective-permute-start | bytes 786440 | tf_op jit(solution)/shard_map/project_q/ppermute | solution.py:262
Sparse Core Ops, SparseCore 0:
  22.2 79.9 all-gather.4

commit v5 on v4

--- a/solution.py
+++ b/solution.py
@@ -253,11 +253,15 @@
         chunks = jnp.sum(chunks.reshape(2, 2, 2, rows // 4, HEAD), axis=(0, 2)).astype(BF16)
         kv = jnp.concatenate([chunks[0], chunks[1]], axis=1)
 
+    with jax.named_scope("project_q"):
+        kv, whole = lax.optimization_barrier((kv, whole))
+        q = project_q(place, whole, swap(whole), wq)
+
     with jax.named_scope("gather_kv"):
-        kv = gather(gather(kv, "zh", 4), "zl", 4)
-
-    with jax.named_scope("project_q"):
-        q = project_q(place, whole, swap(whole), wq)
+        kv, q = lax.optimization_barrier((gather(kv, "zh", 4), q))
+        kv = gather(kv, "zl", 4)
+
+    with jax.named_scope("swap_q"):
         q = (q + lax.ppermute(q, "xh", [(0, 1), (1, 0)])).astype(BF16)
         pair = lax.ppermute(q, "yl", [(0, 1), (1, 0)])
 

time: 164 us -> 167 us (1.018)
  blocking collectives: 94.4 us -> 74.3 us
  starting transfers between devices: 23.3 us -> 34.7 us
  waiting for transfers between devices: 15.6 us -> 26.3 us
  local copies, waits for them, and re-layouts: 5.42 us -> 9.03 us
  Pallas kernels: 9.66 us -> 7.42 us
    all_to_all x1 -> x0, blocking collectives: 23.2 us -> none  [gather(): return lax.all_to_all(jnp.broadcast_to(x[None], (n, *x.shape)), axes, 0, 0)]
    all_gather x1, waiting for transfers between devices: 0.01 us -> 13.4 us  [on_device(): wq = lax.all_gather(w_query, ('zh', 'zl'), axis=0)]
    all_to_all x1 -> x2, starting transfers between devices: 3.47 us -> 12 us  [gather(): return lax.all_to_all(jnp.broadcast_to(x[None], (n, *x.shape)), axes, 0, 0)]
    ppermute x1, waiting for transfers between devices: 4.91 us -> 0.36 us  [on_device(): q = (q + lax.ppermute(q, 'xh', [(0, 1), (1, 0)])).astype(BF16)]
    all_to_all x1, blocking collectives: 17.5 us -> 20.8 us  [on_device(): return merge(lax.all_to_all(out, ('xh', 'yl'), 0, 0))]
    unnamed x6 -> x10, local copies, waits for them, and re-layouts: 3.88 us -> 6.83 us
    ppermute x1, starting transfers between devices: 4 us -> 6.02 us  [on_device(): q = (q + lax.ppermute(q, 'xh', [(0, 1), (1, 0)])).astype(BF16)]
    all_to_all x1 -> x2, waiting for transfers between devices: 4.32 us -> 5.02 us  [gather(): return lax.all_to_all(jnp.broadcast_to(x[None], (n, *x.shape)), axes, 0, 0)]
  transfers between devices with their start and end apart: 7 -> 8, of which waited for: 3 -> 4; matrix products, arithmetic and copies ran while one was open for 1% -> 1% of each run, Pallas kernels for 3% -> 2%
where the time goes in v5:
time: 167 us; the launch traced here: 166 us
  blocking collectives  74.3 us (44%)
  starting transfers between devices  34.7 us (21%)
  waiting for transfers between devices  26.3 us (16%)
  between operations  13.5 us (8%)
  local copies, waits for them, and re-layouts  9.03 us (5%)
  Pallas kernels  7.42 us (4%)
    all_gather x2, blocking collectives, on_device(): wkv = lax.all_gather(lax.all_gather(wkv, 'zh'), 'zl')  41.5 us
    all_to_all x1, blocking collectives, on_device(): return merge(lax.all_to_all(out, ('xh', 'yl'), 0, 0))  20.8 us
    all_gather x1, waiting for transfers between devices, on_device(): wq = lax.all_gather(w_query, ('zh', 'zl'), axis=0)  13.4 us
    all_to_all x1, blocking collectives, on_device(): lax.all_to_all(kv_sum.reshape(8, rows // 4, HEAD), ('xh', 'yl', 'core'),...  12.1 us
    all_to_all x2, starting transfers between devices, gather(): return lax.all_to_all(jnp.broadcast_to(x[None], (n, *x.shape)), axes, 0, 0)  12 us
    all_to_all x1, starting transfers between devices, on_device(): lax.all_to_all(parts.reshape(32, rows + 16, HEAD), ('xh',) + COL, 0, 0)  9.44 us
    ppermute x1, waiting for transfers between devices, on_device(): pair = lax.ppermute(q, 'yl', [(0, 1), (1, 0)])  6.88 us
    unnamed x10, local copies, waits for them, and re-layouts  6.83 us
  transfers between devices with their start and end apart: 8, of which 4 were waited for; matrix products, arithmetic and copies ran while one was open for 1% of the time, Pallas kernels for 2%

profile of v5, /device:TPU:16, one launch (start us, length us, event | category | flops | bytes accessed | tf_op | source)
XLA Modules:
  0.0 166.3 jit_solution(5845335267928916289)
XLA Ops:
  6.5 0.7 reshape.17.gain_ref
  7.2 0.9 copy-done.4
  8.2 0.3 spread.1
  8.5 1.4 copy-done
  9.9 9.4 %all-to-all-start = ((bf16[32,272,128]{2,1,0:T(8,128)(2,1)}), bf16[32,272,128]{2,1,0:T(8,128)(2,1)S(1)}, u32[]{:S(2)}, u32[]{:S(2)}) async-start(bf16[32,272,128]{2,1,0:T(8,128)(2,1)} %bitcast.16), calls=%async_computation | async-start | bytes 4456448 | tf_op jit(solution)/shard_map/spread/all_to_all | solution.py:247
  19.4 0.7 all-gather.5.cloned.1.call-update
  20.1 0.8 dynamic-slice_select_fusion
  20.9 23.9 %all-gather = bf16[512,128]{1,0:T(8,128)(2,1)S(1)} all-gather(bf16[128,128]{1,0:T(8,128)(2,1)S(1)} %dynamic-slice_select_fusion), channel_id=2, replica_groups=mesh['zh'=4,'zl'=4,'xh'=2,'xl'=2,'yh'=2,'yl'=2,'core'=2] {'zh'}, dimensions={0}, use_global_device_ids=true | all-gather | bytes 163840 | tf_op jit(solution)/shard_map/weights/all_gather | solution.py:243
  44.8 17.6 %all-gather.1 = bf16[16,128,128]{2,1,0:T(8,128)(2,1)S(1)} all-gather(bf16[4,128,128]{2,1,0:T(8,128)(2,1)S(1)} %bitcast.21), channel_id=3, replica_groups=mesh['zh'=4,'zl'=4,'xh'=2,'xl'=2,'yh'=2,'yl'=2,'core'=2] {'zl'}, dimensions={0}, use_global_device_ids=true | all-gather | bytes 655360 | tf_op jit(solution)/shard_map/weights/all_gather | solution.py:243
  62.3 1.2 project_kv.1
  63.6 1.3 copy-done.2
  64.9 12.1 %all_to_all.25 = f32[8,64,128]{2,1,0:T(8,128)S(1)} all-to-all(f32[8,64,128]{2,1,0:T(8,128)S(1)} %bitcast.19), channel_id=1, replica_groups=mesh['zh'=4,'zl'=4,'xh'=2,'xl'=2,'yh'=2,'yl'=2,'core'=2] {'xh','yl','core'}, dimensions={0} | all-to-all | bytes 524288 | tf_op jit(solution)/shard_map/project_kv/all_to_all | solution.py:252
  77.1 1.9 %collective-permute-start = (bf16[2,256,2048]{2,1,0:T(8,128)(2,1)}, bf16[2,256,2048]{2,1,0:T(8,128)(2,1)S(1)}, u32[]{:S(2)}, u32[]{:S(2)}) collective-permute-start(bf16[2,256,2048]{2,1,0:T(8,128)(2,1)} %copy-done.2), channel_id=1, source_target_pairs={{0,1},{1,0},{2,3},{3,2},{4,5},{5,4},{6,7},{7,6},{8,9},{9,8},{10,11... | collective-permute-start | bytes 6291464 | tf_op jit(solution)/shard_map/project_q/ppermute | solution.py:26
  79.0 0.7 broadcast_in_dim.4
  79.7 7.9 %all-to-all-start.2 = ((bf16[4,64,256]{2,1,0:T(8,128)(2,1)}), bf16[4,64,256]{2,1,0:T(8,128)(2,1)S(1)}, u32[]{:S(2)}, u32[]{:S(2)}) async-start(bf16[4,64,256]{2,1,0:T(8,128)(2,1)} %broadcast_in_dim.4), calls=%async_computation.2 | async-start | bytes 262144 | tf_op jit(solution)/shard_map/gather_kv/all_to_all | solution.py:22
  87.5 0.1 pad_add_fusion.place
  87.6 13.4 %all-gather.5.cloned.1.call-done = bf16[4096,256]{1,0:T(8,128)(2,1)} async-done(((bf16[256,256]{1,0:T(8,128)(2,1)}), bf16[4096,256]{1,0:T(8,128)(2,1)}) %all-gather.5.cloned.1.call-update) | async-done | bytes 2097168 | tf_op jit(solution)/shard_map/weights/all_gather | solution.py:235
  101.0 1.6 copy-done.1
  102.6 1.6 copy-done.3
  104.2 1.8 %project_q.1 = f32[2,256,256]{2,1,0:T(8,128)S(1)} custom-call(s32[4]{0:T(128)S(1)} %pad_add_fusion.place, bf16[2,256,2048]{2,1,0:T(8,128)(2,1)S(1)} %copy-done.3, bf16[2,256,2048]{2,1,0:T(8,128)(2,1)S(1)} %collective-permute-done.other_ref, bf16[16,256,256]{2,1,0:T(8,128)(2,1)S(1)} %bitcast.17), custom_call_target="tpu_custom_call" | custom-call | flops 1073741824 | bytes 6291456 | tf_op jit(solution)/shard_map/project_q/pallas_call | solution.py:217
  106.0 0.8 broadcast_in_dim.5
  106.8 4.1 %all-to-all-start.3 = ((bf16[4,4,64,256]{3,2,1,0:T(8,128)(2,1)}), bf16[4,4,64,256]{3,2,1,0:T(8,128)(2,1)S(1)}, u32[]{:S(2)}, u32[]{:S(2)}) async-start(bf16[4,4,64,256]{3,2,1,0:T(8,128)(2,1)} %broadcast_in_dim.5), calls=%async_computation.3 | async-start | bytes 1048576 | tf_op jit(solution)/shard_map/gather_kv/all_to_all | solution.py:22
  110.9 6.0 %collective-permute-start.1 = (f32[2,256,256]{2,1,0:T(8,128)S(1)}, f32[2,256,256]{2,1,0:T(8,128)S(1)}, u32[]{:S(2)}, u32[]{:S(2)}) collective-permute-start(f32[2,256,256]{2,1,0:T(8,128)S(1)} %project_q.1), channel_id=1, source_target_pairs={{0,16},{16,0},{1,17},{17,1},{2,18},{18,2},{3,19},{19,3},{4,20},{20... | collective-permute-start | bytes 1572872 | tf_op jit(solution)/shard_map/swap_q/ppermute | solution.py:265
  116.9 5.0 %all-to-all-done.3.mine_ref = bf16[4,4,64,256]{3,2,1,0:T(8,128)(2,1)S(1)} async-done(((bf16[4,4,64,256]{3,2,1,0:T(8,128)(2,1)}), bf16[4,4,64,256]{3,2,1,0:T(8,128)(2,1)S(1)}, u32[]{:S(2)}, u32[]{:S(2)}) %all-to-all-start.3) | async-done | bytes 524320 | tf_op jit(solution)/shard_map/gather_kv/all_to_all | solution.py:22
  122.0 1.9 %collective-permute-start.3 = (bf16[4,4,64,256]{3,2,1,0:T(8,128)(2,1)S(1)}, bf16[4,4,64,256]{3,2,1,0:T(8,128)(2,1)S(1)}, u32[]{:S(2)}, u32[]{:S(2)}) collective-permute-start(bf16[4,4,64,256]{3,2,1,0:T(8,128)(2,1)S(1)} %all-to-all-done.3.mine_ref), channel_id=1, source_target_pairs={{0,1},{1,0},{2,3},{3,2},{4,5},{5,4},{6,7},{7,6},{8,9},{9,8},{10,11... | collective-permute-start | bytes 1572872 | tf_op jit(solution)/shard_map/attend/ppermute | solution.py:26
  123.9 0.4 collective-permute-done.1
  124.2 0.1 add_convert_fusion.own_ref
  124.3 3.4 %collective-permute-start.2 = (bf16[2,256,256]{2,1,0:T(8,128)(2,1)S(1)}, bf16[2,256,256]{2,1,0:T(8,128)(2,1)S(1)}, u32[]{:S(2)}, u32[]{:S(2)}) collective-permute-start(bf16[2,256,256]{2,1,0:T(8,128)(2,1)S(1)} %add_convert_fusion.own_ref), channel_id=1, source_target_pairs={{0,2},{2,0},{1,3},{3,1},{4,6},{6,4},{5,7},{7,5},{8,10},{10,8},{9,1... | collective-permute-start | bytes 786440 | tf_op jit(solution)/shard_map/swap_q/ppermute | solution.py:266
  127.7 6.9 %collective-permute-done.2.pair_ref = bf16[2,256,256]{2,1,0:T(8,128)(2,1)S(1)} collective-permute-done((bf16[2,256,256]{2,1,0:T(8,128)(2,1)S(1)}, bf16[2,256,256]{2,1,0:T(8,128)(2,1)S(1)}, u32[]{:S(2)}, u32[]{:S(2)}) %collective-permute-start.2) | collective-permute-done | bytes 262176 | tf_op jit(solution)/shard_map/swap_q/ppermute | solution.py:266
  134.6 2.9 %attend.2 = f32[4,264,256]{2,1,0:T(8,128)S(1)} custom-call(s32[4]{0:T(128)S(1)} %pad_add_fusion.place, bf16[2,256,256]{2,1,0:T(8,128)(2,1)S(1)} %add_convert_fusion.own_ref, bf16[2,256,256]{2,1,0:T(8,128)(2,1)S(1)} %collective-permute-done.2.pair_ref, bf16[4,4,64,256]{3,2,1,0:T(8,128)(2,1)S(1)} %all-to-all-done.3.mine_ref, ...), custom_call_target="tpu_custom_call" | custom-call | flops 2147483648 | bytes 4194304 | tf_op jit(solution)/shard_map/attend/pallas_call | solution.py:97
  137.5 20.8 %all_to_all.26.parts_ref = f32[4,264,256]{2,1,0:T(8,128)S(1)} all-to-all(f32[4,264,256]{2,1,0:T(8,128)S(1)} %attend.2), channel_id=1, replica_groups=mesh['zh'=4,'zl'=4,'xh'=2,'xl'=2,'yh'=2,'yl'=2,'core'=2] {'xh','yl'}, dimensions={0} | all-to-all | bytes 2162688 | tf_op jit(solution)/shard_map/attend/all_to_all | solution.py:270
  158.3 1.2 attend.3
  (13 shorter events, 0.1 us)
Async XLA Ops:
  7.2 0.9 copy-start.4
  8.5 1.4 copy-start
  9.9 52.5 %all-to-all-start = ((bf16[32,272,128]{2,1,0:T(8,128)(2,1)}), bf16[32,272,128]{2,1,0:T(8,128)(2,1)S(1)}, u32[]{:S(2)}, u32[]{:S(2)}) async-start(bf16[32,272,128]{2,1,0:T(8,128)(2,1)} %bitcast.16), calls=%async_computation | async-start | bytes 4456448 | tf_op jit(solution)/shard_map/spread/all_to_all | solution.py:247
  19.3 81.7 %all-gather.5.cloned.1.call-start = ((), (), s32[]{:S(2)}) async-start(), calls=%async_computation.5 | async-start | bytes 2228224 | tf_op jit(solution)/shard_map/weights/all_gather | solution.py:235
  63.6 1.3 copy-start.2
  77.1 23.9 %collective-permute-start = (bf16[2,256,2048]{2,1,0:T(8,128)(2,1)}, bf16[2,256,2048]{2,1,0:T(8,128)(2,1)S(1)}, u32[]{:S(2)}, u32[]{:S(2)}) collective-permute-start(bf16[2,256,2048]{2,1,0:T(8,128)(2,1)} %copy-done.2), channel_id=1, source_target_pairs={{0,1},{1,0},{2,3},{3,2},{4,5},{5,4},{6,7},{7,6},{8,9},{9,8},{10,11... | collective-permute-start | bytes 6291464 | tf_op jit(solution)/shard_map/project_q/ppermute | solution.py:26
  79.7 26.3 %all-to-all-start.2 = ((bf16[4,64,256]{2,1,0:T(8,128)(2,1)}), bf16[4,64,256]{2,1,0:T(8,128)(2,1)S(1)}, u32[]{:S(2)}, u32[]{:S(2)}) async-start(bf16[4,64,256]{2,1,0:T(8,128)(2,1)} %broadcast_in_dim.4), calls=%async_computation.2 | async-start | bytes 262144 | tf_op jit(solution)/shard_map/gather_kv/all_to_all | solution.py:22
  101.0 1.6 copy-start.1
  102.6 1.6 copy-start.3
  106.8 15.1 %all-to-all-start.3 = ((bf16[4,4,64,256]{3,2,1,0:T(8,128)(2,1)}), bf16[4,4,64,256]{3,2,1,0:T(8,128)(2,1)S(1)}, u32[]{:S(2)}, u32[]{:S(2)}) async-start(bf16[4,4,64,256]{3,2,1,0:T(8,128)(2,1)} %broadcast_in_dim.5), calls=%async_computation.3 | async-start | bytes 1048576 | tf_op jit(solution)/shard_map/gather_kv/all_to_all | solution.py:22
  110.9 13.3 %collective-permute-start.1 = (f32[2,256,256]{2,1,0:T(8,128)S(1)}, f32[2,256,256]{2,1,0:T(8,128)S(1)}, u32[]{:S(2)}, u32[]{:S(2)}) collective-permute-start(f32[2,256,256]{2,1,0:T(8,128)S(1)} %project_q.1), channel_id=1, source_target_pairs={{0,16},{16,0},{1,17},{17,1},{2,18},{18,2},{3,19},{19,3},{4,20},{20... | collective-permute-start | bytes 1572872 | tf_op jit(solution)/shard_map/swap_q/ppermute | solution.py:265
  122.0 12.6 %collective-permute-start.3 = (bf16[4,4,64,256]{3,2,1,0:T(8,128)(2,1)S(1)}, bf16[4,4,64,256]{3,2,1,0:T(8,128)(2,1)S(1)}, u32[]{:S(2)}, u32[]{:S(2)}) collective-permute-start(bf16[4,4,64,256]{3,2,1,0:T(8,128)(2,1)S(1)} %all-to-all-done.3.mine_ref), channel_id=1, source_target_pairs={{0,1},{1,0},{2,3},{3,2},{4,5},{5,4},{6,7},{7,6},{8,9},{9,8},{10,11... | collective-permute-start | bytes 1572872 | tf_op jit(solution)/shard_map/attend/ppermute | solution.py:26
  124.3 10.3 %collective-permute-start.2 = (bf16[2,256,256]{2,1,0:T(8,128)(2,1)S(1)}, bf16[2,256,256]{2,1,0:T(8,128)(2,1)S(1)}, u32[]{:S(2)}, u32[]{:S(2)}) collective-permute-start(bf16[2,256,256]{2,1,0:T(8,128)(2,1)S(1)} %add_convert_fusion.own_ref), channel_id=1, source_target_pairs={{0,2},{2,0},{1,3},{3,1},{4,6},{6,4},{5,7},{7,5},{8,10},{10,8},{9,1... | collective-permute-start | bytes 786440 | tf_op jit(solution)/shard_map/swap_q/ppermute | solution.py:266
Sparse Core Ops, SparseCore 0:
  22.2 78.7 all-gather.4

commit v6 on v5

--- a/solution.py
+++ b/solution.py
@@ -24,6 +24,15 @@
 
 def swap(x):
     return lax.ppermute(x, "core", [(0, 1), (1, 0)])
+
+
+def three(x):
+    pieces = []
+    for _ in range(3):
+        piece = x.astype(BF16).astype(F32)
+        pieces.append(piece)
+        x = x - piece
+    return pieces
 
 
 def attend_kernel(place, own_ref, pair_ref, mine_ref, other_ref, out_ref, m_ref, l_ref, acc_ref):
@@ -84,11 +93,13 @@
             head = side * 2 + i
             total = jnp.sum(l_ref[head], axis=1, keepdims=True)
             stats = jnp.where(lane == i, m_ref[head] * scale + jnp.log2(total), stats)
-            part = acc_ref[head] / total
+            part = (acc_ref[head] / total).astype(BF16)
             for x in range(2):
                 out_ref[2 * x + to, :rows, i * HEAD : (i + 1) * HEAD] = part[x * rows : (x + 1) * rows]
         for x in range(2):
-            out_ref[2 * x + to, rows:, :] = jnp.transpose(stats[x * rows : (x + 1) * rows])[:8]
+            sums = three(jnp.transpose(stats[x * rows : (x + 1) * rows])[:2])
+            sums = jnp.concatenate([*sums, jnp.zeros((10, 2 * HEAD), F32)], axis=0)
+            out_ref[2 * x + to, rows:, :] = sums.astype(BF16)
 
 
 def attend(place, own, pair, mine, other):
@@ -96,7 +107,7 @@
     vmem = pl.BlockSpec(memory_space=pltpu.VMEM)
     return pl.pallas_call(
         attend_kernel,
-        out_shape=jax.ShapeDtypeStruct((4, rows + 8, cols), F32),
+        out_shape=jax.ShapeDtypeStruct((4, rows + 16, cols), BF16),
         in_specs=[pl.BlockSpec(memory_space=pltpu.SMEM), vmem, vmem, vmem, vmem],
         out_specs=vmem,
         scratch_shapes=[pltpu.VMEM((4, 2 * rows, HEAD), F32)] * 3,
@@ -108,61 +119,66 @@
 def merge_kernel(parts_ref, out_ref):
     rows = out_ref.shape[0]
     n = parts_ref.shape[0]
-    sums = [parts_ref[i, rows:, :] for i in range(n)]
+    sums = [parts_ref[i, rows:, :].astype(F32) for i in range(n)]
+    sums = [s[0:2] + s[2:4] + s[4:6] for s in sums]
     most = functools.reduce(jnp.maximum, sums)
     shares = [jnp.exp2(s - most) for s in sums]
     total = functools.reduce(jnp.add, shares)
-    columns = [jnp.transpose(jnp.concatenate([s / total] * (HEAD // 8), axis=0)) for s in shares]
+    columns = [jnp.transpose(jnp.concatenate([s / total] * (HEAD // 2), axis=0)) for s in shares]
     for i in range(2):
         at = slice(i * HEAD, (i + 1) * HEAD)
-        out_ref[:, at] = sum(columns[k][:, i : i + 1] * parts_ref[k, :rows, at] for k in range(n)).astype(BF16)
+        out_ref[:, at] = sum(columns[k][:, i : i + 1] * parts_ref[k, :rows, at].astype(F32) for k in range(n)).astype(BF16)
 
 
 def merge(parts):
     vmem = pl.BlockSpec(memory_space=pltpu.VMEM)
     return pl.pallas_call(
         merge_kernel,
-        out_shape=jax.ShapeDtypeStruct((parts.shape[1] - 8, parts.shape[2]), BF16),
+        out_shape=jax.ShapeDtypeStruct((parts.shape[1] - 16, parts.shape[2]), BF16),
         in_specs=[vmem],
         out_specs=vmem,
         compiler_params=pltpu.CompilerParams(vmem_limit_bytes=40 * 1024 * 1024),
     )(parts)
 
 
-def prep_kernel(tokens_ref, gain_ref, out_ref):
+def prep_kernel(tokens_ref, gain_ref, out_ref, block_ref, sems):
     rows = tokens_ref.shape[0]
     states = tokens_ref[...].astype(F32)
     sums = jnp.sum(states * states, axis=1, keepdims=True)
     left = jnp.transpose(jnp.broadcast_to(sums, (rows, HEAD)))[:1]
-    left = jnp.concatenate([left[:, :HEAD], left[:, HEAD:]], axis=0)
-    pieces = []
-    for _ in range(3):
-        piece = left.astype(BF16).astype(F32)
-        pieces.append(piece)
-        left = left - piece
+    pieces = three(jnp.concatenate([left[:, :HEAD], left[:, HEAD:]], axis=0))
     for q in range(4):
         at = slice(q * HEAD, (q + 1) * HEAD)
         gain = gain_ref[:, at].astype(F32)
-        extra = jnp.concatenate([*pieces, gain, jnp.zeros((9, HEAD), F32)], axis=0).astype(BF16)
-        for to in range(out_ref.shape[1]):
-            out_ref[q // 2, to, q % 2, :rows] = tokens_ref[:, at]
-            out_ref[q // 2, to, q % 2, rows:] = extra
+        extra = jnp.concatenate([*pieces, gain, jnp.zeros((9, HEAD), F32)], axis=0)
+        block_ref[q // 2, q % 2, :rows] = tokens_ref[:, at]
+        block_ref[q // 2, q % 2, rows:] = extra.astype(BF16)
+    copies = [
+        pltpu.make_async_copy(block_ref, out_ref.at[:, to], sems.at[to]) for to in range(out_ref.shape[1])
+    ]
+    for copy in copies:
+        copy.start()
+    for copy in copies:
+        copy.wait()
 
 
 def prep(tokens, gain):
     vmem = pl.BlockSpec(memory_space=pltpu.VMEM)
+    rows = tokens.shape[0] + 16
     return pl.pallas_call(
         prep_kernel,
-        out_shape=jax.ShapeDtypeStruct((2, 8, 2, tokens.shape[0] + 16, HEAD), BF16),
+        out_shape=jax.ShapeDtypeStruct((2, 8, 2, rows, HEAD), BF16),
         in_specs=[vmem, vmem],
-        out_specs=vmem,
-        compiler_params=pltpu.CompilerParams(vmem_limit_bytes=40 * 1024 * 1024),
+        out_specs=pl.BlockSpec(memory_space=pltpu.HBM),
+        scratch_shapes=[pltpu.VMEM((2, 2, rows, HEAD), BF16), pltpu.SemaphoreType.DMA((8,))],
+        compiler_params=pltpu.CompilerParams(vmem_limit_bytes=60 * 1024 * 1024),
     )(tokens, gain)
 
 
-def kv_kernel(parts_ref, w_ref, t_ref, kv_ref):
+def kv_kernel(parts_ref, w_ref, out_ref, kv_ref, t_ref, sems):
     rows = t_ref.shape[1]
     blocks = parts_ref.shape[1]
+    copies = [pltpu.make_async_copy(t_ref.at[xh], out_ref.at[xh], sems.at[xh]) for xh in range(2)]
     for xh in range(2):
         extra = [parts_ref[xh, c, rows:].astype(F32) for c in range(blocks)]
         squares = functools.reduce(jnp.add, extra)
@@ -179,6 +195,9 @@
             w = jnp.concatenate([w_ref[d % 4, d // 4] for d in (c, c + 1)], axis=0)
             total += jnp.dot(t_ref[xh, :, c * HEAD : (c + 2) * HEAD], w, preferred_element_type=F32)
         kv_ref[xh] = total
+        copies[xh].start()
+    for copy in copies:
+        copy.wait()
 
 
 def project_kv(parts, w, rows):
@@ -191,7 +210,8 @@
             jax.ShapeDtypeStruct((2, rows, HEAD), F32),
         ),
         in_specs=[vmem, vmem],
-        out_specs=(vmem, vmem),
+        out_specs=(pl.BlockSpec(memory_space=pltpu.HBM), vmem),
+        scratch_shapes=[pltpu.VMEM((2, rows, blocks * HEAD), BF16), pltpu.SemaphoreType.DMA((2,))],
         compiler_params=pltpu.CompilerParams(vmem_limit_bytes=40 * 1024 * 1024),
         cost_estimate=pl.CostEstimate(flops=2**28, bytes_accessed=5 * 2**20, transcendentals=0),
     )(parts, w)
@@ -200,7 +220,7 @@
 def q_kernel(place, mine_ref, other_ref, w_ref, out_ref):
     core = place[3]
     rows = mine_ref.shape[1]
-    half = w_ref.shape[1] // 2
+    half = mine_ref.shape[2] // w_ref.shape[0]
     for xh in range(2):
         total = jnp.zeros((rows, w_ref.shape[2]), F32)
         for c in range(w_ref.shape[0]):
@@ -232,7 +252,7 @@
     half = w_key.shape[0] // 2
 
     with jax.named_scope("weights"):
-        wq = lax.all_gather(w_query, ("zh", "zl"), axis=0)
+        wq = lax.all_gather(jnp.pad(w_query, ((0, 64), (0, 0))), ("zh", "zl"), axis=0)
         head = at(("xl", "yh"))
         start = (core * half, head * HEAD)
         wkv = jnp.where(

time: 167 us -> 160 us (0.958)
  the two profiles are of different devices: /device:TPU:16 before, /device:TPU:1 now
where the time goes in v6:
time: 160 us; the launch traced here: 159 us
  blocking collectives  67.2 us (42%)
  starting transfers between devices  36.5 us (23%)
  waiting for transfers between devices  22.2 us (14%)
  between operations  13.5 us (8%)
  Pallas kernels  10 us (6%)
  local copies, waits for them, and re-layouts  9.01 us (6%)
    all_gather x2, blocking collectives, on_device(): wkv = lax.all_gather(lax.all_gather(wkv, 'zh'), 'zl')  38.9 us
    all_to_all x1, blocking collectives, on_device(): lax.all_to_all(kv_sum.reshape(8, rows // 4, HEAD), ('xh', 'yl', 'core'),...  16.8 us
    all_to_all x2, waiting for transfers between devices, gather(): return lax.all_to_all(jnp.broadcast_to(x[None], (n, *x.shape)), axes, 0, 0)  15.8 us
    all_to_all x2, starting transfers between devices, gather(): return lax.all_to_all(jnp.broadcast_to(x[None], (n, *x.shape)), axes, 0, 0)  11.6 us
    all_to_all x1, blocking collectives, on_device(): return merge(lax.all_to_all(out, ('xh', 'yl'), 0, 0))  11.6 us
    all_to_all x1, starting transfers between devices, on_device(): lax.all_to_all(parts.reshape(32, rows + 16, HEAD), ('xh',) + COL, 0, 0)  10.6 us
    ppermute x2, starting transfers between devices, swap(): return lax.ppermute(x, 'core', [(0, 1), (1, 0)])  8.14 us
    ppermute x1, waiting for transfers between devices, on_device(): pair = lax.ppermute(q, 'yl', [(0, 1), (1, 0)])  6.32 us
  transfers between devices with their start and end apart: 8, of which 3 were waited for; matrix products, arithmetic and copies ran while one was open for 2% of the time, Pallas kernels for 4%

profile of v6, /device:TPU:1, one launch (start us, length us, event | category | flops | bytes accessed | tf_op | source)
XLA Modules:
  0.0 159.4 jit_solution(2378901286245450741)
XLA Ops:
  6.5 1.6 pad.4
  8.1 0.0 all-gather.5.cloned.1.call-update
  8.1 1.3 reshape.17.gain_ref
  9.4 2.6 %spread.1 = bf16[2,8,2,272,128]{4,3,2,1,0:T(8,128)(2,1)} custom-call(bf16[256,512]{1,0:T(8,128)(2,1)} %tokens_ref.1, bf16[1,512]{1,0:T(2,128)(2,1)} %reshape.17.gain_ref), custom_call_target="tpu_custom_call" | custom-call | tf_op jit(solution)/shard_map/spread/pallas_call | solution.py:168
  12.0 10.6 %all-to-all-start = ((bf16[32,272,128]{2,1,0:T(8,128)(2,1)}), bf16[32,272,128]{2,1,0:T(8,128)(2,1)S(1)}, u32[]{:S(2)}, u32[]{:S(2)}) async-start(bf16[32,272,128]{2,1,0:T(8,128)(2,1)} %bitcast.19), calls=%async_computation | async-start | bytes 4456448 | tf_op jit(solution)/shard_map/spread/all_to_all | solution.py:267
  22.6 0.8 dynamic-slice_select_fusion
  23.4 21.8 %all-gather = bf16[512,128]{1,0:T(8,128)(2,1)S(1)} all-gather(bf16[128,128]{1,0:T(8,128)(2,1)S(1)} %dynamic-slice_select_fusion), channel_id=2, replica_groups=mesh['zh'=4,'zl'=4,'xh'=2,'xl'=2,'yh'=2,'yl'=2,'core'=2] {'zh'}, dimensions={0}, use_global_device_ids=true | all-gather | bytes 163840 | tf_op jit(solution)/shard_map/weights/all_gather | solution.py:263
  45.2 17.1 %all-gather.1 = bf16[16,128,128]{2,1,0:T(8,128)(2,1)S(1)} all-gather(bf16[4,128,128]{2,1,0:T(8,128)(2,1)S(1)} %bitcast.21), channel_id=3, replica_groups=mesh['zh'=4,'zl'=4,'xh'=2,'xl'=2,'yh'=2,'yl'=2,'core'=2] {'zl'}, dimensions={0}, use_global_device_ids=true | all-gather | bytes 655360 | tf_op jit(solution)/shard_map/weights/all_gather | solution.py:263
  62.3 0.0 all-to-all-done
  62.3 1.5 project_kv.1
  63.8 1.3 copy-done.1
  65.2 16.8 %all_to_all.25 = f32[8,64,128]{2,1,0:T(8,128)S(1)} all-to-all(f32[8,64,128]{2,1,0:T(8,128)S(1)} %bitcast.18), channel_id=1, replica_groups=mesh['zh'=4,'zl'=4,'xh'=2,'xl'=2,'yh'=2,'yl'=2,'core'=2] {'xh','yl','core'}, dimensions={0} | all-to-all | bytes 524288 | tf_op jit(solution)/shard_map/project_kv/all_to_all | solution.py:272
  82.0 2.7 %collective-permute-start = (bf16[2,256,2048]{2,1,0:T(8,128)(2,1)}, bf16[2,256,2048]{2,1,0:T(8,128)(2,1)S(1)}, u32[]{:S(2)}, u32[]{:S(2)}) collective-permute-start(bf16[2,256,2048]{2,1,0:T(8,128)(2,1)} %copy-done.1), channel_id=1, source_target_pairs={{0,1},{1,0},{2,3},{3,2},{4,5},{5,4},{6,7},{7,6},{8,9},{9,8},{10,11... | collective-permute-start | bytes 6291464 | tf_op jit(solution)/shard_map/project_q/ppermute | solution.py:26
  84.6 0.7 broadcast_in_dim.4
  85.3 6.8 %all-to-all-start.2 = ((bf16[4,64,256]{2,1,0:T(8,128)(2,1)}), bf16[4,64,256]{2,1,0:T(8,128)(2,1)S(1)}, u32[]{:S(2)}, u32[]{:S(2)}) async-start(bf16[4,64,256]{2,1,0:T(8,128)(2,1)} %broadcast_in_dim.4), calls=%async_computation.2 | async-start | bytes 262144 | tf_op jit(solution)/shard_map/gather_kv/all_to_all | solution.py:22
  92.2 0.1 pad_add_fusion.place
  92.2 1.7 %copy-done = bf16[5120,256]{1,0:T(8,128)(2,1)S(1)} copy-done((bf16[5120,256]{1,0:T(8,128)(2,1)S(1)}, bf16[5120,256]{1,0:T(8,128)(2,1)}, u32[]{:S(2)}) %copy-start) | copy-done | bytes 2621464
  94.0 1.6 copy-done.2
  95.6 1.8 %project_q.1 = f32[2,256,256]{2,1,0:T(8,128)S(1)} custom-call(s32[4]{0:T(128)S(1)} %pad_add_fusion.place, bf16[2,256,2048]{2,1,0:T(8,128)(2,1)S(1)} %copy-done.2, bf16[2,256,2048]{2,1,0:T(8,128)(2,1)S(1)} %collective-permute-done.other_ref, bf16[16,320,256]{2,1,0:T(8,128)(2,1)S(1)} %bitcast.16), custom_call_target="tpu_custom_call" | custom-call | flops 1073741824 | bytes 6291456 | tf_op jit(solution)/shard_map/project_q/pallas_call | solution.py:237
  97.4 7.1 %all-to-all-done.2 = bf16[4,64,256]{2,1,0:T(8,128)(2,1)S(1)} async-done(((bf16[4,64,256]{2,1,0:T(8,128)(2,1)}), bf16[4,64,256]{2,1,0:T(8,128)(2,1)S(1)}, u32[]{:S(2)}, u32[]{:S(2)}) %all-to-all-start.2) | async-done | bytes 131104 | tf_op jit(solution)/shard_map/gather_kv/all_to_all | solution.py:22
  104.4 0.8 broadcast_in_dim.5
  105.3 4.7 %all-to-all-start.3 = ((bf16[4,4,64,256]{3,2,1,0:T(8,128)(2,1)}), bf16[4,4,64,256]{3,2,1,0:T(8,128)(2,1)S(1)}, u32[]{:S(2)}, u32[]{:S(2)}) async-start(bf16[4,4,64,256]{3,2,1,0:T(8,128)(2,1)} %broadcast_in_dim.5), calls=%async_computation.3 | async-start | bytes 1048576 | tf_op jit(solution)/shard_map/gather_kv/all_to_all | solution.py:22
  110.0 3.1 %collective-permute-start.1 = (f32[2,256,256]{2,1,0:T(8,128)S(1)}, f32[2,256,256]{2,1,0:T(8,128)S(1)}, u32[]{:S(2)}, u32[]{:S(2)}) collective-permute-start(f32[2,256,256]{2,1,0:T(8,128)S(1)} %project_q.1), channel_id=1, source_target_pairs={{0,16},{16,0},{1,17},{17,1},{2,18},{18,2},{3,19},{19,3},{4,20},{20... | collective-permute-start | bytes 1572872 | tf_op jit(solution)/shard_map/swap_q/ppermute | solution.py:285
  113.1 8.8 %all-to-all-done.3.mine_ref = bf16[4,4,64,256]{3,2,1,0:T(8,128)(2,1)S(1)} async-done(((bf16[4,4,64,256]{3,2,1,0:T(8,128)(2,1)}), bf16[4,4,64,256]{3,2,1,0:T(8,128)(2,1)S(1)}, u32[]{:S(2)}, u32[]{:S(2)}) %all-to-all-start.3) | async-done | bytes 524320 | tf_op jit(solution)/shard_map/gather_kv/all_to_all | solution.py:22
  121.9 5.5 %collective-permute-start.3 = (bf16[4,4,64,256]{3,2,1,0:T(8,128)(2,1)S(1)}, bf16[4,4,64,256]{3,2,1,0:T(8,128)(2,1)S(1)}, u32[]{:S(2)}, u32[]{:S(2)}) collective-permute-start(bf16[4,4,64,256]{3,2,1,0:T(8,128)(2,1)S(1)} %all-to-all-done.3.mine_ref), channel_id=1, source_target_pairs={{0,1},{1,0},{2,3},{3,2},{4,5},{5,4},{6,7},{7,6},{8,9},{9,8},{10,11... | collective-permute-start | bytes 1572872 | tf_op jit(solution)/shard_map/attend/ppermute | solution.py:26
  127.4 0.0 collective-permute-done.1
  127.4 0.1 add_convert_fusion.own_ref
  127.5 3.1 %collective-permute-start.2 = (bf16[2,256,256]{2,1,0:T(8,128)(2,1)S(1)}, bf16[2,256,256]{2,1,0:T(8,128)(2,1)S(1)}, u32[]{:S(2)}, u32[]{:S(2)}) collective-permute-start(bf16[2,256,256]{2,1,0:T(8,128)(2,1)S(1)} %add_convert_fusion.own_ref), channel_id=1, source_target_pairs={{0,2},{2,0},{1,3},{3,1},{4,6},{6,4},{5,7},{7,5},{8,10},{10,8},{9,1... | collective-permute-start | bytes 786440 | tf_op jit(solution)/shard_map/swap_q/ppermute | solution.py:286
  130.6 6.3 %collective-permute-done.2.pair_ref = bf16[2,256,256]{2,1,0:T(8,128)(2,1)S(1)} collective-permute-done((bf16[2,256,256]{2,1,0:T(8,128)(2,1)S(1)}, bf16[2,256,256]{2,1,0:T(8,128)(2,1)S(1)}, u32[]{:S(2)}, u32[]{:S(2)}) %collective-permute-start.2) | collective-permute-done | bytes 262176 | tf_op jit(solution)/shard_map/swap_q/ppermute | solution.py:286
  136.9 2.9 %attend.2 = bf16[4,272,256]{2,1,0:T(8,128)(2,1)S(1)} custom-call(s32[4]{0:T(128)S(1)} %pad_add_fusion.place, bf16[2,256,256]{2,1,0:T(8,128)(2,1)S(1)} %add_convert_fusion.own_ref, bf16[2,256,256]{2,1,0:T(8,128)(2,1)S(1)} %collective-permute-done.2.pair_ref, bf16[4,4,64,256]{3,2,1,0:T(8,128)(2,1)S(1)} %all-to-all-done.3.mine_ref, ...), custom_call_target="tpu_custom_call" | custom-call | flops 2147483648 | bytes 4194304 | tf_op jit(solution)/shard_map/attend/pallas_call | solution.py:108
  139.8 11.6 %all_to_all.26.parts_ref = bf16[4,272,256]{2,1,0:T(8,128)(2,1)S(1)} all-to-all(bf16[4,272,256]{2,1,0:T(8,128)(2,1)S(1)} %attend.2), channel_id=1, replica_groups=mesh['zh'=4,'zl'=4,'xh'=2,'xl'=2,'yh'=2,'yl'=2,'core'=2] {'xh','yl'}, dimensions={0} | all-to-all | bytes 1114112 | tf_op jit(solution)/shard_map/attend/all_to_all | solution.py:290
  151.4 1.2 attend.3
  (10 shorter events, 0.0 us)
Async XLA Ops:
  6.5 85.7 %all-gather.5.cloned.1.call-start = ((), (), s32[]{:S(2)}) async-start(), calls=%async_computation.5 | async-start | bytes 2785280 | tf_op jit(solution)/shard_map/weights/all_gather | solution.py:255
  12.0 50.3 %all-to-all-start = ((bf16[32,272,128]{2,1,0:T(8,128)(2,1)}), bf16[32,272,128]{2,1,0:T(8,128)(2,1)S(1)}, u32[]{:S(2)}, u32[]{:S(2)}) async-start(bf16[32,272,128]{2,1,0:T(8,128)(2,1)} %bitcast.19), calls=%async_computation | async-start | bytes 4456448 | tf_op jit(solution)/shard_map/spread/all_to_all | solution.py:267
  63.8 1.3 copy-start.1
  82.0 10.2 %collective-permute-start = (bf16[2,256,2048]{2,1,0:T(8,128)(2,1)}, bf16[2,256,2048]{2,1,0:T(8,128)(2,1)S(1)}, u32[]{:S(2)}, u32[]{:S(2)}) collective-permute-start(bf16[2,256,2048]{2,1,0:T(8,128)(2,1)} %copy-done.1), channel_id=1, source_target_pairs={{0,1},{1,0},{2,3},{3,2},{4,5},{5,4},{6,7},{7,6},{8,9},{9,8},{10,11... | collective-permute-start | bytes 6291464 | tf_op jit(solution)/shard_map/project_q/ppermute | solution.py:26
  85.3 19.1 %all-to-all-start.2 = ((bf16[4,64,256]{2,1,0:T(8,128)(2,1)}), bf16[4,64,256]{2,1,0:T(8,128)(2,1)S(1)}, u32[]{:S(2)}, u32[]{:S(2)}) async-start(bf16[4,64,256]{2,1,0:T(8,128)(2,1)} %broadcast_in_dim.4), calls=%async_computation.2 | async-start | bytes 262144 | tf_op jit(solution)/shard_map/gather_kv/all_to_all | solution.py:22
  92.2 1.7 %copy-start = (bf16[5120,256]{1,0:T(8,128)(2,1)S(1)}, bf16[5120,256]{1,0:T(8,128)(2,1)}, u32[]{:S(2)}) copy-start(bf16[5120,256]{1,0:T(8,128)(2,1)} %all-gather.5.cloned.1.call-done) | copy-start | bytes 7864324
  94.0 1.6 copy-start.2
  105.3 16.6 %all-to-all-start.3 = ((bf16[4,4,64,256]{3,2,1,0:T(8,128)(2,1)}), bf16[4,4,64,256]{3,2,1,0:T(8,128)(2,1)S(1)}, u32[]{:S(2)}, u32[]{:S(2)}) async-start(bf16[4,4,64,256]{3,2,1,0:T(8,128)(2,1)} %broadcast_in_dim.5), calls=%async_computation.3 | async-start | bytes 1048576 | tf_op jit(solution)/shard_map/gather_kv/all_to_all | solution.py:22
  110.0 17.4 %collective-permute-start.1 = (f32[2,256,256]{2,1,0:T(8,128)S(1)}, f32[2,256,256]{2,1,0:T(8,128)S(1)}, u32[]{:S(2)}, u32[]{:S(2)}) collective-permute-start(f32[2,256,256]{2,1,0:T(8,128)S(1)} %project_q.1), channel_id=1, source_target_pairs={{0,16},{16,0},{1,17},{17,1},{2,18},{18,2},{3,19},{19,3},{4,20},{20... | collective-permute-start | bytes 1572872 | tf_op jit(solution)/shard_map/swap_q/ppermute | solution.py:285
  121.9 15.0 %collective-permute-start.3 = (bf16[4,4,64,256]{3,2,1,0:T(8,128)(2,1)S(1)}, bf16[4,4,64,256]{3,2,1,0:T(8,128)(2,1)S(1)}, u32[]{:S(2)}, u32[]{:S(2)}) collective-permute-start(bf16[4,4,64,256]{3,2,1,0:T(8,128)(2,1)S(1)} %all-to-all-done.3.mine_ref), channel_id=1, source_target_pairs={{0,1},{1,0},{2,3},{3,2},{4,5},{5,4},{6,7},{7,6},{8,9},{9,8},{10,11... | collective-permute-start | bytes 1572872 | tf_op jit(solution)/shard_map/attend/ppermute | solution.py:26
  127.5 9.4 %collective-permute-start.2 = (bf16[2,256,256]{2,1,0:T(8,128)(2,1)S(1)}, bf16[2,256,256]{2,1,0:T(8,128)(2,1)S(1)}, u32[]{:S(2)}, u32[]{:S(2)}) collective-permute-start(bf16[2,256,256]{2,1,0:T(8,128)(2,1)S(1)} %add_convert_fusion.own_ref), channel_id=1, source_target_pairs={{0,2},{2,0},{1,3},{3,1},{4,6},{6,4},{5,7},{7,5},{8,10},{10,8},{9,1... | collective-permute-start | bytes 786440 | tf_op jit(solution)/shard_map/swap_q/ppermute | solution.py:286
Sparse Core Ops, SparseCore 0:
  9.4 75.0 all-gather.4

commit v7 on v6

--- a/solution.py
+++ b/solution.py
@@ -35,9 +35,9 @@
     return pieces
 
 
-def attend_kernel(place, own_ref, pair_ref, mine_ref, other_ref, out_ref, m_ref, l_ref, acc_ref):
+def attend_kernel(place, q0_ref, q1_ref, q2_ref, q3_ref, mine_ref, other_ref, out_ref, m_ref, l_ref, acc_ref):
     z, xh, yl, core = place[0], place[1], place[2], place[3]
-    rows = own_ref.shape[1]
+    rows = q0_ref.shape[0]
     scale = HEAD**-0.5 * math.log2(math.e)
     m_ref[...] = jnp.full(m_ref.shape, -1e30, F32)
     l_ref[...] = jnp.zeros(l_ref.shape, F32)
@@ -55,12 +55,13 @@
             within = lax.rem(slot, half)
             owner = jnp.where(slot < half, core, 1 - core) + 4 * xh + 2 * yl
             key_pos = lax.div(within, chunk) * (2 * rows) + owner * chunk + lax.rem(within, chunk)
-            query_pos = lax.rem(z, 4) * (2 * rows) + lax.broadcasted_iota(jnp.int32, shape, 0)
+            query = lax.broadcasted_iota(jnp.int32, shape, 0)
+            query = lax.rem(query + xh * rows, 2 * rows)
+            query_pos = lax.rem(z, 4) * (2 * rows) + query
             seen = key_pos <= query_pos
         for head in range(4):
-            q_ref = (own_ref, pair_ref)[head // 2]
-            at = head % 2 * HEAD
-            q = q_ref[:, :, at : at + HEAD].reshape(2 * rows, HEAD)
+            at = slice(head % 2 * HEAD, (head % 2 + 1) * HEAD)
+            q = jnp.concatenate([ref[:, at] for ref in ((q0_ref, q1_ref), (q2_ref, q3_ref))[head // 2]], axis=0)
             s = lax.dot_general(q, kv[:, :HEAD], (((1,), (1,)), ((), ())), preferred_element_type=F32)
             if masked:
                 s = jnp.where(seen, s, -1e30)
@@ -95,25 +96,25 @@
             stats = jnp.where(lane == i, m_ref[head] * scale + jnp.log2(total), stats)
             part = (acc_ref[head] / total).astype(BF16)
             for x in range(2):
-                out_ref[2 * x + to, :rows, i * HEAD : (i + 1) * HEAD] = part[x * rows : (x + 1) * rows]
+                out_ref[2 * (x ^ xh) + to, :rows, i * HEAD : (i + 1) * HEAD] = part[x * rows : (x + 1) * rows]
         for x in range(2):
             sums = three(jnp.transpose(stats[x * rows : (x + 1) * rows])[:2])
             sums = jnp.concatenate([*sums, jnp.zeros((10, 2 * HEAD), F32)], axis=0)
-            out_ref[2 * x + to, rows:, :] = sums.astype(BF16)
-
-
-def attend(place, own, pair, mine, other):
-    rows, cols = own.shape[1:]
+            out_ref[2 * (x ^ xh) + to, rows:, :] = sums.astype(BF16)
+
+
+def attend(place, queries, mine, other):
+    rows, cols = queries[0].shape
     vmem = pl.BlockSpec(memory_space=pltpu.VMEM)
     return pl.pallas_call(
         attend_kernel,
         out_shape=jax.ShapeDtypeStruct((4, rows + 16, cols), BF16),
-        in_specs=[pl.BlockSpec(memory_space=pltpu.SMEM), vmem, vmem, vmem, vmem],
+        in_specs=[pl.BlockSpec(memory_space=pltpu.SMEM)] + [vmem] * 6,
         out_specs=vmem,
         scratch_shapes=[pltpu.VMEM((4, 2 * rows, HEAD), F32)] * 3,
         compiler_params=pltpu.CompilerParams(vmem_limit_bytes=40 * 1024 * 1024),
         cost_estimate=pl.CostEstimate(flops=2**31, bytes_accessed=2**22, transcendentals=2**22),
-    )(place, own, pair, mine, other)
+    )(place, *queries, mine, other)
 
 
 def merge_kernel(parts_ref, out_ref):
@@ -141,7 +142,7 @@
     )(parts)
 
 
-def prep_kernel(tokens_ref, gain_ref, out_ref, block_ref, sems):
+def prep_kernel(tokens_ref, gain_ref, w_ref, out_ref, padded_ref, block_ref, sems):
     rows = tokens_ref.shape[0]
     states = tokens_ref[...].astype(F32)
     sums = jnp.sum(states * states, axis=1, keepdims=True)
@@ -149,7 +150,7 @@
     pieces = three(jnp.concatenate([left[:, :HEAD], left[:, HEAD:]], axis=0))
     for q in range(4):
         at = slice(q * HEAD, (q + 1) * HEAD)
-        gain = gain_ref[:, at].astype(F32)
+        gain = gain_ref[at].astype(F32).reshape(1, HEAD)
         extra = jnp.concatenate([*pieces, gain, jnp.zeros((9, HEAD), F32)], axis=0)
         block_ref[q // 2, q % 2, :rows] = tokens_ref[:, at]
         block_ref[q // 2, q % 2, rows:] = extra.astype(BF16)
@@ -158,21 +159,27 @@
     ]
     for copy in copies:
         copy.start()
+    depth = w_ref.shape[0]
+    padded_ref[:depth] = w_ref[...]
+    padded_ref[depth:] = jnp.zeros((padded_ref.shape[0] - depth, w_ref.shape[1]), BF16)
     for copy in copies:
         copy.wait()
 
 
-def prep(tokens, gain):
+def prep(tokens, gain, w):
     vmem = pl.BlockSpec(memory_space=pltpu.VMEM)
     rows = tokens.shape[0] + 16
     return pl.pallas_call(
         prep_kernel,
-        out_shape=jax.ShapeDtypeStruct((2, 8, 2, rows, HEAD), BF16),
-        in_specs=[vmem, vmem],
-        out_specs=pl.BlockSpec(memory_space=pltpu.HBM),
+        out_shape=(
+            jax.ShapeDtypeStruct((2, 8, 2, rows, HEAD), BF16),
+            jax.ShapeDtypeStruct((w.shape[0] + 64, w.shape[1]), BF16),
+        ),
+        in_specs=[vmem, vmem, vmem],
+        out_specs=(pl.BlockSpec(memory_space=pltpu.HBM), vmem),
         scratch_shapes=[pltpu.VMEM((2, 2, rows, HEAD), BF16), pltpu.SemaphoreType.DMA((8,))],
         compiler_params=pltpu.CompilerParams(vmem_limit_bytes=60 * 1024 * 1024),
-    )(tokens, gain)
+    )(tokens, gain, w)
 
 
 def kv_kernel(parts_ref, w_ref, out_ref, kv_ref, t_ref, sems):
@@ -217,28 +224,28 @@
     )(parts, w)
 
 
-def q_kernel(place, mine_ref, other_ref, w_ref, out_ref):
-    core = place[3]
+def q_kernel(place, mine_ref, other_ref, w_ref, keep_ref, send_ref):
+    xh, core = place[1], place[3]
     rows = mine_ref.shape[1]
     half = mine_ref.shape[2] // w_ref.shape[0]
-    for xh in range(2):
+    for out_ref, x in ((send_ref, 1 - xh), (keep_ref, xh)):
         total = jnp.zeros((rows, w_ref.shape[2]), F32)
         for c in range(w_ref.shape[0]):
-            t = jnp.concatenate([ref[xh, :, c * half : (c + 1) * half] for ref in (mine_ref, other_ref)], axis=1)
+            t = jnp.concatenate([ref[x, :, c * half : (c + 1) * half] for ref in (mine_ref, other_ref)], axis=1)
             w = jnp.concatenate(
                 [w_ref[c, pl.ds(pl.multiple_of(at * half, half), half)] for at in (core, 1 - core)], axis=0
             )
             total += jnp.dot(t, w, preferred_element_type=F32)
-        out_ref[xh] = total
+        out_ref[...] = total.astype(out_ref.dtype)
 
 
 def project_q(place, mine, other, w):
     vmem = pl.BlockSpec(memory_space=pltpu.VMEM)
     return pl.pallas_call(
         q_kernel,
-        out_shape=jax.ShapeDtypeStruct((*mine.shape[:2], w.shape[2]), F32),
+        out_shape=[jax.ShapeDtypeStruct((mine.shape[1], w.shape[2]), kind) for kind in (F32, BF16)],
         in_specs=[pl.BlockSpec(memory_space=pltpu.SMEM), vmem, vmem, vmem],
-        out_specs=vmem,
+        out_specs=[vmem, vmem],
         compiler_params=pltpu.CompilerParams(vmem_limit_bytes=40 * 1024 * 1024),
         cost_estimate=pl.CostEstimate(flops=2**30, bytes_accessed=6 * 2**20, transcendentals=0),
     )(place, mine, other, w)
@@ -251,10 +258,12 @@
     rows, feats = tokens.shape
     half = w_key.shape[0] // 2
 
+    with jax.named_scope("prep"):
+        parts, padded = prep(tokens, norm_gain, w_query)
+
     with jax.named_scope("weights"):
-        wq = lax.all_gather(jnp.pad(w_query, ((0, 64), (0, 0))), ("zh", "zl"), axis=0)
-        head = at(("xl", "yh"))
-        start = (core * half, head * HEAD)
+        wq = lax.all_gather(padded, ("zh", "zl"), axis=0)
+        start = (core * half, at(("xl", "yh")) * HEAD)
         wkv = jnp.where(
             at("yl") == 0,
             lax.dynamic_slice(w_key, start, (half, HEAD)),
@@ -263,7 +272,6 @@
         wkv = lax.all_gather(lax.all_gather(wkv, "zh"), "zl")
 
     with jax.named_scope("spread"):
-        parts = prep(tokens, norm_gain.reshape(1, feats))
         parts = lax.all_to_all(parts.reshape(32, rows + 16, HEAD), ("xh",) + COL, 0, 0)
         parts = parts.reshape(2, 16, rows + 16, HEAD)
 
@@ -275,18 +283,24 @@
 
     with jax.named_scope("project_q"):
         kv, whole = lax.optimization_barrier((kv, whole))
-        q = project_q(place, whole, swap(whole), wq)
+        q_keep, q_send = project_q(place, whole, swap(whole), wq)
+        q = (q_keep + lax.ppermute(q_send, "xh", [(0, 1), (1, 0)]).astype(F32)).astype(BF16)
 
     with jax.named_scope("gather_kv"):
         kv, q = lax.optimization_barrier((gather(kv, "zh", 4), q))
         kv = gather(kv, "zl", 4)
 
     with jax.named_scope("swap_q"):
-        q = (q + lax.ppermute(q, "xh", [(0, 1), (1, 0)])).astype(BF16)
-        pair = lax.ppermute(q, "yl", [(0, 1), (1, 0)])
+        queries = (
+            q,
+            lax.ppermute(q, "xh", [(0, 1), (1, 0)]),
+            lax.ppermute(q, "yl", [(0, 1), (1, 0)]),
+            lax.ppermute(q, ("xh", "yl"), [(0, 3), (1, 2), (2, 1), (3, 0)]),
+        )
 
     with jax.named_scope("attend"):
-        out = attend(place, q, pair, kv, swap(kv))
+        kv, queries = lax.optimization_barrier((kv, queries))
+        out = attend(place, queries, kv, swap(kv))
         return merge(lax.all_to_all(out, ("xh", "yl"), 0, 0))
 
 

time: 160 us -> 161 us (level)
  the two profiles are of different devices: /device:TPU:1 before, /device:TPU:480 now
where the time goes in v7:
time: 161 us; the launch traced here: 160 us
  blocking collectives  63.3 us (39%)
  starting transfers between devices  41.4 us (26%)
  waiting for transfers between devices  18.2 us (11%)
  Pallas kernels  16.5 us (10%)
  between operations  13.5 us (8%)
  local copies, waits for them, and re-layouts  6.19 us (4%)
    all_gather x2, blocking collectives, on_device(): wkv = lax.all_gather(lax.all_gather(wkv, 'zh'), 'zl')  37.2 us
    all_to_all x2, starting transfers between devices, gather(): return lax.all_to_all(jnp.broadcast_to(x[None], (n, *x.shape)), axes, 0, 0)  15.4 us
    all_to_all x1, blocking collectives, on_device(): return merge(lax.all_to_all(out, ('xh', 'yl'), 0, 0))  13.6 us
    all_to_all x1, blocking collectives, on_device(): lax.all_to_all(kv_sum.reshape(8, rows // 4, HEAD), ('xh', 'yl', 'core'),...  12.4 us
    pallas_call x1, Pallas kernels, attend(): pl.pallas_call(attend_kernel, out_shape=jax.ShapeDtypeStruct((4, rows + 1...  8.68 us
    all_to_all x1, starting transfers between devices, on_device(): lax.all_to_all(parts.reshape(32, rows + 16, HEAD), ('xh',) + COL, 0, 0)  7.33 us
    ppermute x1, waiting for transfers between devices, on_device(): lax.ppermute(q, ('xh', 'yl'), [(0, 3), (1, 2), (2, 1), (3, 0)])  6.33 us
    ppermute x1, starting transfers between devices, on_device(): lax.ppermute(q, 'yl', [(0, 1), (1, 0)])  5.49 us
  transfers between devices with their start and end apart: 10, of which 5 were waited for; matrix products, arithmetic and copies ran while one was open for 1% of the time, Pallas kernels for 2%

profile of v7, /device:TPU:480, one launch (start us, length us, event | category | flops | bytes accessed | tf_op | source)
XLA Modules:
  0.0 160.1 jit_solution(6037227350315608927)
XLA Ops:
  6.5 3.3 %prep.1 = (bf16[2,8,2,272,128]{4,3,2,1,0:T(8,128)(2,1)}, bf16[320,256]{1,0:T(8,128)(2,1)}) custom-call(bf16[256,512]{1,0:T(8,128)(2,1)} %tokens_ref.1, bf16[512]{0:T(512)(128)(2,1)} %gain_ref.1, bf16[256,256]{1,0:T(8,128)(2,1)} %w_ref.1), custom_call_target="tpu_custom_call" | custom-call | tf_op jit(solution)/shard_map/prep/pallas_call | solution.py:172
  9.9 0.0 all-gather.5.cloned.1.call-update
  9.9 7.3 %all-to-all-start = ((bf16[32,272,128]{2,1,0:T(8,128)(2,1)}), bf16[32,272,128]{2,1,0:T(8,128)(2,1)S(1)}, u32[]{:S(2)}, u32[]{:S(2)}) async-start(bf16[32,272,128]{2,1,0:T(8,128)(2,1)} %bitcast.19), calls=%async_computation | async-start | bytes 4456448 | tf_op jit(solution)/shard_map/spread/all_to_all | solution.py:275
  17.3 0.8 dynamic-slice_select_fusion
  18.0 18.1 %all-gather = bf16[512,128]{1,0:T(8,128)(2,1)S(1)} all-gather(bf16[128,128]{1,0:T(8,128)(2,1)S(1)} %dynamic-slice_select_fusion), channel_id=2, replica_groups=mesh['zh'=4,'zl'=4,'xh'=2,'xl'=2,'yh'=2,'yl'=2,'core'=2] {'zh'}, dimensions={0}, use_global_device_ids=true | all-gather | bytes 163840 | tf_op jit(solution)/shard_map/weights/all_gather | solution.py:272
  36.1 19.2 %all-gather.1 = bf16[16,128,128]{2,1,0:T(8,128)(2,1)S(1)} all-gather(bf16[4,128,128]{2,1,0:T(8,128)(2,1)S(1)} %bitcast.21), channel_id=3, replica_groups=mesh['zh'=4,'zl'=4,'xh'=2,'xl'=2,'yh'=2,'yl'=2,'core'=2] {'zl'}, dimensions={0}, use_global_device_ids=true | all-gather | bytes 655360 | tf_op jit(solution)/shard_map/weights/all_gather | solution.py:272
  55.3 1.5 project_kv.1
  56.9 1.3 copy-done.1
  58.2 12.4 %all_to_all.25 = f32[8,64,128]{2,1,0:T(8,128)S(1)} all-to-all(f32[8,64,128]{2,1,0:T(8,128)S(1)} %bitcast.18), channel_id=1, replica_groups=mesh['zh'=4,'zl'=4,'xh'=2,'xl'=2,'yh'=2,'yl'=2,'core'=2] {'xh','yl','core'}, dimensions={0} | all-to-all | bytes 524288 | tf_op jit(solution)/shard_map/project_kv/all_to_all | solution.py:280
  70.7 1.9 %collective-permute-start = (bf16[2,256,2048]{2,1,0:T(8,128)(2,1)}, bf16[2,256,2048]{2,1,0:T(8,128)(2,1)S(1)}, u32[]{:S(2)}, u32[]{:S(2)}) collective-permute-start(bf16[2,256,2048]{2,1,0:T(8,128)(2,1)} %copy-done.1), channel_id=1, source_target_pairs={{0,1},{1,0},{2,3},{3,2},{4,5},{5,4},{6,7},{7,6},{8,9},{9,8},{10,11... | collective-permute-start | bytes 6291464 | tf_op jit(solution)/shard_map/project_q/ppermute | solution.py:26
  72.6 0.1 pad_add_fusion.place
  72.7 0.7 broadcast_in_dim.4
  73.3 10.3 %all-to-all-start.2 = ((bf16[4,64,256]{2,1,0:T(8,128)(2,1)}), bf16[4,64,256]{2,1,0:T(8,128)(2,1)S(1)}, u32[]{:S(2)}, u32[]{:S(2)}) async-start(bf16[4,64,256]{2,1,0:T(8,128)(2,1)} %broadcast_in_dim.4), calls=%async_computation.2 | async-start | bytes 262144 | tf_op jit(solution)/shard_map/gather_kv/all_to_all | solution.py:22
  83.6 0.0 collective-permute-done.other_ref
  83.6 4.4 %all-gather.5.cloned.1.call-done = bf16[5120,256]{1,0:T(8,128)(2,1)} async-done(((bf16[320,256]{1,0:T(8,128)(2,1)}), bf16[5120,256]{1,0:T(8,128)(2,1)}) %all-gather.5.cloned.1.call-update) | async-done | bytes 2621456 | tf_op jit(solution)/shard_map/weights/all_gather | solution.py:265
  88.0 1.7 %copy-done = bf16[5120,256]{1,0:T(8,128)(2,1)S(1)} copy-done((bf16[5120,256]{1,0:T(8,128)(2,1)S(1)}, bf16[5120,256]{1,0:T(8,128)(2,1)}, u32[]{:S(2)}) %copy-start) | copy-done | bytes 2621464
  89.7 1.6 copy-done.2
  91.3 1.8 %project_q.1 = (f32[256,256]{1,0:T(8,128)S(1)}, bf16[256,256]{1,0:T(8,128)(2,1)S(1)}) custom-call(s32[4]{0:T(128)S(1)} %pad_add_fusion.place, bf16[2,256,2048]{2,1,0:T(8,128)(2,1)S(1)} %copy-done.2, bf16[2,256,2048]{2,1,0:T(8,128)(2,1)S(1)} %collective-permute-done.other_ref, bf16[16,320,256]{2,1,0:T(8,128)(2,1)S(1)} %bitcast.16), custom_call_target="tpu_custom_call" | custom-call | flops 1073741824 | bytes 6291456 | tf_op jit(solution)/shard_map/project_q/pallas_call | solution.py:244
  93.1 3.8 %collective-permute-start.1 = (bf16[256,256]{1,0:T(8,128)(2,1)S(1)}, bf16[256,256]{1,0:T(8,128)(2,1)S(1)}, u32[]{:S(2)}, u32[]{:S(2)}) collective-permute-start(bf16[256,256]{1,0:T(8,128)(2,1)S(1)} %get-tuple-element.27), channel_id=1, source_target_pairs={{0,16},{16,0},{1,17},{17,1},{2,18},{18,2},{3,19},{19,3},{4,20},{20... | collective-permute-start | bytes 393224 | tf_op jit(solution)/shard_map/project_q/ppermute | solution.py:287
  96.9 4.6 %collective-permute-done.1 = bf16[256,256]{1,0:T(8,128)(2,1)S(1)} collective-permute-done((bf16[256,256]{1,0:T(8,128)(2,1)S(1)}, bf16[256,256]{1,0:T(8,128)(2,1)S(1)}, u32[]{:S(2)}, u32[]{:S(2)}) %collective-permute-start.1) | collective-permute-done | bytes 131104 | tf_op jit(solution)/shard_map/project_q/ppermute | solution.py:287
  101.6 0.9 broadcast_in_dim.5
  102.4 5.1 %all-to-all-start.3 = ((bf16[4,4,64,256]{3,2,1,0:T(8,128)(2,1)}), bf16[4,4,64,256]{3,2,1,0:T(8,128)(2,1)S(1)}, u32[]{:S(2)}, u32[]{:S(2)}) async-start(bf16[4,4,64,256]{3,2,1,0:T(8,128)(2,1)} %broadcast_in_dim.5), calls=%async_computation.3 | async-start | bytes 1048576 | tf_op jit(solution)/shard_map/gather_kv/all_to_all | solution.py:22
  107.5 3.7 %collective-permute-start.2 = (bf16[256,256]{1,0:T(8,128)(2,1)S(1)}, bf16[256,256]{1,0:T(8,128)(2,1)S(1)}, u32[]{:S(2)}, u32[]{:S(2)}) collective-permute-start(bf16[256,256]{1,0:T(8,128)(2,1)S(1)} %add_convert_fusion.q0_ref), channel_id=1, source_target_pairs={{0,16},{16,0},{1,17},{17,1},{2,18},{18,2},{3,19},{19,3},{4,20},{20... | collective-permute-start | bytes 393224 | tf_op jit(solution)/shard_map/swap_q/ppermute | solution.py:296
  111.3 5.5 %collective-permute-start.3 = (bf16[256,256]{1,0:T(8,128)(2,1)S(1)}, bf16[256,256]{1,0:T(8,128)(2,1)S(1)}, u32[]{:S(2)}, u32[]{:S(2)}) collective-permute-start(bf16[256,256]{1,0:T(8,128)(2,1)S(1)} %add_convert_fusion.q0_ref), channel_id=1, source_target_pairs={{0,2},{2,0},{1,3},{3,1},{4,6},{6,4},{5,7},{7,5},{8,10},{10,8},{9,1... | collective-permute-start | bytes 393224 | tf_op jit(solution)/shard_map/swap_q/ppermute | solution.py:297
  116.8 1.9 %collective-permute-start.4 = (bf16[256,256]{1,0:T(8,128)(2,1)S(1)}, bf16[256,256]{1,0:T(8,128)(2,1)S(1)}, u32[]{:S(2)}, u32[]{:S(2)}) collective-permute-start(bf16[256,256]{1,0:T(8,128)(2,1)S(1)} %add_convert_fusion.q0_ref), channel_id=1, source_target_pairs={{0,18},{2,16},{16,2},{18,0},{1,19},{3,17},{17,3},{19,1},{4,22},{6,... | collective-permute-start | bytes 393224 | tf_op jit(solution)/shard_map/swap_q/ppermute | solution.py:298
  118.7 1.0 collective-permute-done.3.q2_ref
  119.7 6.3 %collective-permute-done.4.q3_ref = bf16[256,256]{1,0:T(8,128)(2,1)S(1)} collective-permute-done((bf16[256,256]{1,0:T(8,128)(2,1)S(1)}, bf16[256,256]{1,0:T(8,128)(2,1)S(1)}, u32[]{:S(2)}, u32[]{:S(2)}) %collective-permute-start.4) | collective-permute-done | bytes 131104 | tf_op jit(solution)/shard_map/swap_q/ppermute | solution.py:298
  126.0 1.9 %collective-permute-start.5 = (bf16[4,4,64,256]{3,2,1,0:T(8,128)(2,1)S(1)}, bf16[4,4,64,256]{3,2,1,0:T(8,128)(2,1)S(1)}, u32[]{:S(2)}, u32[]{:S(2)}) collective-permute-start(bf16[4,4,64,256]{3,2,1,0:T(8,128)(2,1)S(1)} %all-to-all-done.3.mine_ref), channel_id=1, source_target_pairs={{0,1},{1,0},{2,3},{3,2},{4,5},{5,4},{6,7},{7,6},{8,9},{9,8},{10,11... | collective-permute-start | bytes 1572872 | tf_op jit(solution)/shard_map/attend/ppermute | solution.py:26
  127.9 1.9 %collective-permute-done.5.other_ref = bf16[4,4,64,256]{3,2,1,0:T(8,128)(2,1)S(1)} collective-permute-done((bf16[4,4,64,256]{3,2,1,0:T(8,128)(2,1)S(1)}, bf16[4,4,64,256]{3,2,1,0:T(8,128)(2,1)S(1)}, u32[]{:S(2)}, u32[]{:S(2)}) %collective-permute-start.5) | collective-permute-done | bytes 524320 | tf_op jit(solution)/shard_map/attend/ppermute | solution.py:26
  129.8 8.7 %attend.2 = bf16[4,272,256]{2,1,0:T(8,128)(2,1)S(1)} custom-call(s32[4]{0:T(128)S(1)} %pad_add_fusion.place, bf16[256,256]{1,0:T(8,128)(2,1)S(1)} %add_convert_fusion.q0_ref, bf16[256,256]{1,0:T(8,128)(2,1)S(1)} %collective-permute-done.2.q1_ref, bf16[256,256]{1,0:T(8,128)(2,1)S(1)} %collective-permute-done.3.q2_ref, ...), custom_call_target="tpu_custom_call" | custom-call | flops 2147483648 | bytes 4194304 | tf_op jit(solution)/shard_map/attend/pallas_call | solution.py:109
  138.5 13.6 %all_to_all.26.parts_ref = bf16[4,272,256]{2,1,0:T(8,128)(2,1)S(1)} all-to-all(bf16[4,272,256]{2,1,0:T(8,128)(2,1)S(1)} %attend.2), channel_id=1, replica_groups=mesh['zh'=4,'zl'=4,'xh'=2,'xl'=2,'yh'=2,'yl'=2,'core'=2] {'xh','yl'}, dimensions={0} | all-to-all | bytes 1114112 | tf_op jit(solution)/shard_map/attend/all_to_all | solution.py:304
  152.1 1.2 attend.3
  (12 shorter events, 0.1 us)
Async XLA Ops:
  6.5 81.5 %all-gather.5.cloned.1.call-start = ((), (), s32[]{:S(2)}) async-start(), calls=%async_computation.5 | async-start | bytes 2785280 | tf_op jit(solution)/shard_map/weights/all_gather | solution.py:265
  9.9 45.4 %all-to-all-start = ((bf16[32,272,128]{2,1,0:T(8,128)(2,1)}), bf16[32,272,128]{2,1,0:T(8,128)(2,1)S(1)}, u32[]{:S(2)}, u32[]{:S(2)}) async-start(bf16[32,272,128]{2,1,0:T(8,128)(2,1)} %bitcast.19), calls=%async_computation | async-start | bytes 4456448 | tf_op jit(solution)/shard_map/spread/all_to_all | solution.py:275
  56.8 1.3 copy-start.1
  70.7 13.0 %collective-permute-start = (bf16[2,256,2048]{2,1,0:T(8,128)(2,1)}, bf16[2,256,2048]{2,1,0:T(8,128)(2,1)S(1)}, u32[]{:S(2)}, u32[]{:S(2)}) collective-permute-start(bf16[2,256,2048]{2,1,0:T(8,128)(2,1)} %copy-done.1), channel_id=1, source_target_pairs={{0,1},{1,0},{2,3},{3,2},{4,5},{5,4},{6,7},{7,6},{8,9},{9,8},{10,11... | collective-permute-start | bytes 6291464 | tf_op jit(solution)/shard_map/project_q/ppermute | solution.py:26
  73.3 28.2 %all-to-all-start.2 = ((bf16[4,64,256]{2,1,0:T(8,128)(2,1)}), bf16[4,64,256]{2,1,0:T(8,128)(2,1)S(1)}, u32[]{:S(2)}, u32[]{:S(2)}) async-start(bf16[4,64,256]{2,1,0:T(8,128)(2,1)} %broadcast_in_dim.4), calls=%async_computation.2 | async-start | bytes 262144 | tf_op jit(solution)/shard_map/gather_kv/all_to_all | solution.py:22
  88.0 1.7 %copy-start = (bf16[5120,256]{1,0:T(8,128)(2,1)S(1)}, bf16[5120,256]{1,0:T(8,128)(2,1)}, u32[]{:S(2)}) copy-start(bf16[5120,256]{1,0:T(8,128)(2,1)} %all-gather.5.cloned.1.call-done) | copy-start | bytes 7864324
  89.7 1.6 copy-start.2
  93.1 8.4 %collective-permute-start.1 = (bf16[256,256]{1,0:T(8,128)(2,1)S(1)}, bf16[256,256]{1,0:T(8,128)(2,1)S(1)}, u32[]{:S(2)}, u32[]{:S(2)}) collective-permute-start(bf16[256,256]{1,0:T(8,128)(2,1)S(1)} %get-tuple-element.27), channel_id=1, source_target_pairs={{0,16},{16,0},{1,17},{17,1},{2,18},{18,2},{3,19},{19,3},{4,20},{20... | collective-permute-start | bytes 393224 | tf_op jit(solution)/shard_map/project_q/ppermute | solution.py:287
  102.4 23.6 %all-to-all-start.3 = ((bf16[4,4,64,256]{3,2,1,0:T(8,128)(2,1)}), bf16[4,4,64,256]{3,2,1,0:T(8,128)(2,1)S(1)}, u32[]{:S(2)}, u32[]{:S(2)}) async-start(bf16[4,4,64,256]{3,2,1,0:T(8,128)(2,1)} %broadcast_in_dim.5), calls=%async_computation.3 | async-start | bytes 1048576 | tf_op jit(solution)/shard_map/gather_kv/all_to_all | solution.py:22
  107.5 11.2 %collective-permute-start.2 = (bf16[256,256]{1,0:T(8,128)(2,1)S(1)}, bf16[256,256]{1,0:T(8,128)(2,1)S(1)}, u32[]{:S(2)}, u32[]{:S(2)}) collective-permute-start(bf16[256,256]{1,0:T(8,128)(2,1)S(1)} %add_convert_fusion.q0_ref), channel_id=1, source_target_pairs={{0,16},{16,0},{1,17},{17,1},{2,18},{18,2},{3,19},{19,3},{4,20},{20... | collective-permute-start | bytes 393224 | tf_op jit(solution)/shard_map/swap_q/ppermute | solution.py:296
  111.3 8.4 %collective-permute-start.3 = (bf16[256,256]{1,0:T(8,128)(2,1)S(1)}, bf16[256,256]{1,0:T(8,128)(2,1)S(1)}, u32[]{:S(2)}, u32[]{:S(2)}) collective-permute-start(bf16[256,256]{1,0:T(8,128)(2,1)S(1)} %add_convert_fusion.q0_ref), channel_id=1, source_target_pairs={{0,2},{2,0},{1,3},{3,1},{4,6},{6,4},{5,7},{7,5},{8,10},{10,8},{9,1... | collective-permute-start | bytes 393224 | tf_op jit(solution)/shard_map/swap_q/ppermute | solution.py:297
  116.8 9.3 %collective-permute-start.4 = (bf16[256,256]{1,0:T(8,128)(2,1)S(1)}, bf16[256,256]{1,0:T(8,128)(2,1)S(1)}, u32[]{:S(2)}, u32[]{:S(2)}) collective-permute-start(bf16[256,256]{1,0:T(8,128)(2,1)S(1)} %add_convert_fusion.q0_ref), channel_id=1, source_target_pairs={{0,18},{2,16},{16,2},{18,0},{1,19},{3,17},{17,3},{19,1},{4,22},{6,... | collective-permute-start | bytes 393224 | tf_op jit(solution)/shard_map/swap_q/ppermute | solution.py:298
  126.0 3.8 %collective-permute-start.5 = (bf16[4,4,64,256]{3,2,1,0:T(8,128)(2,1)S(1)}, bf16[4,4,64,256]{3,2,1,0:T(8,128)(2,1)S(1)}, u32[]{:S(2)}, u32[]{:S(2)}) collective-permute-start(bf16[4,4,64,256]{3,2,1,0:T(8,128)(2,1)S(1)} %all-to-all-done.3.mine_ref), channel_id=1, source_target_pairs={{0,1},{1,0},{2,3},{3,2},{4,5},{5,4},{6,7},{7,6},{8,9},{9,8},{10,11... | collective-permute-start | bytes 1572872 | tf_op jit(solution)/shard_map/attend/ppermute | solution.py:26
Sparse Core Ops, SparseCore 0:
  10.0 77.9 all-gather.4

commit v8 on v7

--- a/solution.py
+++ b/solution.py
@@ -35,9 +35,10 @@
     return pieces
 
 
-def attend_kernel(place, q0_ref, q1_ref, q2_ref, q3_ref, mine_ref, other_ref, out_ref, m_ref, l_ref, acc_ref):
+def attend_kernel(side, place, q_ref, mine_ref, other_ref, *refs):
+    out_ref, m_ref, l_ref, acc_ref = refs[-4:]
     z, xh, yl, core = place[0], place[1], place[2], place[3]
-    rows = q0_ref.shape[0]
+    rows = q_ref.shape[1]
     scale = HEAD**-0.5 * math.log2(math.e)
     m_ref[...] = jnp.full(m_ref.shape, -1e30, F32)
     l_ref[...] = jnp.zeros(l_ref.shape, F32)
@@ -55,13 +56,10 @@
             within = lax.rem(slot, half)
             owner = jnp.where(slot < half, core, 1 - core) + 4 * xh + 2 * yl
             key_pos = lax.div(within, chunk) * (2 * rows) + owner * chunk + lax.rem(within, chunk)
-            query = lax.broadcasted_iota(jnp.int32, shape, 0)
-            query = lax.rem(query + xh * rows, 2 * rows)
-            query_pos = lax.rem(z, 4) * (2 * rows) + query
+            query_pos = lax.rem(z, 4) * (2 * rows) + lax.broadcasted_iota(jnp.int32, shape, 0)
             seen = key_pos <= query_pos
-        for head in range(4):
-            at = slice(head % 2 * HEAD, (head % 2 + 1) * HEAD)
-            q = jnp.concatenate([ref[:, at] for ref in ((q0_ref, q1_ref), (q2_ref, q3_ref))[head // 2]], axis=0)
+        for head in range(2):
+            q = q_ref[:, :, head * HEAD : (head + 1) * HEAD].reshape(2 * rows, HEAD)
             s = lax.dot_general(q, kv[:, :HEAD], (((1,), (1,)), ((), ())), preferred_element_type=F32)
             if masked:
                 s = jnp.where(seen, s, -1e30)
@@ -79,42 +77,41 @@
             m_ref[head] = m_new
             acc_ref[head] = acc_ref[head] * alpha + jnp.dot(p, kv[:, HEAD:], preferred_element_type=F32)
 
-    mine_group = lax.div(z, 4)
-
-    @pl.loop(0, mine_group)
+    last = lax.div(z, 4)
+
+    @pl.loop(0, last)
     def _(group):
         block(group, False)
 
-    block(mine_group, True)
+    block(last, True)
     lane = lax.broadcasted_iota(jnp.int32, (2 * rows, HEAD), 1)
-    for side in range(2):
-        to = yl if side == 0 else 1 - yl
-        stats = jnp.zeros((2 * rows, HEAD), F32)
-        for i in range(2):
-            head = side * 2 + i
-            total = jnp.sum(l_ref[head], axis=1, keepdims=True)
-            stats = jnp.where(lane == i, m_ref[head] * scale + jnp.log2(total), stats)
-            part = (acc_ref[head] / total).astype(BF16)
-            for x in range(2):
-                out_ref[2 * (x ^ xh) + to, :rows, i * HEAD : (i + 1) * HEAD] = part[x * rows : (x + 1) * rows]
+    to = yl if side == 0 else 1 - yl
+    stats = jnp.zeros((2 * rows, HEAD), F32)
+    for head in range(2):
+        total = jnp.sum(l_ref[head], axis=1, keepdims=True)
+        stats = jnp.where(lane == head, m_ref[head] * scale + jnp.log2(total), stats)
+        part = (acc_ref[head] / total).astype(BF16)
         for x in range(2):
-            sums = three(jnp.transpose(stats[x * rows : (x + 1) * rows])[:2])
-            sums = jnp.concatenate([*sums, jnp.zeros((10, 2 * HEAD), F32)], axis=0)
-            out_ref[2 * (x ^ xh) + to, rows:, :] = sums.astype(BF16)
-
-
-def attend(place, queries, mine, other):
-    rows, cols = queries[0].shape
-    vmem = pl.BlockSpec(memory_space=pltpu.VMEM)
-    return pl.pallas_call(
-        attend_kernel,
+            out_ref[2 * x + to, :rows, head * HEAD : (head + 1) * HEAD] = part[x * rows : (x + 1) * rows]
+    for x in range(2):
+        sums = three(jnp.transpose(stats[x * rows : (x + 1) * rows])[:2])
+        sums = jnp.concatenate([*sums, jnp.zeros((10, 2 * HEAD), F32)], axis=0)
+        out_ref[2 * x + to, rows:, :] = sums.astype(BF16)
+
+
+def attend(side, place, q, mine, other, *first):
+    rows, cols = q.shape[1:]
+    vmem = pl.BlockSpec(memory_space=pltpu.VMEM)
+    return pl.pallas_call(
+        functools.partial(attend_kernel, side),
         out_shape=jax.ShapeDtypeStruct((4, rows + 16, cols), BF16),
-        in_specs=[pl.BlockSpec(memory_space=pltpu.SMEM)] + [vmem] * 6,
+        in_specs=[pl.BlockSpec(memory_space=pltpu.SMEM)] + [vmem] * (3 + len(first)),
         out_specs=vmem,
-        scratch_shapes=[pltpu.VMEM((4, 2 * rows, HEAD), F32)] * 3,
+        scratch_shapes=[pltpu.VMEM((2, 2 * rows, HEAD), F32)] * 3,
+        input_output_aliases={4: 0} if first else {},
         compiler_params=pltpu.CompilerParams(vmem_limit_bytes=40 * 1024 * 1024),
-        cost_estimate=pl.CostEstimate(flops=2**31, bytes_accessed=2**22, transcendentals=2**22),
-    )(place, *queries, mine, other)
+        cost_estimate=pl.CostEstimate(flops=2**30, bytes_accessed=2**22, transcendentals=2**21),
+    )(place, q, mine, other, *first)
 
 
 def merge_kernel(parts_ref, out_ref):
@@ -224,11 +221,11 @@
     )(parts, w)
 
 
-def q_kernel(place, mine_ref, other_ref, w_ref, keep_ref, send_ref):
-    xh, core = place[1], place[3]
+def q_kernel(place, mine_ref, other_ref, w_ref, out_ref):
+    core = place[3]
     rows = mine_ref.shape[1]
     half = mine_ref.shape[2] // w_ref.shape[0]
-    for out_ref, x in ((send_ref, 1 - xh), (keep_ref, xh)):
+    for x in range(2):
         total = jnp.zeros((rows, w_ref.shape[2]), F32)
         for c in range(w_ref.shape[0]):
             t = jnp.concatenate([ref[x, :, c * half : (c + 1) * half] for ref in (mine_ref, other_ref)], axis=1)
@@ -236,16 +233,16 @@
                 [w_ref[c, pl.ds(pl.multiple_of(at * half, half), half)] for at in (core, 1 - core)], axis=0
             )
             total += jnp.dot(t, w, preferred_element_type=F32)
-        out_ref[...] = total.astype(out_ref.dtype)
+        out_ref[x] = total
 
 
 def project_q(place, mine, other, w):
     vmem = pl.BlockSpec(memory_space=pltpu.VMEM)
     return pl.pallas_call(
         q_kernel,
-        out_shape=[jax.ShapeDtypeStruct((mine.shape[1], w.shape[2]), kind) for kind in (F32, BF16)],
+        out_shape=jax.ShapeDtypeStruct((*mine.shape[:2], w.shape[2]), F32),
         in_specs=[pl.BlockSpec(memory_space=pltpu.SMEM), vmem, vmem, vmem],
-        out_specs=[vmem, vmem],
+        out_specs=vmem,
         compiler_params=pltpu.CompilerParams(vmem_limit_bytes=40 * 1024 * 1024),
         cost_estimate=pl.CostEstimate(flops=2**30, bytes_accessed=6 * 2**20, transcendentals=0),
     )(place, mine, other, w)
@@ -281,26 +278,19 @@
         chunks = jnp.sum(chunks.reshape(2, 2, 2, rows // 4, HEAD), axis=(0, 2)).astype(BF16)
         kv = jnp.concatenate([chunks[0], chunks[1]], axis=1)
 
+    with jax.named_scope("gather_kv"):
+        kv, wq = lax.optimization_barrier((lax.all_gather(kv, "zh"), wq))
+        kv = gather(kv, "zl", 4)
+
     with jax.named_scope("project_q"):
-        kv, whole = lax.optimization_barrier((kv, whole))
-        q_keep, q_send = project_q(place, whole, swap(whole), wq)
-        q = (q_keep + lax.ppermute(q_send, "xh", [(0, 1), (1, 0)]).astype(F32)).astype(BF16)
-
-    with jax.named_scope("gather_kv"):
-        kv, q = lax.optimization_barrier((gather(kv, "zh", 4), q))
-        kv = gather(kv, "zl", 4)
-
-    with jax.named_scope("swap_q"):
-        queries = (
-            q,
-            lax.ppermute(q, "xh", [(0, 1), (1, 0)]),
-            lax.ppermute(q, "yl", [(0, 1), (1, 0)]),
-            lax.ppermute(q, ("xh", "yl"), [(0, 3), (1, 2), (2, 1), (3, 0)]),
-        )
+        q = project_q(place, whole, swap(whole), wq)
+        q = (q + lax.ppermute(q, "xh", [(0, 1), (1, 0)])).astype(BF16)
+        pair = lax.ppermute(q, "yl", [(0, 1), (1, 0)])
 
     with jax.named_scope("attend"):
-        kv, queries = lax.optimization_barrier((kv, queries))
-        out = attend(place, queries, kv, swap(kv))
+        swapped = swap(kv)
+        out = attend(0, place, q, kv, swapped)
+        out = attend(1, place, pair, kv, swapped, out)
         return merge(lax.all_to_all(out, ("xh", "yl"), 0, 0))
 
 

time: 161 us -> 153 us (0.950)
  the two profiles are of different devices: /device:TPU:480 before, /device:TPU:16 now
where the time goes in v8:
time: 153 us
  blocking collectives  86.3 us (56%)
  starting transfers between devices  24.1 us (16%)
  between operations  13.5 us (9%)
  Pallas kernels  13.1 us (9%)
  waiting for transfers between devices  11.9 us (8%)
  local copies, waits for them, and re-layouts  2.6 us (2%)
    all_gather x2, blocking collectives, on_device(): wkv = lax.all_gather(lax.all_gather(wkv, 'zh'), 'zl')  42.2 us
    all_gather x1, blocking collectives, on_device(): kv, wq = lax.optimization_barrier((lax.all_gather(kv, 'zh'), wq))  19.9 us
    all_to_all x1, blocking collectives, on_device(): lax.all_to_all(kv_sum.reshape(8, rows // 4, HEAD), ('xh', 'yl', 'core'),...  12.2 us
    all_to_all x1, blocking collectives, on_device(): return merge(lax.all_to_all(out, ('xh', 'yl'), 0, 0))  12 us
    all_to_all x1, starting transfers between devices, on_device(): lax.all_to_all(parts.reshape(32, rows + 16, HEAD), ('xh',) + COL, 0, 0)  9.45 us
    ppermute x1, waiting for transfers between devices, on_device(): q = (q + lax.ppermute(q, 'xh', [(0, 1), (1, 0)])).astype(BF16)  5.09 us
    ppermute x1, starting transfers between devices, on_device(): q = (q + lax.ppermute(q, 'xh', [(0, 1), (1, 0)])).astype(BF16)  4.36 us
    ppermute x2, starting transfers between devices, swap(): return lax.ppermute(x, 'core', [(0, 1), (1, 0)])  3.83 us
  transfers between devices with their start and end apart: 7, of which 3 were waited for; matrix products, arithmetic and copies ran while one was open for 1% of the time, Pallas kernels for 4%

profile of v8, /device:TPU:16, one launch (start us, length us, event | category | flops | bytes accessed | tf_op | source)
XLA Modules:
  0.0 152.5 jit_solution(1520588873340987771)
XLA Ops:
  6.5 0.0 all-gather.6.cloned.1.call-start
  6.5 3.3 %prep.1 = (bf16[2,8,2,272,128]{4,3,2,1,0:T(8,128)(2,1)}, bf16[320,256]{1,0:T(8,128)(2,1)}) custom-call(bf16[256,512]{1,0:T(8,128)(2,1)} %tokens_ref.1, bf16[512]{0:T(512)(128)(2,1)} %gain_ref.1, bf16[256,256]{1,0:T(8,128)(2,1)} %w_ref.1), custom_call_target="tpu_custom_call" | custom-call | tf_op jit(solution)/shard_map/prep/pallas_call | solution.py:169
  9.8 0.0 all-gather.6.cloned.1.call-update
  9.9 9.4 %all-to-all-start = ((bf16[32,272,128]{2,1,0:T(8,128)(2,1)}), bf16[32,272,128]{2,1,0:T(8,128)(2,1)S(1)}, u32[]{:S(2)}, u32[]{:S(2)}) async-start(bf16[32,272,128]{2,1,0:T(8,128)(2,1)} %bitcast.20), calls=%async_computation | async-start | bytes 4456448 | tf_op jit(solution)/shard_map/spread/all_to_all | solution.py:272
  19.3 0.8 dynamic-slice_select_fusion
  20.1 24.1 %all-gather = bf16[512,128]{1,0:T(8,128)(2,1)S(1)} all-gather(bf16[128,128]{1,0:T(8,128)(2,1)S(1)} %dynamic-slice_select_fusion), channel_id=2, replica_groups=mesh['zh'=4,'zl'=4,'xh'=2,'xl'=2,'yh'=2,'yl'=2,'core'=2] {'zh'}, dimensions={0}, use_global_device_ids=true | all-gather | bytes 163840 | tf_op jit(solution)/shard_map/weights/all_gather | solution.py:269
  44.2 18.0 %all-gather.1 = bf16[16,128,128]{2,1,0:T(8,128)(2,1)S(1)} all-gather(bf16[4,128,128]{2,1,0:T(8,128)(2,1)S(1)} %bitcast.23), channel_id=3, replica_groups=mesh['zh'=4,'zl'=4,'xh'=2,'xl'=2,'yh'=2,'yl'=2,'core'=2] {'zl'}, dimensions={0}, use_global_device_ids=true | all-gather | bytes 655360 | tf_op jit(solution)/shard_map/weights/all_gather | solution.py:269
  62.3 0.0 all-to-all-done
  62.3 2.1 %project_kv.1 = (bf16[2,256,2048]{2,1,0:T(8,128)(2,1)}, f32[2,256,128]{2,1,0:T(8,128)S(1)}) custom-call(bf16[2,16,272,128]{3,2,1,0:T(8,128)(2,1)S(1)} %bitcast.16, bf16[4,4,128,128]{3,2,1,0:T(8,128)(2,1)S(1)} %bitcast.18), custom_call_target="tpu_custom_call" | custom-call | flops 268435456 | bytes 5242880 | tf_op jit(solution)/shard_map/project_kv/pallas_call | solution.py:210
  64.4 1.9 %collective-permute-start = (bf16[2,256,2048]{2,1,0:T(8,128)(2,1)}, bf16[2,256,2048]{2,1,0:T(8,128)(2,1)S(1)}, u32[]{:S(2)}, u32[]{:S(2)}) collective-permute-start(bf16[2,256,2048]{2,1,0:T(8,128)(2,1)} %get-tuple-element.12.mine_ref), channel_id=1, source_target_pairs={{0,1},{1,0},{2,3},{3,2},{4,5},{5,4},{6,7},{7,6},{8,9},{9,8},{10,11... | collective-permute-start | bytes 6291464 | tf_op jit(solution)/shard_map/project_q/ppermute | solution.py:26
  66.3 12.2 %all_to_all.20 = f32[8,64,128]{2,1,0:T(8,128)S(1)} all-to-all(f32[8,64,128]{2,1,0:T(8,128)S(1)} %bitcast.19), channel_id=1, replica_groups=mesh['zh'=4,'zl'=4,'xh'=2,'xl'=2,'yh'=2,'yl'=2,'core'=2] {'xh','yl','core'}, dimensions={0} | all-to-all | bytes 524288 | tf_op jit(solution)/shard_map/project_kv/all_to_all | solution.py:277
  78.6 19.9 %all-gather.2 = bf16[256,256]{1,0:T(8,128)(2,1)S(1)} all-gather(bf16[64,256]{1,0:T(8,128)(2,1)S(1)} %pad_maximum_fusion), channel_id=4, replica_groups=mesh['zh'=4,'zl'=4,'xh'=2,'xl'=2,'yh'=2,'yl'=2,'core'=2] {'zh'}, dimensions={0}, use_global_device_ids=true | all-gather | bytes 163840 | tf_op jit(solution)/shard_map/gather_kv/all_gather | solution.py:282
  98.5 0.0 all-gather.6.cloned.1.call-done
  98.5 0.9 broadcast_in_dim.2
  99.4 3.5 %all-to-all-start.2 = ((bf16[4,4,64,256]{3,2,1,0:T(8,128)(2,1)}), bf16[4,4,64,256]{3,2,1,0:T(8,128)(2,1)S(1)}, u32[]{:S(2)}, u32[]{:S(2)}) async-start(bf16[4,4,64,256]{3,2,1,0:T(8,128)(2,1)} %broadcast_in_dim.2), calls=%async_computation.2 | async-start | bytes 1048576 | tf_op jit(solution)/shard_map/gather_kv/all_to_all | solution.py:22
  102.8 0.1 pad_add_fusion.place
  102.9 0.0 collective-permute-done.other_ref
  102.9 0.0 copy-start
  102.9 1.7 %copy-done = bf16[5120,256]{1,0:T(8,128)(2,1)S(1)} copy-done((bf16[5120,256]{1,0:T(8,128)(2,1)S(1)}, bf16[5120,256]{1,0:T(8,128)(2,1)}, u32[]{:S(2)}) %copy-start) | copy-done | bytes 2621464
  104.7 2.9 %project_q.1 = f32[2,256,256]{2,1,0:T(8,128)S(1)} custom-call(s32[4]{0:T(128)S(1)} %pad_add_fusion.place, bf16[2,256,2048]{2,1,0:T(8,128)(2,1)} %get-tuple-element.12.mine_ref, bf16[2,256,2048]{2,1,0:T(8,128)(2,1)S(1)} %collective-permute-done.other_ref, bf16[16,320,256]{2,1,0:T(8,128)(2,1)S(1)} %bitcast.17), custom_call_target="tpu_custom_call" | custom-call | flops 1073741824 | bytes 6291456 | tf_op jit(solution)/shard_map/project_q/pallas_call | solution.py:241
  107.5 4.4 %collective-permute-start.1 = (f32[2,256,256]{2,1,0:T(8,128)S(1)}, f32[2,256,256]{2,1,0:T(8,128)S(1)}, u32[]{:S(2)}, u32[]{:S(2)}) collective-permute-start(f32[2,256,256]{2,1,0:T(8,128)S(1)} %project_q.1), channel_id=1, source_target_pairs={{0,16},{16,0},{1,17},{17,1},{2,18},{18,2},{3,19},{19,3},{4,20},{20... | collective-permute-start | bytes 1572872 | tf_op jit(solution)/shard_map/project_q/ppermute | solution.py:287
  111.9 3.4 %all-to-all-done.2.mine_ref = bf16[4,4,64,256]{3,2,1,0:T(8,128)(2,1)S(1)} async-done(((bf16[4,4,64,256]{3,2,1,0:T(8,128)(2,1)}), bf16[4,4,64,256]{3,2,1,0:T(8,128)(2,1)S(1)}, u32[]{:S(2)}, u32[]{:S(2)}) %all-to-all-start.2) | async-done | bytes 524320 | tf_op jit(solution)/shard_map/gather_kv/all_to_all | solution.py:22
  115.3 1.9 %collective-permute-start.3 = (bf16[4,4,64,256]{3,2,1,0:T(8,128)(2,1)S(1)}, bf16[4,4,64,256]{3,2,1,0:T(8,128)(2,1)S(1)}, u32[]{:S(2)}, u32[]{:S(2)}) collective-permute-start(bf16[4,4,64,256]{3,2,1,0:T(8,128)(2,1)S(1)} %all-to-all-done.2.mine_ref), channel_id=1, source_target_pairs={{0,1},{1,0},{2,3},{3,2},{4,5},{5,4},{6,7},{7,6},{8,9},{9,8},{10,11... | collective-permute-start | bytes 1572872 | tf_op jit(solution)/shard_map/attend/ppermute | solution.py:26
  117.2 5.1 %collective-permute-done.1 = f32[2,256,256]{2,1,0:T(8,128)S(1)} collective-permute-done((f32[2,256,256]{2,1,0:T(8,128)S(1)}, f32[2,256,256]{2,1,0:T(8,128)S(1)}, u32[]{:S(2)}, u32[]{:S(2)}) %collective-permute-start.1) | collective-permute-done | bytes 524320 | tf_op jit(solution)/shard_map/project_q/ppermute | solution.py:287
  122.3 0.1 add_convert_fusion.q_ref
  122.4 3.0 %collective-permute-start.2 = (bf16[2,256,256]{2,1,0:T(8,128)(2,1)S(1)}, bf16[2,256,256]{2,1,0:T(8,128)(2,1)S(1)}, u32[]{:S(2)}, u32[]{:S(2)}) collective-permute-start(bf16[2,256,256]{2,1,0:T(8,128)(2,1)S(1)} %add_convert_fusion.q_ref), channel_id=1, source_target_pairs={{0,2},{2,0},{1,3},{3,1},{4,6},{6,4},{5,7},{7,5},{8,10},{10,8},{9,1... | collective-permute-start | bytes 786440 | tf_op jit(solution)/shard_map/project_q/ppermute | solution.py:288
  125.4 0.0 collective-permute-done.3.other_ref
  125.4 1.8 %attend.3.refs_0_ = bf16[4,272,256]{2,1,0:T(8,128)(2,1)S(1)} custom-call(s32[4]{0:T(128)S(1)} %pad_add_fusion.place, bf16[2,256,256]{2,1,0:T(8,128)(2,1)S(1)} %add_convert_fusion.q_ref, bf16[4,4,64,256]{3,2,1,0:T(8,128)(2,1)S(1)} %all-to-all-done.2.mine_ref, bf16[4,4,64,256]{3,2,1,0:T(8,128)(2,1)S(1)} %collective-permute-done.3.other_ref), custom_call_target="tpu_custom_call" | custom-call | flops 1073741824 | bytes 4194304 | tf_op jit(solution)/shard_map/attend/pallas_call | solution.py:105
  127.2 3.4 %collective-permute-done.2.q_ref = bf16[2,256,256]{2,1,0:T(8,128)(2,1)S(1)} collective-permute-done((bf16[2,256,256]{2,1,0:T(8,128)(2,1)S(1)}, bf16[2,256,256]{2,1,0:T(8,128)(2,1)S(1)}, u32[]{:S(2)}, u32[]{:S(2)}) %collective-permute-start.2) | collective-permute-done | bytes 262176 | tf_op jit(solution)/shard_map/project_q/ppermute | solution.py:288
  130.6 1.8 %attend.4 = bf16[4,272,256]{2,1,0:T(8,128)(2,1)S(1)} custom-call(s32[4]{0:T(128)S(1)} %pad_add_fusion.place, bf16[2,256,256]{2,1,0:T(8,128)(2,1)S(1)} %collective-permute-done.2.q_ref, bf16[4,4,64,256]{3,2,1,0:T(8,128)(2,1)S(1)} %all-to-all-done.2.mine_ref, ...), custom_call_target="tpu_custom_call", output_to_operand_aliasing={{}: (4, {})} | custom-call | flops 1073741824 | bytes 4194304 | tf_op jit(solution)/shard_map/attend/pallas_call | solution.py:105
  132.5 12.0 %all_to_all.21.parts_ref = bf16[4,272,256]{2,1,0:T(8,128)(2,1)S(1)} all-to-all(bf16[4,272,256]{2,1,0:T(8,128)(2,1)S(1)} %attend.4), channel_id=1, replica_groups=mesh['zh'=4,'zl'=4,'xh'=2,'xl'=2,'yh'=2,'yl'=2,'core'=2] {'xh','yl'}, dimensions={0} | all-to-all | bytes 1114112 | tf_op jit(solution)/shard_map/attend/all_to_all | solution.py:294
  144.5 1.2 attend.5
  (3 shorter events, 0.0 us)
Async XLA Ops:
  6.5 92.0 %all-gather.6.cloned.1.call-start = ((), (), s32[]{:S(2)}) async-start(), calls=%async_computation.4 | async-start | bytes 2785280 | tf_op jit(solution)/shard_map/weights/all_gather | solution.py:262
  9.9 52.4 %all-to-all-start = ((bf16[32,272,128]{2,1,0:T(8,128)(2,1)}), bf16[32,272,128]{2,1,0:T(8,128)(2,1)S(1)}, u32[]{:S(2)}, u32[]{:S(2)}) async-start(bf16[32,272,128]{2,1,0:T(8,128)(2,1)} %bitcast.20), calls=%async_computation | async-start | bytes 4456448 | tf_op jit(solution)/shard_map/spread/all_to_all | solution.py:272
  64.4 38.5 %collective-permute-start = (bf16[2,256,2048]{2,1,0:T(8,128)(2,1)}, bf16[2,256,2048]{2,1,0:T(8,128)(2,1)S(1)}, u32[]{:S(2)}, u32[]{:S(2)}) collective-permute-start(bf16[2,256,2048]{2,1,0:T(8,128)(2,1)} %get-tuple-element.12.mine_ref), channel_id=1, source_target_pairs={{0,1},{1,0},{2,3},{3,2},{4,5},{5,4},{6,7},{7,6},{8,9},{9,8},{10,11... | collective-permute-start | bytes 6291464 | tf_op jit(solution)/shard_map/project_q/ppermute | solution.py:26
  99.4 15.9 %all-to-all-start.2 = ((bf16[4,4,64,256]{3,2,1,0:T(8,128)(2,1)}), bf16[4,4,64,256]{3,2,1,0:T(8,128)(2,1)S(1)}, u32[]{:S(2)}, u32[]{:S(2)}) async-start(bf16[4,4,64,256]{3,2,1,0:T(8,128)(2,1)} %broadcast_in_dim.2), calls=%async_computation.2 | async-start | bytes 1048576 | tf_op jit(solution)/shard_map/gather_kv/all_to_all | solution.py:22
  102.9 1.7 %copy-start = (bf16[5120,256]{1,0:T(8,128)(2,1)S(1)}, bf16[5120,256]{1,0:T(8,128)(2,1)}, u32[]{:S(2)}) copy-start(bf16[5120,256]{1,0:T(8,128)(2,1)} %all-gather.6.cloned.1.call-done) | copy-start | bytes 7864324
  107.5 14.8 %collective-permute-start.1 = (f32[2,256,256]{2,1,0:T(8,128)S(1)}, f32[2,256,256]{2,1,0:T(8,128)S(1)}, u32[]{:S(2)}, u32[]{:S(2)}) collective-permute-start(f32[2,256,256]{2,1,0:T(8,128)S(1)} %project_q.1), channel_id=1, source_target_pairs={{0,16},{16,0},{1,17},{17,1},{2,18},{18,2},{3,19},{19,3},{4,20},{20... | collective-permute-start | bytes 1572872 | tf_op jit(solution)/shard_map/project_q/ppermute | solution.py:287
  115.3 10.1 %collective-permute-start.3 = (bf16[4,4,64,256]{3,2,1,0:T(8,128)(2,1)S(1)}, bf16[4,4,64,256]{3,2,1,0:T(8,128)(2,1)S(1)}, u32[]{:S(2)}, u32[]{:S(2)}) collective-permute-start(bf16[4,4,64,256]{3,2,1,0:T(8,128)(2,1)S(1)} %all-to-all-done.2.mine_ref), channel_id=1, source_target_pairs={{0,1},{1,0},{2,3},{3,2},{4,5},{5,4},{6,7},{7,6},{8,9},{9,8},{10,11... | collective-permute-start | bytes 1572872 | tf_op jit(solution)/shard_map/attend/ppermute | solution.py:26
  122.4 8.3 %collective-permute-start.2 = (bf16[2,256,256]{2,1,0:T(8,128)(2,1)S(1)}, bf16[2,256,256]{2,1,0:T(8,128)(2,1)S(1)}, u32[]{:S(2)}, u32[]{:S(2)}) collective-permute-start(bf16[2,256,256]{2,1,0:T(8,128)(2,1)S(1)} %add_convert_fusion.q_ref), channel_id=1, source_target_pairs={{0,2},{2,0},{1,3},{3,1},{4,6},{6,4},{5,7},{7,5},{8,10},{10,8},{9,1... | collective-permute-start | bytes 786440 | tf_op jit(solution)/shard_map/project_q/ppermute | solution.py:288
Sparse Core Ops, SparseCore 0:
  10.0 82.9 all-gather.5

commit v9 on v8

--- a/solution.py
+++ b/solution.py
@@ -36,67 +36,61 @@
 
 
 def attend_kernel(side, place, q_ref, mine_ref, other_ref, *refs):
-    out_ref, m_ref, l_ref, acc_ref = refs[-4:]
+    out_ref = refs[-1]
     z, xh, yl, core = place[0], place[1], place[2], place[3]
     rows = q_ref.shape[1]
     scale = HEAD**-0.5 * math.log2(math.e)
-    m_ref[...] = jnp.full(m_ref.shape, -1e30, F32)
-    l_ref[...] = jnp.zeros(l_ref.shape, F32)
-    acc_ref[...] = jnp.zeros(acc_ref.shape, F32)
     chunk = mine_ref.shape[2]
     half = 4 * chunk
-
-    def block(group, masked):
-        kv = jnp.concatenate(
-            [mine_ref[:, group].reshape(half, 2 * HEAD), other_ref[:, group].reshape(half, 2 * HEAD)], axis=0
+    to = yl if side == 0 else 1 - yl
+    lane = lax.broadcasted_iota(jnp.int32, (rows, HEAD), 1)
+
+    def block(group):
+        return jnp.concatenate(
+            [ref[:, group].reshape(half, 2 * HEAD) for ref in (mine_ref, other_ref)], axis=0
         )
-        if masked:
-            shape = (2 * rows, 2 * half)
-            slot = lax.broadcasted_iota(jnp.int32, shape, 1)
-            within = lax.rem(slot, half)
-            owner = jnp.where(slot < half, core, 1 - core) + 4 * xh + 2 * yl
-            key_pos = lax.div(within, chunk) * (2 * rows) + owner * chunk + lax.rem(within, chunk)
-            query_pos = lax.rem(z, 4) * (2 * rows) + lax.broadcasted_iota(jnp.int32, shape, 0)
-            seen = key_pos <= query_pos
+
+    def run(last, x):
+        shape = (rows, 2 * half)
+        slot = lax.broadcasted_iota(jnp.int32, shape, 1)
+        within = lax.rem(slot, half)
+        owner = jnp.where(slot < half, core, 1 - core) + 4 * xh + 2 * yl
+        key_pos = lax.div(within, chunk) * (2 * rows) + owner * chunk + lax.rem(within, chunk)
+        query_pos = lax.rem(z, 4) * (2 * rows) + x * rows + lax.broadcasted_iota(jnp.int32, shape, 0)
+        seen = key_pos <= query_pos
+        stats = jnp.zeros((rows, HEAD), F32)
         for head in range(2):
-            q = q_ref[:, :, head * HEAD : (head + 1) * HEAD].reshape(2 * rows, HEAD)
-            s = lax.dot_general(q, kv[:, :HEAD], (((1,), (1,)), ((), ())), preferred_element_type=F32)
-            if masked:
-                s = jnp.where(seen, s, -1e30)
-            m_old = m_ref[head]
-            m_new = jnp.maximum(m_old, jnp.max(s, axis=1, keepdims=True))
-            alpha = jnp.exp2((m_old - m_new) * scale)
-            total = l_ref[head] * alpha
-            weights = []
-            for j in range(0, s.shape[1], HEAD):
-                w = jnp.exp2((s[:, j : j + HEAD] - m_new) * scale)
-                total = total + w
-                weights.append(w.astype(BF16))
-            p = jnp.concatenate(weights, axis=1)
-            l_ref[head] = total
-            m_ref[head] = m_new
-            acc_ref[head] = acc_ref[head] * alpha + jnp.dot(p, kv[:, HEAD:], preferred_element_type=F32)
-
-    last = lax.div(z, 4)
-
-    @pl.loop(0, last)
-    def _(group):
-        block(group, False)
-
-    block(last, True)
-    lane = lax.broadcasted_iota(jnp.int32, (2 * rows, HEAD), 1)
-    to = yl if side == 0 else 1 - yl
-    stats = jnp.zeros((2 * rows, HEAD), F32)
-    for head in range(2):
-        total = jnp.sum(l_ref[head], axis=1, keepdims=True)
-        stats = jnp.where(lane == head, m_ref[head] * scale + jnp.log2(total), stats)
-        part = (acc_ref[head] / total).astype(BF16)
-        for x in range(2):
-            out_ref[2 * x + to, :rows, head * HEAD : (head + 1) * HEAD] = part[x * rows : (x + 1) * rows]
-    for x in range(2):
-        sums = three(jnp.transpose(stats[x * rows : (x + 1) * rows])[:2])
-        sums = jnp.concatenate([*sums, jnp.zeros((10, 2 * HEAD), F32)], axis=0)
+            q = q_ref[x, :, head * HEAD : (head + 1) * HEAD]
+            scores = [
+                lax.dot_general(q, block(g)[:, :HEAD], (((1,), (1,)), ((), ())), preferred_element_type=F32)
+                for g in range(last + 1)
+            ]
+            scores[last] = jnp.where(seen, scores[last], -1e30)
+            pieces = [part[:, j : j + HEAD] for part in scores for j in range(0, 2 * half, HEAD)]
+            most = jnp.max(functools.reduce(jnp.maximum, pieces), axis=1, keepdims=True)
+            total = jnp.zeros((rows, HEAD), F32)
+            acc = jnp.zeros((rows, HEAD), F32)
+            for g in range(last + 1):
+                weights = []
+                for j in range(0, 2 * half, HEAD):
+                    w = jnp.exp2((scores[g][:, j : j + HEAD] - most) * scale)
+                    total = total + w
+                    weights.append(w.astype(BF16))
+                p = jnp.concatenate(weights, axis=1)
+                acc = acc + jnp.dot(p, block(g)[:, HEAD:], preferred_element_type=F32)
+            total = jnp.sum(total, axis=1, keepdims=True)
+            stats = jnp.where(lane == head, most * scale + jnp.log2(total), stats)
+            out_ref[2 * x + to, :rows, head * HEAD : (head + 1) * HEAD] = (acc / total).astype(BF16)
+        sums = three(jnp.transpose(stats)[:2])
+        sums = jnp.concatenate([*sums, jnp.zeros((10, rows), F32)], axis=0)
         out_ref[2 * x + to, rows:, :] = sums.astype(BF16)
+
+    for last in range(4):
+
+        @pl.when(lax.div(z, 4) == last)
+        def _():
+            for x in range(2):
+                run(last, x)
 
 
 def attend(side, place, q, mine, other, *first):
@@ -107,7 +101,6 @@
         out_shape=jax.ShapeDtypeStruct((4, rows + 16, cols), BF16),
         in_specs=[pl.BlockSpec(memory_space=pltpu.SMEM)] + [vmem] * (3 + len(first)),
         out_specs=vmem,
-        scratch_shapes=[pltpu.VMEM((2, 2 * rows, HEAD), F32)] * 3,
         input_output_aliases={4: 0} if first else {},
         compiler_params=pltpu.CompilerParams(vmem_limit_bytes=40 * 1024 * 1024),
         cost_estimate=pl.CostEstimate(flops=2**30, bytes_accessed=2**22, transcendentals=2**21),
@@ -139,44 +132,84 @@
     )(parts)
 
 
-def prep_kernel(tokens_ref, gain_ref, w_ref, out_ref, padded_ref, block_ref, sems):
+def prep_kernel(
+    place, tokens_ref, gain_ref, query_ref, key_ref, value_ref, out_ref, padded_ref, own_ref, block_ref, zeros_ref, sems
+):
     rows = tokens_ref.shape[0]
+    n = out_ref.shape[1]
+    depth = query_ref.shape[0]
+    yl, core, head = place[2], place[3], place[4]
+    zeros_ref[...] = jnp.zeros(zeros_ref.shape, BF16)
+    at = (pl.ds(pl.multiple_of(core * HEAD, HEAD), HEAD), pl.ds(pl.multiple_of(head * HEAD, HEAD), HEAD))
+    keys = pltpu.make_async_copy(key_ref.at[at], own_ref, sems.at[2 * n])
+    values = pltpu.make_async_copy(value_ref.at[at], own_ref, sems.at[2 * n + 1])
+    pads = [
+        pltpu.make_async_copy(query_ref, padded_ref.at[:depth], sems.at[2 * n + 2]),
+        pltpu.make_async_copy(zeros_ref, padded_ref.at[depth:], sems.at[2 * n + 3]),
+    ]
+    for q in range(4):
+        block_ref[q // 2, q % 2, :rows] = tokens_ref[:, q * HEAD : (q + 1) * HEAD]
+    body = [
+        pltpu.make_async_copy(block_ref.at[:, :, :rows], out_ref.at[:, to, :, :rows], sems.at[to]) for to in range(n)
+    ]
+    tail = [
+        pltpu.make_async_copy(block_ref.at[:, :, rows:], out_ref.at[:, to, :, rows:], sems.at[n + to]) for to in range(n)
+    ]
+    for copy in (*pads, *body):
+        copy.start()
+
+    @pl.when(yl == 0)
+    def _():
+        keys.start()
+
+    @pl.when(yl == 1)
+    def _():
+        values.start()
+
     states = tokens_ref[...].astype(F32)
     sums = jnp.sum(states * states, axis=1, keepdims=True)
     left = jnp.transpose(jnp.broadcast_to(sums, (rows, HEAD)))[:1]
     pieces = three(jnp.concatenate([left[:, :HEAD], left[:, HEAD:]], axis=0))
     for q in range(4):
-        at = slice(q * HEAD, (q + 1) * HEAD)
-        gain = gain_ref[at].astype(F32).reshape(1, HEAD)
+        gain = gain_ref[q * HEAD : (q + 1) * HEAD].astype(F32).reshape(1, HEAD)
         extra = jnp.concatenate([*pieces, gain, jnp.zeros((9, HEAD), F32)], axis=0)
-        block_ref[q // 2, q % 2, :rows] = tokens_ref[:, at]
         block_ref[q // 2, q % 2, rows:] = extra.astype(BF16)
-    copies = [
-        pltpu.make_async_copy(block_ref, out_ref.at[:, to], sems.at[to]) for to in range(out_ref.shape[1])
-    ]
-    for copy in copies:
+    for copy in tail:
         copy.start()
-    depth = w_ref.shape[0]
-    padded_ref[:depth] = w_ref[...]
-    padded_ref[depth:] = jnp.zeros((padded_ref.shape[0] - depth, w_ref.shape[1]), BF16)
-    for copy in copies:
+
+    @pl.when(yl == 0)
+    def _():
+        keys.wait()
+
+    @pl.when(yl == 1)
+    def _():
+        values.wait()
+
+    for copy in (*pads, *body, *tail):
         copy.wait()
 
 
-def prep(tokens, gain, w):
-    vmem = pl.BlockSpec(memory_space=pltpu.VMEM)
+def prep(place, tokens, gain, w_query, w_key, w_value):
+    vmem = pl.BlockSpec(memory_space=pltpu.VMEM)
+    hbm = pl.BlockSpec(memory_space=pltpu.HBM)
     rows = tokens.shape[0] + 16
+    depth, cols = w_query.shape
     return pl.pallas_call(
         prep_kernel,
         out_shape=(
             jax.ShapeDtypeStruct((2, 8, 2, rows, HEAD), BF16),
-            jax.ShapeDtypeStruct((w.shape[0] + 64, w.shape[1]), BF16),
+            jax.ShapeDtypeStruct((depth + 64, cols), BF16),
+            jax.ShapeDtypeStruct((HEAD, HEAD), BF16),
         ),
-        in_specs=[vmem, vmem, vmem],
-        out_specs=(pl.BlockSpec(memory_space=pltpu.HBM), vmem),
-        scratch_shapes=[pltpu.VMEM((2, 2, rows, HEAD), BF16), pltpu.SemaphoreType.DMA((8,))],
+        in_specs=[pl.BlockSpec(memory_space=pltpu.SMEM), vmem, vmem, hbm, hbm, hbm],
+        out_specs=(hbm, hbm, hbm),
+        scratch_shapes=[
+            pltpu.VMEM((2, 2, rows, HEAD), BF16),
+            pltpu.VMEM((64, cols), BF16),
+            pltpu.SemaphoreType.DMA((20,)),
+        ],
         compiler_params=pltpu.CompilerParams(vmem_limit_bytes=60 * 1024 * 1024),
-    )(tokens, gain, w)
+    )(place, tokens, gain, w_query, w_key, w_value)
 
 
 def kv_kernel(parts_ref, w_ref, out_ref, kv_ref, t_ref, sems):
@@ -250,22 +283,14 @@
 
 def on_device(tokens, norm_gain, w_query, w_key, w_value):
     at = lax.axis_index
-    core = at("core")
-    place = jnp.stack([at(("zh", "zl")), at("xh"), at("yl"), core]).astype(jnp.int32)
-    rows, feats = tokens.shape
-    half = w_key.shape[0] // 2
+    place = jnp.stack([at(("zh", "zl")), at("xh"), at("yl"), at("core"), at(("xl", "yh"))]).astype(jnp.int32)
+    rows = tokens.shape[0]
 
     with jax.named_scope("prep"):
-        parts, padded = prep(tokens, norm_gain, w_query)
+        parts, padded, wkv = prep(place, tokens, norm_gain, w_query, w_key, w_value)
 
     with jax.named_scope("weights"):
         wq = lax.all_gather(padded, ("zh", "zl"), axis=0)
-        start = (core * half, at(("xl", "yh")) * HEAD)
-        wkv = jnp.where(
-            at("yl") == 0,
-            lax.dynamic_slice(w_key, start, (half, HEAD)),
-            lax.dynamic_slice(w_value, start, (half, HEAD)),
-        )
         wkv = lax.all_gather(lax.all_gather(wkv, "zh"), "zl")
 
     with jax.named_scope("spread"):

time: 153 us -> 157 us (1.026)
  Pallas kernels: 13.1 us -> 17.8 us
    pallas_call x1, Pallas kernels: 3.29 us -> 7.28 us  [prep(): pl.pallas_call(prep_kernel, out_shape=(jax.ShapeDtypeStruct((2, 8, 2, row...]
  transfers between devices with their start and end apart: 7 -> 7, of which waited for: 3 -> 3; matrix products, arithmetic and copies ran while one was open for 1% -> 1% of each run, Pallas kernels for 4% -> 5%
where the time goes in v9:
time: 157 us; the launch traced here: 156 us
  blocking collectives  86.6 us (55%)
  starting transfers between devices  23.1 us (15%)
  Pallas kernels  17.8 us (11%)
  between operations  13.6 us (9%)
  waiting for transfers between devices  12 us (8%)
  local copies, waits for them, and re-layouts  3.22 us (2%)
    all_gather x2, blocking collectives, on_device(): wkv = lax.all_gather(lax.all_gather(wkv, 'zh'), 'zl')  42.2 us
    all_gather x1, blocking collectives, on_device(): kv, wq = lax.optimization_barrier((lax.all_gather(kv, 'zh'), wq))  20.5 us
    all_to_all x1, blocking collectives, on_device(): lax.all_to_all(kv_sum.reshape(8, rows // 4, HEAD), ('xh', 'yl', 'core'),...  12.2 us
    all_to_all x1, blocking collectives, on_device(): return merge(lax.all_to_all(out, ('xh', 'yl'), 0, 0))  11.6 us
    all_to_all x1, starting transfers between devices, on_device(): lax.all_to_all(parts.reshape(32, rows + 16, HEAD), ('xh',) + COL, 0, 0)  9.45 us
    pallas_call x1, Pallas kernels, prep(): pl.pallas_call(prep_kernel, out_shape=(jax.ShapeDtypeStruct((2, 8, 2, row...  7.28 us
    ppermute x1, waiting for transfers between devices, on_device(): q = (q + lax.ppermute(q, 'xh', [(0, 1), (1, 0)])).astype(BF16)  5.04 us
    pallas_call x2, Pallas kernels, attend(): pl.pallas_call(functools.partial(attend_kernel, side), out_shape=jax.Shap...  4.32 us
  transfers between devices with their start and end apart: 7, of which 3 were waited for; matrix products, arithmetic and copies ran while one was open for 1% of the time, Pallas kernels for 5%

profile of v9, /device:TPU:16, one launch (start us, length us, event | category | flops | bytes accessed | tf_op | source)
XLA Modules:
  0.0 156.4 jit_solution(17683380345077881803)
XLA Ops:
  6.5 0.0 all-gather.6.cloned.1.call-start
  6.5 0.6 stack.23.place
  7.2 7.3 %prep.1 = (bf16[2,8,2,272,128]{4,3,2,1,0:T(8,128)(2,1)}, bf16[320,256]{1,0:T(8,128)(2,1)}, bf16[128,128]{1,0:T(8,128)(2,1)}) custom-call(s32[5]{0:T(128)} %stack.23.place, bf16[256,512]{1,0:T(8,128)(2,1)} %tokens_ref.1, bf16[512]{0:T(512)(128)(2,1)} %gain_ref.1, bf16[256,256]{1,0:T(8,128)(2,1)} %query_ref.1, bf16[256,512]{1,0:T(8,128)(2,1)} %key_ref.1, ...), custom_call_target="tpu_custom_call" | custom-call | tf_op jit(solution)/shard_map/prep/pallas_call | solution.py:197
  14.4 0.0 all-gather.6.cloned.1.call-update
  14.5 0.0 copy-start.2
  14.5 9.4 %all-to-all-start = ((bf16[32,272,128]{2,1,0:T(8,128)(2,1)}), bf16[32,272,128]{2,1,0:T(8,128)(2,1)S(1)}, u32[]{:S(2)}, u32[]{:S(2)}) async-start(bf16[32,272,128]{2,1,0:T(8,128)(2,1)} %bitcast.21), calls=%async_computation | async-start | bytes 4456448 | tf_op jit(solution)/shard_map/spread/all_to_all | solution.py:297
  23.9 0.0 copy-done.2
  23.9 24.1 %all-gather = bf16[512,128]{1,0:T(8,128)(2,1)S(1)} all-gather(bf16[128,128]{1,0:T(8,128)(2,1)S(1)} %copy-done.2), channel_id=2, replica_groups=mesh['zh'=4,'zl'=4,'xh'=2,'xl'=2,'yh'=2,'yl'=2,'core'=2] {'zh'}, dimensions={0}, use_global_device_ids=true | all-gather | bytes 163840 | tf_op jit(solution)/shard_map/weights/all_gather | solution.py:294
  48.1 18.1 %all-gather.1 = bf16[16,128,128]{2,1,0:T(8,128)(2,1)S(1)} all-gather(bf16[4,128,128]{2,1,0:T(8,128)(2,1)S(1)} %bitcast.24), channel_id=3, replica_groups=mesh['zh'=4,'zl'=4,'xh'=2,'xl'=2,'yh'=2,'yl'=2,'core'=2] {'zl'}, dimensions={0}, use_global_device_ids=true | all-gather | bytes 655360 | tf_op jit(solution)/shard_map/weights/all_gather | solution.py:294
  66.2 0.0 all-to-all-done
  66.2 2.1 %project_kv.1 = (bf16[2,256,2048]{2,1,0:T(8,128)(2,1)}, f32[2,256,128]{2,1,0:T(8,128)S(1)}) custom-call(bf16[2,16,272,128]{3,2,1,0:T(8,128)(2,1)S(1)} %bitcast.17, bf16[4,4,128,128]{3,2,1,0:T(8,128)(2,1)S(1)} %bitcast.19), custom_call_target="tpu_custom_call" | custom-call | flops 268435456 | bytes 5242880 | tf_op jit(solution)/shard_map/project_kv/pallas_call | solution.py:243
  68.3 1.9 %collective-permute-start = (bf16[2,256,2048]{2,1,0:T(8,128)(2,1)}, bf16[2,256,2048]{2,1,0:T(8,128)(2,1)S(1)}, u32[]{:S(2)}, u32[]{:S(2)}) collective-permute-start(bf16[2,256,2048]{2,1,0:T(8,128)(2,1)} %get-tuple-element.14.mine_ref), channel_id=1, source_target_pairs={{0,1},{1,0},{2,3},{3,2},{4,5},{5,4},{6,7},{7,6},{8,9},{9,8},{10,11... | collective-permute-start | bytes 6291464 | tf_op jit(solution)/shard_map/project_q/ppermute | solution.py:26
  70.2 12.2 %all_to_all.20 = f32[8,64,128]{2,1,0:T(8,128)S(1)} all-to-all(f32[8,64,128]{2,1,0:T(8,128)S(1)} %bitcast.20), channel_id=1, replica_groups=mesh['zh'=4,'zl'=4,'xh'=2,'xl'=2,'yh'=2,'yl'=2,'core'=2] {'xh','yl','core'}, dimensions={0} | all-to-all | bytes 524288 | tf_op jit(solution)/shard_map/project_kv/all_to_all | solution.py:302
  82.5 20.5 %all-gather.2 = bf16[256,256]{1,0:T(8,128)(2,1)S(1)} all-gather(bf16[64,256]{1,0:T(8,128)(2,1)S(1)} %pad_maximum_fusion), channel_id=4, replica_groups=mesh['zh'=4,'zl'=4,'xh'=2,'xl'=2,'yh'=2,'yl'=2,'core'=2] {'zh'}, dimensions={0}, use_global_device_ids=true | all-gather | bytes 163840 | tf_op jit(solution)/shard_map/gather_kv/all_gather | solution.py:307
  103.0 0.8 broadcast_in_dim.2
  103.9 3.5 %all-to-all-start.2 = ((bf16[4,4,64,256]{3,2,1,0:T(8,128)(2,1)}), bf16[4,4,64,256]{3,2,1,0:T(8,128)(2,1)S(1)}, u32[]{:S(2)}, u32[]{:S(2)}) async-start(bf16[4,4,64,256]{3,2,1,0:T(8,128)(2,1)} %broadcast_in_dim.2), calls=%async_computation.2 | async-start | bytes 1048576 | tf_op jit(solution)/shard_map/gather_kv/all_to_all | solution.py:22
  107.4 0.0 collective-permute-done.other_ref
  107.4 0.0 copy-done.1
  107.4 1.7 %copy-done = bf16[5120,256]{1,0:T(8,128)(2,1)S(1)} copy-done((bf16[5120,256]{1,0:T(8,128)(2,1)S(1)}, bf16[5120,256]{1,0:T(8,128)(2,1)}, u32[]{:S(2)}) %copy-start) | copy-done | bytes 2621464
  109.1 2.9 %project_q.1 = f32[2,256,256]{2,1,0:T(8,128)S(1)} custom-call(s32[5]{0:T(128)S(1)} %copy-done.1, bf16[2,256,2048]{2,1,0:T(8,128)(2,1)} %get-tuple-element.14.mine_ref, bf16[2,256,2048]{2,1,0:T(8,128)(2,1)S(1)} %collective-permute-done.other_ref, bf16[16,320,256]{2,1,0:T(8,128)(2,1)S(1)} %bitcast.18), custom_call_target="tpu_custom_call" | custom-call | flops 1073741824 | bytes 6291456 | tf_op jit(solution)/shard_map/project_q/pallas_call | solution.py:274
  112.0 3.5 %collective-permute-start.1 = (f32[2,256,256]{2,1,0:T(8,128)S(1)}, f32[2,256,256]{2,1,0:T(8,128)S(1)}, u32[]{:S(2)}, u32[]{:S(2)}) collective-permute-start(f32[2,256,256]{2,1,0:T(8,128)S(1)} %project_q.1), channel_id=1, source_target_pairs={{0,16},{16,0},{1,17},{17,1},{2,18},{18,2},{3,19},{19,3},{4,20},{20... | collective-permute-start | bytes 1572872 | tf_op jit(solution)/shard_map/project_q/ppermute | solution.py:312
  115.5 3.8 %all-to-all-done.2.mine_ref = bf16[4,4,64,256]{3,2,1,0:T(8,128)(2,1)S(1)} async-done(((bf16[4,4,64,256]{3,2,1,0:T(8,128)(2,1)}), bf16[4,4,64,256]{3,2,1,0:T(8,128)(2,1)S(1)}, u32[]{:S(2)}, u32[]{:S(2)}) %all-to-all-start.2) | async-done | bytes 524320 | tf_op jit(solution)/shard_map/gather_kv/all_to_all | solution.py:22
  119.2 1.9 %collective-permute-start.3 = (bf16[4,4,64,256]{3,2,1,0:T(8,128)(2,1)S(1)}, bf16[4,4,64,256]{3,2,1,0:T(8,128)(2,1)S(1)}, u32[]{:S(2)}, u32[]{:S(2)}) collective-permute-start(bf16[4,4,64,256]{3,2,1,0:T(8,128)(2,1)S(1)} %all-to-all-done.2.mine_ref), channel_id=1, source_target_pairs={{0,1},{1,0},{2,3},{3,2},{4,5},{5,4},{6,7},{7,6},{8,9},{9,8},{10,11... | collective-permute-start | bytes 1572872 | tf_op jit(solution)/shard_map/attend/ppermute | solution.py:26
  121.2 5.0 %collective-permute-done.1 = f32[2,256,256]{2,1,0:T(8,128)S(1)} collective-permute-done((f32[2,256,256]{2,1,0:T(8,128)S(1)}, f32[2,256,256]{2,1,0:T(8,128)S(1)}, u32[]{:S(2)}, u32[]{:S(2)}) %collective-permute-start.1) | collective-permute-done | bytes 524320 | tf_op jit(solution)/shard_map/project_q/ppermute | solution.py:312
  126.2 0.1 add_convert_fusion.q_ref
  126.3 2.9 %collective-permute-start.2 = (bf16[2,256,256]{2,1,0:T(8,128)(2,1)S(1)}, bf16[2,256,256]{2,1,0:T(8,128)(2,1)S(1)}, u32[]{:S(2)}, u32[]{:S(2)}) collective-permute-start(bf16[2,256,256]{2,1,0:T(8,128)(2,1)S(1)} %add_convert_fusion.q_ref), channel_id=1, source_target_pairs={{0,2},{2,0},{1,3},{3,1},{4,6},{6,4},{5,7},{7,5},{8,10},{10,8},{9,1... | collective-permute-start | bytes 786440 | tf_op jit(solution)/shard_map/project_q/ppermute | solution.py:313
  129.2 0.0 collective-permute-done.3.other_ref
  129.2 2.1 %attend.3.refs_0_ = bf16[4,272,256]{2,1,0:T(8,128)(2,1)S(1)} custom-call(s32[5]{0:T(128)S(1)} %copy-done.1, bf16[2,256,256]{2,1,0:T(8,128)(2,1)S(1)} %add_convert_fusion.q_ref, bf16[4,4,64,256]{3,2,1,0:T(8,128)(2,1)S(1)} %all-to-all-done.2.mine_ref, bf16[4,4,64,256]{3,2,1,0:T(8,128)(2,1)S(1)} %collective-permute-done.3.other_ref), custom_call_target="tpu_custom_call" | custom-call | flops 1073741824 | bytes 4194304 | tf_op jit(solution)/shard_map/attend/pallas_call | solution.py:99
  131.3 3.2 %collective-permute-done.2.q_ref = bf16[2,256,256]{2,1,0:T(8,128)(2,1)S(1)} collective-permute-done((bf16[2,256,256]{2,1,0:T(8,128)(2,1)S(1)}, bf16[2,256,256]{2,1,0:T(8,128)(2,1)S(1)}, u32[]{:S(2)}, u32[]{:S(2)}) %collective-permute-start.2) | collective-permute-done | bytes 262176 | tf_op jit(solution)/shard_map/project_q/ppermute | solution.py:313
  134.6 2.2 %attend.4 = bf16[4,272,256]{2,1,0:T(8,128)(2,1)S(1)} custom-call(s32[5]{0:T(128)S(1)} %copy-done.1, bf16[2,256,256]{2,1,0:T(8,128)(2,1)S(1)} %collective-permute-done.2.q_ref, bf16[4,4,64,256]{3,2,1,0:T(8,128)(2,1)S(1)} %all-to-all-done.2.mine_ref, bf16[4,4,64,256]{3,2,1,0:T(8,128)(2,1)S(1)} %collective-permute-done.3.other_ref, ...), custom_call_target="tpu_custom_call", output_to_operand_aliasing={{}: (4, {})} | custom-call | flops 1073741824 | bytes 4194304 | tf_op jit(solution)/shard_map/attend/pallas_call | solution.py:99
  136.7 11.6 %all_to_all.21.parts_ref = bf16[4,272,256]{2,1,0:T(8,128)(2,1)S(1)} all-to-all(bf16[4,272,256]{2,1,0:T(8,128)(2,1)S(1)} %attend.4), channel_id=1, replica_groups=mesh['zh'=4,'zl'=4,'xh'=2,'xl'=2,'yh'=2,'yl'=2,'core'=2] {'xh','yl'}, dimensions={0} | all-to-all | bytes 1114112 | tf_op jit(solution)/shard_map/attend/all_to_all | solution.py:319
  148.3 1.2 attend.5
  (6 shorter events, 0.0 us)
Async XLA Ops:
  6.5 96.5 %all-gather.6.cloned.1.call-start = ((), (), s32[]{:S(2)}) async-start(), calls=%async_computation.4 | async-start | bytes 2785280 | tf_op jit(solution)/shard_map/weights/all_gather | solution.py:293
  14.5 9.5 %copy-start.2 = (bf16[128,128]{1,0:T(8,128)(2,1)S(1)}, bf16[128,128]{1,0:T(8,128)(2,1)}, u32[]{:S(2)}) copy-start(bf16[128,128]{1,0:T(8,128)(2,1)} %get-tuple-element.13) | copy-start | bytes 98308
  14.5 51.7 %all-to-all-start = ((bf16[32,272,128]{2,1,0:T(8,128)(2,1)}), bf16[32,272,128]{2,1,0:T(8,128)(2,1)S(1)}, u32[]{:S(2)}, u32[]{:S(2)}) async-start(bf16[32,272,128]{2,1,0:T(8,128)(2,1)} %bitcast.21), calls=%async_computation | async-start | bytes 4456448 | tf_op jit(solution)/shard_map/spread/all_to_all | solution.py:297
  66.2 41.2 %copy-start.1 = (s32[5]{0:T(128)S(1)}, s32[5]{0:T(128)}, u32[]{:S(2)}) copy-start(s32[5]{0:T(128)} %stack.23.place) | copy-start | bytes 64
  68.3 39.1 %collective-permute-start = (bf16[2,256,2048]{2,1,0:T(8,128)(2,1)}, bf16[2,256,2048]{2,1,0:T(8,128)(2,1)S(1)}, u32[]{:S(2)}, u32[]{:S(2)}) collective-permute-start(bf16[2,256,2048]{2,1,0:T(8,128)(2,1)} %get-tuple-element.14.mine_ref), channel_id=1, source_target_pairs={{0,1},{1,0},{2,3},{3,2},{4,5},{5,4},{6,7},{7,6},{8,9},{9,8},{10,11... | collective-permute-start | bytes 6291464 | tf_op jit(solution)/shard_map/project_q/ppermute | solution.py:26
  103.9 15.4 %all-to-all-start.2 = ((bf16[4,4,64,256]{3,2,1,0:T(8,128)(2,1)}), bf16[4,4,64,256]{3,2,1,0:T(8,128)(2,1)S(1)}, u32[]{:S(2)}, u32[]{:S(2)}) async-start(bf16[4,4,64,256]{3,2,1,0:T(8,128)(2,1)} %broadcast_in_dim.2), calls=%async_computation.2 | async-start | bytes 1048576 | tf_op jit(solution)/shard_map/gather_kv/all_to_all | solution.py:22
  107.4 1.7 %copy-start = (bf16[5120,256]{1,0:T(8,128)(2,1)S(1)}, bf16[5120,256]{1,0:T(8,128)(2,1)}, u32[]{:S(2)}) copy-start(bf16[5120,256]{1,0:T(8,128)(2,1)} %all-gather.6.cloned.1.call-done) | copy-start | bytes 7864324
  112.0 14.2 %collective-permute-start.1 = (f32[2,256,256]{2,1,0:T(8,128)S(1)}, f32[2,256,256]{2,1,0:T(8,128)S(1)}, u32[]{:S(2)}, u32[]{:S(2)}) collective-permute-start(f32[2,256,256]{2,1,0:T(8,128)S(1)} %project_q.1), channel_id=1, source_target_pairs={{0,16},{16,0},{1,17},{17,1},{2,18},{18,2},{3,19},{19,3},{4,20},{20... | collective-permute-start | bytes 1572872 | tf_op jit(solution)/shard_map/project_q/ppermute | solution.py:312
  119.2 9.9 %collective-permute-start.3 = (bf16[4,4,64,256]{3,2,1,0:T(8,128)(2,1)S(1)}, bf16[4,4,64,256]{3,2,1,0:T(8,128)(2,1)S(1)}, u32[]{:S(2)}, u32[]{:S(2)}) collective-permute-start(bf16[4,4,64,256]{3,2,1,0:T(8,128)(2,1)S(1)} %all-to-all-done.2.mine_ref), channel_id=1, source_target_pairs={{0,1},{1,0},{2,3},{3,2},{4,5},{5,4},{6,7},{7,6},{8,9},{9,8},{10,11... | collective-permute-start | bytes 1572872 | tf_op jit(solution)/shard_map/attend/ppermute | solution.py:26
  126.3 8.3 %collective-permute-start.2 = (bf16[2,256,256]{2,1,0:T(8,128)(2,1)S(1)}, bf16[2,256,256]{2,1,0:T(8,128)(2,1)S(1)}, u32[]{:S(2)}, u32[]{:S(2)}) collective-permute-start(bf16[2,256,256]{2,1,0:T(8,128)(2,1)S(1)} %add_convert_fusion.q_ref), channel_id=1, source_target_pairs={{0,2},{2,0},{1,3},{3,1},{4,6},{6,4},{5,7},{7,5},{8,10},{10,8},{9,1... | collective-permute-start | bytes 786440 | tf_op jit(solution)/shard_map/project_q/ppermute | solution.py:313
Sparse Core Ops, SparseCore 0:
  14.6 82.2 all-gather.5

commit v10 on v9

--- a/solution.py
+++ b/solution.py
@@ -40,14 +40,14 @@
     z, xh, yl, core = place[0], place[1], place[2], place[3]
     rows = q_ref.shape[1]
     scale = HEAD**-0.5 * math.log2(math.e)
-    chunk = mine_ref.shape[2]
+    chunk = mine_ref.shape[1]
     half = 4 * chunk
     to = yl if side == 0 else 1 - yl
     lane = lax.broadcasted_iota(jnp.int32, (rows, HEAD), 1)
 
     def block(group):
         return jnp.concatenate(
-            [ref[:, group].reshape(half, 2 * HEAD) for ref in (mine_ref, other_ref)], axis=0
+            [ref[4 * group : 4 * group + 4].reshape(half, 2 * HEAD) for ref in (mine_ref, other_ref)], axis=0
         )
 
     def run(last, x):
@@ -132,84 +132,44 @@
     )(parts)
 
 
-def prep_kernel(
-    place, tokens_ref, gain_ref, query_ref, key_ref, value_ref, out_ref, padded_ref, own_ref, block_ref, zeros_ref, sems
-):
+def prep_kernel(tokens_ref, gain_ref, w_ref, out_ref, padded_ref, block_ref, sems):
     rows = tokens_ref.shape[0]
-    n = out_ref.shape[1]
-    depth = query_ref.shape[0]
-    yl, core, head = place[2], place[3], place[4]
-    zeros_ref[...] = jnp.zeros(zeros_ref.shape, BF16)
-    at = (pl.ds(pl.multiple_of(core * HEAD, HEAD), HEAD), pl.ds(pl.multiple_of(head * HEAD, HEAD), HEAD))
-    keys = pltpu.make_async_copy(key_ref.at[at], own_ref, sems.at[2 * n])
-    values = pltpu.make_async_copy(value_ref.at[at], own_ref, sems.at[2 * n + 1])
-    pads = [
-        pltpu.make_async_copy(query_ref, padded_ref.at[:depth], sems.at[2 * n + 2]),
-        pltpu.make_async_copy(zeros_ref, padded_ref.at[depth:], sems.at[2 * n + 3]),
-    ]
-    for q in range(4):
-        block_ref[q // 2, q % 2, :rows] = tokens_ref[:, q * HEAD : (q + 1) * HEAD]
-    body = [
-        pltpu.make_async_copy(block_ref.at[:, :, :rows], out_ref.at[:, to, :, :rows], sems.at[to]) for to in range(n)
-    ]
-    tail = [
-        pltpu.make_async_copy(block_ref.at[:, :, rows:], out_ref.at[:, to, :, rows:], sems.at[n + to]) for to in range(n)
-    ]
-    for copy in (*pads, *body):
-        copy.start()
-
-    @pl.when(yl == 0)
-    def _():
-        keys.start()
-
-    @pl.when(yl == 1)
-    def _():
-        values.start()
-
     states = tokens_ref[...].astype(F32)
     sums = jnp.sum(states * states, axis=1, keepdims=True)
     left = jnp.transpose(jnp.broadcast_to(sums, (rows, HEAD)))[:1]
     pieces = three(jnp.concatenate([left[:, :HEAD], left[:, HEAD:]], axis=0))
     for q in range(4):
-        gain = gain_ref[q * HEAD : (q + 1) * HEAD].astype(F32).reshape(1, HEAD)
+        at = slice(q * HEAD, (q + 1) * HEAD)
+        gain = gain_ref[at].astype(F32).reshape(1, HEAD)
         extra = jnp.concatenate([*pieces, gain, jnp.zeros((9, HEAD), F32)], axis=0)
+        block_ref[q // 2, q % 2, :rows] = tokens_ref[:, at]
         block_ref[q // 2, q % 2, rows:] = extra.astype(BF16)
-    for copy in tail:
+    copies = [
+        pltpu.make_async_copy(block_ref, out_ref.at[:, to], sems.at[to]) for to in range(out_ref.shape[1])
+    ]
+    for copy in copies:
         copy.start()
-
-    @pl.when(yl == 0)
-    def _():
-        keys.wait()
-
-    @pl.when(yl == 1)
-    def _():
-        values.wait()
-
-    for copy in (*pads, *body, *tail):
+    depth = w_ref.shape[0]
+    padded_ref[:depth] = w_ref[...]
+    padded_ref[depth:] = jnp.zeros((padded_ref.shape[0] - depth, w_ref.shape[1]), BF16)
+    for copy in copies:
         copy.wait()
 
 
-def prep(place, tokens, gain, w_query, w_key, w_value):
-    vmem = pl.BlockSpec(memory_space=pltpu.VMEM)
-    hbm = pl.BlockSpec(memory_space=pltpu.HBM)
+def prep(tokens, gain, w):
+    vmem = pl.BlockSpec(memory_space=pltpu.VMEM)
     rows = tokens.shape[0] + 16
-    depth, cols = w_query.shape
     return pl.pallas_call(
         prep_kernel,
         out_shape=(
             jax.ShapeDtypeStruct((2, 8, 2, rows, HEAD), BF16),
-            jax.ShapeDtypeStruct((depth + 64, cols), BF16),
-            jax.ShapeDtypeStruct((HEAD, HEAD), BF16),
+            jax.ShapeDtypeStruct((w.shape[0] + 64, w.shape[1]), BF16),
         ),
-        in_specs=[pl.BlockSpec(memory_space=pltpu.SMEM), vmem, vmem, hbm, hbm, hbm],
-        out_specs=(hbm, hbm, hbm),
-        scratch_shapes=[
-            pltpu.VMEM((2, 2, rows, HEAD), BF16),
-            pltpu.VMEM((64, cols), BF16),
-            pltpu.SemaphoreType.DMA((20,)),
-        ],
+        in_specs=[vmem, vmem, vmem],
+        out_specs=(pl.BlockSpec(memory_space=pltpu.HBM), vmem),
+        scratch_shapes=[pltpu.VMEM((2, 2, rows, HEAD), BF16), pltpu.SemaphoreType.DMA((8,))],
         compiler_params=pltpu.CompilerParams(vmem_limit_bytes=60 * 1024 * 1024),
-    )(place, tokens, gain, w_query, w_key, w_value)
+    )(tokens, gain, w)
 
 
 def kv_kernel(parts_ref, w_ref, out_ref, kv_ref, t_ref, sems):
@@ -283,14 +243,22 @@
 
 def on_device(tokens, norm_gain, w_query, w_key, w_value):
     at = lax.axis_index
-    place = jnp.stack([at(("zh", "zl")), at("xh"), at("yl"), at("core"), at(("xl", "yh"))]).astype(jnp.int32)
-    rows = tokens.shape[0]
+    core = at("core")
+    place = jnp.stack([at(("zh", "zl")), at("xh"), at("yl"), core]).astype(jnp.int32)
+    rows, feats = tokens.shape
+    half = w_key.shape[0] // 2
 
     with jax.named_scope("prep"):
-        parts, padded, wkv = prep(place, tokens, norm_gain, w_query, w_key, w_value)
+        parts, padded = prep(tokens, norm_gain, w_query)
 
     with jax.named_scope("weights"):
         wq = lax.all_gather(padded, ("zh", "zl"), axis=0)
+        start = (core * half, at(("xl", "yh")) * HEAD)
+        wkv = jnp.where(
+            at("yl") == 0,
+            lax.dynamic_slice(w_key, start, (half, HEAD)),
+            lax.dynamic_slice(w_value, start, (half, HEAD)),
+        )
         wkv = lax.all_gather(lax.all_gather(wkv, "zh"), "zl")
 
     with jax.named_scope("spread"):
@@ -304,8 +272,7 @@
         kv = jnp.concatenate([chunks[0], chunks[1]], axis=1)
 
     with jax.named_scope("gather_kv"):
-        kv, wq = lax.optimization_barrier((lax.all_gather(kv, "zh"), wq))
-        kv = gather(kv, "zl", 4)
+        kv = gather(kv, ("zh", "zl"), 16)
 
     with jax.named_scope("project_q"):
         q = project_q(place, whole, swap(whole), wq)

time: 157 us -> 155 us (0.987)
  the two profiles are of different devices: /device:TPU:16 before, /device:TPU:32 now
where the time goes in v10:
time: 155 us; the launch traced here: 154 us
  blocking collectives  69.5 us (45%)
  starting transfers between devices  30.1 us (19%)
  waiting for transfers between devices  23.6 us (15%)
  Pallas kernels  13.7 us (9%)
  between operations  13.5 us (9%)
  local copies, waits for them, and re-layouts  2.59 us (2%)
    all_gather x2, blocking collectives, on_device(): wkv = lax.all_gather(lax.all_gather(wkv, 'zh'), 'zl')  42.9 us
    all_to_all x1, waiting for transfers between devices, gather(): return lax.all_to_all(jnp.broadcast_to(x[None], (n, *x.shape)), axes, 0, 0)  16.3 us
    all_to_all x1, blocking collectives, on_device(): return merge(lax.all_to_all(out, ('xh', 'yl'), 0, 0))  14.3 us
    all_to_all x1, blocking collectives, on_device(): lax.all_to_all(kv_sum.reshape(8, rows // 4, HEAD), ('xh', 'yl', 'core'),...  12.4 us
    all_to_all x1, starting transfers between devices, gather(): return lax.all_to_all(jnp.broadcast_to(x[None], (n, *x.shape)), axes, 0, 0)  10.7 us
    all_to_all x1, starting transfers between devices, on_device(): lax.all_to_all(parts.reshape(32, rows + 16, HEAD), ('xh',) + COL, 0, 0)  7.33 us
    ppermute x1, waiting for transfers between devices, on_device(): pair = lax.ppermute(q, 'yl', [(0, 1), (1, 0)])  5.39 us
    ppermute x1, starting transfers between devices, on_device(): q = (q + lax.ppermute(q, 'xh', [(0, 1), (1, 0)])).astype(BF16)  5.16 us
  transfers between devices with their start and end apart: 7, of which 3 were waited for; matrix products, arithmetic and copies ran while one was open for 1% of the time, Pallas kernels for 5%

profile of v10, /device:TPU:32, one launch (start us, length us, event | category | flops | bytes accessed | tf_op | source)
XLA Modules:
  0.0 154.1 jit_solution(14117967945165469484)
XLA Ops:
  6.5 0.0 all-gather.5.cloned.1.call-start
  6.5 3.3 %prep.1 = (bf16[2,8,2,272,128]{4,3,2,1,0:T(8,128)(2,1)}, bf16[320,256]{1,0:T(8,128)(2,1)}) custom-call(bf16[256,512]{1,0:T(8,128)(2,1)} %tokens_ref.1, bf16[512]{0:T(512)(128)(2,1)} %gain_ref.1, bf16[256,256]{1,0:T(8,128)(2,1)} %w_ref.1), custom_call_target="tpu_custom_call" | custom-call | tf_op jit(solution)/shard_map/prep/pallas_call | solution.py:162
  9.8 0.0 all-gather.5.cloned.1.call-update
  9.9 7.3 %all-to-all-start = ((bf16[32,272,128]{2,1,0:T(8,128)(2,1)}), bf16[32,272,128]{2,1,0:T(8,128)(2,1)S(1)}, u32[]{:S(2)}, u32[]{:S(2)}) async-start(bf16[32,272,128]{2,1,0:T(8,128)(2,1)} %bitcast.19), calls=%async_computation | async-start | bytes 4456448 | tf_op jit(solution)/shard_map/spread/all_to_all | solution.py:265
  17.2 0.8 dynamic-slice_select_fusion
  18.0 25.5 %all-gather = bf16[512,128]{1,0:T(8,128)(2,1)S(1)} all-gather(bf16[128,128]{1,0:T(8,128)(2,1)S(1)} %dynamic-slice_select_fusion), channel_id=2, replica_groups=mesh['zh'=4,'zl'=4,'xh'=2,'xl'=2,'yh'=2,'yl'=2,'core'=2] {'zh'}, dimensions={0}, use_global_device_ids=true | all-gather | bytes 163840 | tf_op jit(solution)/shard_map/weights/all_gather | solution.py:262
  43.6 17.3 %all-gather.1 = bf16[16,128,128]{2,1,0:T(8,128)(2,1)S(1)} all-gather(bf16[4,128,128]{2,1,0:T(8,128)(2,1)S(1)} %bitcast.21), channel_id=3, replica_groups=mesh['zh'=4,'zl'=4,'xh'=2,'xl'=2,'yh'=2,'yl'=2,'core'=2] {'zl'}, dimensions={0}, use_global_device_ids=true | all-gather | bytes 655360 | tf_op jit(solution)/shard_map/weights/all_gather | solution.py:262
  60.9 0.0 all-to-all-done
  60.9 2.1 %project_kv.1 = (bf16[2,256,2048]{2,1,0:T(8,128)(2,1)}, f32[2,256,128]{2,1,0:T(8,128)S(1)}) custom-call(bf16[2,16,272,128]{3,2,1,0:T(8,128)(2,1)S(1)} %bitcast.15, bf16[4,4,128,128]{3,2,1,0:T(8,128)(2,1)S(1)} %bitcast.17), custom_call_target="tpu_custom_call" | custom-call | flops 268435456 | bytes 5242880 | tf_op jit(solution)/shard_map/project_kv/pallas_call | solution.py:203
  63.0 1.9 %collective-permute-start = (bf16[2,256,2048]{2,1,0:T(8,128)(2,1)}, bf16[2,256,2048]{2,1,0:T(8,128)(2,1)S(1)}, u32[]{:S(2)}, u32[]{:S(2)}) collective-permute-start(bf16[2,256,2048]{2,1,0:T(8,128)(2,1)} %get-tuple-element.10.mine_ref), channel_id=1, source_target_pairs={{0,1},{1,0},{2,3},{3,2},{4,5},{5,4},{6,7},{7,6},{8,9},{9,8},{10,11... | collective-permute-start | bytes 6291464 | tf_op jit(solution)/shard_map/project_q/ppermute | solution.py:26
  64.9 12.4 %all_to_all.20 = f32[8,64,128]{2,1,0:T(8,128)S(1)} all-to-all(f32[8,64,128]{2,1,0:T(8,128)S(1)} %bitcast.18), channel_id=1, replica_groups=mesh['zh'=4,'zl'=4,'xh'=2,'xl'=2,'yh'=2,'yl'=2,'core'=2] {'xh','yl','core'}, dimensions={0} | all-to-all | bytes 524288 | tf_op jit(solution)/shard_map/project_kv/all_to_all | solution.py:270
  77.3 0.8 broadcast_in_dim.2
  78.2 10.7 %all-to-all-start.2 = ((bf16[16,64,256]{2,1,0:T(8,128)(2,1)}), bf16[16,64,256]{2,1,0:T(8,128)(2,1)S(1)}, u32[]{:S(2)}, u32[]{:S(2)}) async-start(bf16[16,64,256]{2,1,0:T(8,128)(2,1)} %broadcast_in_dim.2), calls=%async_computation.2 | async-start | bytes 1048576 | tf_op jit(solution)/shard_map/gather_kv/all_to_all | solution.py:22
  88.9 0.1 pad_add_fusion.place
  89.0 0.0 collective-permute-done.other_ref
  89.0 1.9 %all-gather.5.cloned.1.call-done = bf16[5120,256]{1,0:T(8,128)(2,1)} async-done(((bf16[320,256]{1,0:T(8,128)(2,1)}), bf16[5120,256]{1,0:T(8,128)(2,1)}) %all-gather.5.cloned.1.call-update) | async-done | bytes 2621456 | tf_op jit(solution)/shard_map/weights/all_gather | solution.py:255
  90.9 0.0 copy-start
  90.9 1.7 %copy-done = bf16[5120,256]{1,0:T(8,128)(2,1)S(1)} copy-done((bf16[5120,256]{1,0:T(8,128)(2,1)S(1)}, bf16[5120,256]{1,0:T(8,128)(2,1)}, u32[]{:S(2)}) %copy-start) | copy-done | bytes 2621464
  92.7 2.8 %project_q.1 = f32[2,256,256]{2,1,0:T(8,128)S(1)} custom-call(s32[4]{0:T(128)S(1)} %pad_add_fusion.place, bf16[2,256,2048]{2,1,0:T(8,128)(2,1)} %get-tuple-element.10.mine_ref, bf16[2,256,2048]{2,1,0:T(8,128)(2,1)S(1)} %collective-permute-done.other_ref, bf16[16,320,256]{2,1,0:T(8,128)(2,1)S(1)} %bitcast.16), custom_call_target="tpu_custom_call" | custom-call | flops 1073741824 | bytes 6291456 | tf_op jit(solution)/shard_map/project_q/pallas_call | solution.py:234
  95.5 5.2 %collective-permute-start.1 = (f32[2,256,256]{2,1,0:T(8,128)S(1)}, f32[2,256,256]{2,1,0:T(8,128)S(1)}, u32[]{:S(2)}, u32[]{:S(2)}) collective-permute-start(f32[2,256,256]{2,1,0:T(8,128)S(1)} %project_q.1), channel_id=1, source_target_pairs={{0,16},{16,0},{1,17},{17,1},{2,18},{18,2},{3,19},{19,3},{4,20},{20... | collective-permute-start | bytes 1572872 | tf_op jit(solution)/shard_map/project_q/ppermute | solution.py:279
  100.7 16.3 %all-to-all-done.2.mine_ref = bf16[16,64,256]{2,1,0:T(8,128)(2,1)S(1)} async-done(((bf16[16,64,256]{2,1,0:T(8,128)(2,1)}), bf16[16,64,256]{2,1,0:T(8,128)(2,1)S(1)}, u32[]{:S(2)}, u32[]{:S(2)}) %all-to-all-start.2) | async-done | bytes 524320 | tf_op jit(solution)/shard_map/gather_kv/all_to_all | solution.py:22
  116.9 1.9 %collective-permute-start.3 = (bf16[16,64,256]{2,1,0:T(8,128)(2,1)S(1)}, bf16[16,64,256]{2,1,0:T(8,128)(2,1)S(1)}, u32[]{:S(2)}, u32[]{:S(2)}) collective-permute-start(bf16[16,64,256]{2,1,0:T(8,128)(2,1)S(1)} %all-to-all-done.2.mine_ref), channel_id=1, source_target_pairs={{0,1},{1,0},{2,3},{3,2},{4,5},{5,4},{6,7},{7,6},{8,9},{9,8},{10,11... | collective-permute-start | bytes 1572872 | tf_op jit(solution)/shard_map/attend/ppermute | solution.py:26
  118.9 0.0 collective-permute-done.1
  118.9 0.1 add_convert_fusion.q_ref
  119.0 3.1 %collective-permute-start.2 = (bf16[2,256,256]{2,1,0:T(8,128)(2,1)S(1)}, bf16[2,256,256]{2,1,0:T(8,128)(2,1)S(1)}, u32[]{:S(2)}, u32[]{:S(2)}) collective-permute-start(bf16[2,256,256]{2,1,0:T(8,128)(2,1)S(1)} %add_convert_fusion.q_ref), channel_id=1, source_target_pairs={{0,2},{2,0},{1,3},{3,1},{4,6},{6,4},{5,7},{7,5},{8,10},{10,8},{9,1... | collective-permute-start | bytes 786440 | tf_op jit(solution)/shard_map/project_q/ppermute | solution.py:280
  122.0 0.0 collective-permute-done.3.other_ref
  122.0 2.1 %attend.3.refs_0_ = bf16[4,272,256]{2,1,0:T(8,128)(2,1)S(1)} custom-call(s32[4]{0:T(128)S(1)} %pad_add_fusion.place, bf16[2,256,256]{2,1,0:T(8,128)(2,1)S(1)} %add_convert_fusion.q_ref, bf16[16,64,256]{2,1,0:T(8,128)(2,1)S(1)} %all-to-all-done.2.mine_ref, bf16[16,64,256]{2,1,0:T(8,128)(2,1)S(1)} %collective-permute-done.3.other_ref), custom_call_target="tpu_custom_call" | custom-call | flops 1073741824 | bytes 4194304 | tf_op jit(solution)/shard_map/attend/pallas_call | solution.py:99
  124.2 5.4 %collective-permute-done.2.q_ref = bf16[2,256,256]{2,1,0:T(8,128)(2,1)S(1)} collective-permute-done((bf16[2,256,256]{2,1,0:T(8,128)(2,1)S(1)}, bf16[2,256,256]{2,1,0:T(8,128)(2,1)S(1)}, u32[]{:S(2)}, u32[]{:S(2)}) %collective-permute-start.2) | collective-permute-done | bytes 262176 | tf_op jit(solution)/shard_map/project_q/ppermute | solution.py:280
  129.6 2.2 %attend.4 = bf16[4,272,256]{2,1,0:T(8,128)(2,1)S(1)} custom-call(s32[4]{0:T(128)S(1)} %pad_add_fusion.place, bf16[2,256,256]{2,1,0:T(8,128)(2,1)S(1)} %collective-permute-done.2.q_ref, bf16[16,64,256]{2,1,0:T(8,128)(2,1)S(1)} %all-to-all-done.2.mine_ref, bf16[16,64,256]{2,1,0:T(8,128)(2,1)S(1)} %collective-permute-done.3.other_ref, ...), custom_call_target="tpu_custom_call", output_to_operand_aliasing={{}: (4, {})} | custom-call | flops 1073741824 | bytes 4194304 | tf_op jit(solution)/shard_map/attend/pallas_call | solution.py:99
  131.7 14.3 %all_to_all.21.parts_ref = bf16[4,272,256]{2,1,0:T(8,128)(2,1)S(1)} all-to-all(bf16[4,272,256]{2,1,0:T(8,128)(2,1)S(1)} %attend.4), channel_id=1, replica_groups=mesh['zh'=4,'zl'=4,'xh'=2,'xl'=2,'yh'=2,'yl'=2,'core'=2] {'xh','yl'}, dimensions={0} | all-to-all | bytes 1114112 | tf_op jit(solution)/shard_map/attend/all_to_all | solution.py:286
  146.0 1.2 attend.5
  (3 shorter events, 0.0 us)
Async XLA Ops:
  6.5 84.4 %all-gather.5.cloned.1.call-start = ((), (), s32[]{:S(2)}) async-start(), calls=%async_computation.4 | async-start | bytes 2785280 | tf_op jit(solution)/shard_map/weights/all_gather | solution.py:255
  9.9 51.0 %all-to-all-start = ((bf16[32,272,128]{2,1,0:T(8,128)(2,1)}), bf16[32,272,128]{2,1,0:T(8,128)(2,1)S(1)}, u32[]{:S(2)}, u32[]{:S(2)}) async-start(bf16[32,272,128]{2,1,0:T(8,128)(2,1)} %bitcast.19), calls=%async_computation | async-start | bytes 4456448 | tf_op jit(solution)/shard_map/spread/all_to_all | solution.py:265
  63.0 26.0 %collective-permute-start = (bf16[2,256,2048]{2,1,0:T(8,128)(2,1)}, bf16[2,256,2048]{2,1,0:T(8,128)(2,1)S(1)}, u32[]{:S(2)}, u32[]{:S(2)}) collective-permute-start(bf16[2,256,2048]{2,1,0:T(8,128)(2,1)} %get-tuple-element.10.mine_ref), channel_id=1, source_target_pairs={{0,1},{1,0},{2,3},{3,2},{4,5},{5,4},{6,7},{7,6},{8,9},{9,8},{10,11... | collective-permute-start | bytes 6291464 | tf_op jit(solution)/shard_map/project_q/ppermute | solution.py:26
  78.2 38.8 %all-to-all-start.2 = ((bf16[16,64,256]{2,1,0:T(8,128)(2,1)}), bf16[16,64,256]{2,1,0:T(8,128)(2,1)S(1)}, u32[]{:S(2)}, u32[]{:S(2)}) async-start(bf16[16,64,256]{2,1,0:T(8,128)(2,1)} %broadcast_in_dim.2), calls=%async_computation.2 | async-start | bytes 1048576 | tf_op jit(solution)/shard_map/gather_kv/all_to_all | solution.py:22
  90.9 1.7 %copy-start = (bf16[5120,256]{1,0:T(8,128)(2,1)S(1)}, bf16[5120,256]{1,0:T(8,128)(2,1)}, u32[]{:S(2)}) copy-start(bf16[5120,256]{1,0:T(8,128)(2,1)} %all-gather.5.cloned.1.call-done) | copy-start | bytes 7864324
  95.5 23.4 %collective-permute-start.1 = (f32[2,256,256]{2,1,0:T(8,128)S(1)}, f32[2,256,256]{2,1,0:T(8,128)S(1)}, u32[]{:S(2)}, u32[]{:S(2)}) collective-permute-start(f32[2,256,256]{2,1,0:T(8,128)S(1)} %project_q.1), channel_id=1, source_target_pairs={{0,16},{16,0},{1,17},{17,1},{2,18},{18,2},{3,19},{19,3},{4,20},{20... | collective-permute-start | bytes 1572872 | tf_op jit(solution)/shard_map/project_q/ppermute | solution.py:279
  116.9 5.1 %collective-permute-start.3 = (bf16[16,64,256]{2,1,0:T(8,128)(2,1)S(1)}, bf16[16,64,256]{2,1,0:T(8,128)(2,1)S(1)}, u32[]{:S(2)}, u32[]{:S(2)}) collective-permute-start(bf16[16,64,256]{2,1,0:T(8,128)(2,1)S(1)} %all-to-all-done.2.mine_ref), channel_id=1, source_target_pairs={{0,1},{1,0},{2,3},{3,2},{4,5},{5,4},{6,7},{7,6},{8,9},{9,8},{10,11... | collective-permute-start | bytes 1572872 | tf_op jit(solution)/shard_map/attend/ppermute | solution.py:26
  119.0 10.6 %collective-permute-start.2 = (bf16[2,256,256]{2,1,0:T(8,128)(2,1)S(1)}, bf16[2,256,256]{2,1,0:T(8,128)(2,1)S(1)}, u32[]{:S(2)}, u32[]{:S(2)}) collective-permute-start(bf16[2,256,256]{2,1,0:T(8,128)(2,1)S(1)} %add_convert_fusion.q_ref), channel_id=1, source_target_pairs={{0,2},{2,0},{1,3},{3,1},{4,6},{6,4},{5,7},{7,5},{8,10},{10,8},{9,1... | collective-permute-start | bytes 786440 | tf_op jit(solution)/shard_map/project_q/ppermute | solution.py:280
Sparse Core Ops, SparseCore 0:
  10.0 80.8 all-gather.4

commit v11 on v10

--- a/solution.py
+++ b/solution.py
@@ -35,14 +35,12 @@
     return pieces
 
 
-def attend_kernel(side, place, q_ref, mine_ref, other_ref, *refs):
-    out_ref = refs[-1]
+def attend_kernel(place, own_ref, pair_ref, mine_ref, other_ref, out_ref):
     z, xh, yl, core = place[0], place[1], place[2], place[3]
-    rows = q_ref.shape[1]
+    rows = own_ref.shape[1]
     scale = HEAD**-0.5 * math.log2(math.e)
     chunk = mine_ref.shape[1]
     half = 4 * chunk
-    to = yl if side == 0 else 1 - yl
     lane = lax.broadcasted_iota(jnp.int32, (rows, HEAD), 1)
 
     def block(group):
@@ -58,6 +56,10 @@
         key_pos = lax.div(within, chunk) * (2 * rows) + owner * chunk + lax.rem(within, chunk)
         query_pos = lax.rem(z, 4) * (2 * rows) + x * rows + lax.broadcasted_iota(jnp.int32, shape, 0)
         seen = key_pos <= query_pos
+        for q_ref, to in ((own_ref, yl), (pair_ref, 1 - yl)):
+            share(last, x, seen, q_ref, to)
+
+    def share(last, x, seen, q_ref, to):
         stats = jnp.zeros((rows, HEAD), F32)
         for head in range(2):
             q = q_ref[x, :, head * HEAD : (head + 1) * HEAD]
@@ -93,18 +95,17 @@
                 run(last, x)
 
 
-def attend(side, place, q, mine, other, *first):
-    rows, cols = q.shape[1:]
-    vmem = pl.BlockSpec(memory_space=pltpu.VMEM)
-    return pl.pallas_call(
-        functools.partial(attend_kernel, side),
+def attend(place, own, pair, mine, other):
+    rows, cols = own.shape[1:]
+    vmem = pl.BlockSpec(memory_space=pltpu.VMEM)
+    return pl.pallas_call(
+        attend_kernel,
         out_shape=jax.ShapeDtypeStruct((4, rows + 16, cols), BF16),
-        in_specs=[pl.BlockSpec(memory_space=pltpu.SMEM)] + [vmem] * (3 + len(first)),
+        in_specs=[pl.BlockSpec(memory_space=pltpu.SMEM), vmem, vmem, vmem, vmem],
         out_specs=vmem,
-        input_output_aliases={4: 0} if first else {},
-        compiler_params=pltpu.CompilerParams(vmem_limit_bytes=40 * 1024 * 1024),
-        cost_estimate=pl.CostEstimate(flops=2**30, bytes_accessed=2**22, transcendentals=2**21),
-    )(place, q, mine, other, *first)
+        compiler_params=pltpu.CompilerParams(vmem_limit_bytes=40 * 1024 * 1024),
+        cost_estimate=pl.CostEstimate(flops=2**31, bytes_accessed=2**22, transcendentals=2**22),
+    )(place, own, pair, mine, other)
 
 
 def merge_kernel(parts_ref, out_ref):
@@ -280,9 +281,8 @@
         pair = lax.ppermute(q, "yl", [(0, 1), (1, 0)])
 
     with jax.named_scope("attend"):
-        swapped = swap(kv)
-        out = attend(0, place, q, kv, swapped)
-        out = attend(1, place, pair, kv, swapped, out)
+        kv, pair = lax.optimization_barrier((kv, pair))
+        out = attend(place, q, pair, kv, swap(kv))
         return merge(lax.all_to_all(out, ("xh", "yl"), 0, 0))
 
 

time: 155 us -> 155 us (level)
  the two profiles are of different devices: /device:TPU:32 before, /device:TPU:16 now
where the time goes in v11:
time: 155 us
  blocking collectives  70.8 us (46%)
  starting transfers between devices  28.8 us (19%)
  waiting for transfers between devices  25 us (16%)
  between operations  13.5 us (9%)
  Pallas kernels  13.1 us (8%)
  local copies, waits for them, and re-layouts  2.59 us (2%)
    all_gather x2, blocking collectives, on_device(): wkv = lax.all_gather(lax.all_gather(wkv, 'zh'), 'zl')  42.3 us
    all_to_all x1, blocking collectives, on_device(): return merge(lax.all_to_all(out, ('xh', 'yl'), 0, 0))  16.4 us
    all_to_all x1, blocking collectives, on_device(): lax.all_to_all(kv_sum.reshape(8, rows // 4, HEAD), ('xh', 'yl', 'core'),...  12.1 us
    all_to_all x1, starting transfers between devices, on_device(): lax.all_to_all(parts.reshape(32, rows + 16, HEAD), ('xh',) + COL, 0, 0)  9.45 us
    ppermute x1, waiting for transfers between devices, on_device(): q = (q + lax.ppermute(q, 'xh', [(0, 1), (1, 0)])).astype(BF16)  9.23 us
    all_gather x1, waiting for transfers between devices, on_device(): wq = lax.all_gather(padded, ('zh', 'zl'), axis=0)  8.97 us
    all_to_all x1, starting transfers between devices, gather(): return lax.all_to_all(jnp.broadcast_to(x[None], (n, *x.shape)), axes, 0, 0)  8.85 us
    ppermute x1, waiting for transfers between devices, on_device(): pair = lax.ppermute(q, 'yl', [(0, 1), (1, 0)])  4.9 us
  transfers between devices with their start and end apart: 7, of which 4 were waited for; matrix products, arithmetic and copies ran while one was open for 1% of the time, Pallas kernels for 3%

profile of v11, /device:TPU:16, one launch (start us, length us, event | category | flops | bytes accessed | tf_op | source)
XLA Modules:
  0.0 154.8 jit_solution(12167178855629540520)
XLA Ops:
  6.5 0.0 all-gather.5.cloned.1.call-start
  6.5 3.3 %prep.1 = (bf16[2,8,2,272,128]{4,3,2,1,0:T(8,128)(2,1)}, bf16[320,256]{1,0:T(8,128)(2,1)}) custom-call(bf16[256,512]{1,0:T(8,128)(2,1)} %tokens_ref.1, bf16[512]{0:T(512)(128)(2,1)} %gain_ref.1, bf16[256,256]{1,0:T(8,128)(2,1)} %w_ref.1), custom_call_target="tpu_custom_call" | custom-call | tf_op jit(solution)/shard_map/prep/pallas_call | solution.py:163
  9.8 0.0 all-gather.5.cloned.1.call-update
  9.9 9.4 %all-to-all-start = ((bf16[32,272,128]{2,1,0:T(8,128)(2,1)}), bf16[32,272,128]{2,1,0:T(8,128)(2,1)S(1)}, u32[]{:S(2)}, u32[]{:S(2)}) async-start(bf16[32,272,128]{2,1,0:T(8,128)(2,1)} %bitcast.19), calls=%async_computation | async-start | bytes 4456448 | tf_op jit(solution)/shard_map/spread/all_to_all | solution.py:266
  19.3 0.8 dynamic-slice_select_fusion
  20.1 24.1 %all-gather = bf16[512,128]{1,0:T(8,128)(2,1)S(1)} all-gather(bf16[128,128]{1,0:T(8,128)(2,1)S(1)} %dynamic-slice_select_fusion), channel_id=2, replica_groups=mesh['zh'=4,'zl'=4,'xh'=2,'xl'=2,'yh'=2,'yl'=2,'core'=2] {'zh'}, dimensions={0}, use_global_device_ids=true | all-gather | bytes 163840 | tf_op jit(solution)/shard_map/weights/all_gather | solution.py:263
  44.2 18.2 %all-gather.1 = bf16[16,128,128]{2,1,0:T(8,128)(2,1)S(1)} all-gather(bf16[4,128,128]{2,1,0:T(8,128)(2,1)S(1)} %bitcast.21), channel_id=3, replica_groups=mesh['zh'=4,'zl'=4,'xh'=2,'xl'=2,'yh'=2,'yl'=2,'core'=2] {'zl'}, dimensions={0}, use_global_device_ids=true | all-gather | bytes 655360 | tf_op jit(solution)/shard_map/weights/all_gather | solution.py:263
  62.4 0.0 all-to-all-done
  62.4 2.1 %project_kv.1 = (bf16[2,256,2048]{2,1,0:T(8,128)(2,1)}, f32[2,256,128]{2,1,0:T(8,128)S(1)}) custom-call(bf16[2,16,272,128]{3,2,1,0:T(8,128)(2,1)S(1)} %bitcast.15, bf16[4,4,128,128]{3,2,1,0:T(8,128)(2,1)S(1)} %bitcast.17), custom_call_target="tpu_custom_call" | custom-call | flops 268435456 | bytes 5242880 | tf_op jit(solution)/shard_map/project_kv/pallas_call | solution.py:204
  64.5 1.9 %collective-permute-start = (bf16[2,256,2048]{2,1,0:T(8,128)(2,1)}, bf16[2,256,2048]{2,1,0:T(8,128)(2,1)S(1)}, u32[]{:S(2)}, u32[]{:S(2)}) collective-permute-start(bf16[2,256,2048]{2,1,0:T(8,128)(2,1)} %get-tuple-element.12.mine_ref), channel_id=1, source_target_pairs={{0,1},{1,0},{2,3},{3,2},{4,5},{5,4},{6,7},{7,6},{8,9},{9,8},{10,11... | collective-permute-start | bytes 6291464 | tf_op jit(solution)/shard_map/project_q/ppermute | solution.py:26
  66.4 12.1 %all_to_all.20 = f32[8,64,128]{2,1,0:T(8,128)S(1)} all-to-all(f32[8,64,128]{2,1,0:T(8,128)S(1)} %bitcast.18), channel_id=1, replica_groups=mesh['zh'=4,'zl'=4,'xh'=2,'xl'=2,'yh'=2,'yl'=2,'core'=2] {'xh','yl','core'}, dimensions={0} | all-to-all | bytes 524288 | tf_op jit(solution)/shard_map/project_kv/all_to_all | solution.py:271
  78.6 0.8 broadcast_in_dim.2
  79.5 8.8 %all-to-all-start.2 = ((bf16[16,64,256]{2,1,0:T(8,128)(2,1)}), bf16[16,64,256]{2,1,0:T(8,128)(2,1)S(1)}, u32[]{:S(2)}, u32[]{:S(2)}) async-start(bf16[16,64,256]{2,1,0:T(8,128)(2,1)} %broadcast_in_dim.2), calls=%async_computation.2 | async-start | bytes 1048576 | tf_op jit(solution)/shard_map/gather_kv/all_to_all | solution.py:22
  88.3 0.1 pad_add_fusion.place
  88.4 0.0 collective-permute-done.other_ref
  88.4 9.0 %all-gather.5.cloned.1.call-done = bf16[5120,256]{1,0:T(8,128)(2,1)} async-done(((bf16[320,256]{1,0:T(8,128)(2,1)}), bf16[5120,256]{1,0:T(8,128)(2,1)}) %all-gather.5.cloned.1.call-update) | async-done | bytes 2621456 | tf_op jit(solution)/shard_map/weights/all_gather | solution.py:256
  97.4 0.0 copy-start
  97.4 1.7 %copy-done = bf16[5120,256]{1,0:T(8,128)(2,1)S(1)} copy-done((bf16[5120,256]{1,0:T(8,128)(2,1)S(1)}, bf16[5120,256]{1,0:T(8,128)(2,1)}, u32[]{:S(2)}) %copy-start) | copy-done | bytes 2621464
  99.1 2.8 %project_q.1 = f32[2,256,256]{2,1,0:T(8,128)S(1)} custom-call(s32[4]{0:T(128)S(1)} %pad_add_fusion.place, bf16[2,256,2048]{2,1,0:T(8,128)(2,1)} %get-tuple-element.12.mine_ref, bf16[2,256,2048]{2,1,0:T(8,128)(2,1)S(1)} %collective-permute-done.other_ref, bf16[16,320,256]{2,1,0:T(8,128)(2,1)S(1)} %bitcast.16), custom_call_target="tpu_custom_call" | custom-call | flops 1073741824 | bytes 6291456 | tf_op jit(solution)/shard_map/project_q/pallas_call | solution.py:235
  102.0 3.3 %collective-permute-start.1 = (f32[2,256,256]{2,1,0:T(8,128)S(1)}, f32[2,256,256]{2,1,0:T(8,128)S(1)}, u32[]{:S(2)}, u32[]{:S(2)}) collective-permute-start(f32[2,256,256]{2,1,0:T(8,128)S(1)} %project_q.1), channel_id=1, source_target_pairs={{0,16},{16,0},{1,17},{17,1},{2,18},{18,2},{3,19},{19,3},{4,20},{20... | collective-permute-start | bytes 1572872 | tf_op jit(solution)/shard_map/project_q/ppermute | solution.py:280
  105.3 9.2 %collective-permute-done.1 = f32[2,256,256]{2,1,0:T(8,128)S(1)} collective-permute-done((f32[2,256,256]{2,1,0:T(8,128)S(1)}, f32[2,256,256]{2,1,0:T(8,128)S(1)}, u32[]{:S(2)}, u32[]{:S(2)}) %collective-permute-start.1) | collective-permute-done | bytes 524320 | tf_op jit(solution)/shard_map/project_q/ppermute | solution.py:280
  114.5 0.1 add_convert_fusion.own_ref
  114.6 3.3 %collective-permute-start.2 = (bf16[2,256,256]{2,1,0:T(8,128)(2,1)S(1)}, bf16[2,256,256]{2,1,0:T(8,128)(2,1)S(1)}, u32[]{:S(2)}, u32[]{:S(2)}) collective-permute-start(bf16[2,256,256]{2,1,0:T(8,128)(2,1)S(1)} %add_convert_fusion.own_ref), channel_id=1, source_target_pairs={{0,2},{2,0},{1,3},{3,1},{4,6},{6,4},{5,7},{7,5},{8,10},{10,8},{9,1... | collective-permute-start | bytes 786440 | tf_op jit(solution)/shard_map/project_q/ppermute | solution.py:281
  118.0 0.0 all-to-all-done.2.mine_ref
  118.0 4.9 %collective-permute-done.2.pair_ref = bf16[2,256,256]{2,1,0:T(8,128)(2,1)S(1)} collective-permute-done((bf16[2,256,256]{2,1,0:T(8,128)(2,1)S(1)}, bf16[2,256,256]{2,1,0:T(8,128)(2,1)S(1)}, u32[]{:S(2)}, u32[]{:S(2)}) %collective-permute-start.2) | collective-permute-done | bytes 262176 | tf_op jit(solution)/shard_map/project_q/ppermute | solution.py:281
  122.9 1.9 %collective-permute-start.3 = (bf16[16,64,256]{2,1,0:T(8,128)(2,1)S(1)}, bf16[16,64,256]{2,1,0:T(8,128)(2,1)S(1)}, u32[]{:S(2)}, u32[]{:S(2)}) collective-permute-start(bf16[16,64,256]{2,1,0:T(8,128)(2,1)S(1)} %all-to-all-done.2.mine_ref), channel_id=1, source_target_pairs={{0,1},{1,0},{2,3},{3,2},{4,5},{5,4},{6,7},{7,6},{8,9},{9,8},{10,11... | collective-permute-start | bytes 1572872 | tf_op jit(solution)/shard_map/attend/ppermute | solution.py:26
  124.8 1.9 %collective-permute-done.3.other_ref = bf16[16,64,256]{2,1,0:T(8,128)(2,1)S(1)} collective-permute-done((bf16[16,64,256]{2,1,0:T(8,128)(2,1)S(1)}, bf16[16,64,256]{2,1,0:T(8,128)(2,1)S(1)}, u32[]{:S(2)}, u32[]{:S(2)}) %collective-permute-start.3) | collective-permute-done | bytes 524320 | tf_op jit(solution)/shard_map/attend/ppermute | solution.py:26
  126.7 3.6 %attend.2 = bf16[4,272,256]{2,1,0:T(8,128)(2,1)S(1)} custom-call(s32[4]{0:T(128)S(1)} %pad_add_fusion.place, bf16[2,256,256]{2,1,0:T(8,128)(2,1)S(1)} %add_convert_fusion.own_ref, bf16[2,256,256]{2,1,0:T(8,128)(2,1)S(1)} %collective-permute-done.2.pair_ref, bf16[16,64,256]{2,1,0:T(8,128)(2,1)S(1)} %all-to-all-done.2.mine_ref, ...), custom_call_target="tpu_custom_call" | custom-call | flops 2147483648 | bytes 4194304 | tf_op jit(solution)/shard_map/attend/pallas_call | solution.py:101
  130.3 16.4 %all_to_all.21.parts_ref = bf16[4,272,256]{2,1,0:T(8,128)(2,1)S(1)} all-to-all(bf16[4,272,256]{2,1,0:T(8,128)(2,1)S(1)} %attend.2), channel_id=1, replica_groups=mesh['zh'=4,'zl'=4,'xh'=2,'xl'=2,'yh'=2,'yl'=2,'core'=2] {'xh','yl'}, dimensions={0} | all-to-all | bytes 1114112 | tf_op jit(solution)/shard_map/attend/all_to_all | solution.py:286
  146.8 1.2 attend.3
  (3 shorter events, 0.0 us)
Async XLA Ops:
  6.5 90.8 %all-gather.5.cloned.1.call-start = ((), (), s32[]{:S(2)}) async-start(), calls=%async_computation.4 | async-start | bytes 2785280 | tf_op jit(solution)/shard_map/weights/all_gather | solution.py:256
  9.9 52.5 %all-to-all-start = ((bf16[32,272,128]{2,1,0:T(8,128)(2,1)}), bf16[32,272,128]{2,1,0:T(8,128)(2,1)S(1)}, u32[]{:S(2)}, u32[]{:S(2)}) async-start(bf16[32,272,128]{2,1,0:T(8,128)(2,1)} %bitcast.19), calls=%async_computation | async-start | bytes 4456448 | tf_op jit(solution)/shard_map/spread/all_to_all | solution.py:266
  64.5 23.9 %collective-permute-start = (bf16[2,256,2048]{2,1,0:T(8,128)(2,1)}, bf16[2,256,2048]{2,1,0:T(8,128)(2,1)S(1)}, u32[]{:S(2)}, u32[]{:S(2)}) collective-permute-start(bf16[2,256,2048]{2,1,0:T(8,128)(2,1)} %get-tuple-element.12.mine_ref), channel_id=1, source_target_pairs={{0,1},{1,0},{2,3},{3,2},{4,5},{5,4},{6,7},{7,6},{8,9},{9,8},{10,11... | collective-permute-start | bytes 6291464 | tf_op jit(solution)/shard_map/project_q/ppermute | solution.py:26
  79.5 38.5 %all-to-all-start.2 = ((bf16[16,64,256]{2,1,0:T(8,128)(2,1)}), bf16[16,64,256]{2,1,0:T(8,128)(2,1)S(1)}, u32[]{:S(2)}, u32[]{:S(2)}) async-start(bf16[16,64,256]{2,1,0:T(8,128)(2,1)} %broadcast_in_dim.2), calls=%async_computation.2 | async-start | bytes 1048576 | tf_op jit(solution)/shard_map/gather_kv/all_to_all | solution.py:22
  97.4 1.7 %copy-start = (bf16[5120,256]{1,0:T(8,128)(2,1)S(1)}, bf16[5120,256]{1,0:T(8,128)(2,1)}, u32[]{:S(2)}) copy-start(bf16[5120,256]{1,0:T(8,128)(2,1)} %all-gather.5.cloned.1.call-done) | copy-start | bytes 7864324
  102.0 12.6 %collective-permute-start.1 = (f32[2,256,256]{2,1,0:T(8,128)S(1)}, f32[2,256,256]{2,1,0:T(8,128)S(1)}, u32[]{:S(2)}, u32[]{:S(2)}) collective-permute-start(f32[2,256,256]{2,1,0:T(8,128)S(1)} %project_q.1), channel_id=1, source_target_pairs={{0,16},{16,0},{1,17},{17,1},{2,18},{18,2},{3,19},{19,3},{4,20},{20... | collective-permute-start | bytes 1572872 | tf_op jit(solution)/shard_map/project_q/ppermute | solution.py:280
  114.6 8.3 %collective-permute-start.2 = (bf16[2,256,256]{2,1,0:T(8,128)(2,1)S(1)}, bf16[2,256,256]{2,1,0:T(8,128)(2,1)S(1)}, u32[]{:S(2)}, u32[]{:S(2)}) collective-permute-start(bf16[2,256,256]{2,1,0:T(8,128)(2,1)S(1)} %add_convert_fusion.own_ref), channel_id=1, source_target_pairs={{0,2},{2,0},{1,3},{3,1},{4,6},{6,4},{5,7},{7,5},{8,10},{10,8},{9,1... | collective-permute-start | bytes 786440 | tf_op jit(solution)/shard_map/project_q/ppermute | solution.py:281
  122.9 3.8 %collective-permute-start.3 = (bf16[16,64,256]{2,1,0:T(8,128)(2,1)S(1)}, bf16[16,64,256]{2,1,0:T(8,128)(2,1)S(1)}, u32[]{:S(2)}, u32[]{:S(2)}) collective-permute-start(bf16[16,64,256]{2,1,0:T(8,128)(2,1)S(1)} %all-to-all-done.2.mine_ref), channel_id=1, source_target_pairs={{0,1},{1,0},{2,3},{3,2},{4,5},{5,4},{6,7},{7,6},{8,9},{9,8},{10,11... | collective-permute-start | bytes 1572872 | tf_op jit(solution)/shard_map/attend/ppermute | solution.py:26
Sparse Core Ops, SparseCore 0:
  10.0 87.3 all-gather.4

commit v12 on v10

--- a/solution.py
+++ b/solution.py
@@ -214,29 +214,56 @@
     )(parts, w)
 
 
-def q_kernel(place, mine_ref, other_ref, w_ref, out_ref):
+def q_kernel(place, mine_hbm, other_hbm, w_hbm, out_ref, mine_ref, other_ref, w_ref, sems):
     core = place[3]
+    blocks, depth = w_ref.shape[:2]
+    half = depth // 2
     rows = mine_ref.shape[1]
-    half = mine_ref.shape[2] // w_ref.shape[0]
-    for x in range(2):
-        total = jnp.zeros((rows, w_ref.shape[2]), F32)
-        for c in range(w_ref.shape[0]):
-            t = jnp.concatenate([ref[x, :, c * half : (c + 1) * half] for ref in (mine_ref, other_ref)], axis=1)
+    step = blocks // 4
+    copies = []
+    for i in range(4):
+        at = pl.ds(i * step, step)
+        wide = pl.ds(i * step * half, step * half)
+        copies.append(
+            [
+                pltpu.make_async_copy(mine_hbm.at[:, :, wide], mine_ref.at[:, :, wide], sems.at[3 * i]),
+                pltpu.make_async_copy(other_hbm.at[:, :, wide], other_ref.at[:, :, wide], sems.at[3 * i + 1]),
+                pltpu.make_async_copy(w_hbm.at[at, :depth], w_ref.at[at], sems.at[3 * i + 2]),
+            ]
+        )
+    for group in copies:
+        for copy in group:
+            copy.start()
+    totals = [jnp.zeros((rows, w_ref.shape[2]), F32) for _ in range(2)]
+    for i in range(4):
+        for copy in copies[i]:
+            copy.wait()
+        for c in range(i * step, (i + 1) * step):
             w = jnp.concatenate(
                 [w_ref[c, pl.ds(pl.multiple_of(at * half, half), half)] for at in (core, 1 - core)], axis=0
             )
-            total += jnp.dot(t, w, preferred_element_type=F32)
-        out_ref[x] = total
+            for x in range(2):
+                t = jnp.concatenate([ref[x, :, c * half : (c + 1) * half] for ref in (mine_ref, other_ref)], axis=1)
+                totals[x] += jnp.dot(t, w, preferred_element_type=F32)
+    for x in range(2):
+        out_ref[x] = totals[x]
 
 
 def project_q(place, mine, other, w):
     vmem = pl.BlockSpec(memory_space=pltpu.VMEM)
+    hbm = pl.BlockSpec(memory_space=pltpu.HBM)
     return pl.pallas_call(
         q_kernel,
         out_shape=jax.ShapeDtypeStruct((*mine.shape[:2], w.shape[2]), F32),
-        in_specs=[pl.BlockSpec(memory_space=pltpu.SMEM), vmem, vmem, vmem],
+        in_specs=[pl.BlockSpec(memory_space=pltpu.SMEM), hbm, hbm, hbm],
         out_specs=vmem,
-        compiler_params=pltpu.CompilerParams(vmem_limit_bytes=40 * 1024 * 1024),
+        scratch_shapes=[
+            pltpu.VMEM(mine.shape, BF16),
+            pltpu.VMEM(other.shape, BF16),
+            pltpu.VMEM((w.shape[0], w.shape[1] - 64, w.shape[2]), BF16),
+            pltpu.SemaphoreType.DMA((12,)),
+        ],
+        compiler_params=pltpu.CompilerParams(vmem_limit_bytes=57 * 1024 * 1024),
         cost_estimate=pl.CostEstimate(flops=2**30, bytes_accessed=6 * 2**20, transcendentals=0),
     )(place, mine, other, w)
 
@@ -280,6 +307,7 @@
         pair = lax.ppermute(q, "yl", [(0, 1), (1, 0)])
 
     with jax.named_scope("attend"):
+        kv, q = lax.optimization_barrier((kv, q))
         swapped = swap(kv)
         out = attend(0, place, q, kv, swapped)
         out = attend(1, place, pair, kv, swapped, out)

time: 155 us -> 156 us (level)
  the two profiles are of different devices: /device:TPU:32 before, /device:TPU:16 now
where the time goes in v12:
time: 156 us; the launch traced here: 155 us
  blocking collectives  69.6 us (45%)
  starting transfers between devices  28.8 us (18%)
  waiting for transfers between devices  23.8 us (15%)
  Pallas kernels  15.8 us (10%)
  between operations  13.5 us (9%)
  other arithmetic  2.5 us (2%)
    all_gather x2, blocking collectives, on_device(): wkv = lax.all_gather(lax.all_gather(wkv, 'zh'), 'zl')  42.3 us
    all_to_all x1, blocking collectives, on_device(): return merge(lax.all_to_all(out, ('xh', 'yl'), 0, 0))  15.2 us
    all_to_all x1, blocking collectives, on_device(): lax.all_to_all(kv_sum.reshape(8, rows // 4, HEAD), ('xh', 'yl', 'core'),...  12.1 us
    all_to_all x1, starting transfers between devices, on_device(): lax.all_to_all(parts.reshape(32, rows + 16, HEAD), ('xh',) + COL, 0, 0)  9.45 us
    ppermute x1, waiting for transfers between devices, on_device(): q = (q + lax.ppermute(q, 'xh', [(0, 1), (1, 0)])).astype(BF16)  9.45 us
    all_to_all x1, starting transfers between devices, gather(): return lax.all_to_all(jnp.broadcast_to(x[None], (n, *x.shape)), axes, 0, 0)  8.85 us
    all_gather x1, waiting for transfers between devices, on_device(): wq = lax.all_gather(padded, ('zh', 'zl'), axis=0)  8.46 us
    ppermute x1, waiting for transfers between devices, on_device(): pair = lax.ppermute(q, 'yl', [(0, 1), (1, 0)])  5.06 us
  transfers between devices with their start and end apart: 7, of which 4 were waited for; matrix products, arithmetic and copies ran while one was open for 2% of the time, Pallas kernels for 6%

profile of v12, /device:TPU:16, one launch (start us, length us, event | category | flops | bytes accessed | tf_op | source)
XLA Modules:
  0.0 154.9 jit_solution(8094608648944408264)
XLA Ops:
  6.5 0.0 all-gather.5.cloned.1.call-start
  6.5 3.3 %prep.1 = (bf16[2,8,2,272,128]{4,3,2,1,0:T(8,128)(2,1)}, bf16[320,256]{1,0:T(8,128)(2,1)}) custom-call(bf16[256,512]{1,0:T(8,128)(2,1)} %tokens_ref.1, bf16[512]{0:T(512)(128)(2,1)} %gain_ref.1, bf16[256,256]{1,0:T(8,128)(2,1)} %w_ref.1), custom_call_target="tpu_custom_call" | custom-call | tf_op jit(solution)/shard_map/prep/pallas_call | solution.py:162
  9.8 0.0 all-gather.5.cloned.1.call-update
  9.9 9.4 %all-to-all-start = ((bf16[32,272,128]{2,1,0:T(8,128)(2,1)}), bf16[32,272,128]{2,1,0:T(8,128)(2,1)S(1)}, u32[]{:S(2)}, u32[]{:S(2)}) async-start(bf16[32,272,128]{2,1,0:T(8,128)(2,1)} %bitcast.19), calls=%async_computation | async-start | bytes 4456448 | tf_op jit(solution)/shard_map/spread/all_to_all | solution.py:292
  19.3 0.8 dynamic-slice_select_fusion
  20.1 24.1 %all-gather = bf16[512,128]{1,0:T(8,128)(2,1)S(1)} all-gather(bf16[128,128]{1,0:T(8,128)(2,1)S(1)} %dynamic-slice_select_fusion), channel_id=2, replica_groups=mesh['zh'=4,'zl'=4,'xh'=2,'xl'=2,'yh'=2,'yl'=2,'core'=2] {'zh'}, dimensions={0}, use_global_device_ids=true | all-gather | bytes 163840 | tf_op jit(solution)/shard_map/weights/all_gather | solution.py:289
  44.2 18.2 %all-gather.1 = bf16[16,128,128]{2,1,0:T(8,128)(2,1)S(1)} all-gather(bf16[4,128,128]{2,1,0:T(8,128)(2,1)S(1)} %bitcast.21), channel_id=3, replica_groups=mesh['zh'=4,'zl'=4,'xh'=2,'xl'=2,'yh'=2,'yl'=2,'core'=2] {'zl'}, dimensions={0}, use_global_device_ids=true | all-gather | bytes 655360 | tf_op jit(solution)/shard_map/weights/all_gather | solution.py:289
  62.4 0.0 all-to-all-done
  62.4 2.1 %project_kv.1 = (bf16[2,256,2048]{2,1,0:T(8,128)(2,1)}, f32[2,256,128]{2,1,0:T(8,128)S(1)}) custom-call(bf16[2,16,272,128]{3,2,1,0:T(8,128)(2,1)S(1)} %bitcast.15, bf16[4,4,128,128]{3,2,1,0:T(8,128)(2,1)S(1)} %bitcast.16), custom_call_target="tpu_custom_call" | custom-call | flops 268435456 | bytes 5242880 | tf_op jit(solution)/shard_map/project_kv/pallas_call | solution.py:203
  64.5 1.9 %collective-permute-start = (bf16[2,256,2048]{2,1,0:T(8,128)(2,1)}, bf16[2,256,2048]{2,1,0:T(8,128)(2,1)S(1)}, u32[]{:S(2)}, u32[]{:S(2)}) collective-permute-start(bf16[2,256,2048]{2,1,0:T(8,128)(2,1)} %get-tuple-element.12.mine_hbm), channel_id=1, source_target_pairs={{0,1},{1,0},{2,3},{3,2},{4,5},{5,4},{6,7},{7,6},{8,9},{9,8},{10,11... | collective-permute-start | bytes 6291464 | tf_op jit(solution)/shard_map/project_q/ppermute | solution.py:26
  66.4 12.1 %all_to_all.20 = f32[8,64,128]{2,1,0:T(8,128)S(1)} all-to-all(f32[8,64,128]{2,1,0:T(8,128)S(1)} %bitcast.17), channel_id=1, replica_groups=mesh['zh'=4,'zl'=4,'xh'=2,'xl'=2,'yh'=2,'yl'=2,'core'=2] {'xh','yl','core'}, dimensions={0} | all-to-all | bytes 524288 | tf_op jit(solution)/shard_map/project_kv/all_to_all | solution.py:297
  78.6 0.8 broadcast_in_dim.2
  79.4 8.8 %all-to-all-start.2 = ((bf16[16,64,256]{2,1,0:T(8,128)(2,1)}), bf16[16,64,256]{2,1,0:T(8,128)(2,1)S(1)}, u32[]{:S(2)}, u32[]{:S(2)}) async-start(bf16[16,64,256]{2,1,0:T(8,128)(2,1)} %broadcast_in_dim.2), calls=%async_computation.2 | async-start | bytes 1048576 | tf_op jit(solution)/shard_map/gather_kv/all_to_all | solution.py:22
  88.3 0.6 pad_add_fusion.place
  88.9 0.0 collective-permute-done.other_hbm
  88.9 0.0 copy-start.1
  88.9 8.5 %all-gather.5.cloned.1.call-done = bf16[5120,256]{1,0:T(8,128)(2,1)} async-done(((bf16[320,256]{1,0:T(8,128)(2,1)}), bf16[5120,256]{1,0:T(8,128)(2,1)}) %all-gather.5.cloned.1.call-update) | async-done | bytes 2621456 | tf_op jit(solution)/shard_map/weights/all_gather | solution.py:282
  97.3 0.0 copy-done.1
  97.4 4.9 %project_q.1 = f32[2,256,256]{2,1,0:T(8,128)} custom-call(s32[4]{0:T(128)} %pad_add_fusion.place, bf16[2,256,2048]{2,1,0:T(8,128)(2,1)} %get-tuple-element.12.mine_hbm, bf16[2,256,2048]{2,1,0:T(8,128)(2,1)} %copy-done.1, bf16[16,320,256]{2,1,0:T(8,128)(2,1)} %bitcast.18), custom_call_target="tpu_custom_call" | custom-call | flops 1073741824 | bytes 6291456 | tf_op jit(solution)/shard_map/project_q/pallas_call | solution.py:255
  102.3 3.3 %collective-permute-start.1 = (f32[2,256,256]{2,1,0:T(8,128)}, f32[2,256,256]{2,1,0:T(8,128)S(1)}, u32[]{:S(2)}, u32[]{:S(2)}) collective-permute-start(f32[2,256,256]{2,1,0:T(8,128)} %project_q.1), channel_id=1, source_target_pairs={{0,16},{16,0},{1,17},{17,1},{2,18},{18,2},{3,19},{19,3},{4,20},{20... | collective-permute-start | bytes 1572872 | tf_op jit(solution)/shard_map/project_q/ppermute | solution.py:306
  105.6 9.4 %collective-permute-done.1 = f32[2,256,256]{2,1,0:T(8,128)S(1)} collective-permute-done((f32[2,256,256]{2,1,0:T(8,128)}, f32[2,256,256]{2,1,0:T(8,128)S(1)}, u32[]{:S(2)}, u32[]{:S(2)}) %collective-permute-start.1) | collective-permute-done | bytes 524320 | tf_op jit(solution)/shard_map/project_q/ppermute | solution.py:306
  115.1 1.1 add_convert_fusion.q_ref
  116.2 0.8 all-to-all-done.2.mine_ref
  117.0 1.9 %collective-permute-start.3 = (bf16[16,64,256]{2,1,0:T(8,128)(2,1)S(1)}, bf16[16,64,256]{2,1,0:T(8,128)(2,1)S(1)}, u32[]{:S(2)}, u32[]{:S(2)}) collective-permute-start(bf16[16,64,256]{2,1,0:T(8,128)(2,1)S(1)} %all-to-all-done.2.mine_ref), channel_id=1, source_target_pairs={{0,1},{1,0},{2,3},{3,2},{4,5},{5,4},{6,7},{7,6},{8,9},{9,8},{10,11... | collective-permute-start | bytes 1572872 | tf_op jit(solution)/shard_map/attend/ppermute | solution.py:26
  118.9 3.4 %collective-permute-start.2 = (bf16[2,256,256]{2,1,0:T(8,128)(2,1)S(1)}, bf16[2,256,256]{2,1,0:T(8,128)(2,1)S(1)}, u32[]{:S(2)}, u32[]{:S(2)}) collective-permute-start(bf16[2,256,256]{2,1,0:T(8,128)(2,1)S(1)} %add_convert_fusion.q_ref), channel_id=1, source_target_pairs={{0,2},{2,0},{1,3},{3,1},{4,6},{6,4},{5,7},{7,5},{8,10},{10,8},{9,1... | collective-permute-start | bytes 786440 | tf_op jit(solution)/shard_map/project_q/ppermute | solution.py:307
  122.3 0.0 collective-permute-done.3.other_ref
  122.3 0.0 copy-done
  122.3 2.1 %attend.3.refs_0_ = bf16[4,272,256]{2,1,0:T(8,128)(2,1)S(1)} custom-call(s32[4]{0:T(128)S(1)} %copy-done, bf16[2,256,256]{2,1,0:T(8,128)(2,1)S(1)} %add_convert_fusion.q_ref, bf16[16,64,256]{2,1,0:T(8,128)(2,1)S(1)} %all-to-all-done.2.mine_ref, bf16[16,64,256]{2,1,0:T(8,128)(2,1)S(1)} %collective-permute-done.3.other_ref), custom_call_target="tpu_custom_call" | custom-call | flops 1073741824 | bytes 4194304 | tf_op jit(solution)/shard_map/attend/pallas_call | solution.py:99
  124.4 5.1 %collective-permute-done.2.q_ref = bf16[2,256,256]{2,1,0:T(8,128)(2,1)S(1)} collective-permute-done((bf16[2,256,256]{2,1,0:T(8,128)(2,1)S(1)}, bf16[2,256,256]{2,1,0:T(8,128)(2,1)S(1)}, u32[]{:S(2)}, u32[]{:S(2)}) %collective-permute-start.2) | collective-permute-done | bytes 262176 | tf_op jit(solution)/shard_map/project_q/ppermute | solution.py:307
  129.5 2.2 %attend.4 = bf16[4,272,256]{2,1,0:T(8,128)(2,1)S(1)} custom-call(s32[4]{0:T(128)S(1)} %copy-done, bf16[2,256,256]{2,1,0:T(8,128)(2,1)S(1)} %collective-permute-done.2.q_ref, bf16[16,64,256]{2,1,0:T(8,128)(2,1)S(1)} %all-to-all-done.2.mine_ref, bf16[16,64,256]{2,1,0:T(8,128)(2,1)S(1)} %collective-permute-done.3.other_ref, ...), custom_call_target="tpu_custom_call", output_to_operand_aliasing={{}: (4, {})} | custom-call | flops 1073741824 | bytes 4194304 | tf_op jit(solution)/shard_map/attend/pallas_call | solution.py:99
  131.7 15.2 %all_to_all.21.parts_ref = bf16[4,272,256]{2,1,0:T(8,128)(2,1)S(1)} all-to-all(bf16[4,272,256]{2,1,0:T(8,128)(2,1)S(1)} %attend.4), channel_id=1, replica_groups=mesh['zh'=4,'zl'=4,'xh'=2,'xl'=2,'yh'=2,'yl'=2,'core'=2] {'xh','yl'}, dimensions={0} | all-to-all | bytes 1114112 | tf_op jit(solution)/shard_map/attend/all_to_all | solution.py:314
  146.9 1.2 attend.5
  (4 shorter events, 0.0 us)
Async XLA Ops:
  6.5 90.8 %all-gather.5.cloned.1.call-start = ((), (), s32[]{:S(2)}) async-start(), calls=%async_computation.4 | async-start | bytes 2785280 | tf_op jit(solution)/shard_map/weights/all_gather | solution.py:282
  9.9 52.5 %all-to-all-start = ((bf16[32,272,128]{2,1,0:T(8,128)(2,1)}), bf16[32,272,128]{2,1,0:T(8,128)(2,1)S(1)}, u32[]{:S(2)}, u32[]{:S(2)}) async-start(bf16[32,272,128]{2,1,0:T(8,128)(2,1)} %bitcast.19), calls=%async_computation | async-start | bytes 4456448 | tf_op jit(solution)/shard_map/spread/all_to_all | solution.py:292
  64.5 24.4 %collective-permute-start = (bf16[2,256,2048]{2,1,0:T(8,128)(2,1)}, bf16[2,256,2048]{2,1,0:T(8,128)(2,1)S(1)}, u32[]{:S(2)}, u32[]{:S(2)}) collective-permute-start(bf16[2,256,2048]{2,1,0:T(8,128)(2,1)} %get-tuple-element.12.mine_hbm), channel_id=1, source_target_pairs={{0,1},{1,0},{2,3},{3,2},{4,5},{5,4},{6,7},{7,6},{8,9},{9,8},{10,11... | collective-permute-start | bytes 6291464 | tf_op jit(solution)/shard_map/project_q/ppermute | solution.py:26
  79.4 37.6 %all-to-all-start.2 = ((bf16[16,64,256]{2,1,0:T(8,128)(2,1)}), bf16[16,64,256]{2,1,0:T(8,128)(2,1)S(1)}, u32[]{:S(2)}, u32[]{:S(2)}) async-start(bf16[16,64,256]{2,1,0:T(8,128)(2,1)} %broadcast_in_dim.2), calls=%async_computation.2 | async-start | bytes 1048576 | tf_op jit(solution)/shard_map/gather_kv/all_to_all | solution.py:22
  88.9 8.5 %copy-start.1 = (bf16[2,256,2048]{2,1,0:T(8,128)(2,1)}, bf16[2,256,2048]{2,1,0:T(8,128)(2,1)S(1)}, u32[]{:S(2)}) copy-start(bf16[2,256,2048]{2,1,0:T(8,128)(2,1)S(1)} %collective-permute-done.other_hbm) | copy-start | bytes 6291460
  97.4 24.9 %copy-start = (s32[4]{0:T(128)S(1)}, s32[4]{0:T(128)}, u32[]{:S(2)}) copy-start(s32[4]{0:T(128)} %pad_add_fusion.place) | copy-start | bytes 52
  102.3 12.8 %collective-permute-start.1 = (f32[2,256,256]{2,1,0:T(8,128)}, f32[2,256,256]{2,1,0:T(8,128)S(1)}, u32[]{:S(2)}, u32[]{:S(2)}) collective-permute-start(f32[2,256,256]{2,1,0:T(8,128)} %project_q.1), channel_id=1, source_target_pairs={{0,16},{16,0},{1,17},{17,1},{2,18},{18,2},{3,19},{19,3},{4,20},{20... | collective-permute-start | bytes 1572872 | tf_op jit(solution)/shard_map/project_q/ppermute | solution.py:306
  117.0 5.3 %collective-permute-start.3 = (bf16[16,64,256]{2,1,0:T(8,128)(2,1)S(1)}, bf16[16,64,256]{2,1,0:T(8,128)(2,1)S(1)}, u32[]{:S(2)}, u32[]{:S(2)}) collective-permute-start(bf16[16,64,256]{2,1,0:T(8,128)(2,1)S(1)} %all-to-all-done.2.mine_ref), channel_id=1, source_target_pairs={{0,1},{1,0},{2,3},{3,2},{4,5},{5,4},{6,7},{7,6},{8,9},{9,8},{10,11... | collective-permute-start | bytes 1572872 | tf_op jit(solution)/shard_map/attend/ppermute | solution.py:26
  118.9 10.6 %collective-permute-start.2 = (bf16[2,256,256]{2,1,0:T(8,128)(2,1)S(1)}, bf16[2,256,256]{2,1,0:T(8,128)(2,1)S(1)}, u32[]{:S(2)}, u32[]{:S(2)}) collective-permute-start(bf16[2,256,256]{2,1,0:T(8,128)(2,1)S(1)} %add_convert_fusion.q_ref), channel_id=1, source_target_pairs={{0,2},{2,0},{1,3},{3,1},{4,6},{6,4},{5,7},{7,5},{8,10},{10,8},{9,1... | collective-permute-start | bytes 786440 | tf_op jit(solution)/shard_map/project_q/ppermute | solution.py:307
Sparse Core Ops, SparseCore 0:
  10.0 87.3 all-gather.4

commit v13 on v10

--- a/solution.py
+++ b/solution.py
@@ -40,14 +40,14 @@
     z, xh, yl, core = place[0], place[1], place[2], place[3]
     rows = q_ref.shape[1]
     scale = HEAD**-0.5 * math.log2(math.e)
-    chunk = mine_ref.shape[1]
+    chunk = mine_ref.shape[2]
     half = 4 * chunk
     to = yl if side == 0 else 1 - yl
     lane = lax.broadcasted_iota(jnp.int32, (rows, HEAD), 1)
 
     def block(group):
         return jnp.concatenate(
-            [ref[4 * group : 4 * group + 4].reshape(half, 2 * HEAD) for ref in (mine_ref, other_ref)], axis=0
+            [ref[:, group].reshape(half, 2 * HEAD) for ref in (mine_ref, other_ref)], axis=0
         )
 
     def run(last, x):
@@ -272,7 +272,8 @@
         kv = jnp.concatenate([chunks[0], chunks[1]], axis=1)
 
     with jax.named_scope("gather_kv"):
-        kv = gather(kv, ("zh", "zl"), 16)
+        kv, wq = lax.optimization_barrier((lax.all_gather(kv, "zh"), wq))
+        kv = gather(kv, "zl", 4)
 
     with jax.named_scope("project_q"):
         q = project_q(place, whole, swap(whole), wq)

time: 155 us -> 154 us (level)
  the two profiles are of different devices: /device:TPU:32 before, /device:TPU:16 now
where the time goes in v13:
time: 154 us; the launch traced here: 153 us
  blocking collectives  86.4 us (56%)
  starting transfers between devices  24.1 us (16%)
  Pallas kernels  13.7 us (9%)
  between operations  13.5 us (9%)
  waiting for transfers between devices  11.6 us (8%)
  local copies, waits for them, and re-layouts  2.6 us (2%)
    all_gather x2, blocking collectives, on_device(): wkv = lax.all_gather(lax.all_gather(wkv, 'zh'), 'zl')  42.2 us
    all_gather x1, blocking collectives, on_device(): kv, wq = lax.optimization_barrier((lax.all_gather(kv, 'zh'), wq))  19.9 us
    all_to_all x1, blocking collectives, on_device(): lax.all_to_all(kv_sum.reshape(8, rows // 4, HEAD), ('xh', 'yl', 'core'),...  12.2 us
    all_to_all x1, blocking collectives, on_device(): return merge(lax.all_to_all(out, ('xh', 'yl'), 0, 0))  12.1 us
    all_to_all x1, starting transfers between devices, on_device(): lax.all_to_all(parts.reshape(32, rows + 16, HEAD), ('xh',) + COL, 0, 0)  9.45 us
    ppermute x1, waiting for transfers between devices, on_device(): q = (q + lax.ppermute(q, 'xh', [(0, 1), (1, 0)])).astype(BF16)  5.1 us
    ppermute x1, starting transfers between devices, on_device(): q = (q + lax.ppermute(q, 'xh', [(0, 1), (1, 0)])).astype(BF16)  4.37 us
    pallas_call x2, Pallas kernels, attend(): pl.pallas_call(functools.partial(attend_kernel, side), out_shape=jax.Shap...  4.3 us
  transfers between devices with their start and end apart: 7, of which 3 were waited for; matrix products, arithmetic and copies ran while one was open for 1% of the time, Pallas kernels for 5%

profile of v13, /device:TPU:16, one launch (start us, length us, event | category | flops | bytes accessed | tf_op | source)
XLA Modules:
  0.0 153.0 jit_solution(1084282486111205625)
XLA Ops:
  6.5 0.0 all-gather.6.cloned.1.call-start
  6.5 3.3 %prep.1 = (bf16[2,8,2,272,128]{4,3,2,1,0:T(8,128)(2,1)}, bf16[320,256]{1,0:T(8,128)(2,1)}) custom-call(bf16[256,512]{1,0:T(8,128)(2,1)} %tokens_ref.1, bf16[512]{0:T(512)(128)(2,1)} %gain_ref.1, bf16[256,256]{1,0:T(8,128)(2,1)} %w_ref.1), custom_call_target="tpu_custom_call" | custom-call | tf_op jit(solution)/shard_map/prep/pallas_call | solution.py:162
  9.8 0.0 all-gather.6.cloned.1.call-update
  9.9 9.4 %all-to-all-start = ((bf16[32,272,128]{2,1,0:T(8,128)(2,1)}), bf16[32,272,128]{2,1,0:T(8,128)(2,1)S(1)}, u32[]{:S(2)}, u32[]{:S(2)}) async-start(bf16[32,272,128]{2,1,0:T(8,128)(2,1)} %bitcast.20), calls=%async_computation | async-start | bytes 4456448 | tf_op jit(solution)/shard_map/spread/all_to_all | solution.py:265
  19.3 0.8 dynamic-slice_select_fusion
  20.1 24.1 %all-gather = bf16[512,128]{1,0:T(8,128)(2,1)S(1)} all-gather(bf16[128,128]{1,0:T(8,128)(2,1)S(1)} %dynamic-slice_select_fusion), channel_id=2, replica_groups=mesh['zh'=4,'zl'=4,'xh'=2,'xl'=2,'yh'=2,'yl'=2,'core'=2] {'zh'}, dimensions={0}, use_global_device_ids=true | all-gather | bytes 163840 | tf_op jit(solution)/shard_map/weights/all_gather | solution.py:262
  44.2 18.0 %all-gather.1 = bf16[16,128,128]{2,1,0:T(8,128)(2,1)S(1)} all-gather(bf16[4,128,128]{2,1,0:T(8,128)(2,1)S(1)} %bitcast.23), channel_id=3, replica_groups=mesh['zh'=4,'zl'=4,'xh'=2,'xl'=2,'yh'=2,'yl'=2,'core'=2] {'zl'}, dimensions={0}, use_global_device_ids=true | all-gather | bytes 655360 | tf_op jit(solution)/shard_map/weights/all_gather | solution.py:262
  62.3 0.0 all-to-all-done
  62.3 2.1 %project_kv.1 = (bf16[2,256,2048]{2,1,0:T(8,128)(2,1)}, f32[2,256,128]{2,1,0:T(8,128)S(1)}) custom-call(bf16[2,16,272,128]{3,2,1,0:T(8,128)(2,1)S(1)} %bitcast.16, bf16[4,4,128,128]{3,2,1,0:T(8,128)(2,1)S(1)} %bitcast.18), custom_call_target="tpu_custom_call" | custom-call | flops 268435456 | bytes 5242880 | tf_op jit(solution)/shard_map/project_kv/pallas_call | solution.py:203
  64.4 1.9 %collective-permute-start = (bf16[2,256,2048]{2,1,0:T(8,128)(2,1)}, bf16[2,256,2048]{2,1,0:T(8,128)(2,1)S(1)}, u32[]{:S(2)}, u32[]{:S(2)}) collective-permute-start(bf16[2,256,2048]{2,1,0:T(8,128)(2,1)} %get-tuple-element.12.mine_ref), channel_id=1, source_target_pairs={{0,1},{1,0},{2,3},{3,2},{4,5},{5,4},{6,7},{7,6},{8,9},{9,8},{10,11... | collective-permute-start | bytes 6291464 | tf_op jit(solution)/shard_map/project_q/ppermute | solution.py:26
  66.3 12.2 %all_to_all.20 = f32[8,64,128]{2,1,0:T(8,128)S(1)} all-to-all(f32[8,64,128]{2,1,0:T(8,128)S(1)} %bitcast.19), channel_id=1, replica_groups=mesh['zh'=4,'zl'=4,'xh'=2,'xl'=2,'yh'=2,'yl'=2,'core'=2] {'xh','yl','core'}, dimensions={0} | all-to-all | bytes 524288 | tf_op jit(solution)/shard_map/project_kv/all_to_all | solution.py:270
  78.6 19.9 %all-gather.2 = bf16[256,256]{1,0:T(8,128)(2,1)S(1)} all-gather(bf16[64,256]{1,0:T(8,128)(2,1)S(1)} %pad_maximum_fusion), channel_id=4, replica_groups=mesh['zh'=4,'zl'=4,'xh'=2,'xl'=2,'yh'=2,'yl'=2,'core'=2] {'zh'}, dimensions={0}, use_global_device_ids=true | all-gather | bytes 163840 | tf_op jit(solution)/shard_map/gather_kv/all_gather | solution.py:275
  98.5 0.0 all-gather.6.cloned.1.call-done
  98.5 0.9 broadcast_in_dim.2
  99.4 3.5 %all-to-all-start.2 = ((bf16[4,4,64,256]{3,2,1,0:T(8,128)(2,1)}), bf16[4,4,64,256]{3,2,1,0:T(8,128)(2,1)S(1)}, u32[]{:S(2)}, u32[]{:S(2)}) async-start(bf16[4,4,64,256]{3,2,1,0:T(8,128)(2,1)} %broadcast_in_dim.2), calls=%async_computation.2 | async-start | bytes 1048576 | tf_op jit(solution)/shard_map/gather_kv/all_to_all | solution.py:22
  102.8 0.1 pad_add_fusion.place
  102.9 0.0 collective-permute-done.other_ref
  102.9 0.0 copy-start
  102.9 1.7 %copy-done = bf16[5120,256]{1,0:T(8,128)(2,1)S(1)} copy-done((bf16[5120,256]{1,0:T(8,128)(2,1)S(1)}, bf16[5120,256]{1,0:T(8,128)(2,1)}, u32[]{:S(2)}) %copy-start) | copy-done | bytes 2621464
  104.7 2.8 %project_q.1 = f32[2,256,256]{2,1,0:T(8,128)S(1)} custom-call(s32[4]{0:T(128)S(1)} %pad_add_fusion.place, bf16[2,256,2048]{2,1,0:T(8,128)(2,1)} %get-tuple-element.12.mine_ref, bf16[2,256,2048]{2,1,0:T(8,128)(2,1)S(1)} %collective-permute-done.other_ref, bf16[16,320,256]{2,1,0:T(8,128)(2,1)S(1)} %bitcast.17), custom_call_target="tpu_custom_call" | custom-call | flops 1073741824 | bytes 6291456 | tf_op jit(solution)/shard_map/project_q/pallas_call | solution.py:234
  107.5 4.4 %collective-permute-start.1 = (f32[2,256,256]{2,1,0:T(8,128)S(1)}, f32[2,256,256]{2,1,0:T(8,128)S(1)}, u32[]{:S(2)}, u32[]{:S(2)}) collective-permute-start(f32[2,256,256]{2,1,0:T(8,128)S(1)} %project_q.1), channel_id=1, source_target_pairs={{0,16},{16,0},{1,17},{17,1},{2,18},{18,2},{3,19},{19,3},{4,20},{20... | collective-permute-start | bytes 1572872 | tf_op jit(solution)/shard_map/project_q/ppermute | solution.py:280
  111.9 3.4 %all-to-all-done.2.mine_ref = bf16[4,4,64,256]{3,2,1,0:T(8,128)(2,1)S(1)} async-done(((bf16[4,4,64,256]{3,2,1,0:T(8,128)(2,1)}), bf16[4,4,64,256]{3,2,1,0:T(8,128)(2,1)S(1)}, u32[]{:S(2)}, u32[]{:S(2)}) %all-to-all-start.2) | async-done | bytes 524320 | tf_op jit(solution)/shard_map/gather_kv/all_to_all | solution.py:22
  115.3 1.9 %collective-permute-start.3 = (bf16[4,4,64,256]{3,2,1,0:T(8,128)(2,1)S(1)}, bf16[4,4,64,256]{3,2,1,0:T(8,128)(2,1)S(1)}, u32[]{:S(2)}, u32[]{:S(2)}) collective-permute-start(bf16[4,4,64,256]{3,2,1,0:T(8,128)(2,1)S(1)} %all-to-all-done.2.mine_ref), channel_id=1, source_target_pairs={{0,1},{1,0},{2,3},{3,2},{4,5},{5,4},{6,7},{7,6},{8,9},{9,8},{10,11... | collective-permute-start | bytes 1572872 | tf_op jit(solution)/shard_map/attend/ppermute | solution.py:26
  117.2 5.1 %collective-permute-done.1 = f32[2,256,256]{2,1,0:T(8,128)S(1)} collective-permute-done((f32[2,256,256]{2,1,0:T(8,128)S(1)}, f32[2,256,256]{2,1,0:T(8,128)S(1)}, u32[]{:S(2)}, u32[]{:S(2)}) %collective-permute-start.1) | collective-permute-done | bytes 524320 | tf_op jit(solution)/shard_map/project_q/ppermute | solution.py:280
  122.3 0.1 add_convert_fusion.q_ref
  122.4 3.0 %collective-permute-start.2 = (bf16[2,256,256]{2,1,0:T(8,128)(2,1)S(1)}, bf16[2,256,256]{2,1,0:T(8,128)(2,1)S(1)}, u32[]{:S(2)}, u32[]{:S(2)}) collective-permute-start(bf16[2,256,256]{2,1,0:T(8,128)(2,1)S(1)} %add_convert_fusion.q_ref), channel_id=1, source_target_pairs={{0,2},{2,0},{1,3},{3,1},{4,6},{6,4},{5,7},{7,5},{8,10},{10,8},{9,1... | collective-permute-start | bytes 786440 | tf_op jit(solution)/shard_map/project_q/ppermute | solution.py:281
  125.4 0.0 collective-permute-done.3.other_ref
  125.4 2.1 %attend.3.refs_0_ = bf16[4,272,256]{2,1,0:T(8,128)(2,1)S(1)} custom-call(s32[4]{0:T(128)S(1)} %pad_add_fusion.place, bf16[2,256,256]{2,1,0:T(8,128)(2,1)S(1)} %add_convert_fusion.q_ref, bf16[4,4,64,256]{3,2,1,0:T(8,128)(2,1)S(1)} %all-to-all-done.2.mine_ref, bf16[4,4,64,256]{3,2,1,0:T(8,128)(2,1)S(1)} %collective-permute-done.3.other_ref), custom_call_target="tpu_custom_call" | custom-call | flops 1073741824 | bytes 4194304 | tf_op jit(solution)/shard_map/attend/pallas_call | solution.py:99
  127.5 3.1 %collective-permute-done.2.q_ref = bf16[2,256,256]{2,1,0:T(8,128)(2,1)S(1)} collective-permute-done((bf16[2,256,256]{2,1,0:T(8,128)(2,1)S(1)}, bf16[2,256,256]{2,1,0:T(8,128)(2,1)S(1)}, u32[]{:S(2)}, u32[]{:S(2)}) %collective-permute-start.2) | collective-permute-done | bytes 262176 | tf_op jit(solution)/shard_map/project_q/ppermute | solution.py:281
  130.6 2.2 %attend.4 = bf16[4,272,256]{2,1,0:T(8,128)(2,1)S(1)} custom-call(s32[4]{0:T(128)S(1)} %pad_add_fusion.place, bf16[2,256,256]{2,1,0:T(8,128)(2,1)S(1)} %collective-permute-done.2.q_ref, bf16[4,4,64,256]{3,2,1,0:T(8,128)(2,1)S(1)} %all-to-all-done.2.mine_ref, ...), custom_call_target="tpu_custom_call", output_to_operand_aliasing={{}: (4, {})} | custom-call | flops 1073741824 | bytes 4194304 | tf_op jit(solution)/shard_map/attend/pallas_call | solution.py:99
  132.8 12.1 %all_to_all.21.parts_ref = bf16[4,272,256]{2,1,0:T(8,128)(2,1)S(1)} all-to-all(bf16[4,272,256]{2,1,0:T(8,128)(2,1)S(1)} %attend.4), channel_id=1, replica_groups=mesh['zh'=4,'zl'=4,'xh'=2,'xl'=2,'yh'=2,'yl'=2,'core'=2] {'xh','yl'}, dimensions={0} | all-to-all | bytes 1114112 | tf_op jit(solution)/shard_map/attend/all_to_all | solution.py:287
  144.9 1.2 attend.5
  (3 shorter events, 0.0 us)
Async XLA Ops:
  6.5 92.0 %all-gather.6.cloned.1.call-start = ((), (), s32[]{:S(2)}) async-start(), calls=%async_computation.4 | async-start | bytes 2785280 | tf_op jit(solution)/shard_map/weights/all_gather | solution.py:255
  9.9 52.4 %all-to-all-start = ((bf16[32,272,128]{2,1,0:T(8,128)(2,1)}), bf16[32,272,128]{2,1,0:T(8,128)(2,1)S(1)}, u32[]{:S(2)}, u32[]{:S(2)}) async-start(bf16[32,272,128]{2,1,0:T(8,128)(2,1)} %bitcast.20), calls=%async_computation | async-start | bytes 4456448 | tf_op jit(solution)/shard_map/spread/all_to_all | solution.py:265
  64.4 38.5 %collective-permute-start = (bf16[2,256,2048]{2,1,0:T(8,128)(2,1)}, bf16[2,256,2048]{2,1,0:T(8,128)(2,1)S(1)}, u32[]{:S(2)}, u32[]{:S(2)}) collective-permute-start(bf16[2,256,2048]{2,1,0:T(8,128)(2,1)} %get-tuple-element.12.mine_ref), channel_id=1, source_target_pairs={{0,1},{1,0},{2,3},{3,2},{4,5},{5,4},{6,7},{7,6},{8,9},{9,8},{10,11... | collective-permute-start | bytes 6291464 | tf_op jit(solution)/shard_map/project_q/ppermute | solution.py:26
  99.4 15.9 %all-to-all-start.2 = ((bf16[4,4,64,256]{3,2,1,0:T(8,128)(2,1)}), bf16[4,4,64,256]{3,2,1,0:T(8,128)(2,1)S(1)}, u32[]{:S(2)}, u32[]{:S(2)}) async-start(bf16[4,4,64,256]{3,2,1,0:T(8,128)(2,1)} %broadcast_in_dim.2), calls=%async_computation.2 | async-start | bytes 1048576 | tf_op jit(solution)/shard_map/gather_kv/all_to_all | solution.py:22
  102.9 1.7 %copy-start = (bf16[5120,256]{1,0:T(8,128)(2,1)S(1)}, bf16[5120,256]{1,0:T(8,128)(2,1)}, u32[]{:S(2)}) copy-start(bf16[5120,256]{1,0:T(8,128)(2,1)} %all-gather.6.cloned.1.call-done) | copy-start | bytes 7864324
  107.5 14.8 %collective-permute-start.1 = (f32[2,256,256]{2,1,0:T(8,128)S(1)}, f32[2,256,256]{2,1,0:T(8,128)S(1)}, u32[]{:S(2)}, u32[]{:S(2)}) collective-permute-start(f32[2,256,256]{2,1,0:T(8,128)S(1)} %project_q.1), channel_id=1, source_target_pairs={{0,16},{16,0},{1,17},{17,1},{2,18},{18,2},{3,19},{19,3},{4,20},{20... | collective-permute-start | bytes 1572872 | tf_op jit(solution)/shard_map/project_q/ppermute | solution.py:280
  115.3 10.1 %collective-permute-start.3 = (bf16[4,4,64,256]{3,2,1,0:T(8,128)(2,1)S(1)}, bf16[4,4,64,256]{3,2,1,0:T(8,128)(2,1)S(1)}, u32[]{:S(2)}, u32[]{:S(2)}) collective-permute-start(bf16[4,4,64,256]{3,2,1,0:T(8,128)(2,1)S(1)} %all-to-all-done.2.mine_ref), channel_id=1, source_target_pairs={{0,1},{1,0},{2,3},{3,2},{4,5},{5,4},{6,7},{7,6},{8,9},{9,8},{10,11... | collective-permute-start | bytes 1572872 | tf_op jit(solution)/shard_map/attend/ppermute | solution.py:26
  122.4 8.3 %collective-permute-start.2 = (bf16[2,256,256]{2,1,0:T(8,128)(2,1)S(1)}, bf16[2,256,256]{2,1,0:T(8,128)(2,1)S(1)}, u32[]{:S(2)}, u32[]{:S(2)}) collective-permute-start(bf16[2,256,256]{2,1,0:T(8,128)(2,1)S(1)} %add_convert_fusion.q_ref), channel_id=1, source_target_pairs={{0,2},{2,0},{1,3},{3,1},{4,6},{6,4},{5,7},{7,5},{8,10},{10,8},{9,1... | collective-permute-start | bytes 786440 | tf_op jit(solution)/shard_map/project_q/ppermute | solution.py:281
Sparse Core Ops, SparseCore 0:
  10.0 82.9 all-gather.5

commit v14 on v13

--- a/solution.py
+++ b/solution.py
@@ -272,11 +272,12 @@
         kv = jnp.concatenate([chunks[0], chunks[1]], axis=1)
 
     with jax.named_scope("gather_kv"):
+        other = swap(whole)
         kv, wq = lax.optimization_barrier((lax.all_gather(kv, "zh"), wq))
-        kv = gather(kv, "zl", 4)
 
     with jax.named_scope("project_q"):
-        q = project_q(place, whole, swap(whole), wq)
+        kv, q = lax.optimization_barrier((kv, project_q(place, whole, other, wq)))
+        kv = lax.all_gather(kv, "zl")
         q = (q + lax.ppermute(q, "xh", [(0, 1), (1, 0)])).astype(BF16)
         pair = lax.ppermute(q, "yl", [(0, 1), (1, 0)])
 

time: 154 us -> 160 us (1.039)
  the two profiles are of different devices: /device:TPU:16 before, /device:TPU:2 now
where the time goes in v14:
time: 160 us
  blocking collectives  92.2 us (58%)
  starting transfers between devices  24.1 us (15%)
  Pallas kernels  14.5 us (9%)
  between operations  13.5 us (8%)
  waiting for transfers between devices  12.7 us (8%)
  local copies, waits for them, and re-layouts  1.75 us (1%)
    all_gather x2, blocking collectives, on_device(): wkv = lax.all_gather(lax.all_gather(wkv, 'zh'), 'zl')  42.1 us
    all_gather x1, blocking collectives, on_device(): kv, wq = lax.optimization_barrier((lax.all_gather(kv, 'zh'), wq))  20 us
    all_to_all x1, blocking collectives, on_device(): return merge(lax.all_to_all(out, ('xh', 'yl'), 0, 0))  15.2 us
    all_gather x1, blocking collectives, on_device(): kv = lax.all_gather(kv, 'zl')  14.8 us
    all_to_all x1, starting transfers between devices, on_device(): lax.all_to_all(parts.reshape(32, rows + 16, HEAD), ('xh',) + COL, 0, 0)  9.67 us
    all_to_all x1, waiting for transfers between devices, on_device(): lax.all_to_all(kv_sum.reshape(8, rows // 4, HEAD), ('xh', 'yl', 'core'),...  7.46 us
    ppermute x1, waiting for transfers between devices, on_device(): pair = lax.ppermute(q, 'yl', [(0, 1), (1, 0)])  5.17 us
    all_to_all x1, starting transfers between devices, on_device(): lax.all_to_all(kv_sum.reshape(8, rows // 4, HEAD), ('xh', 'yl', 'core'),...  4.49 us
  transfers between devices with their start and end apart: 7, of which 2 were waited for; matrix products, arithmetic and copies ran while one was open for 1% of the time, Pallas kernels for 3%

profile of v14, /device:TPU:2, one launch (start us, length us, event | category | flops | bytes accessed | tf_op | source)
XLA Modules:
  0.0 159.7 jit_solution(13887185490440223006)
XLA Ops:
  6.5 0.0 all-gather.7.cloned.1.call-start
  6.5 3.3 %prep.1 = (bf16[2,8,2,272,128]{4,3,2,1,0:T(8,128)(2,1)}, bf16[320,256]{1,0:T(8,128)(2,1)}) custom-call(bf16[256,512]{1,0:T(8,128)(2,1)} %tokens_ref.1, bf16[512]{0:T(512)(128)(2,1)} %gain_ref.1, bf16[256,256]{1,0:T(8,128)(2,1)} %w_ref.1), custom_call_target="tpu_custom_call" | custom-call | tf_op jit(solution)/shard_map/prep/pallas_call | solution.py:162
  9.8 0.0 all-gather.7.cloned.1.call-update
  9.9 9.7 %all-to-all-start = ((bf16[32,272,128]{2,1,0:T(8,128)(2,1)}), bf16[32,272,128]{2,1,0:T(8,128)(2,1)S(1)}, u32[]{:S(2)}, u32[]{:S(2)}) async-start(bf16[32,272,128]{2,1,0:T(8,128)(2,1)} %bitcast.23), calls=%async_computation | async-start | bytes 4456448 | tf_op jit(solution)/shard_map/spread/all_to_all | solution.py:265
  19.6 0.8 dynamic-slice_select_fusion
  20.4 24.2 %all-gather = bf16[512,128]{1,0:T(8,128)(2,1)S(1)} all-gather(bf16[128,128]{1,0:T(8,128)(2,1)S(1)} %dynamic-slice_select_fusion), channel_id=2, replica_groups=mesh['zh'=4,'zl'=4,'xh'=2,'xl'=2,'yh'=2,'yl'=2,'core'=2] {'zh'}, dimensions={0}, use_global_device_ids=true | all-gather | bytes 163840 | tf_op jit(solution)/shard_map/weights/all_gather | solution.py:262
  44.6 17.9 %all-gather.1 = bf16[16,128,128]{2,1,0:T(8,128)(2,1)S(1)} all-gather(bf16[4,128,128]{2,1,0:T(8,128)(2,1)S(1)} %bitcast.26), channel_id=3, replica_groups=mesh['zh'=4,'zl'=4,'xh'=2,'xl'=2,'yh'=2,'yl'=2,'core'=2] {'zl'}, dimensions={0}, use_global_device_ids=true | all-gather | bytes 655360 | tf_op jit(solution)/shard_map/weights/all_gather | solution.py:262
  62.5 0.0 all-to-all-done
  62.5 2.8 %project_kv.1 = (bf16[2,256,2048]{2,1,0:T(8,128)(2,1)}, f32[2,256,128]{2,1,0:T(8,128)}) custom-call(bf16[2,16,272,128]{3,2,1,0:T(8,128)(2,1)S(1)} %bitcast.17, bf16[4,4,128,128]{3,2,1,0:T(8,128)(2,1)S(1)} %bitcast.19), custom_call_target="tpu_custom_call" | custom-call | flops 268435456 | bytes 5242880 | tf_op jit(solution)/shard_map/project_kv/pallas_call | solution.py:203
  65.3 1.9 %collective-permute-start = (bf16[2,256,2048]{2,1,0:T(8,128)(2,1)}, bf16[2,256,2048]{2,1,0:T(8,128)(2,1)S(1)}, u32[]{:S(2)}, u32[]{:S(2)}) collective-permute-start(bf16[2,256,2048]{2,1,0:T(8,128)(2,1)} %get-tuple-element.17.mine_ref), channel_id=1, source_target_pairs={{0,1},{1,0},{2,3},{3,2},{4,5},{5,4},{6,7},{7,6},{8,9},{9,8},{10,11... | collective-permute-start | bytes 6291464 | tf_op jit(solution)/shard_map/gather_kv/ppermute | solution.py:26
  67.2 4.5 %all-to-all-start.1 = ((f32[8,64,128]{2,1,0:T(8,128)}), f32[8,64,128]{2,1,0:T(8,128)S(1)}, u32[]{:S(2)}, u32[]{:S(2)}) async-start(f32[8,64,128]{2,1,0:T(8,128)} %bitcast.8), calls=%async_computation.1 | async-start | bytes 524288 | tf_op jit(solution)/shard_map/project_kv/all_to_all | solution.py:270
  71.7 0.1 pad_add_fusion.place
  71.8 7.5 %all-to-all-done.1 = f32[8,64,128]{2,1,0:T(8,128)S(1)} async-done(((f32[8,64,128]{2,1,0:T(8,128)}), f32[8,64,128]{2,1,0:T(8,128)S(1)}, u32[]{:S(2)}, u32[]{:S(2)}) %all-to-all-start.1) | async-done | bytes 262176 | tf_op jit(solution)/shard_map/project_kv/all_to_all | solution.py:270
  79.3 20.0 %all-gather.2 = bf16[256,256]{1,0:T(8,128)(2,1)S(1)} all-gather(bf16[64,256]{1,0:T(8,128)(2,1)S(1)} %pad_maximum_fusion), channel_id=4, replica_groups=mesh['zh'=4,'zl'=4,'xh'=2,'xl'=2,'yh'=2,'yl'=2,'core'=2] {'zh'}, dimensions={0}, use_global_device_ids=true | all-gather | bytes 163840 | tf_op jit(solution)/shard_map/gather_kv/all_gather | solution.py:276
  99.3 0.0 all-gather.7.cloned.1.call-done
  99.3 0.0 collective-permute-done.other_ref
  99.3 0.0 copy-start
  99.3 1.7 %copy-done = bf16[5120,256]{1,0:T(8,128)(2,1)S(1)} copy-done((bf16[5120,256]{1,0:T(8,128)(2,1)S(1)}, bf16[5120,256]{1,0:T(8,128)(2,1)}, u32[]{:S(2)}) %copy-start) | copy-done | bytes 2621464
  101.1 2.8 %project_q.1 = f32[2,256,256]{2,1,0:T(8,128)S(1)} custom-call(s32[4]{0:T(128)S(1)} %pad_add_fusion.place, bf16[2,256,2048]{2,1,0:T(8,128)(2,1)} %get-tuple-element.17.mine_ref, bf16[2,256,2048]{2,1,0:T(8,128)(2,1)S(1)} %collective-permute-done.other_ref, bf16[16,320,256]{2,1,0:T(8,128)(2,1)S(1)} %bitcast.18), custom_call_target="tpu_custom_call" | custom-call | flops 1073741824 | bytes 6291456 | tf_op jit(solution)/shard_map/project_q/pallas_call | solution.py:234
  103.9 2.9 %collective-permute-start.1 = (f32[2,256,256]{2,1,0:T(8,128)S(1)}, f32[2,256,256]{2,1,0:T(8,128)S(1)}, u32[]{:S(2)}, u32[]{:S(2)}) collective-permute-start(f32[2,256,256]{2,1,0:T(8,128)S(1)} %project_q.1), channel_id=1, source_target_pairs={{0,16},{16,0},{1,17},{17,1},{2,18},{18,2},{3,19},{19,3},{4,20},{20... | collective-permute-start | bytes 1572872 | tf_op jit(solution)/shard_map/project_q/ppermute | solution.py:281
  106.8 14.8 %all-gather.4 = bf16[16,64,256]{2,1,0:T(8,128)(2,1)S(1)} all-gather(bf16[4,64,256]{2,1,0:T(8,128)(2,1)S(1)} %bitcast.25), channel_id=6, replica_groups=mesh['zh'=4,'zl'=4,'xh'=2,'xl'=2,'yh'=2,'yl'=2,'core'=2] {'zl'}, dimensions={0}, use_global_device_ids=true | all-gather | bytes 655360 | tf_op jit(solution)/shard_map/project_q/all_gather | solution.py:280
  121.6 1.9 %collective-permute-start.3 = (bf16[4,4,64,256]{3,2,1,0:T(8,128)(2,1)S(1)}, bf16[4,4,64,256]{3,2,1,0:T(8,128)(2,1)S(1)}, u32[]{:S(2)}, u32[]{:S(2)}) collective-permute-start(bf16[4,4,64,256]{3,2,1,0:T(8,128)(2,1)S(1)} %bitcast.20), channel_id=1, source_target_pairs={{0,1},{1,0},{2,3},{3,2},{4,5},{5,4},{6,7},{7,6},{8,9},{9,8},{10,11... | collective-permute-start | bytes 1572872 | tf_op jit(solution)/shard_map/attend/ppermute | solution.py:26
  123.5 0.0 collective-permute-done.1
  123.5 0.1 add_convert_fusion.q_ref
  123.6 3.3 %collective-permute-start.2 = (bf16[2,256,256]{2,1,0:T(8,128)(2,1)S(1)}, bf16[2,256,256]{2,1,0:T(8,128)(2,1)S(1)}, u32[]{:S(2)}, u32[]{:S(2)}) collective-permute-start(bf16[2,256,256]{2,1,0:T(8,128)(2,1)S(1)} %add_convert_fusion.q_ref), channel_id=1, source_target_pairs={{0,2},{2,0},{1,3},{3,1},{4,6},{6,4},{5,7},{7,5},{8,10},{10,8},{9,1... | collective-permute-start | bytes 786440 | tf_op jit(solution)/shard_map/project_q/ppermute | solution.py:282
  126.9 0.0 collective-permute-done.3.other_ref
  126.9 2.1 %attend.3.refs_0_ = bf16[4,272,256]{2,1,0:T(8,128)(2,1)S(1)} custom-call(s32[4]{0:T(128)S(1)} %pad_add_fusion.place, bf16[2,256,256]{2,1,0:T(8,128)(2,1)S(1)} %add_convert_fusion.q_ref, bf16[4,4,64,256]{3,2,1,0:T(8,128)(2,1)S(1)} %bitcast.21, bf16[4,4,64,256]{3,2,1,0:T(8,128)(2,1)S(1)} %collective-permute-done.3.other_ref), custom_call_target="tpu_custom_call" | custom-call | flops 1073741824 | bytes 4194304 | tf_op jit(solution)/shard_map/attend/pallas_call | solution.py:99
  129.0 5.2 %collective-permute-done.2.q_ref = bf16[2,256,256]{2,1,0:T(8,128)(2,1)S(1)} collective-permute-done((bf16[2,256,256]{2,1,0:T(8,128)(2,1)S(1)}, bf16[2,256,256]{2,1,0:T(8,128)(2,1)S(1)}, u32[]{:S(2)}, u32[]{:S(2)}) %collective-permute-start.2) | collective-permute-done | bytes 262176 | tf_op jit(solution)/shard_map/project_q/ppermute | solution.py:282
  134.2 2.2 %attend.4 = bf16[4,272,256]{2,1,0:T(8,128)(2,1)S(1)} custom-call(s32[4]{0:T(128)S(1)} %pad_add_fusion.place, bf16[2,256,256]{2,1,0:T(8,128)(2,1)S(1)} %collective-permute-done.2.q_ref, bf16[4,4,64,256]{3,2,1,0:T(8,128)(2,1)S(1)} %bitcast.22, bf16[4,4,64,256]{3,2,1,0:T(8,128)(2,1)S(1)} %collective-permute-done.3.other_ref, ...), custom_call_target="tpu_custom_call", output_to_operand_aliasing={{}: (4, {})} | custom-call | flops 1073741824 | bytes 4194304 | tf_op jit(solution)/shard_map/attend/pallas_call | solution.py:99
  136.4 15.2 %all_to_all.15.parts_ref = bf16[4,272,256]{2,1,0:T(8,128)(2,1)S(1)} all-to-all(bf16[4,272,256]{2,1,0:T(8,128)(2,1)S(1)} %attend.4), channel_id=1, replica_groups=mesh['zh'=4,'zl'=4,'xh'=2,'xl'=2,'yh'=2,'yl'=2,'core'=2] {'xh','yl'}, dimensions={0} | all-to-all | bytes 1114112 | tf_op jit(solution)/shard_map/attend/all_to_all | solution.py:288
  151.6 1.2 attend.5
  (3 shorter events, 0.0 us)
Async XLA Ops:
  6.5 92.8 %all-gather.7.cloned.1.call-start = ((), (), s32[]{:S(2)}) async-start(), calls=%async_computation.3 | async-start | bytes 2785280 | tf_op jit(solution)/shard_map/weights/all_gather | solution.py:255
  9.9 52.6 %all-to-all-start = ((bf16[32,272,128]{2,1,0:T(8,128)(2,1)}), bf16[32,272,128]{2,1,0:T(8,128)(2,1)S(1)}, u32[]{:S(2)}, u32[]{:S(2)}) async-start(bf16[32,272,128]{2,1,0:T(8,128)(2,1)} %bitcast.23), calls=%async_computation | async-start | bytes 4456448 | tf_op jit(solution)/shard_map/spread/all_to_all | solution.py:265
  65.3 34.0 %collective-permute-start = (bf16[2,256,2048]{2,1,0:T(8,128)(2,1)}, bf16[2,256,2048]{2,1,0:T(8,128)(2,1)S(1)}, u32[]{:S(2)}, u32[]{:S(2)}) collective-permute-start(bf16[2,256,2048]{2,1,0:T(8,128)(2,1)} %get-tuple-element.17.mine_ref), channel_id=1, source_target_pairs={{0,1},{1,0},{2,3},{3,2},{4,5},{5,4},{6,7},{7,6},{8,9},{9,8},{10,11... | collective-permute-start | bytes 6291464 | tf_op jit(solution)/shard_map/gather_kv/ppermute | solution.py:26
  67.2 12.0 %all-to-all-start.1 = ((f32[8,64,128]{2,1,0:T(8,128)}), f32[8,64,128]{2,1,0:T(8,128)S(1)}, u32[]{:S(2)}, u32[]{:S(2)}) async-start(f32[8,64,128]{2,1,0:T(8,128)} %bitcast.8), calls=%async_computation.1 | async-start | bytes 524288 | tf_op jit(solution)/shard_map/project_kv/all_to_all | solution.py:270
  99.3 1.7 %copy-start = (bf16[5120,256]{1,0:T(8,128)(2,1)S(1)}, bf16[5120,256]{1,0:T(8,128)(2,1)}, u32[]{:S(2)}) copy-start(bf16[5120,256]{1,0:T(8,128)(2,1)} %all-gather.7.cloned.1.call-done) | copy-start | bytes 7864324
  103.9 19.6 %collective-permute-start.1 = (f32[2,256,256]{2,1,0:T(8,128)S(1)}, f32[2,256,256]{2,1,0:T(8,128)S(1)}, u32[]{:S(2)}, u32[]{:S(2)}) collective-permute-start(f32[2,256,256]{2,1,0:T(8,128)S(1)} %project_q.1), channel_id=1, source_target_pairs={{0,16},{16,0},{1,17},{17,1},{2,18},{18,2},{3,19},{19,3},{4,20},{20... | collective-permute-start | bytes 1572872 | tf_op jit(solution)/shard_map/project_q/ppermute | solution.py:281
  121.6 5.3 %collective-permute-start.3 = (bf16[4,4,64,256]{3,2,1,0:T(8,128)(2,1)S(1)}, bf16[4,4,64,256]{3,2,1,0:T(8,128)(2,1)S(1)}, u32[]{:S(2)}, u32[]{:S(2)}) collective-permute-start(bf16[4,4,64,256]{3,2,1,0:T(8,128)(2,1)S(1)} %bitcast.20), channel_id=1, source_target_pairs={{0,1},{1,0},{2,3},{3,2},{4,5},{5,4},{6,7},{7,6},{8,9},{9,8},{10,11... | collective-permute-start | bytes 1572872 | tf_op jit(solution)/shard_map/attend/ppermute | solution.py:26
  123.6 10.6 %collective-permute-start.2 = (bf16[2,256,256]{2,1,0:T(8,128)(2,1)S(1)}, bf16[2,256,256]{2,1,0:T(8,128)(2,1)S(1)}, u32[]{:S(2)}, u32[]{:S(2)}) collective-permute-start(bf16[2,256,256]{2,1,0:T(8,128)(2,1)S(1)} %add_convert_fusion.q_ref), channel_id=1, source_target_pairs={{0,2},{2,0},{1,3},{3,1},{4,6},{6,4},{5,7},{7,5},{8,10},{10,8},{9,1... | collective-permute-start | bytes 786440 | tf_op jit(solution)/shard_map/project_q/ppermute | solution.py:282
Sparse Core Ops, SparseCore 0:
  10.0 82.2 all-gather.6

commit v15 on v8

--- a/solution.py
+++ b/solution.py
@@ -40,9 +40,6 @@
     z, xh, yl, core = place[0], place[1], place[2], place[3]
     rows = q_ref.shape[1]
     scale = HEAD**-0.5 * math.log2(math.e)
-    m_ref[...] = jnp.full(m_ref.shape, -1e30, F32)
-    l_ref[...] = jnp.zeros(l_ref.shape, F32)
-    acc_ref[...] = jnp.zeros(acc_ref.shape, F32)
     chunk = mine_ref.shape[2]
     half = 4 * chunk
 
@@ -63,10 +60,13 @@
             s = lax.dot_general(q, kv[:, :HEAD], (((1,), (1,)), ((), ())), preferred_element_type=F32)
             if masked:
                 s = jnp.where(seen, s, -1e30)
-            m_old = m_ref[head]
-            m_new = jnp.maximum(m_old, jnp.max(s, axis=1, keepdims=True))
-            alpha = jnp.exp2((m_old - m_new) * scale)
-            total = l_ref[head] * alpha
+            m_new = jnp.broadcast_to(jnp.max(s, axis=1, keepdims=True), (2 * rows, HEAD))
+            total = jnp.zeros((2 * rows, HEAD), F32)
+            if not masked:
+                m_old = m_ref[head]
+                m_new = jnp.maximum(m_old, m_new)
+                alpha = jnp.exp2((m_old - m_new) * scale)
+                total = l_ref[head] * alpha
             weights = []
             for j in range(0, s.shape[1], HEAD):
                 w = jnp.exp2((s[:, j : j + HEAD] - m_new) * scale)
@@ -75,15 +75,17 @@
             p = jnp.concatenate(weights, axis=1)
             l_ref[head] = total
             m_ref[head] = m_new
-            acc_ref[head] = acc_ref[head] * alpha + jnp.dot(p, kv[:, HEAD:], preferred_element_type=F32)
+            mixed = jnp.dot(p, kv[:, HEAD:], preferred_element_type=F32)
+            acc_ref[head] = mixed if masked else acc_ref[head] * alpha + mixed
 
     last = lax.div(z, 4)
+
+    block(last, True)
 
     @pl.loop(0, last)
     def _(group):
         block(group, False)
 
-    block(last, True)
     lane = lax.broadcasted_iota(jnp.int32, (2 * rows, HEAD), 1)
     to = yl if side == 0 else 1 - yl
     stats = jnp.zeros((2 * rows, HEAD), F32)

time: 153 us -> 153 us (level)
  transfers between devices with their start and end apart: 7 -> 7, of which waited for: 3 -> 3; matrix products, arithmetic and copies ran while one was open for 1% -> 1% of each run, Pallas kernels for 4% -> 5%
where the time goes in v15:
time: 153 us
  blocking collectives  86.3 us (56%)
  starting transfers between devices  24.1 us (16%)
  between operations  13.5 us (9%)
  Pallas kernels  13.3 us (9%)
  waiting for transfers between devices  11.8 us (8%)
  local copies, waits for them, and re-layouts  2.6 us (2%)
    all_gather x2, blocking collectives, on_device(): wkv = lax.all_gather(lax.all_gather(wkv, 'zh'), 'zl')  42.2 us
    all_gather x1, blocking collectives, on_device(): kv, wq = lax.optimization_barrier((lax.all_gather(kv, 'zh'), wq))  19.9 us
    all_to_all x1, blocking collectives, on_device(): lax.all_to_all(kv_sum.reshape(8, rows // 4, HEAD), ('xh', 'yl', 'core'),...  12.2 us
    all_to_all x1, blocking collectives, on_device(): return merge(lax.all_to_all(out, ('xh', 'yl'), 0, 0))  12 us
    all_to_all x1, starting transfers between devices, on_device(): lax.all_to_all(parts.reshape(32, rows + 16, HEAD), ('xh',) + COL, 0, 0)  9.45 us
    ppermute x1, waiting for transfers between devices, on_device(): q = (q + lax.ppermute(q, 'xh', [(0, 1), (1, 0)])).astype(BF16)  5.09 us
    ppermute x1, starting transfers between devices, on_device(): q = (q + lax.ppermute(q, 'xh', [(0, 1), (1, 0)])).astype(BF16)  4.36 us
    pallas_call x2, Pallas kernels, attend(): pl.pallas_call(functools.partial(attend_kernel, side), out_shape=jax.Shap...  3.89 us
  transfers between devices with their start and end apart: 7, of which 3 were waited for; matrix products, arithmetic and copies ran while one was open for 1% of the time, Pallas kernels for 5%

profile of v15, /device:TPU:16, one launch (start us, length us, event | category | flops | bytes accessed | tf_op | source)
XLA Modules:
  0.0 152.6 jit_solution(13993056352239110230)
XLA Ops:
  6.5 0.0 all-gather.6.cloned.1.call-start
  6.5 3.3 %prep.1 = (bf16[2,8,2,272,128]{4,3,2,1,0:T(8,128)(2,1)}, bf16[320,256]{1,0:T(8,128)(2,1)}) custom-call(bf16[256,512]{1,0:T(8,128)(2,1)} %tokens_ref.1, bf16[512]{0:T(512)(128)(2,1)} %gain_ref.1, bf16[256,256]{1,0:T(8,128)(2,1)} %w_ref.1), custom_call_target="tpu_custom_call" | custom-call | tf_op jit(solution)/shard_map/prep/pallas_call | solution.py:171
  9.8 0.0 all-gather.6.cloned.1.call-update
  9.9 9.4 %all-to-all-start = ((bf16[32,272,128]{2,1,0:T(8,128)(2,1)}), bf16[32,272,128]{2,1,0:T(8,128)(2,1)S(1)}, u32[]{:S(2)}, u32[]{:S(2)}) async-start(bf16[32,272,128]{2,1,0:T(8,128)(2,1)} %bitcast.20), calls=%async_computation | async-start | bytes 4456448 | tf_op jit(solution)/shard_map/spread/all_to_all | solution.py:274
  19.3 0.8 dynamic-slice_select_fusion
  20.1 24.1 %all-gather = bf16[512,128]{1,0:T(8,128)(2,1)S(1)} all-gather(bf16[128,128]{1,0:T(8,128)(2,1)S(1)} %dynamic-slice_select_fusion), channel_id=2, replica_groups=mesh['zh'=4,'zl'=4,'xh'=2,'xl'=2,'yh'=2,'yl'=2,'core'=2] {'zh'}, dimensions={0}, use_global_device_ids=true | all-gather | bytes 163840 | tf_op jit(solution)/shard_map/weights/all_gather | solution.py:271
  44.2 18.0 %all-gather.1 = bf16[16,128,128]{2,1,0:T(8,128)(2,1)S(1)} all-gather(bf16[4,128,128]{2,1,0:T(8,128)(2,1)S(1)} %bitcast.23), channel_id=3, replica_groups=mesh['zh'=4,'zl'=4,'xh'=2,'xl'=2,'yh'=2,'yl'=2,'core'=2] {'zl'}, dimensions={0}, use_global_device_ids=true | all-gather | bytes 655360 | tf_op jit(solution)/shard_map/weights/all_gather | solution.py:271
  62.3 0.0 all-to-all-done
  62.3 2.1 %project_kv.1 = (bf16[2,256,2048]{2,1,0:T(8,128)(2,1)}, f32[2,256,128]{2,1,0:T(8,128)S(1)}) custom-call(bf16[2,16,272,128]{3,2,1,0:T(8,128)(2,1)S(1)} %bitcast.16, bf16[4,4,128,128]{3,2,1,0:T(8,128)(2,1)S(1)} %bitcast.18), custom_call_target="tpu_custom_call" | custom-call | flops 268435456 | bytes 5242880 | tf_op jit(solution)/shard_map/project_kv/pallas_call | solution.py:212
  64.4 1.9 %collective-permute-start = (bf16[2,256,2048]{2,1,0:T(8,128)(2,1)}, bf16[2,256,2048]{2,1,0:T(8,128)(2,1)S(1)}, u32[]{:S(2)}, u32[]{:S(2)}) collective-permute-start(bf16[2,256,2048]{2,1,0:T(8,128)(2,1)} %get-tuple-element.12.mine_ref), channel_id=1, source_target_pairs={{0,1},{1,0},{2,3},{3,2},{4,5},{5,4},{6,7},{7,6},{8,9},{9,8},{10,11... | collective-permute-start | bytes 6291464 | tf_op jit(solution)/shard_map/project_q/ppermute | solution.py:26
  66.3 12.2 %all_to_all.20 = f32[8,64,128]{2,1,0:T(8,128)S(1)} all-to-all(f32[8,64,128]{2,1,0:T(8,128)S(1)} %bitcast.19), channel_id=1, replica_groups=mesh['zh'=4,'zl'=4,'xh'=2,'xl'=2,'yh'=2,'yl'=2,'core'=2] {'xh','yl','core'}, dimensions={0} | all-to-all | bytes 524288 | tf_op jit(solution)/shard_map/project_kv/all_to_all | solution.py:279
  78.6 19.9 %all-gather.2 = bf16[256,256]{1,0:T(8,128)(2,1)S(1)} all-gather(bf16[64,256]{1,0:T(8,128)(2,1)S(1)} %pad_maximum_fusion), channel_id=4, replica_groups=mesh['zh'=4,'zl'=4,'xh'=2,'xl'=2,'yh'=2,'yl'=2,'core'=2] {'zh'}, dimensions={0}, use_global_device_ids=true | all-gather | bytes 163840 | tf_op jit(solution)/shard_map/gather_kv/all_gather | solution.py:284
  98.5 0.0 all-gather.6.cloned.1.call-done
  98.5 0.9 broadcast_in_dim.2
  99.4 3.5 %all-to-all-start.2 = ((bf16[4,4,64,256]{3,2,1,0:T(8,128)(2,1)}), bf16[4,4,64,256]{3,2,1,0:T(8,128)(2,1)S(1)}, u32[]{:S(2)}, u32[]{:S(2)}) async-start(bf16[4,4,64,256]{3,2,1,0:T(8,128)(2,1)} %broadcast_in_dim.2), calls=%async_computation.2 | async-start | bytes 1048576 | tf_op jit(solution)/shard_map/gather_kv/all_to_all | solution.py:22
  102.8 0.1 pad_add_fusion.place
  102.9 0.0 collective-permute-done.other_ref
  102.9 0.0 copy-start
  102.9 1.7 %copy-done = bf16[5120,256]{1,0:T(8,128)(2,1)S(1)} copy-done((bf16[5120,256]{1,0:T(8,128)(2,1)S(1)}, bf16[5120,256]{1,0:T(8,128)(2,1)}, u32[]{:S(2)}) %copy-start) | copy-done | bytes 2621464
  104.7 2.9 %project_q.1 = f32[2,256,256]{2,1,0:T(8,128)S(1)} custom-call(s32[4]{0:T(128)S(1)} %pad_add_fusion.place, bf16[2,256,2048]{2,1,0:T(8,128)(2,1)} %get-tuple-element.12.mine_ref, bf16[2,256,2048]{2,1,0:T(8,128)(2,1)S(1)} %collective-permute-done.other_ref, bf16[16,320,256]{2,1,0:T(8,128)(2,1)S(1)} %bitcast.17), custom_call_target="tpu_custom_call" | custom-call | flops 1073741824 | bytes 6291456 | tf_op jit(solution)/shard_map/project_q/pallas_call | solution.py:243
  107.5 4.4 %collective-permute-start.1 = (f32[2,256,256]{2,1,0:T(8,128)S(1)}, f32[2,256,256]{2,1,0:T(8,128)S(1)}, u32[]{:S(2)}, u32[]{:S(2)}) collective-permute-start(f32[2,256,256]{2,1,0:T(8,128)S(1)} %project_q.1), channel_id=1, source_target_pairs={{0,16},{16,0},{1,17},{17,1},{2,18},{18,2},{3,19},{19,3},{4,20},{20... | collective-permute-start | bytes 1572872 | tf_op jit(solution)/shard_map/project_q/ppermute | solution.py:289
  111.9 3.4 %all-to-all-done.2.mine_ref = bf16[4,4,64,256]{3,2,1,0:T(8,128)(2,1)S(1)} async-done(((bf16[4,4,64,256]{3,2,1,0:T(8,128)(2,1)}), bf16[4,4,64,256]{3,2,1,0:T(8,128)(2,1)S(1)}, u32[]{:S(2)}, u32[]{:S(2)}) %all-to-all-start.2) | async-done | bytes 524320 | tf_op jit(solution)/shard_map/gather_kv/all_to_all | solution.py:22
  115.3 1.9 %collective-permute-start.3 = (bf16[4,4,64,256]{3,2,1,0:T(8,128)(2,1)S(1)}, bf16[4,4,64,256]{3,2,1,0:T(8,128)(2,1)S(1)}, u32[]{:S(2)}, u32[]{:S(2)}) collective-permute-start(bf16[4,4,64,256]{3,2,1,0:T(8,128)(2,1)S(1)} %all-to-all-done.2.mine_ref), channel_id=1, source_target_pairs={{0,1},{1,0},{2,3},{3,2},{4,5},{5,4},{6,7},{7,6},{8,9},{9,8},{10,11... | collective-permute-start | bytes 1572872 | tf_op jit(solution)/shard_map/attend/ppermute | solution.py:26
  117.2 5.1 %collective-permute-done.1 = f32[2,256,256]{2,1,0:T(8,128)S(1)} collective-permute-done((f32[2,256,256]{2,1,0:T(8,128)S(1)}, f32[2,256,256]{2,1,0:T(8,128)S(1)}, u32[]{:S(2)}, u32[]{:S(2)}) %collective-permute-start.1) | collective-permute-done | bytes 524320 | tf_op jit(solution)/shard_map/project_q/ppermute | solution.py:289
  122.3 0.1 add_convert_fusion.q_ref
  122.4 3.0 %collective-permute-start.2 = (bf16[2,256,256]{2,1,0:T(8,128)(2,1)S(1)}, bf16[2,256,256]{2,1,0:T(8,128)(2,1)S(1)}, u32[]{:S(2)}, u32[]{:S(2)}) collective-permute-start(bf16[2,256,256]{2,1,0:T(8,128)(2,1)S(1)} %add_convert_fusion.q_ref), channel_id=1, source_target_pairs={{0,2},{2,0},{1,3},{3,1},{4,6},{6,4},{5,7},{7,5},{8,10},{10,8},{9,1... | collective-permute-start | bytes 786440 | tf_op jit(solution)/shard_map/project_q/ppermute | solution.py:290
  125.4 0.0 collective-permute-done.3.other_ref
  125.4 1.9 %attend.3.refs_0_ = bf16[4,272,256]{2,1,0:T(8,128)(2,1)S(1)} custom-call(s32[4]{0:T(128)S(1)} %pad_add_fusion.place, bf16[2,256,256]{2,1,0:T(8,128)(2,1)S(1)} %add_convert_fusion.q_ref, bf16[4,4,64,256]{3,2,1,0:T(8,128)(2,1)S(1)} %all-to-all-done.2.mine_ref, bf16[4,4,64,256]{3,2,1,0:T(8,128)(2,1)S(1)} %collective-permute-done.3.other_ref), custom_call_target="tpu_custom_call" | custom-call | flops 1073741824 | bytes 4194304 | tf_op jit(solution)/shard_map/attend/pallas_call | solution.py:107
  127.3 3.3 %collective-permute-done.2.q_ref = bf16[2,256,256]{2,1,0:T(8,128)(2,1)S(1)} collective-permute-done((bf16[2,256,256]{2,1,0:T(8,128)(2,1)S(1)}, bf16[2,256,256]{2,1,0:T(8,128)(2,1)S(1)}, u32[]{:S(2)}, u32[]{:S(2)}) %collective-permute-start.2) | collective-permute-done | bytes 262176 | tf_op jit(solution)/shard_map/project_q/ppermute | solution.py:290
  130.6 1.9 %attend.4 = bf16[4,272,256]{2,1,0:T(8,128)(2,1)S(1)} custom-call(s32[4]{0:T(128)S(1)} %pad_add_fusion.place, bf16[2,256,256]{2,1,0:T(8,128)(2,1)S(1)} %collective-permute-done.2.q_ref, bf16[4,4,64,256]{3,2,1,0:T(8,128)(2,1)S(1)} %all-to-all-done.2.mine_ref, ...), custom_call_target="tpu_custom_call", output_to_operand_aliasing={{}: (4, {})} | custom-call | flops 1073741824 | bytes 4194304 | tf_op jit(solution)/shard_map/attend/pallas_call | solution.py:107
  132.6 12.0 %all_to_all.21.parts_ref = bf16[4,272,256]{2,1,0:T(8,128)(2,1)S(1)} all-to-all(bf16[4,272,256]{2,1,0:T(8,128)(2,1)S(1)} %attend.4), channel_id=1, replica_groups=mesh['zh'=4,'zl'=4,'xh'=2,'xl'=2,'yh'=2,'yl'=2,'core'=2] {'xh','yl'}, dimensions={0} | all-to-all | bytes 1114112 | tf_op jit(solution)/shard_map/attend/all_to_all | solution.py:296
  144.6 1.2 attend.5
  (3 shorter events, 0.0 us)
Async XLA Ops:
  6.5 92.0 %all-gather.6.cloned.1.call-start = ((), (), s32[]{:S(2)}) async-start(), calls=%async_computation.4 | async-start | bytes 2785280 | tf_op jit(solution)/shard_map/weights/all_gather | solution.py:264
  9.9 52.4 %all-to-all-start = ((bf16[32,272,128]{2,1,0:T(8,128)(2,1)}), bf16[32,272,128]{2,1,0:T(8,128)(2,1)S(1)}, u32[]{:S(2)}, u32[]{:S(2)}) async-start(bf16[32,272,128]{2,1,0:T(8,128)(2,1)} %bitcast.20), calls=%async_computation | async-start | bytes 4456448 | tf_op jit(solution)/shard_map/spread/all_to_all | solution.py:274
  64.4 38.5 %collective-permute-start = (bf16[2,256,2048]{2,1,0:T(8,128)(2,1)}, bf16[2,256,2048]{2,1,0:T(8,128)(2,1)S(1)}, u32[]{:S(2)}, u32[]{:S(2)}) collective-permute-start(bf16[2,256,2048]{2,1,0:T(8,128)(2,1)} %get-tuple-element.12.mine_ref), channel_id=1, source_target_pairs={{0,1},{1,0},{2,3},{3,2},{4,5},{5,4},{6,7},{7,6},{8,9},{9,8},{10,11... | collective-permute-start | bytes 6291464 | tf_op jit(solution)/shard_map/project_q/ppermute | solution.py:26
  99.4 15.9 %all-to-all-start.2 = ((bf16[4,4,64,256]{3,2,1,0:T(8,128)(2,1)}), bf16[4,4,64,256]{3,2,1,0:T(8,128)(2,1)S(1)}, u32[]{:S(2)}, u32[]{:S(2)}) async-start(bf16[4,4,64,256]{3,2,1,0:T(8,128)(2,1)} %broadcast_in_dim.2), calls=%async_computation.2 | async-start | bytes 1048576 | tf_op jit(solution)/shard_map/gather_kv/all_to_all | solution.py:22
  102.9 1.7 %copy-start = (bf16[5120,256]{1,0:T(8,128)(2,1)S(1)}, bf16[5120,256]{1,0:T(8,128)(2,1)}, u32[]{:S(2)}) copy-start(bf16[5120,256]{1,0:T(8,128)(2,1)} %all-gather.6.cloned.1.call-done) | copy-start | bytes 7864324
  107.5 14.8 %collective-permute-start.1 = (f32[2,256,256]{2,1,0:T(8,128)S(1)}, f32[2,256,256]{2,1,0:T(8,128)S(1)}, u32[]{:S(2)}, u32[]{:S(2)}) collective-permute-start(f32[2,256,256]{2,1,0:T(8,128)S(1)} %project_q.1), channel_id=1, source_target_pairs={{0,16},{16,0},{1,17},{17,1},{2,18},{18,2},{3,19},{19,3},{4,20},{20... | collective-permute-start | bytes 1572872 | tf_op jit(solution)/shard_map/project_q/ppermute | solution.py:289
  115.3 10.1 %collective-permute-start.3 = (bf16[4,4,64,256]{3,2,1,0:T(8,128)(2,1)S(1)}, bf16[4,4,64,256]{3,2,1,0:T(8,128)(2,1)S(1)}, u32[]{:S(2)}, u32[]{:S(2)}) collective-permute-start(bf16[4,4,64,256]{3,2,1,0:T(8,128)(2,1)S(1)} %all-to-all-done.2.mine_ref), channel_id=1, source_target_pairs={{0,1},{1,0},{2,3},{3,2},{4,5},{5,4},{6,7},{7,6},{8,9},{9,8},{10,11... | collective-permute-start | bytes 1572872 | tf_op jit(solution)/shard_map/attend/ppermute | solution.py:26
  122.4 8.3 %collective-permute-start.2 = (bf16[2,256,256]{2,1,0:T(8,128)(2,1)S(1)}, bf16[2,256,256]{2,1,0:T(8,128)(2,1)S(1)}, u32[]{:S(2)}, u32[]{:S(2)}) collective-permute-start(bf16[2,256,256]{2,1,0:T(8,128)(2,1)S(1)} %add_convert_fusion.q_ref), channel_id=1, source_target_pairs={{0,2},{2,0},{1,3},{3,1},{4,6},{6,4},{5,7},{7,5},{8,10},{10,8},{9,1... | collective-permute-start | bytes 786440 | tf_op jit(solution)/shard_map/project_q/ppermute | solution.py:290
Sparse Core Ops, SparseCore 0:
  10.0 82.9 all-gather.5

commit v16 on v8

--- a/solution.py
+++ b/solution.py
@@ -279,11 +279,13 @@
         kv = jnp.concatenate([chunks[0], chunks[1]], axis=1)
 
     with jax.named_scope("gather_kv"):
+        kv, whole = lax.optimization_barrier((kv, whole))
+        other = swap(whole)
         kv, wq = lax.optimization_barrier((lax.all_gather(kv, "zh"), wq))
         kv = gather(kv, "zl", 4)
 
     with jax.named_scope("project_q"):
-        q = project_q(place, whole, swap(whole), wq)
+        q = project_q(place, whole, other, wq)
         q = (q + lax.ppermute(q, "xh", [(0, 1), (1, 0)])).astype(BF16)
         pair = lax.ppermute(q, "yl", [(0, 1), (1, 0)])
 

time: 153 us -> 155 us (1.013)
    all_to_all x1, waiting for transfers between devices: 3.39 us -> 5.04 us  [gather(): return lax.all_to_all(jnp.broadcast_to(x[None], (n, *x.shape)), axes, 0, 0)]
    unnamed x2 -> x6, local copies, waits for them, and re-layouts: 1.74 us -> 3.11 us
where the time goes in v16:
time: 155 us
  blocking collectives  87.1 us (56%)
  starting transfers between devices  23.3 us (15%)
  between operations  13.5 us (9%)
  waiting for transfers between devices  13.3 us (9%)
  Pallas kernels  12.5 us (8%)
  local copies, waits for them, and re-layouts  3.96 us (3%)
    all_gather x2, blocking collectives, on_device(): wkv = lax.all_gather(lax.all_gather(wkv, 'zh'), 'zl')  42.2 us
    all_gather x1, blocking collectives, on_device(): kv, wq = lax.optimization_barrier((lax.all_gather(kv, 'zh'), wq))  21.1 us
    all_to_all x1, blocking collectives, on_device(): lax.all_to_all(kv_sum.reshape(8, rows // 4, HEAD), ('xh', 'yl', 'core'),...  12.2 us
    all_to_all x1, blocking collectives, on_device(): return merge(lax.all_to_all(out, ('xh', 'yl'), 0, 0))  11.6 us
    all_to_all x1, starting transfers between devices, on_device(): lax.all_to_all(parts.reshape(32, rows + 16, HEAD), ('xh',) + COL, 0, 0)  9.45 us
    ppermute x1, waiting for transfers between devices, on_device(): q = (q + lax.ppermute(q, 'xh', [(0, 1), (1, 0)])).astype(BF16)  5.1 us
    all_to_all x1, waiting for transfers between devices, gather(): return lax.all_to_all(jnp.broadcast_to(x[None], (n, *x.shape)), axes, 0, 0)  5.04 us
    ppermute x2, starting transfers between devices, swap(): return lax.ppermute(x, 'core', [(0, 1), (1, 0)])  3.83 us
  transfers between devices with their start and end apart: 7, of which 3 were waited for; matrix products, arithmetic and copies ran while one was open for 1% of the time, Pallas kernels for 4%

profile of v16, /device:TPU:16, one launch (start us, length us, event | category | flops | bytes accessed | tf_op | source)
XLA Modules:
  0.0 154.6 jit_solution(1364402935875197686)
XLA Ops:
  6.5 0.0 all-gather.6.cloned.1.call-start
  6.5 3.3 %prep.1 = (bf16[2,8,2,272,128]{4,3,2,1,0:T(8,128)(2,1)}, bf16[320,256]{1,0:T(8,128)(2,1)}) custom-call(bf16[256,512]{1,0:T(8,128)(2,1)} %tokens_ref.1, bf16[512]{0:T(512)(128)(2,1)} %gain_ref.1, bf16[256,256]{1,0:T(8,128)(2,1)} %w_ref.1), custom_call_target="tpu_custom_call" | custom-call | tf_op jit(solution)/shard_map/prep/pallas_call | solution.py:169
  9.9 0.0 all-gather.6.cloned.1.call-update
  9.9 9.4 %all-to-all-start = ((bf16[32,272,128]{2,1,0:T(8,128)(2,1)}), bf16[32,272,128]{2,1,0:T(8,128)(2,1)S(1)}, u32[]{:S(2)}, u32[]{:S(2)}) async-start(bf16[32,272,128]{2,1,0:T(8,128)(2,1)} %bitcast.20), calls=%async_computation | async-start | bytes 4456448 | tf_op jit(solution)/shard_map/spread/all_to_all | solution.py:272
  19.3 0.8 dynamic-slice_select_fusion
  20.1 24.1 %all-gather = bf16[512,128]{1,0:T(8,128)(2,1)S(1)} all-gather(bf16[128,128]{1,0:T(8,128)(2,1)S(1)} %dynamic-slice_select_fusion), channel_id=2, replica_groups=mesh['zh'=4,'zl'=4,'xh'=2,'xl'=2,'yh'=2,'yl'=2,'core'=2] {'zh'}, dimensions={0}, use_global_device_ids=true | all-gather | bytes 163840 | tf_op jit(solution)/shard_map/weights/all_gather | solution.py:269
  44.3 18.0 %all-gather.1 = bf16[16,128,128]{2,1,0:T(8,128)(2,1)S(1)} all-gather(bf16[4,128,128]{2,1,0:T(8,128)(2,1)S(1)} %bitcast.23), channel_id=3, replica_groups=mesh['zh'=4,'zl'=4,'xh'=2,'xl'=2,'yh'=2,'yl'=2,'core'=2] {'zl'}, dimensions={0}, use_global_device_ids=true | all-gather | bytes 655360 | tf_op jit(solution)/shard_map/weights/all_gather | solution.py:269
  62.3 0.0 all-to-all-done
  62.3 1.5 project_kv.1
  63.9 0.0 copy-start.1
  63.9 1.4 copy-done.1
  65.2 12.2 %all_to_all.20 = f32[8,64,128]{2,1,0:T(8,128)S(1)} all-to-all(f32[8,64,128]{2,1,0:T(8,128)S(1)} %bitcast.19), channel_id=1, replica_groups=mesh['zh'=4,'zl'=4,'xh'=2,'xl'=2,'yh'=2,'yl'=2,'core'=2] {'xh','yl','core'}, dimensions={0} | all-to-all | bytes 524288 | tf_op jit(solution)/shard_map/project_kv/all_to_all | solution.py:277
  77.5 1.9 %collective-permute-start = (bf16[2,256,2048]{2,1,0:T(8,128)(2,1)}, bf16[2,256,2048]{2,1,0:T(8,128)(2,1)}, u32[]{:S(2)}, u32[]{:S(2)}) collective-permute-start(bf16[2,256,2048]{2,1,0:T(8,128)(2,1)} %copy-done.1), channel_id=1, source_target_pairs={{0,1},{1,0},{2,3},{3,2},{4,5},{5,4},{6,7},{7,6},{8,9},{9,8},{10,11... | collective-permute-start | bytes 6291464 | tf_op jit(solution)/shard_map/gather_kv/ppermute | solution.py:26
  79.5 21.1 %all-gather.2 = bf16[256,256]{1,0:T(8,128)(2,1)S(1)} all-gather(bf16[64,256]{1,0:T(8,128)(2,1)S(1)} %pad_maximum_fusion), channel_id=4, replica_groups=mesh['zh'=4,'zl'=4,'xh'=2,'xl'=2,'yh'=2,'yl'=2,'core'=2] {'zh'}, dimensions={0}, use_global_device_ids=true | all-gather | bytes 163840 | tf_op jit(solution)/shard_map/gather_kv/all_gather | solution.py:284
  100.6 0.9 broadcast_in_dim.2
  101.4 3.5 %all-to-all-start.2 = ((bf16[4,4,64,256]{3,2,1,0:T(8,128)(2,1)}), bf16[4,4,64,256]{3,2,1,0:T(8,128)(2,1)S(1)}, u32[]{:S(2)}, u32[]{:S(2)}) async-start(bf16[4,4,64,256]{3,2,1,0:T(8,128)(2,1)} %broadcast_in_dim.2), calls=%async_computation.2 | async-start | bytes 1048576 | tf_op jit(solution)/shard_map/gather_kv/all_to_all | solution.py:22
  104.9 0.1 pad_add_fusion.place
  105.0 0.0 collective-permute-done.other_ref
  105.0 1.7 %copy-done = bf16[5120,256]{1,0:T(8,128)(2,1)S(1)} copy-done((bf16[5120,256]{1,0:T(8,128)(2,1)S(1)}, bf16[5120,256]{1,0:T(8,128)(2,1)}, u32[]{:S(2)}) %copy-start) | copy-done | bytes 2621464
  106.7 2.8 %project_q.1 = f32[2,256,256]{2,1,0:T(8,128)S(1)} custom-call(s32[4]{0:T(128)S(1)} %pad_add_fusion.place, bf16[2,256,2048]{2,1,0:T(8,128)(2,1)S(1)} %copy-done.2, bf16[2,256,2048]{2,1,0:T(8,128)(2,1)} %collective-permute-done.other_ref, bf16[16,320,256]{2,1,0:T(8,128)(2,1)S(1)} %bitcast.17), custom_call_target="tpu_custom_call" | custom-call | flops 1073741824 | bytes 6291456 | tf_op jit(solution)/shard_map/project_q/pallas_call | solution.py:241
  109.6 3.2 %collective-permute-start.1 = (f32[2,256,256]{2,1,0:T(8,128)S(1)}, f32[2,256,256]{2,1,0:T(8,128)S(1)}, u32[]{:S(2)}, u32[]{:S(2)}) collective-permute-start(f32[2,256,256]{2,1,0:T(8,128)S(1)} %project_q.1), channel_id=1, source_target_pairs={{0,16},{16,0},{1,17},{17,1},{2,18},{18,2},{3,19},{19,3},{4,20},{20... | collective-permute-start | bytes 1572872 | tf_op jit(solution)/shard_map/project_q/ppermute | solution.py:289
  112.8 5.0 %all-to-all-done.2.mine_ref = bf16[4,4,64,256]{3,2,1,0:T(8,128)(2,1)S(1)} async-done(((bf16[4,4,64,256]{3,2,1,0:T(8,128)(2,1)}), bf16[4,4,64,256]{3,2,1,0:T(8,128)(2,1)S(1)}, u32[]{:S(2)}, u32[]{:S(2)}) %all-to-all-start.2) | async-done | bytes 524320 | tf_op jit(solution)/shard_map/gather_kv/all_to_all | solution.py:22
  117.8 1.9 %collective-permute-start.3 = (bf16[4,4,64,256]{3,2,1,0:T(8,128)(2,1)S(1)}, bf16[4,4,64,256]{3,2,1,0:T(8,128)(2,1)S(1)}, u32[]{:S(2)}, u32[]{:S(2)}) collective-permute-start(bf16[4,4,64,256]{3,2,1,0:T(8,128)(2,1)S(1)} %all-to-all-done.2.mine_ref), channel_id=1, source_target_pairs={{0,1},{1,0},{2,3},{3,2},{4,5},{5,4},{6,7},{7,6},{8,9},{9,8},{10,11... | collective-permute-start | bytes 1572872 | tf_op jit(solution)/shard_map/attend/ppermute | solution.py:26
  119.8 5.1 %collective-permute-done.1 = f32[2,256,256]{2,1,0:T(8,128)S(1)} collective-permute-done((f32[2,256,256]{2,1,0:T(8,128)S(1)}, f32[2,256,256]{2,1,0:T(8,128)S(1)}, u32[]{:S(2)}, u32[]{:S(2)}) %collective-permute-start.1) | collective-permute-done | bytes 524320 | tf_op jit(solution)/shard_map/project_q/ppermute | solution.py:289
  124.9 0.1 add_convert_fusion.q_ref
  124.9 3.3 %collective-permute-start.2 = (bf16[2,256,256]{2,1,0:T(8,128)(2,1)S(1)}, bf16[2,256,256]{2,1,0:T(8,128)(2,1)S(1)}, u32[]{:S(2)}, u32[]{:S(2)}) collective-permute-start(bf16[2,256,256]{2,1,0:T(8,128)(2,1)S(1)} %add_convert_fusion.q_ref), channel_id=1, source_target_pairs={{0,2},{2,0},{1,3},{3,1},{4,6},{6,4},{5,7},{7,5},{8,10},{10,8},{9,1... | collective-permute-start | bytes 786440 | tf_op jit(solution)/shard_map/project_q/ppermute | solution.py:290
  128.2 0.0 collective-permute-done.3.other_ref
  128.2 1.8 %attend.3.refs_0_ = bf16[4,272,256]{2,1,0:T(8,128)(2,1)S(1)} custom-call(s32[4]{0:T(128)S(1)} %pad_add_fusion.place, bf16[2,256,256]{2,1,0:T(8,128)(2,1)S(1)} %add_convert_fusion.q_ref, bf16[4,4,64,256]{3,2,1,0:T(8,128)(2,1)S(1)} %all-to-all-done.2.mine_ref, bf16[4,4,64,256]{3,2,1,0:T(8,128)(2,1)S(1)} %collective-permute-done.3.other_ref), custom_call_target="tpu_custom_call" | custom-call | flops 1073741824 | bytes 4194304 | tf_op jit(solution)/shard_map/attend/pallas_call | solution.py:105
  130.1 3.1 %collective-permute-done.2.q_ref = bf16[2,256,256]{2,1,0:T(8,128)(2,1)S(1)} collective-permute-done((bf16[2,256,256]{2,1,0:T(8,128)(2,1)S(1)}, bf16[2,256,256]{2,1,0:T(8,128)(2,1)S(1)}, u32[]{:S(2)}, u32[]{:S(2)}) %collective-permute-start.2) | collective-permute-done | bytes 262176 | tf_op jit(solution)/shard_map/project_q/ppermute | solution.py:290
  133.2 1.8 %attend.4 = bf16[4,272,256]{2,1,0:T(8,128)(2,1)S(1)} custom-call(s32[4]{0:T(128)S(1)} %pad_add_fusion.place, bf16[2,256,256]{2,1,0:T(8,128)(2,1)S(1)} %collective-permute-done.2.q_ref, bf16[4,4,64,256]{3,2,1,0:T(8,128)(2,1)S(1)} %all-to-all-done.2.mine_ref, ...), custom_call_target="tpu_custom_call", output_to_operand_aliasing={{}: (4, {})} | custom-call | flops 1073741824 | bytes 4194304 | tf_op jit(solution)/shard_map/attend/pallas_call | solution.py:105
  135.0 11.6 %all_to_all.21.parts_ref = bf16[4,272,256]{2,1,0:T(8,128)(2,1)S(1)} all-to-all(bf16[4,272,256]{2,1,0:T(8,128)(2,1)S(1)} %attend.4), channel_id=1, replica_groups=mesh['zh'=4,'zl'=4,'xh'=2,'xl'=2,'yh'=2,'yl'=2,'core'=2] {'xh','yl'}, dimensions={0} | all-to-all | bytes 1114112 | tf_op jit(solution)/shard_map/attend/all_to_all | solution.py:296
  146.6 1.2 attend.5
  (7 shorter events, 0.0 us)
Async XLA Ops:
  6.5 94.0 %all-gather.6.cloned.1.call-start = ((), (), s32[]{:S(2)}) async-start(), calls=%async_computation.4 | async-start | bytes 2785280 | tf_op jit(solution)/shard_map/weights/all_gather | solution.py:262
  9.9 52.4 %all-to-all-start = ((bf16[32,272,128]{2,1,0:T(8,128)(2,1)}), bf16[32,272,128]{2,1,0:T(8,128)(2,1)S(1)}, u32[]{:S(2)}, u32[]{:S(2)}) async-start(bf16[32,272,128]{2,1,0:T(8,128)(2,1)} %bitcast.20), calls=%async_computation | async-start | bytes 4456448 | tf_op jit(solution)/shard_map/spread/all_to_all | solution.py:272
  63.9 1.4 copy-start.1
  65.2 39.7 %copy-start.2 = (bf16[2,256,2048]{2,1,0:T(8,128)(2,1)S(1)}, bf16[2,256,2048]{2,1,0:T(8,128)(2,1)}, u32[]{:S(2)}) copy-start(bf16[2,256,2048]{2,1,0:T(8,128)(2,1)} %copy-done.1) | copy-start | bytes 6291460
  77.5 27.4 %collective-permute-start = (bf16[2,256,2048]{2,1,0:T(8,128)(2,1)}, bf16[2,256,2048]{2,1,0:T(8,128)(2,1)}, u32[]{:S(2)}, u32[]{:S(2)}) collective-permute-start(bf16[2,256,2048]{2,1,0:T(8,128)(2,1)} %copy-done.1), channel_id=1, source_target_pairs={{0,1},{1,0},{2,3},{3,2},{4,5},{5,4},{6,7},{7,6},{8,9},{9,8},{10,11... | collective-permute-start | bytes 6291464 | tf_op jit(solution)/shard_map/gather_kv/ppermute | solution.py:26
  101.4 16.4 %all-to-all-start.2 = ((bf16[4,4,64,256]{3,2,1,0:T(8,128)(2,1)}), bf16[4,4,64,256]{3,2,1,0:T(8,128)(2,1)S(1)}, u32[]{:S(2)}, u32[]{:S(2)}) async-start(bf16[4,4,64,256]{3,2,1,0:T(8,128)(2,1)} %broadcast_in_dim.2), calls=%async_computation.2 | async-start | bytes 1048576 | tf_op jit(solution)/shard_map/gather_kv/all_to_all | solution.py:22
  105.0 1.7 %copy-start = (bf16[5120,256]{1,0:T(8,128)(2,1)S(1)}, bf16[5120,256]{1,0:T(8,128)(2,1)}, u32[]{:S(2)}) copy-start(bf16[5120,256]{1,0:T(8,128)(2,1)} %all-gather.6.cloned.1.call-done) | copy-start | bytes 7864324
  109.6 15.3 %collective-permute-start.1 = (f32[2,256,256]{2,1,0:T(8,128)S(1)}, f32[2,256,256]{2,1,0:T(8,128)S(1)}, u32[]{:S(2)}, u32[]{:S(2)}) collective-permute-start(f32[2,256,256]{2,1,0:T(8,128)S(1)} %project_q.1), channel_id=1, source_target_pairs={{0,16},{16,0},{1,17},{17,1},{2,18},{18,2},{3,19},{19,3},{4,20},{20... | collective-permute-start | bytes 1572872 | tf_op jit(solution)/shard_map/project_q/ppermute | solution.py:289
  117.8 10.4 %collective-permute-start.3 = (bf16[4,4,64,256]{3,2,1,0:T(8,128)(2,1)S(1)}, bf16[4,4,64,256]{3,2,1,0:T(8,128)(2,1)S(1)}, u32[]{:S(2)}, u32[]{:S(2)}) collective-permute-start(bf16[4,4,64,256]{3,2,1,0:T(8,128)(2,1)S(1)} %all-to-all-done.2.mine_ref), channel_id=1, source_target_pairs={{0,1},{1,0},{2,3},{3,2},{4,5},{5,4},{6,7},{7,6},{8,9},{9,8},{10,11... | collective-permute-start | bytes 1572872 | tf_op jit(solution)/shard_map/attend/ppermute | solution.py:26
  124.9 8.3 %collective-permute-start.2 = (bf16[2,256,256]{2,1,0:T(8,128)(2,1)S(1)}, bf16[2,256,256]{2,1,0:T(8,128)(2,1)S(1)}, u32[]{:S(2)}, u32[]{:S(2)}) collective-permute-start(bf16[2,256,256]{2,1,0:T(8,128)(2,1)S(1)} %add_convert_fusion.q_ref), channel_id=1, source_target_pairs={{0,2},{2,0},{1,3},{3,1},{4,6},{6,4},{5,7},{7,5},{8,10},{10,8},{9,1... | collective-permute-start | bytes 786440 | tf_op jit(solution)/shard_map/project_q/ppermute | solution.py:290
Sparse Core Ops, SparseCore 0:
  10.0 82.7 all-gather.5
